TPU v7x, 32 devices: a whole 2x2x4 slice. The times are simulated.
32 devices in a mesh: row: 2 (over x), col: 4 (over y, core), depth: 4 (over z).
Axes of the slice: x: 2, y: 2, z: 4, core: 2. Of those that a mesh axis runs over, the one named last changes fastest.
Arguments:
- tokens: bfloat16 [768, 8192], P(('depth', 'col'), 'row'), may hold values from -6 to 6
- gate_weight: bfloat16 [8192, 14336], P('row', ('col', 'depth')), may hold values from -0.0625 to 0.0625
- up_weight: bfloat16 [8192, 14336], P('row', ('col', 'depth')), may hold values from -0.0625 to 0.0625
- down_weight: bfloat16 [14336, 8192], P(('col', 'depth'), 'row'), may hold values from -0.046875 to 0.046875
- cotangent: bfloat16 [768, 8192], P(('depth', 'col'), 'row'), may hold values from -0.86328125 to 0.86328125
Outputs:
- mixed: float32 [768, 8192], P(('depth', 'col'), 'row')
- token_grad: float32 [768, 8192], P(('depth', 'col'), 'row')
- gate_weight_grad: float32 [8192, 14336], P('row', ('col', 'depth'))
- up_weight_grad: float32 [8192, 14336], P('row', ('col', 'depth'))
- down_weight_grad: float32 [14336, 8192], P(('col', 'depth'), 'row')
All inputs are finite; a program needn't handle non-finite values.
Results may differ from a plain program's by a relative error of at most 0.012.
Values may be sent and summed in bfloat16 or wider, within the bound.
No kernel may reach another device: no remote copies, remote signals or barrier semaphores. Data moves between devices by JAX's collectives and lax.ppermute only.
A program may use at most 384 MiB of HBM per device.

v0:
```python
import jax
import jax.numpy as jnp
from jax import lax
from jax.sharding import PartitionSpec as P


def swish_parts(gate):
    sigma_gate = jax.nn.sigmoid(gate)
    return (gate * sigma_gate, sigma_gate)


def product(left_side, right_side):
    return jnp.dot(left_side, right_side, preferred_element_type=jnp.float32)


def product_transposed(left_side, right_side):
    return lax.dot_general(
        left_side, right_side, (((1,), (1,)), ((), ())), preferred_element_type=jnp.float32
    )


def rounded_partial(left_side, right_side):
    partial_term = lax.dot_general(
        left_side, right_side, (((0,), (0,)), ((), ())), preferred_element_type=jnp.float32
    ).astype(jnp.bfloat16)
    return lax.optimization_barrier(partial_term).astype(jnp.float32)


def body(tokens, gate_weight, up_weight, down_weight, cotangent):
    gate_panel, up_panel, down_panel = (
        lax.all_gather(gate_weight, "depth", axis=1, tiled=True),
        lax.all_gather(up_weight, "depth", axis=1, tiled=True),
        lax.all_gather(down_weight, "depth", axis=0, tiled=True),
    )
    token_all, cotangent_all = (
        lax.all_gather(tokens, "col", axis=0, tiled=True),
        lax.all_gather(cotangent, "col", axis=0, tiled=True),
    )
    panel_width = gate_panel.shape[1]
    segment = token_all
    paired = lax.psum_scatter(
        jnp.concatenate([product(segment, gate_panel), product(segment, up_panel)], axis=1),
        "row",
        scatter_dimension=0,
        tiled=True,
    )
    gate_mine = paired[:, :panel_width]
    up_mine = paired[:, panel_width:]
    activated_mine, sigma_mine = swish_parts(gate_mine)
    hidden_mine = (activated_mine * up_mine).astype(jnp.bfloat16)
    hidden_all = lax.all_gather(hidden_mine, "row", axis=0, tiled=True)
    segment = hidden_all
    mixed = lax.psum_scatter(product(segment, down_panel), "col", scatter_dimension=0, tiled=True)
    segment = cotangent_all
    hidden_grad = lax.psum_scatter(
        product_transposed(segment, down_panel), "row", scatter_dimension=0, tiled=True
    )
    activated, sigma_gate = swish_parts(gate_mine)
    gate_grad = (
        hidden_grad * up_mine * sigma_gate * (1.0 + gate_mine * (1.0 - sigma_gate))
    ).astype(jnp.bfloat16)
    up_grad = (hidden_grad * activated).astype(jnp.bfloat16)
    gate_grad_all, up_grad_all = (
        lax.all_gather(gate_grad, "row", axis=0, tiled=True),
        lax.all_gather(up_grad, "row", axis=0, tiled=True),
    )
    token_grad = lax.psum_scatter(
        product_transposed(gate_grad_all, gate_panel) + product_transposed(up_grad_all, up_panel),
        "col",
        scatter_dimension=0,
        tiled=True,
    )
    gate_total, up_total, down_total = (
        lax.psum_scatter(
            rounded_partial(token_all, gate_grad_all).astype(jnp.bfloat16),
            "depth",
            scatter_dimension=1,
            tiled=True,
        ).astype(jnp.float32),
        lax.psum_scatter(
            rounded_partial(token_all, up_grad_all).astype(jnp.bfloat16),
            "depth",
            scatter_dimension=1,
            tiled=True,
        ).astype(jnp.float32),
        lax.psum_scatter(
            rounded_partial(hidden_all, cotangent_all).astype(jnp.bfloat16),
            "depth",
            scatter_dimension=0,
            tiled=True,
        ).astype(jnp.float32),
    )
    return (mixed, token_grad, gate_total, up_total, down_total)


def solution(mesh):
    placed = (
        P(("depth", "col"), "row"),
        P("row", ("col", "depth")),
        P("row", ("col", "depth")),
        P(("col", "depth"), "row"),
        P(("depth", "col"), "row"),
    )
    return jax.shard_map(
        body,
        mesh=mesh,
        in_specs=placed,
        out_specs=(
            P(("depth", "col"), "row"),
            P(("depth", "col"), "row"),
            P("row", ("col", "depth")),
            P("row", ("col", "depth")),
            P(("col", "depth"), "row"),
        ),
        check_vma=False,
    )
```

profile of v0, /device:TPU:0, one launch (start us, length us, event | category | flops | bytes accessed | tf_op | source)
XLA Modules:
  0.0 3275.5 jit_solution(1531984546047915065)
XLA Ops:
  7.2 0.7 all-gather.19.cloned.1.call-update
  7.9 0.0 all-gather.17.cloned.1.call-start
  7.9 0.7 all-gather.17.cloned.1.call-update
  8.7 0.7 all-gather.9.cloned.1.call-update
  9.4 0.5 all-gather.11.cloned.1.call-update
  10.0 0.5 all-gather.13.cloned.1.call-update
  10.5 0.0 reduce-scatter.12.cloned.1.call-start
  10.6 21.4 all-gather.19.cloned.1.call-done
  32.0 494.7 %all-gather.17.cloned.1.call-done = bf16[3584,4096]{1,0:T(8,128)(2,1)} async-done(((bf16[896,4096]{1,0:T(8,128)(2,1)}), bf16[3584,4096]{1,0:T(8,128)(2,1)}) %all-gather.17.cloned.1.call-update) | async-done | bytes 29360144 | tf_op jit(solution)/shard_map/all_gather | solution.py:33
  526.7 16.2 fusion.6
  542.9 0.0 reduce-scatter.8.cloned.1.call-start
  543.0 3.2 all-gather.9.cloned.1.call-done
  546.1 494.6 %all-gather.11.cloned.1.call-done = bf16[4096,3584]{1,0:T(8,128)(2,1)} async-done(((bf16[4096,896]{1,0:T(8,128)(2,1)}), bf16[4096,3584]{1,0:T(8,128)(2,1)}) %all-gather.11.cloned.1.call-update) | async-done | bytes 29360144 | tf_op jit(solution)/shard_map/all_gather | solution.py:31
  1040.8 17.6 fusion.3
  1058.3 475.2 %all-gather.13.cloned.1.call-done = bf16[4096,3584]{1,0:T(8,128)(2,1)} async-done(((bf16[4096,896]{1,0:T(8,128)(2,1)}), bf16[4096,3584]{1,0:T(8,128)(2,1)}) %all-gather.13.cloned.1.call-update) | async-done | bytes 29360144 | tf_op jit(solution)/shard_map/all_gather | solution.py:32
  1533.6 13.4 fusion.4
  1547.0 2.8 pad_maximum_fusion
  1549.9 0.0 all-gather.21.cloned.1.call-start
  1549.9 23.6 reduce-scatter.12.cloned.1.call-done
  1573.5 71.5 %reduce-scatter.8.cloned.1.call-done = f32[96,7168]{1,0:T(8,128)} async-done(((f32[192,7168]{1,0:T(8,128)}), f32[96,7168]{1,0:T(8,128)}) %reduce-scatter.8.cloned.1.call-update) | async-done | bytes 2752528 | tf_op jit(solution)/shard_map/reduce_scatter | solution.py:41
  1645.0 4.2 multiply_convert_fusion
  1649.2 0.0 all-gather.23.cloned.1.call-start
  1649.3 0.7 all-gather.23.cloned.1.call-update
  1650.0 0.5 all-gather.15.cloned.1.call-update
  1650.6 0.2 reduce-scatter.16.cloned.1.call-start
  1650.8 23.6 all-gather.21.cloned.1.call-done
  1674.4 15.4 fusion
  1689.8 0.0 reduce-scatter.18.cloned.1.call-start
  1689.8 11.7 all-gather.23.cloned.1.call-done
  1701.5 15.3 fusion.1
  1716.9 0.0 reduce-scatter.20.cloned.1.call-start
  1717.0 11.6 all-gather.15.cloned.1.call-done
  1728.5 16.0 convolution_convert_fusion
  1744.6 0.3 reduce-scatter.14.cloned.1.call-start
  1744.9 1.0 copy-done.2
  1745.9 14.4 fusion.7
  1760.3 16.8 convolution_add_fusion
  1777.1 0.0 reduce-scatter.10.cloned.1.call-start
  1777.1 1.3 copy-done.3
  1778.4 14.4 fusion.5
  1792.8 419.8 %reduce-scatter.16.cloned.1.call-done = bf16[4096,896]{0,1:T(8,128)(2,1)} async-done(((bf16[4096,3584]{0,1:T(8,128)(2,1)}), bf16[4096,896]{0,1:T(8,128)(2,1)}) %reduce-scatter.16.cloned.1.call-update) | async-done | bytes 7340048 | tf_op jit(solution)/shard_map/reduce_scatter | solution.py:74
  2212.6 11.7 copy.10
  2224.3 474.5 %reduce-scatter.18.cloned.1.call-done = bf16[4096,896]{0,1:T(8,128)(2,1)} async-done(((bf16[4096,3584]{0,1:T(8,128)(2,1)}), bf16[4096,896]{0,1:T(8,128)(2,1)}) %reduce-scatter.18.cloned.1.call-update) | async-done | bytes 7340048 | tf_op jit(solution)/shard_map/reduce_scatter | solution.py:80
  2698.7 11.6 copy.11
  2710.4 474.5 %reduce-scatter.20.cloned.1.call-done = bf16[896,4096]{1,0:T(8,128)(2,1)} async-done(((bf16[3584,4096]{1,0:T(8,128)(2,1)}), bf16[896,4096]{1,0:T(8,128)(2,1)}) %reduce-scatter.20.cloned.1.call-update) | async-done | bytes 7340048 | tf_op jit(solution)/shard_map/reduce_scatter | solution.py:86
  3184.8 10.5 convert_element_type.49
  3195.4 32.7 reduce-scatter.14.cloned.1.call-done
  3228.0 40.9 %reduce-scatter.10.cloned.1.call-done = f32[48,4096]{1,0:T(8,128)} async-done(((f32[192,4096]{1,0:T(8,128)}), f32[48,4096]{1,0:T(8,128)}) %reduce-scatter.10.cloned.1.call-update) | async-done | bytes 786448 | tf_op jit(solution)/shard_map/reduce_scatter | solution.py:53
  (23 shorter events, 0.3 us)
Async XLA Ops:
  7.2 24.8 all-gather.19.cloned.1.call-start
  7.9 518.8 %all-gather.17.cloned.1.call-start = ((), (), s32[]{:S(2)}) async-start(), calls=%async_computation.12 | async-start | bytes 36700160 | tf_op jit(solution)/shard_map/all_gather | solution.py:33
  8.6 537.5 %all-gather.9.cloned.1.call-start = ((), (), s32[]{:S(2)}) async-start(), calls=%async_computation.7 | async-start | bytes 1966080 | tf_op jit(solution)/shard_map/all_gather | solution.py:36
  9.4 1031.4 %all-gather.11.cloned.1.call-start = ((), (), s32[]{:S(2)}) async-start(), calls=%async_computation.8 | async-start | bytes 36700160 | tf_op jit(solution)/shard_map/all_gather | solution.py:31
  10.0 1523.6 %all-gather.13.cloned.1.call-start = ((), (), s32[]{:S(2)}) async-start(), calls=%async_computation.9 | async-start | bytes 36700160 | tf_op jit(solution)/shard_map/all_gather | solution.py:32
  10.5 1563.0 %reduce-scatter.12.cloned.1.call-start = ((), (), s32[]{:S(2)}) async-start(), calls=%async_computation.15 | async-start | bytes 4128768 | tf_op jit(solution)/shard_map/reduce_scatter | solution.py:55
  542.9 1102.1 %reduce-scatter.8.cloned.1.call-start = ((), (), s32[]{:S(2)}) async-start(), calls=%async_computation.10 | async-start | bytes 8257536 | tf_op jit(solution)/shard_map/reduce_scatter | solution.py:41
  546.1 987.4 %copy-start = (bf16[192,4096]{1,0:T(8,128)(2,1)S(1)}, bf16[192,4096]{1,0:T(8,128)(2,1)}, u32[]{:S(2)}) copy-start(bf16[192,4096]{1,0:T(8,128)(2,1)} %all-gather.9.cloned.1.call-done) | copy-start | bytes 4718596
  1533.6 13.5 copy-start.1
  1549.9 124.5 %all-gather.21.cloned.1.call-start = ((), (), s32[]{:S(2)}) async-start(), calls=%async_computation.16 | async-start | bytes 2064384 | tf_op jit(solution)/shard_map/all_gather | solution.py:64
  1649.2 52.3 %all-gather.23.cloned.1.call-start = ((), (), s32[]{:S(2)}) async-start(), calls=%async_computation.17 | async-start | bytes 2064384 | tf_op jit(solution)/shard_map/all_gather | solution.py:65
  1650.0 78.6 %all-gather.15.cloned.1.call-start = ((), (), s32[]{:S(2)}) async-start(), calls=%async_computation.11 | async-start | bytes 2064384 | tf_op jit(solution)/shard_map/all_gather | solution.py:51
  1650.6 562.0 %reduce-scatter.16.cloned.1.call-start = ((), (), s32[]{:S(2)}) async-start(), calls=%async_computation.19 | async-start | bytes 36700160 | tf_op jit(solution)/shard_map/reduce_scatter | solution.py:74
  1689.8 1008.9 %reduce-scatter.18.cloned.1.call-start = ((), (), s32[]{:S(2)}) async-start(), calls=%async_computation.20 | async-start | bytes 36700160 | tf_op jit(solution)/shard_map/reduce_scatter | solution.py:80
  1716.9 11.6 copy-start.5
  1716.9 1467.9 %reduce-scatter.20.cloned.1.call-start = ((), (), s32[]{:S(2)}) async-start(), calls=%async_computation.21 | async-start | bytes 36700160 | tf_op jit(solution)/shard_map/reduce_scatter | solution.py:86
  1744.6 1.3 copy-start.2
  1744.6 15.7 copy-start.4
  1744.6 1483.4 %reduce-scatter.14.cloned.1.call-start = ((), (), s32[]{:S(2)}) async-start(), calls=%async_computation.18 | async-start | bytes 3932160 | tf_op jit(solution)/shard_map/reduce_scatter | solution.py:67
  1777.0 1.3 copy-start.3
  1777.1 1491.9 %reduce-scatter.10.cloned.1.call-start = ((), (), s32[]{:S(2)}) async-start(), calls=%async_computation.13 | async-start | bytes 3932160 | tf_op jit(solution)/shard_map/reduce_scatter | solution.py:53
Sparse Core Ops, SparseCore 0:
  9.6 22.3 all-gather.18
  33.5 493.1 all-gather.16
  528.3 17.8 all-gather.8
  547.6 493.1 all-gather.10
  1042.2 491.2 all-gather.12
  1536.2 37.2 reduce-scatter.11
  1576.5 68.5 reduce-scatter.7
  1649.4 24.9 all-gather.20
  1676.5 24.9 all-gather.22
  1703.5 24.9 all-gather.14
  1730.9 481.6 reduce-scatter.15
  2214.9 483.7 reduce-scatter.17
  2701.1 483.6 reduce-scatter.19
  3187.9 40.0 reduce-scatter.13
  3231.0 37.9 reduce-scatter.9
where the time goes:
time: 3280 us
  waiting for transfers between devices  3080 us (94%)
  matrix products  139 us (4%)
    all_gather x1, waiting for transfers between devices, body(): lax.all_gather(down_weight, 'depth', axis=0, tiled=True)  495 us
    all_gather x1, waiting for transfers between devices, body(): lax.all_gather(gate_weight, 'depth', axis=1, tiled=True)  495 us
    all_gather x1, waiting for transfers between devices, body(): lax.all_gather(up_weight, 'depth', axis=1, tiled=True)  475 us
    reduce_scatter x1, waiting for transfers between devices, body(): lax.psum_scatter(rounded_partial(hidden_all, cotangent_all).astype(jnp.bf...  474 us
    reduce_scatter x1, waiting for transfers between devices, body(): lax.psum_scatter(rounded_partial(token_all, up_grad_all).astype(jnp.bfloa...  474 us
    reduce_scatter x1, waiting for transfers between devices, body(): lax.psum_scatter(rounded_partial(token_all, gate_grad_all).astype(jnp.bfl...  420 us
    reduce_scatter x1, waiting for transfers between devices, body(): lax.psum_scatter(jnp.concatenate([product(segment, gate_panel), product(s...  71.5 us
  transfers between devices with their start and end apart: 15, of which 15 were waited for; matrix products, arithmetic and copies ran while one was open for 5% of the time, Pallas kernels for 0%

commit v1 on v0

v1 whole, which is shorter than its diff:
```python
import jax
import jax.numpy as jnp
from jax import lax
from jax.sharding import PartitionSpec as P

TOKEN_AXES = ("depth", "col")


def dot(left, right, left_dim, right_dim):
    return lax.dot_general(
        left, right, (((left_dim,), (right_dim,)), ((), ())), preferred_element_type=jnp.float32
    )


def row_sum(partial):
    n = lax.axis_size("row")
    sent = partial.astype(jnp.bfloat16)
    total = partial
    for step in range(1, n):
        moved = lax.ppermute(sent, "row", [(i, (i + step) % n) for i in range(n)])
        total = total + moved.astype(jnp.float32)
    return total


def token_scatter(partial):
    return lax.psum_scatter(
        partial.astype(jnp.bfloat16), TOKEN_AXES, scatter_dimension=0, tiled=True
    ).astype(jnp.float32)


def body(tokens, gate_weight, up_weight, down_weight, cotangent):
    token_all = lax.all_gather(tokens, TOKEN_AXES, axis=0, tiled=True)
    cotangent_all = lax.all_gather(cotangent, TOKEN_AXES, axis=0, tiled=True)
    gate = row_sum(dot(token_all, gate_weight, 1, 0))
    up = row_sum(dot(token_all, up_weight, 1, 0))
    hidden_grad = row_sum(dot(cotangent_all, down_weight, 1, 1))
    sigma = jax.nn.sigmoid(gate)
    activated = gate * sigma
    hidden = (activated * up).astype(jnp.bfloat16)
    mixed = token_scatter(dot(hidden, down_weight, 1, 0))
    gate_grad = (hidden_grad * up * sigma * (1.0 + gate * (1.0 - sigma))).astype(jnp.bfloat16)
    up_grad = (hidden_grad * activated).astype(jnp.bfloat16)
    token_grad = token_scatter(
        dot(gate_grad, gate_weight, 1, 1) + dot(up_grad, up_weight, 1, 1)
    )
    gate_total = dot(token_all, gate_grad, 0, 0)
    up_total = dot(token_all, up_grad, 0, 0)
    down_total = dot(hidden, cotangent_all, 0, 0)
    return (mixed, token_grad, gate_total, up_total, down_total)


def solution(mesh):
    activations = P(("depth", "col"), "row")
    wide = P("row", ("col", "depth"))
    tall = P(("col", "depth"), "row")
    return jax.shard_map(
        body,
        mesh=mesh,
        in_specs=(activations, wide, wide, tall, activations),
        out_specs=(activations, activations, wide, wide, tall),
        check_vma=False,
    )
```

time: 3280 us -> 392 us (0.12)
  waiting for transfers between devices: 3080 us -> 229 us
  matrix products: 139 us -> 104 us
    reduce_scatter x7 -> x2, waiting for transfers between devices: 1540 us -> 92.5 us  [token_scatter(): lax.psum_scatter(partial.astype(jnp.bfloat16), TOKEN_AXES, scatter_dimens...]
    all_gather x8 -> x2, waiting for transfers between devices: 1540 us -> 104 us  [the longest x1 66.2 us: body(): token_all = lax.all_gather(tokens, TOKEN_AXES, axis=0, tiled=True)]
    dot_general x9, matrix products: 139 us -> 104 us  [dot(): lax.dot_general(left, right, (((left_dim,), (right_dim,)), ((), ())), pre...]
  transfers between devices with their start and end apart: 15 -> 7, of which waited for: 15 -> 5; matrix products, arithmetic and copies ran while one was open for 5% -> 29% of each run, Pallas kernels for 0% -> 0%
where the time goes in v1:
time: 392 us; the launch traced here: 391 us
  waiting for transfers between devices  229 us (58%)
  matrix products  104 us (27%)
  local copies, waits for them, and re-layouts  32.4 us (8%)
  between operations  13.8 us (4%)
  other arithmetic  8.32 us (2%)
    dot_general x9, matrix products, dot(): lax.dot_general(left, right, (((left_dim,), (right_dim,)), ((), ())), pre...  104 us
    reduce_scatter x2, waiting for transfers between devices, token_scatter(): lax.psum_scatter(partial.astype(jnp.bfloat16), TOKEN_AXES, scatter_dimens...  92.5 us
    all_gather x1, waiting for transfers between devices, body(): token_all = lax.all_gather(tokens, TOKEN_AXES, axis=0, tiled=True)  66.2 us
    all_gather x1, waiting for transfers between devices, body(): cotangent_all = lax.all_gather(cotangent, TOKEN_AXES, axis=0, tiled=True)  38.1 us
    unnamed x14, local copies, waits for them, and re-layouts  32.4 us
    ppermute x3, waiting for transfers between devices, row_sum(): moved = lax.ppermute(sent, 'row', [(i, (i + step) % n) for i in range(n)])  30.9 us
  transfers between devices with their start and end apart: 7, of which 5 were waited for; matrix products, arithmetic and copies ran while one was open for 29% of the time, Pallas kernels for 0%

profile of v1, /device:TPU:0, one launch (start us, length us, event | category | flops | bytes accessed | tf_op | source)
XLA Modules:
  0.0 390.7 jit_solution(6260893742973775077)
XLA Ops:
  7.2 0.0 all-gather.3.cloned.1.call-start
  7.2 0.7 all-gather.3.cloned.1.call-update
  7.9 0.0 all-gather.5.cloned.1.call-start
  7.9 0.7 all-gather.5.cloned.1.call-update
  8.6 0.0 reduce-scatter.5.cloned.1.call-start
  8.7 66.2 %all-gather.3.cloned.1.call-done = bf16[768,4096]{1,0:T(8,128)(2,1)} async-done(((bf16[48,4096]{1,0:T(8,128)(2,1)}), bf16[768,4096]{1,0:T(8,128)(2,1)}) %all-gather.3.cloned.1.call-update) | async-done | bytes 6291472 | tf_op jit(solution)/shard_map/all_gather | solution.py:32
  74.9 0.0 copy-start
  74.9 12.3 %fusion.2 = (bf16[768,896]{1,0:T(8,128)(2,1)}, f32[768,896]{1,0:T(8,128)}) fusion(bf16[768,4096]{1,0:T(8,128)(2,1)} %all-gather.3.cloned.1.call-done, bf16[4096,896]{1,0:T(8,128)(2,1)} %param.6), kind=kOutput, calls=%fused_computation.13 | convolution fusion | flops 5637832704 | bytes 17760256 | tf_op jit(solution)/shard_map/dot_general | solution.py:10
  87.2 1.5 collective-permute-start
  88.6 0.0 copy-done
  88.6 10.4 %fusion.3 = (bf16[768,896]{1,0:T(8,128)(2,1)}, f32[768,896]{1,0:T(8,128)}) fusion(bf16[768,4096]{1,0:T(8,128)(2,1)S(1)} %copy-done, bf16[4096,896]{1,0:T(8,128)(2,1)} %param.7), kind=kOutput, calls=%fused_computation.14 | convolution fusion | flops 5637832704 | bytes 17760256 | tf_op jit(solution)/shard_map/dot_general | solution.py:10
  99.0 0.6 collective-permute-start.1
  99.6 38.1 %all-gather.5.cloned.1.call-done = bf16[768,4096]{1,0:T(8,128)(2,1)} async-done(((bf16[48,4096]{1,0:T(8,128)(2,1)}), bf16[768,4096]{1,0:T(8,128)(2,1)}) %all-gather.5.cloned.1.call-update) | async-done | bytes 6291472 | tf_op jit(solution)/shard_map/all_gather | solution.py:33
  137.6 11.0 %fusion.1 = (bf16[768,896]{1,0:T(8,128)(2,1)S(1)}, f32[768,896]{1,0:T(8,128)S(1)}) fusion(bf16[768,4096]{1,0:T(8,128)(2,1)} %all-gather.5.cloned.1.call-done, bf16[896,4096]{1,0:T(8,128)(2,1)} %param.8), kind=kOutput, calls=%fused_computation.12 | convolution fusion | flops 5637832704 | bytes 17760256 | tf_op jit(solution)/shard_map/dot_general | solution.py:10
  148.6 1.5 collective-permute-start.2
  150.1 0.0 collective-permute-done
  150.1 0.0 copy-start.2
  150.1 0.0 collective-permute-done.1
  150.1 0.0 copy-start.3
  150.1 30.9 %collective-permute-done.2 = bf16[768,896]{1,0:T(8,128)(2,1)S(1)} collective-permute-done((bf16[768,896]{1,0:T(8,128)(2,1)S(1)}, bf16[768,896]{1,0:T(8,128)(2,1)S(1)}, u32[]{:S(2)}, u32[]{:S(2)}) %collective-permute-start.2) | collective-permute-done | bytes 1376288 | tf_op jit(solution)/shard_map/ppermute | solution.py:20
  181.0 0.0 copy-done.2
  181.0 0.0 copy-done.3
  181.0 0.0 slice-start
  181.0 4.5 %multiply_convert_fusion = (bf16[768,896]{1,0:T(8,128)(2,1)S(1)}, bf16[768,896]{1,0:T(8,128)(2,1)S(1)}, bf16[768,896]{1,0:T(8,128)(2,1)S(1)}) fusion(f32[768,896]{1,0:T(8,128)S(1)} %get-tuple-element.14, bf16[768,896]{1,0:T(8,128)(2,1)S(1)} %collective-permute-done.2, f32[768,896]{1,0:T(8,128)} %get-tuple-element.16, bf16[768,896]{1,0:T(8,128)(2,1)} %copy-done.2, ...), kind=kLoop, calls=%fused_computation.4 | loop fusion | flops 14450688 | bytes 16515072 | tf_op jit(solution)/shard_map/convert_element_type | solution.py:42
  185.5 0.0 copy-start.1
  185.5 0.0 slice-start.1
  185.5 12.7 %fusion.4 = f32[768,4096]{1,0:T(8,128)} fusion(bf16[768,896]{1,0:T(8,128)(2,1)S(1)} %get-tuple-element.11, bf16[4096,896]{1,0:T(8,128)(2,1)} %param.6), kind=kOutput, calls=%fused_computation.15 | convolution fusion | flops 5637144576 | bytes 21299200 | tf_op jit(solution)/shard_map/dot_general | solution.py:10
  198.2 0.0 copy-done.1
  198.3 0.0 slice-done
  198.3 0.0 slice-done.1
  198.3 11.4 %add_convert_fusion = bf16[768,4096]{1,0:T(8,128)(2,1)} fusion(f32[768,4096]{1,0:T(8,128)} %fusion.4, bf16[768,896]{1,0:T(8,128)(2,1)S(1)} %get-tuple-element.10, bf16[4096,896]{1,0:T(8,128)(2,1)S(1)} %bitcast.23), kind=kOutput, calls=%fused_computation | convolution fusion | flops 5643436032 | bytes 27590656 | tf_op jit(solution)/shard_map/dot_general | solution.py:10
  209.6 0.0 reduce-scatter.5.cloned.1.call-update
  209.7 0.0 reduce-scatter.3.cloned.1.call-start
  209.7 11.8 %convolution_convert_fusion = bf16[768,4096]{1,0:T(8,128)(2,1)} fusion(bf16[768,896]{1,0:T(8,128)(2,1)S(1)} %get-tuple-element.12, bf16[896,4096]{1,0:T(8,128)(2,1)} %param.8), kind=kOutput, calls=%fused_computation.3 | convolution fusion | flops 5640290304 | bytes 15007744 | tf_op jit(solution)/shard_map/dot_general | solution.py:10
  221.5 0.0 reduce-scatter.3.cloned.1.call-update
  221.5 11.8 %convolution_bitcast_fusion.1 = f32[4096,896]{0,1:T(8,128)} fusion(bf16[768,896]{1,0:T(8,128)(2,1)} %copy-done.1, bf16[768,4096]{1,0:T(8,128)(2,1)} %all-gather.3.cloned.1.call-done), kind=kOutput, calls=%fused_computation.2 | convolution fusion | flops 5637144576 | bytes 22347776 | tf_op jit(solution)/shard_map/dot_general | solution.py:10
  233.3 16.2 %copy.10 = f32[4096,896]{1,0:T(8,128)} copy(f32[4096,896]{0,1:T(8,128)} %convolution_bitcast_fusion.1) | data formatting | bytes 29360128
  249.6 11.1 %convolution_bitcast_fusion = f32[4096,896]{0,1:T(8,128)} fusion(bf16[768,896]{1,0:T(8,128)(2,1)S(1)} %get-tuple-element.10, bf16[768,4096]{1,0:T(8,128)(2,1)} %all-gather.3.cloned.1.call-done), kind=kOutput, calls=%fused_computation.1 | convolution fusion | flops 5637144576 | bytes 22347776 | tf_op jit(solution)/shard_map/dot_general | solution.py:10
  260.6 16.1 %copy.11 = f32[4096,896]{1,0:T(8,128)} copy(f32[4096,896]{0,1:T(8,128)} %convolution_bitcast_fusion) | data formatting | bytes 29360128
  276.8 11.1 %fusion.5 = f32[896,4096]{1,0:T(8,128)} fusion(bf16[768,896]{1,0:T(8,128)(2,1)S(1)} %get-tuple-element.12, bf16[768,4096]{1,0:T(8,128)(2,1)} %all-gather.5.cloned.1.call-done), kind=kOutput, calls=%fused_computation.16 | convolution fusion | flops 5637144576 | bytes 22347776 | tf_op jit(solution)/shard_map/dot_general | solution.py:10
  287.9 5.7 %reduce-scatter.5.cloned.1.call-done = bf16[48,4096]{1,0:T(8,128)(2,1)} async-done(((bf16[768,4096]{1,0:T(8,128)(2,1)}), bf16[48,4096]{1,0:T(8,128)(2,1)}) %reduce-scatter.5.cloned.1.call-update) | async-done | bytes 393232 | tf_op jit(solution)/shard_map/reduce_scatter | solution.py:26
  293.6 1.9 convert_element_type.51
  295.5 86.8 %reduce-scatter.3.cloned.1.call-done = bf16[48,4096]{1,0:T(8,128)(2,1)} async-done(((bf16[768,4096]{1,0:T(8,128)(2,1)}), bf16[48,4096]{1,0:T(8,128)(2,1)}) %reduce-scatter.3.cloned.1.call-update) | async-done | bytes 393232 | tf_op jit(solution)/shard_map/reduce_scatter | solution.py:26
  382.3 1.9 convert_element_type.45
  (1 shorter events, 0.0 us)
Async XLA Ops:
  7.2 67.7 %all-gather.3.cloned.1.call-start = ((), (), s32[]{:S(2)}) async-start(), calls=%async_computation.2 | async-start | bytes 6684672 | tf_op jit(solution)/shard_map/all_gather | solution.py:32
  7.9 129.7 %all-gather.5.cloned.1.call-start = ((), (), s32[]{:S(2)}) async-start(), calls=%async_computation.4 | async-start | bytes 6684672 | tf_op jit(solution)/shard_map/all_gather | solution.py:33
  8.6 285.0 %reduce-scatter.5.cloned.1.call-start = ((), (), s32[]{:S(2)}) async-start(), calls=%async_computation.5 | async-start | bytes 6684672 | tf_op jit(solution)/shard_map/reduce_scatter | solution.py:26
  74.9 13.8 %copy-start = (bf16[768,4096]{1,0:T(8,128)(2,1)S(1)}, bf16[768,4096]{1,0:T(8,128)(2,1)}, u32[]{:S(2)}) copy-start(bf16[768,4096]{1,0:T(8,128)(2,1)} %all-gather.3.cloned.1.call-done) | copy-start | bytes 18874372
  87.2 62.9 %collective-permute-start = (bf16[768,896]{1,0:T(8,128)(2,1)}, bf16[768,896]{1,0:T(8,128)(2,1)S(1)}, u32[]{:S(2)}, u32[]{:S(2)}) collective-permute-start(bf16[768,896]{1,0:T(8,128)(2,1)} %get-tuple-element.15), channel_id=1, source_target_pairs={{0,16},{16,0},{1,17},{17,1},{2,18},{18,2},{3,19},{19,3},{4,20},{20... | collective-permute-start | bytes 4128776 | tf_op jit(solution)/shard_map/ppermute | solution.py:20
  99.0 51.1 %collective-permute-start.1 = (bf16[768,896]{1,0:T(8,128)(2,1)}, bf16[768,896]{1,0:T(8,128)(2,1)S(1)}, u32[]{:S(2)}, u32[]{:S(2)}) collective-permute-start(bf16[768,896]{1,0:T(8,128)(2,1)} %get-tuple-element.17), channel_id=1, source_target_pairs={{0,16},{16,0},{1,17},{17,1},{2,18},{18,2},{3,19},{19,3},{4,20},{20... | collective-permute-start | bytes 4128776 | tf_op jit(solution)/shard_map/ppermute | solution.py:20
  148.6 32.4 %collective-permute-start.2 = (bf16[768,896]{1,0:T(8,128)(2,1)S(1)}, bf16[768,896]{1,0:T(8,128)(2,1)S(1)}, u32[]{:S(2)}, u32[]{:S(2)}) collective-permute-start(bf16[768,896]{1,0:T(8,128)(2,1)S(1)} %get-tuple-element.13), channel_id=1, source_target_pairs={{0,16},{16,0},{1,17},{17,1},{2,18},{18,2},{3,19},{19,3},{4,20},{20... | collective-permute-start | bytes 4128776 | tf_op jit(solution)/shard_map/ppermute | solution.py:20
  150.1 30.9 %copy-start.2 = (bf16[768,896]{1,0:T(8,128)(2,1)}, bf16[768,896]{1,0:T(8,128)(2,1)S(1)}, u32[]{:S(2)}) copy-start(bf16[768,896]{1,0:T(8,128)(2,1)S(1)} %collective-permute-done) | copy-start | bytes 4128772
  150.1 30.9 %copy-start.3 = (bf16[768,896]{1,0:T(8,128)(2,1)}, bf16[768,896]{1,0:T(8,128)(2,1)S(1)}, u32[]{:S(2)}) copy-start(bf16[768,896]{1,0:T(8,128)(2,1)S(1)} %collective-permute-done.1) | copy-start | bytes 4128772
  181.0 17.2 %slice-start = ((s8[7340032]{0:T(1024)(128)(4,1)}), s8[4194304]{0:T(1024)(128)(4,1)S(1)}, s32[]{:S(2)}) async-start(s8[7340032]{0:T(1024)(128)(4,1)} %bitcast.22), calls=%async_computation.6 | async-start | bytes 8388608
  185.5 12.8 %copy-start.1 = (bf16[768,896]{1,0:T(8,128)(2,1)}, bf16[768,896]{1,0:T(8,128)(2,1)S(1)}, u32[]{:S(2)}) copy-start(bf16[768,896]{1,0:T(8,128)(2,1)S(1)} %get-tuple-element.11) | copy-start | bytes 4128772
  185.5 12.8 %slice-start.1 = ((s8[7340032]{0:T(1024)(128)(4,1)}), s8[3145728]{0:T(1024)(128)(4,1)S(1)}, s32[]{:S(2)}) async-start(s8[7340032]{0:T(1024)(128)(4,1)} %bitcast.22), calls=%async_computation.7 | async-start | bytes 6291456
  209.7 172.6 %reduce-scatter.3.cloned.1.call-start = ((), (), s32[]{:S(2)}) async-start(), calls=%async_computation.3 | async-start | bytes 6684672 | tf_op jit(solution)/shard_map/reduce_scatter | solution.py:26
Sparse Core Ops, SparseCore 0:
  10.3 64.5 all-gather.2
  77.1 60.4 all-gather.4
  209.8 83.7 reduce-scatter.4
  297.9 84.3 reduce-scatter.2

commit v2 on v1

v2 whole, which is shorter than its diff:
```python
import jax
import jax.numpy as jnp
from jax import lax
from jax.sharding import PartitionSpec as P

CORE, CHIP = 1, 2


def dot(left, right, left_dim, right_dim):
    return lax.dot_general(
        left, right, (((left_dim,), (right_dim,)), ((), ())), preferred_element_type=jnp.float32
    )


def after(array, *others):
    return lax.optimization_barrier((array, *others))[0]


def shift(block, step):
    n = lax.axis_size("depth")
    return lax.ppermute(block, "depth", [(i, (i + step) % n) for i in range(n)])


def swap(block, bit):
    n = lax.axis_size("col")
    return lax.ppermute(block, "col", [(i, i ^ bit) for i in range(n)])


def row_sum(partial):
    n = lax.axis_size("row")
    sent = partial.astype(jnp.bfloat16)
    total = partial
    for step in range(1, n):
        moved = lax.ppermute(sent, "row", [(i, (i + step) % n) for i in range(n)])
        total = total + moved.astype(jnp.float32)
    return total


def gather(shard, hold=None):
    near = [shard] + [shift(shard, k) for k in range(1, lax.axis_size("depth"))]
    mine = jnp.concatenate(near, axis=0)
    first = jnp.concatenate([mine, swap(mine, CORE)], axis=0)
    passed = near if hold is None else [near[0]] + hold(near[1:], first)
    mine = jnp.concatenate([swap(block, CHIP) for block in passed], axis=0)
    second = jnp.concatenate([mine, swap(mine, CORE)], axis=0)
    return first, second, near


def scatter(near, far):
    n = lax.axis_size("depth")
    half = near.shape[0] // 2
    size = half // n

    def wide(block):
        return block.astype(jnp.float32)

    far_core = swap(far[half:], CORE)
    near_core = swap(near[half:], CORE)
    total, to_chip, to_depth = None, [], []
    for k in reversed(range(n)):
        rows = slice(k * size, (k + 1) * size)
        far_sum = (wide(far[rows]) + wide(far_core[rows])).astype(jnp.bfloat16)
        to_chip.append(far_sum)
        block = wide(near[rows]) + wide(near_core[rows]) + wide(swap(far_sum, CHIP))
        if k:
            sent = block.astype(jnp.bfloat16)
            to_depth.append(sent)
            block = wide(shift(sent, -k))
        total = block if total is None else total + block
    return total, to_chip, to_depth


def body(tokens, gate_weight, up_weight, down_weight, cotangent):
    token_first, token_second, token_near = gather(tokens)
    gate_first = dot(token_first, gate_weight, 1, 0)
    up_first = dot(token_first, up_weight, 1, 0)
    gates, ups = [row_sum(gate_first)], [row_sum(up_first)]

    def hold(blocks, first):
        return list(lax.optimization_barrier((*blocks, gate_first, up_first))[: len(blocks)])

    cotangent_first, cotangent_second, _ = gather(after(cotangent, *token_near), hold)
    gates.append(row_sum(dot(token_second, gate_weight, 1, 0)))
    ups.append(row_sum(dot(token_second, up_weight, 1, 0)))
    hidden_grads = [
        row_sum(dot(group, down_weight, 1, 1)) for group in (cotangent_first, cotangent_second)
    ]
    hiddens, mixes = [], []
    for gate, up in zip(gates, ups):
        hidden = (gate * jax.nn.sigmoid(gate) * up).astype(jnp.bfloat16)
        hiddens.append(hidden)
        mixes.append(dot(hidden, down_weight, 1, 0).astype(jnp.bfloat16))
    mixed, to_chip, _ = scatter(*mixes)
    cotangent_all = jnp.concatenate([cotangent_first, cotangent_second], axis=0)
    hidden_all = after(jnp.concatenate(hiddens, axis=0), *to_chip)
    down_total = dot(hidden_all, cotangent_all, 0, 0)
    gate_grads, up_grads, token_grads = [], [], []
    for gate, up, hidden_grad in zip(gates, ups, hidden_grads):
        sigma = jax.nn.sigmoid(gate)
        gate_grad = (hidden_grad * up * sigma * (1.0 + gate * (1.0 - sigma))).astype(jnp.bfloat16)
        up_grad = (hidden_grad * (gate * sigma)).astype(jnp.bfloat16)
        gate_grads.append(gate_grad)
        up_grads.append(up_grad)
        token_grads.append(
            (dot(gate_grad, gate_weight, 1, 1) + dot(up_grad, up_weight, 1, 1)).astype(jnp.bfloat16)
        )
    token_grad, to_chip, to_depth = scatter(*token_grads)
    token_all = jnp.concatenate([token_first, token_second], axis=0)
    gate_total = dot(token_all, after(jnp.concatenate(gate_grads, axis=0), *to_chip), 0, 0)
    up_total = dot(token_all, after(jnp.concatenate(up_grads, axis=0), *to_depth), 0, 0)
    return (mixed, token_grad, gate_total, up_total, down_total)


def solution(mesh):
    activations = P(("depth", "col"), "row")
    wide = P("row", ("col", "depth"))
    tall = P(("col", "depth"), "row")
    return jax.shard_map(
        body,
        mesh=mesh,
        in_specs=(activations, wide, wide, tall, activations),
        out_specs=(activations, activations, wide, wide, tall),
        check_vma=False,
    )
```

time: 392 us -> 385 us (0.982)
  waiting for transfers between devices: 229 us -> 186 us
  starting transfers between devices: 3.7 us -> 41.9 us
  matrix products: 104 us -> 125 us
  local copies, waits for them, and re-layouts: 32.4 us -> 13.8 us
  between operations: 13.8 us -> 1.47 us
  other arithmetic: 8.32 us -> 13.4 us
    ppermute x0 -> x36, waiting for transfers between devices: none -> 136 us  [the longest x12 90.6 us: shift(): return lax.ppermute(block, 'depth', [(i, (i + step) % n) for i in range(n)])]
    all_gather x2 -> x0, waiting for transfers between devices: 104 us -> none  [the longest x1 66.2 us: body(): token_all = lax.all_gather(tokens, TOKEN_AXES, axis=0, tiled=True)]
    reduce_scatter x2 -> x0, waiting for transfers between devices: 92.5 us -> none  [token_scatter(): lax.psum_scatter(partial.astype(jnp.bfloat16), TOKEN_AXES, scatter_dimens...]
    ppermute x0 -> x36, starting transfers between devices: none -> 34.7 us  [the longest x24 20.4 us: swap(): return lax.ppermute(block, 'col', [(i, i ^ bit) for i in range(n)])]
    unnamed x14 -> x46, local copies, waits for them, and re-layouts: 32.4 us -> 9.23 us
    dot_general x9 -> x15, matrix products: 104 us -> 125 us  [dot(): lax.dot_general(left, right, (((left_dim,), (right_dim,)), ((), ())), pre...]
    ppermute x3 -> x6, waiting for transfers between devices: 30.9 us -> 50.4 us  [row_sum(): moved = lax.ppermute(sent, 'row', [(i, (i + step) % n) for i in range(n)])]
    convert_element_type x3 -> x6, other arithmetic: 8.32 us -> 8.11 us  [the longest x2 3.77 us: scatter(): far_sum = (wide(far[rows]) + wide(far_core[rows])).astype(jnp.bfloat16)]
  transfers between devices with their start and end apart: 7 -> 42, of which waited for: 5 -> 17; matrix products, arithmetic and copies ran while one was open for 29% -> 38% of each run, Pallas kernels for 0% -> 0%
where the time goes in v2:
time: 385 us; the launch traced here: 382 us
  waiting for transfers between devices  186 us (48%)
  matrix products  125 us (32%)
  starting transfers between devices  41.9 us (11%)
  local copies, waits for them, and re-layouts  13.8 us (4%)
  other arithmetic  13.4 us (3%)
    dot_general x15, matrix products, dot(): lax.dot_general(left, right, (((left_dim,), (right_dim,)), ((), ())), pre...  125 us
    ppermute x12, waiting for transfers between devices, shift(): return lax.ppermute(block, 'depth', [(i, (i + step) % n) for i in range(n)])  90.6 us
    ppermute x6, waiting for transfers between devices, row_sum(): moved = lax.ppermute(sent, 'row', [(i, (i + step) % n) for i in range(n)])  50.4 us
    ppermute x24, waiting for transfers between devices, swap(): return lax.ppermute(block, 'col', [(i, i ^ bit) for i in range(n)])  44.9 us
    ppermute x24, starting transfers between devices, swap(): return lax.ppermute(block, 'col', [(i, i ^ bit) for i in range(n)])  20.4 us
    ppermute x12, starting transfers between devices, shift(): return lax.ppermute(block, 'depth', [(i, (i + step) % n) for i in range(n)])  14.4 us
    unnamed x46, local copies, waits for them, and re-layouts  9.23 us
  transfers between devices with their start and end apart: 42, of which 17 were waited for; matrix products, arithmetic and copies ran while one was open for 38% of the time, Pallas kernels for 0%

profile of v2, /device:TPU:0, one launch (start us, length us, event | category | flops | bytes accessed | tf_op | source)
XLA Modules:
  0.0 381.8 jit_solution(10347979651661478624)
XLA Ops:
  0.6 3.0 collective-permute-start.7
  3.7 3.6 collective-permute-start.2
  9.4 7.8 %collective-permute-done.2 = bf16[48,4096]{1,0:T(8,128)(2,1)S(1)} collective-permute-done((bf16[48,4096]{1,0:T(8,128)(2,1)}, bf16[48,4096]{1,0:T(8,128)(2,1)S(1)}, u32[]{:S(2)}, u32[]{:S(2)}) %collective-permute-start.2) | collective-permute-done | bytes 393248 | tf_op jit(solution)/shard_map/ppermute | solution.py:21
  17.2 23.6 %collective-permute-done.1 = bf16[48,4096]{1,0:T(8,128)(2,1)S(1)} collective-permute-done((bf16[48,4096]{1,0:T(8,128)(2,1)}, bf16[48,4096]{1,0:T(8,128)(2,1)S(1)}, u32[]{:S(2)}, u32[]{:S(2)}) %collective-permute-start.1) | collective-permute-done | bytes 393248 | tf_op jit(solution)/shard_map/ppermute | solution.py:21
  41.3 2.8 collective-permute-start.23
  44.1 2.0 collective-permute-start.22
  48.6 2.6 collective-permute-done.24
  52.8 25.0 %collective-permute-done.23 = bf16[48,4096]{1,0:T(8,128)(2,1)S(1)} collective-permute-done((bf16[48,4096]{1,0:T(8,128)(2,1)}, bf16[48,4096]{1,0:T(8,128)(2,1)S(1)}, u32[]{:S(2)}, u32[]{:S(2)}) %collective-permute-start.23) | collective-permute-done | bytes 393248 | tf_op jit(solution)/shard_map/ppermute | solution.py:21
  80.5 9.3 %collective-permute-done.9 = bf16[48,4096]{1,0:T(8,128)(2,1)S(1)} collective-permute-done((bf16[48,4096]{1,0:T(8,128)(2,1)S(1)}, bf16[48,4096]{1,0:T(8,128)(2,1)S(1)}, u32[]{:S(2)}, u32[]{:S(2)}) %collective-permute-start.9) | collective-permute-done | bytes 393248 | tf_op jit(solution)/shard_map/ppermute | solution.py:26
  89.8 5.7 %collective-permute-done.8 = bf16[48,4096]{1,0:T(8,128)(2,1)S(1)} collective-permute-done((bf16[48,4096]{1,0:T(8,128)(2,1)S(1)}, bf16[48,4096]{1,0:T(8,128)(2,1)S(1)}, u32[]{:S(2)}, u32[]{:S(2)}) %collective-permute-start.8) | collective-permute-done | bytes 393248 | tf_op jit(solution)/shard_map/ppermute | solution.py:26
  96.3 7.8 %fusion.7 = (bf16[384,896]{1,0:T(8,128)(2,1)S(1)}, f32[384,896]{1,0:T(8,128)S(1)}) fusion(bf16[384,4096]{1,0:T(8,128)(2,1)S(1)} %get-tuple-element.46, bf16[4096,896]{1,0:T(8,128)(2,1)} %param.7), kind=kOutput, calls=%fused_computation.88 | convolution fusion | flops 2818916352 | bytes 12550144 | tf_op jit(solution)/shard_map/dot_general | solution.py:10
  104.1 7.3 %fusion.6 = (bf16[384,896]{1,0:T(8,128)(2,1)S(1)}, f32[384,896]{1,0:T(8,128)S(1)}) fusion(bf16[384,4096]{1,0:T(8,128)(2,1)S(1)} %get-tuple-element.46, bf16[4096,896]{1,0:T(8,128)(2,1)} %param.6), kind=kOutput, calls=%fused_computation.87 | convolution fusion | flops 2818916352 | bytes 12550144 | tf_op jit(solution)/shard_map/dot_general | solution.py:10
  111.4 1.6 collective-permute-start.29
  113.8 1.6 collective-permute-start.31
  115.8 8.9 %fusion.4 = (bf16[384,896]{1,0:T(8,128)(2,1)}, f32[384,896]{1,0:T(8,128)S(1)}) fusion(bf16[384,4096]{1,0:T(8,128)(2,1)S(1)} %get-tuple-element.44, bf16[4096,896]{1,0:T(8,128)(2,1)} %param.7), kind=kOutput, calls=%fused_computation.85 | convolution fusion | flops 2818916352 | bytes 12550144 | tf_op jit(solution)/shard_map/dot_general | solution.py:10
  124.7 6.6 %fusion.3 = (bf16[384,896]{1,0:T(8,128)(2,1)}, f32[384,896]{1,0:T(8,128)S(1)}) fusion(bf16[384,4096]{1,0:T(8,128)(2,1)S(1)} %get-tuple-element.44, bf16[4096,896]{1,0:T(8,128)(2,1)} %param.6), kind=kOutput, calls=%fused_computation.84 | convolution fusion | flops 2818916352 | bytes 12550144 | tf_op jit(solution)/shard_map/dot_general | solution.py:10
  133.1 7.4 %fusion.5 = (bf16[384,896]{1,0:T(8,128)(2,1)S(1)}, f32[384,896]{1,0:T(8,128)S(1)}) fusion(bf16[384,4096]{1,0:T(8,128)(2,1)S(1)} %get-tuple-element.42, bf16[896,4096]{1,0:T(8,128)(2,1)} %param.8), kind=kOutput, calls=%fused_computation.86 | convolution fusion | flops 2818916352 | bytes 12550144 | tf_op jit(solution)/shard_map/dot_general | solution.py:10
  143.8 5.8 %collective-permute-done.5 = bf16[384,896]{1,0:T(8,128)(2,1)S(1)} collective-permute-done((bf16[384,896]{1,0:T(8,128)(2,1)S(1)}, bf16[384,896]{1,0:T(8,128)(2,1)S(1)}, u32[]{:S(2)}, u32[]{:S(2)}) %collective-permute-start.5) | collective-permute-done | bytes 688160 | tf_op jit(solution)/shard_map/ppermute | solution.py:34
  151.1 13.3 %collective-permute-done.4 = bf16[384,896]{1,0:T(8,128)(2,1)S(1)} collective-permute-done((bf16[384,896]{1,0:T(8,128)(2,1)S(1)}, bf16[384,896]{1,0:T(8,128)(2,1)S(1)}, u32[]{:S(2)}, u32[]{:S(2)}) %collective-permute-start.4) | collective-permute-done | bytes 688160 | tf_op jit(solution)/shard_map/ppermute | solution.py:34
  164.4 14.7 %collective-permute-done.26 = bf16[384,896]{1,0:T(8,128)(2,1)S(1)} collective-permute-done((bf16[384,896]{1,0:T(8,128)(2,1)S(1)}, bf16[384,896]{1,0:T(8,128)(2,1)S(1)}, u32[]{:S(2)}, u32[]{:S(2)}) %collective-permute-start.26) | collective-permute-done | bytes 688160 | tf_op jit(solution)/shard_map/ppermute | solution.py:34
  181.0 3.7 convolution_convert_fusion.1
  186.4 7.5 %fusion.2 = (bf16[384,896]{1,0:T(8,128)(2,1)S(1)}, f32[384,896]{1,0:T(8,128)S(1)}) fusion(bf16[384,4096]{1,0:T(8,128)(2,1)S(1)} %get-tuple-element.40, bf16[896,4096]{1,0:T(8,128)(2,1)} %param.8), kind=kOutput, calls=%fused_computation.83 | convolution fusion | flops 2818916352 | bytes 12550144 | tf_op jit(solution)/shard_map/dot_general | solution.py:10
  193.8 1.5 collective-permute-start.33
  195.4 10.0 %fusion.8 = f32[384,4096]{1,0:T(8,128)} fusion(bf16[384,896]{1,0:T(8,128)(2,1)S(1)} %get-tuple-element.34, bf16[4096,896]{1,0:T(8,128)(2,1)} %param.6), kind=kOutput, calls=%fused_computation.89 | convolution fusion | flops 2818572288 | bytes 14319616 | tf_op jit(solution)/shard_map/dot_general | solution.py:10
  205.4 3.2 collective-permute-done.12
  208.6 13.4 %collective-permute-done.33 = bf16[384,896]{1,0:T(8,128)(2,1)S(1)} collective-permute-done((bf16[384,896]{1,0:T(8,128)(2,1)S(1)}, bf16[384,896]{1,0:T(8,128)(2,1)S(1)}, u32[]{:S(2)}, u32[]{:S(2)}) %collective-permute-start.33) | collective-permute-done | bytes 688160 | tf_op jit(solution)/shard_map/ppermute | solution.py:34
  223.0 7.4 %convolution_convert_fusion = bf16[384,4096]{1,0:T(8,128)(2,1)S(1)} fusion(bf16[384,896]{1,0:T(8,128)(2,1)S(1)} %get-tuple-element.38, bf16[896,4096]{1,0:T(8,128)(2,1)} %param.8), kind=kOutput, calls=%fused_computation.2 | convolution fusion | flops 2820145152 | bytes 11173888 | tf_op jit(solution)/shard_map/dot_general | solution.py:10
  230.5 1.7 copy-done
  233.4 5.3 %fusion.9 = f32[384,4096]{1,0:T(8,128)} fusion(bf16[384,896]{1,0:T(8,128)(2,1)S(1)} %get-tuple-element.37, bf16[4096,896]{1,0:T(8,128)(2,1)S(1)} %bitcast.33), kind=kOutput, calls=%fused_computation.90 | convolution fusion | flops 2818572288 | bytes 14319616 | tf_op jit(solution)/shard_map/dot_general | solution.py:10
  238.7 9.6 %add_convert_fusion = bf16[384,4096]{1,0:T(8,128)(2,1)S(1)} fusion(f32[384,4096]{1,0:T(8,128)} %fusion.9, bf16[384,896]{1,0:T(8,128)(2,1)S(1)} %get-tuple-element.36, bf16[4096,896]{1,0:T(8,128)(2,1)} %param.7), kind=kOutput, calls=%fused_computation | convolution fusion | flops 2821718016 | bytes 17465344 | tf_op jit(solution)/shard_map/dot_general | solution.py:10
  250.0 9.4 %add_convert_fusion.1 = bf16[384,4096]{1,0:T(8,128)(2,1)S(1)} fusion(f32[384,4096]{1,0:T(8,128)} %fusion.8, bf16[384,896]{1,0:T(8,128)(2,1)S(1)} %get-tuple-element.33, bf16[4096,896]{1,0:T(8,128)(2,1)} %param.7), kind=kOutput, calls=%fused_computation.1 | convolution fusion | flops 2821718016 | bytes 17465344 | tf_op jit(solution)/shard_map/dot_general | solution.py:10
  261.2 1.6 copy-done.1
  262.8 1.9 add_convert_fusion.15
  267.3 1.9 add_convert_fusion.8
  269.2 12.5 %fusion.10 = f32[4096,896]{1,0:T(8,128)} fusion(bf16[768,4096]{1,0:T(8,128)(2,1)} %copy-done.9, bf16[768,896]{1,0:T(8,128)(2,1)S(1)} %get-tuple-element.16), kind=kOutput, calls=%fused_computation.91 | convolution fusion | flops 5637144576 | bytes 22347776 | tf_op jit(solution)/shard_map/dot_general | solution.py:10
  281.7 9.5 %fusion.12 = f32[896,4096]{1,0:T(8,128)} fusion(bf16[768,896]{1,0:T(8,128)(2,1)S(1)} %get-tuple-element.18, bf16[768,4096]{1,0:T(8,128)(2,1)S(1)} %get-tuple-element.39), kind=kOutput, calls=%fused_computation.93 | convolution fusion | flops 5637144576 | bytes 22347776 | tf_op jit(solution)/shard_map/dot_general | solution.py:10
  291.2 1.6 collective-permute-start.21
  295.4 1.8 add_convert_fusion.14
  297.2 1.5 collective-permute-start.41
  298.8 13.0 %collective-permute-done.35 = bf16[48,4096]{1,0:T(8,128)(2,1)S(1)} collective-permute-done((bf16[48,4096]{1,0:T(8,128)(2,1)S(1)}, bf16[48,4096]{1,0:T(8,128)(2,1)S(1)}, u32[]{:S(2)}, u32[]{:S(2)}) %collective-permute-start.35) | collective-permute-done | bytes 393248 | tf_op jit(solution)/shard_map/ppermute | solution.py:26
  311.8 8.4 %collective-permute-done.39 = bf16[48,4096]{1,0:T(8,128)(2,1)S(1)} collective-permute-done((bf16[48,4096]{1,0:T(8,128)(2,1)S(1)}, bf16[48,4096]{1,0:T(8,128)(2,1)S(1)}, u32[]{:S(2)}, u32[]{:S(2)}) %collective-permute-start.39) | collective-permute-done | bytes 393248 | tf_op jit(solution)/shard_map/ppermute | solution.py:26
  320.2 8.4 %collective-permute-done.37 = bf16[48,4096]{1,0:T(8,128)(2,1)S(1)} collective-permute-done((bf16[48,4096]{1,0:T(8,128)(2,1)S(1)}, bf16[48,4096]{1,0:T(8,128)(2,1)S(1)}, u32[]{:S(2)}, u32[]{:S(2)}) %collective-permute-start.37) | collective-permute-done | bytes 393248 | tf_op jit(solution)/shard_map/ppermute | solution.py:26
  329.2 12.5 %fusion.11 = f32[4096,896]{1,0:T(8,128)} fusion(bf16[768,4096]{1,0:T(8,128)(2,1)} %copy-done.9, bf16[768,896]{1,0:T(8,128)(2,1)S(1)} %pad_maximum_fusion.5), kind=kOutput, calls=%fused_computation.92 | convolution fusion | flops 5637144576 | bytes 22347776 | tf_op jit(solution)/shard_map/dot_general | solution.py:10
  341.7 3.8 %collective-permute-start.40 = (bf16[48,4096]{1,0:T(8,128)(2,1)S(1)}, bf16[48,4096]{1,0:T(8,128)(2,1)S(1)}, u32[]{:S(2)}, u32[]{:S(2)}) collective-permute-start(bf16[48,4096]{1,0:T(8,128)(2,1)S(1)} %get-tuple-element.20), channel_id=1, source_target_pairs={{0,3},{1,0},{2,1},{3,2},{4,7},{5,4},{6,5},{7,6},{8,11},{9,8},{10,9... | collective-permute-start | bytes 1179656 | tf_op jit(solution)/shard_map/ppermute | solution.py:21
  346.7 11.7 %collective-permute-done.18 = bf16[48,4096]{1,0:T(8,128)(2,1)S(1)} collective-permute-done((bf16[48,4096]{1,0:T(8,128)(2,1)S(1)}, bf16[48,4096]{1,0:T(8,128)(2,1)S(1)}, u32[]{:S(2)}, u32[]{:S(2)}) %collective-permute-start.18) | collective-permute-done | bytes 393248 | tf_op jit(solution)/shard_map/ppermute | solution.py:21
  358.4 2.2 add_add_fusion.1
  360.6 2.9 collective-permute-done.40
  363.5 16.9 %collective-permute-done.38 = bf16[48,4096]{1,0:T(8,128)(2,1)S(1)} collective-permute-done((bf16[48,4096]{1,0:T(8,128)(2,1)S(1)}, bf16[48,4096]{1,0:T(8,128)(2,1)S(1)}, u32[]{:S(2)}, u32[]{:S(2)}) %collective-permute-start.38) | collective-permute-done | bytes 393248 | tf_op jit(solution)/shard_map/ppermute | solution.py:21
  (119 shorter events, 35.1 us)
Async XLA Ops:
  0.6 79.3 %collective-permute-start.7 = (bf16[48,4096]{1,0:T(8,128)(2,1)}, bf16[48,4096]{1,0:T(8,128)(2,1)S(1)}, u32[]{:S(2)}, u32[]{:S(2)}) collective-permute-start(bf16[48,4096]{1,0:T(8,128)(2,1)} %param.5), channel_id=1, source_target_pairs={{0,8},{4,12},{8,0},{12,4},{1,9},{5,13},{9,1},{13,5},{2,10},{6,14},... | collective-permute-start | bytes 1179656 | tf_op jit(solution)/shard_map/ppermute | solution.py:26
  3.7 13.5 %collective-permute-start.2 = (bf16[48,4096]{1,0:T(8,128)(2,1)}, bf16[48,4096]{1,0:T(8,128)(2,1)S(1)}, u32[]{:S(2)}, u32[]{:S(2)}) collective-permute-start(bf16[48,4096]{1,0:T(8,128)(2,1)} %param.5), channel_id=1, source_target_pairs={{0,3},{1,0},{2,1},{3,2},{4,7},{5,4},{6,5},{7,6},{8,11},{9,8},{10,9... | collective-permute-start | bytes 1179656 | tf_op jit(solution)/shard_map/ppermute | solution.py:21
  7.3 33.5 %collective-permute-start.1 = (bf16[48,4096]{1,0:T(8,128)(2,1)}, bf16[48,4096]{1,0:T(8,128)(2,1)S(1)}, u32[]{:S(2)}, u32[]{:S(2)}) collective-permute-start(bf16[48,4096]{1,0:T(8,128)(2,1)} %param.5), channel_id=1, source_target_pairs={{0,2},{1,3},{2,0},{3,1},{4,6},{5,7},{6,4},{7,5},{8,10},{9,11},{10,... | collective-permute-start | bytes 1179656 | tf_op jit(solution)/shard_map/ppermute | solution.py:21
  7.3 33.5 %collective-permute-start = (bf16[48,4096]{1,0:T(8,128)(2,1)}, bf16[48,4096]{1,0:T(8,128)(2,1)S(1)}, u32[]{:S(2)}, u32[]{:S(2)}) collective-permute-start(bf16[48,4096]{1,0:T(8,128)(2,1)} %param.5), channel_id=1, source_target_pairs={{0,1},{1,2},{2,3},{3,0},{4,5},{5,6},{6,7},{7,4},{8,9},{9,10},{10,1... | collective-permute-start | bytes 1179656 | tf_op jit(solution)/shard_map/ppermute | solution.py:21
  40.7 99.8 %collective-permute-start.28 = (bf16[48,4096]{1,0:T(8,128)(2,1)}, bf16[48,4096]{1,0:T(8,128)(2,1)S(1)}, u32[]{:S(2)}, u32[]{:S(2)}) collective-permute-start(bf16[48,4096]{1,0:T(8,128)(2,1)} %param.9), channel_id=1, source_target_pairs={{0,8},{4,12},{8,0},{12,4},{1,9},{5,13},{9,1},{13,5},{2,10},{6,14},... | collective-permute-start | bytes 1179656 | tf_op jit(solution)/shard_map/ppermute | solution.py:26
  41.3 10.0 %collective-permute-start.24 = (bf16[48,4096]{1,0:T(8,128)(2,1)}, bf16[48,4096]{1,0:T(8,128)(2,1)S(1)}, u32[]{:S(2)}, u32[]{:S(2)}) collective-permute-start(bf16[48,4096]{1,0:T(8,128)(2,1)} %param.9), channel_id=1, source_target_pairs={{0,3},{1,0},{2,1},{3,2},{4,7},{5,4},{6,5},{7,6},{8,11},{9,8},{10,9... | collective-permute-start | bytes 1179656 | tf_op jit(solution)/shard_map/ppermute | solution.py:21
  41.3 36.5 %collective-permute-start.23 = (bf16[48,4096]{1,0:T(8,128)(2,1)}, bf16[48,4096]{1,0:T(8,128)(2,1)S(1)}, u32[]{:S(2)}, u32[]{:S(2)}) collective-permute-start(bf16[48,4096]{1,0:T(8,128)(2,1)} %param.9), channel_id=1, source_target_pairs={{0,2},{1,3},{2,0},{3,1},{4,6},{5,7},{6,4},{7,5},{8,10},{9,11},{10,... | collective-permute-start | bytes 1179656 | tf_op jit(solution)/shard_map/ppermute | solution.py:21
  44.1 35.3 %collective-permute-start.22 = (bf16[48,4096]{1,0:T(8,128)(2,1)}, bf16[48,4096]{1,0:T(8,128)(2,1)S(1)}, u32[]{:S(2)}, u32[]{:S(2)}) collective-permute-start(bf16[48,4096]{1,0:T(8,128)(2,1)} %param.9), channel_id=1, source_target_pairs={{0,1},{1,2},{2,3},{3,0},{4,5},{5,6},{6,7},{7,4},{8,9},{9,10},{10,1... | collective-permute-start | bytes 1179656 | tf_op jit(solution)/shard_map/ppermute | solution.py:21
  47.2 32.6 %copy-start.8 = (bf16[48,4096]{1,0:T(8,128)(2,1)S(1)}, bf16[48,4096]{1,0:T(8,128)(2,1)}, u32[]{:S(2)}) copy-start(bf16[48,4096]{1,0:T(8,128)(2,1)} %param.9) | copy-start | bytes 1179652
  51.3 28.8 %collective-permute-start.10 = (bf16[48,4096]{1,0:T(8,128)(2,1)S(1)}, bf16[48,4096]{1,0:T(8,128)(2,1)S(1)}, u32[]{:S(2)}, u32[]{:S(2)}) collective-permute-start(bf16[48,4096]{1,0:T(8,128)(2,1)S(1)} %collective-permute-done.2), channel_id=1, source_target_pairs={{0,8},{4,12},{8,0},{12,4},{1,9},{5,13},{9,1},{13,5},{2,10},{6,14},... | collective-permute-start | bytes 1179656 | tf_op jit(solution)/shard_map/ppermute | solution.py:26
  77.8 12.1 %collective-permute-start.9 = (bf16[48,4096]{1,0:T(8,128)(2,1)S(1)}, bf16[48,4096]{1,0:T(8,128)(2,1)S(1)}, u32[]{:S(2)}, u32[]{:S(2)}) collective-permute-start(bf16[48,4096]{1,0:T(8,128)(2,1)S(1)} %collective-permute-done.1), channel_id=1, source_target_pairs={{0,8},{4,12},{8,0},{12,4},{1,9},{5,13},{9,1},{13,5},{2,10},{6,14},... | collective-permute-start | bytes 1179656 | tf_op jit(solution)/shard_map/ppermute | solution.py:26
  79.3 16.2 %collective-permute-start.8 = (bf16[48,4096]{1,0:T(8,128)(2,1)S(1)}, bf16[48,4096]{1,0:T(8,128)(2,1)S(1)}, u32[]{:S(2)}, u32[]{:S(2)}) collective-permute-start(bf16[48,4096]{1,0:T(8,128)(2,1)S(1)} %collective-permute-done), channel_id=1, source_target_pairs={{0,8},{4,12},{8,0},{12,4},{1,9},{5,13},{9,1},{13,5},{2,10},{6,14},... | collective-permute-start | bytes 1179656 | tf_op jit(solution)/shard_map/ppermute | solution.py:26
  79.9 16.0 %collective-permute-start.3 = (bf16[192,4096]{1,0:T(8,128)(2,1)S(1)}, bf16[192,4096]{1,0:T(8,128)(2,1)S(1)}, u32[]{:S(2)}, u32[]{:S(2)}) collective-permute-start(bf16[192,4096]{1,0:T(8,128)(2,1)S(1)} %pad_maximum_fusion), channel_id=1, source_target_pairs={{0,4},{4,0},{8,12},{12,8},{1,5},{5,1},{9,13},{13,9},{2,6},{6,2},{1... | collective-permute-start | bytes 4718600 | tf_op jit(solution)/shard_map/ppermute | solution.py:26
  80.0 51.2 %collective-permute-start.25 = (bf16[192,4096]{1,0:T(8,128)(2,1)S(1)}, bf16[192,4096]{1,0:T(8,128)(2,1)S(1)}, u32[]{:S(2)}, u32[]{:S(2)}) collective-permute-start(bf16[192,4096]{1,0:T(8,128)(2,1)S(1)} %pad_maximum_fusion.2), channel_id=1, source_target_pairs={{0,4},{4,0},{8,12},{12,8},{1,5},{5,1},{9,13},{13,9},{2,6},{6,2},{1... | collective-permute-start | bytes 4718600 | tf_op jit(solution)/shard_map/ppermute | solution.py:26
  95.6 18.2 %collective-permute-start.11 = (bf16[192,4096]{1,0:T(8,128)(2,1)S(1)}, bf16[192,4096]{1,0:T(8,128)(2,1)S(1)}, u32[]{:S(2)}, u32[]{:S(2)}) collective-permute-start(bf16[192,4096]{1,0:T(8,128)(2,1)S(1)} %pad_maximum_fusion.1), channel_id=1, source_target_pairs={{0,4},{4,0},{8,12},{12,8},{1,5},{5,1},{9,13},{13,9},{2,6},{6,2},{1... | collective-permute-start | bytes 4718600 | tf_op jit(solution)/shard_map/ppermute | solution.py:26
  111.4 29.8 %collective-permute-start.29 = (bf16[48,4096]{1,0:T(8,128)(2,1)S(1)}, bf16[48,4096]{1,0:T(8,128)(2,1)S(1)}, u32[]{:S(2)}, u32[]{:S(2)}) collective-permute-start(bf16[48,4096]{1,0:T(8,128)(2,1)S(1)} %collective-permute-done.22), channel_id=1, source_target_pairs={{0,8},{4,12},{8,0},{12,4},{1,9},{5,13},{9,1},{13,5},{2,10},{6,14},... | collective-permute-start | bytes 1179656 | tf_op jit(solution)/shard_map/ppermute | solution.py:26
  113.0 29.7 %collective-permute-start.30 = (bf16[48,4096]{1,0:T(8,128)(2,1)S(1)}, bf16[48,4096]{1,0:T(8,128)(2,1)S(1)}, u32[]{:S(2)}, u32[]{:S(2)}) collective-permute-start(bf16[48,4096]{1,0:T(8,128)(2,1)S(1)} %collective-permute-done.23), channel_id=1, source_target_pairs={{0,8},{4,12},{8,0},{12,4},{1,9},{5,13},{9,1},{13,5},{2,10},{6,14},... | collective-permute-start | bytes 1179656 | tf_op jit(solution)/shard_map/ppermute | solution.py:26
  113.8 28.9 %collective-permute-start.31 = (bf16[48,4096]{1,0:T(8,128)(2,1)S(1)}, bf16[48,4096]{1,0:T(8,128)(2,1)S(1)}, u32[]{:S(2)}, u32[]{:S(2)}) collective-permute-start(bf16[48,4096]{1,0:T(8,128)(2,1)S(1)} %collective-permute-done.24), channel_id=1, source_target_pairs={{0,8},{4,12},{8,0},{12,4},{1,9},{5,13},{9,1},{13,5},{2,10},{6,14},... | collective-permute-start | bytes 1179656 | tf_op jit(solution)/shard_map/ppermute | solution.py:26
  115.8 8.9 %copy-start.9 = (bf16[768,4096]{1,0:T(8,128)(2,1)}, bf16[768,4096]{1,0:T(8,128)(2,1)S(1)}, u32[]{:S(2)}) copy-start(bf16[768,4096]{1,0:T(8,128)(2,1)S(1)} %get-tuple-element.43) | copy-start | bytes 18874372
  131.3 18.3 %collective-permute-start.5 = (bf16[384,896]{1,0:T(8,128)(2,1)S(1)}, bf16[384,896]{1,0:T(8,128)(2,1)S(1)}, u32[]{:S(2)}, u32[]{:S(2)}) collective-permute-start(bf16[384,896]{1,0:T(8,128)(2,1)S(1)} %get-tuple-element.89), channel_id=1, source_target_pairs={{0,16},{16,0},{1,17},{17,1},{2,18},{18,2},{3,19},{19,3},{4,20},{20... | collective-permute-start | bytes 2064392 | tf_op jit(solution)/shard_map/ppermute | solution.py:34
  140.6 23.8 %collective-permute-start.4 = (bf16[384,896]{1,0:T(8,128)(2,1)S(1)}, bf16[384,896]{1,0:T(8,128)(2,1)S(1)}, u32[]{:S(2)}, u32[]{:S(2)}) collective-permute-start(bf16[384,896]{1,0:T(8,128)(2,1)S(1)} %get-tuple-element.87), channel_id=1, source_target_pairs={{0,16},{16,0},{1,17},{17,1},{2,18},{18,2},{3,19},{19,3},{4,20},{20... | collective-permute-start | bytes 2064392 | tf_op jit(solution)/shard_map/ppermute | solution.py:34
  141.2 37.9 %collective-permute-start.26 = (bf16[384,896]{1,0:T(8,128)(2,1)S(1)}, bf16[384,896]{1,0:T(8,128)(2,1)S(1)}, u32[]{:S(2)}, u32[]{:S(2)}) collective-permute-start(bf16[384,896]{1,0:T(8,128)(2,1)S(1)} %get-tuple-element.85), channel_id=1, source_target_pairs={{0,16},{16,0},{1,17},{17,1},{2,18},{18,2},{3,19},{19,3},{4,20},{20... | collective-permute-start | bytes 2064392 | tf_op jit(solution)/shard_map/ppermute | solution.py:34
  142.7 37.4 %slice-start = ((s8[7340032]{0:T(1024)(128)(4,1)}), s8[4194304]{0:T(1024)(128)(4,1)S(1)}, s32[]{:S(2)}) async-start(s8[7340032]{0:T(1024)(128)(4,1)} %bitcast.30), calls=%async_computation | async-start | bytes 8388608
  142.9 43.1 %collective-permute-start.32 = (bf16[192,4096]{1,0:T(8,128)(2,1)S(1)}, bf16[192,4096]{1,0:T(8,128)(2,1)S(1)}, u32[]{:S(2)}, u32[]{:S(2)}) collective-permute-start(bf16[192,4096]{1,0:T(8,128)(2,1)S(1)} %pad_maximum_fusion.3), channel_id=1, source_target_pairs={{0,4},{4,0},{8,12},{12,8},{1,5},{5,1},{9,13},{13,9},{2,6},{6,2},{1... | collective-permute-start | bytes 4718600 | tf_op jit(solution)/shard_map/ppermute | solution.py:26
  142.9 62.4 %collective-permute-start.13 = (bf16[384,896]{1,0:T(8,128)(2,1)}, bf16[384,896]{1,0:T(8,128)(2,1)S(1)}, u32[]{:S(2)}, u32[]{:S(2)}) collective-permute-start(bf16[384,896]{1,0:T(8,128)(2,1)} %get-tuple-element.83), channel_id=1, source_target_pairs={{0,16},{16,0},{1,17},{17,1},{2,18},{18,2},{3,19},{19,3},{4,20},{20... | collective-permute-start | bytes 2064392 | tf_op jit(solution)/shard_map/ppermute | solution.py:34
  149.6 59.0 %collective-permute-start.12 = (bf16[384,896]{1,0:T(8,128)(2,1)}, bf16[384,896]{1,0:T(8,128)(2,1)S(1)}, u32[]{:S(2)}, u32[]{:S(2)}) collective-permute-start(bf16[384,896]{1,0:T(8,128)(2,1)} %get-tuple-element.81), channel_id=1, source_target_pairs={{0,16},{16,0},{1,17},{17,1},{2,18},{18,2},{3,19},{19,3},{4,20},{20... | collective-permute-start | bytes 2064392 | tf_op jit(solution)/shard_map/ppermute | solution.py:34
  186.0 105.3 %collective-permute-start.6 = (bf16[192,4096]{1,0:T(8,128)(2,1)}, bf16[192,4096]{1,0:T(8,128)(2,1)}, u32[]{:S(2)}, u32[]{:S(2)}) collective-permute-start(bf16[192,4096]{1,0:T(8,128)(2,1)} %slice.145), channel_id=1, source_target_pairs={{0,4},{4,0},{8,12},{12,8},{1,5},{5,1},{9,13},{13,9},{2,6},{6,2},{1... | collective-permute-start | bytes 4718600 | tf_op jit(solution)/shard_map/ppermute | solution.py:26
  193.8 28.2 %collective-permute-start.33 = (bf16[384,896]{1,0:T(8,128)(2,1)S(1)}, bf16[384,896]{1,0:T(8,128)(2,1)S(1)}, u32[]{:S(2)}, u32[]{:S(2)}) collective-permute-start(bf16[384,896]{1,0:T(8,128)(2,1)S(1)} %get-tuple-element.79), channel_id=1, source_target_pairs={{0,16},{16,0},{1,17},{17,1},{2,18},{18,2},{3,19},{19,3},{4,20},{20... | collective-permute-start | bytes 2064392 | tf_op jit(solution)/shard_map/ppermute | solution.py:34
  222.0 11.4 %slice-start.2 = ((s8[7340032]{0:T(1024)(128)(4,1)}), s8[3145728]{0:T(1024)(128)(4,1)S(1)}, s32[]{:S(2)}) async-start(s8[7340032]{0:T(1024)(128)(4,1)} %bitcast.32), calls=%async_computation.2 | async-start | bytes 6291456
  223.0 10.4 %copy-start.4 = (bf16[384,896]{1,0:T(8,128)(2,1)}, bf16[384,896]{1,0:T(8,128)(2,1)S(1)}, u32[]{:S(2)}) copy-start(bf16[384,896]{1,0:T(8,128)(2,1)S(1)} %get-tuple-element.37) | copy-start | bytes 2064388
  223.0 10.4 %slice-start.3 = ((s8[7340032]{0:T(1024)(128)(4,1)}), s8[4194304]{0:T(1024)(128)(4,1)S(1)}, s32[]{:S(2)}) async-start(s8[7340032]{0:T(1024)(128)(4,1)} %bitcast.32), calls=%async_computation.3 | async-start | bytes 8388608
  233.4 27.8 %collective-permute-start.14 = (bf16[192,4096]{1,0:T(8,128)(2,1)}, bf16[192,4096]{1,0:T(8,128)(2,1)}, u32[]{:S(2)}, u32[]{:S(2)}) collective-permute-start(bf16[192,4096]{1,0:T(8,128)(2,1)} %slice.148), channel_id=1, source_target_pairs={{0,4},{4,0},{8,12},{12,8},{1,5},{5,1},{9,13},{13,9},{2,6},{6,2},{1... | collective-permute-start | bytes 4718600 | tf_op jit(solution)/shard_map/ppermute | solution.py:26
  249.5 17.3 %collective-permute-start.34 = (bf16[192,4096]{1,0:T(8,128)(2,1)}, bf16[192,4096]{1,0:T(8,128)(2,1)}, u32[]{:S(2)}, u32[]{:S(2)}) collective-permute-start(bf16[192,4096]{1,0:T(8,128)(2,1)} %slice.166), channel_id=1, source_target_pairs={{0,4},{4,0},{8,12},{12,8},{1,5},{5,1},{9,13},{13,9},{2,6},{6,2},{1... | collective-permute-start | bytes 4718600 | tf_op jit(solution)/shard_map/ppermute | solution.py:26
  259.6 37.7 %collective-permute-start.27 = (bf16[192,4096]{1,0:T(8,128)(2,1)S(1)}, bf16[192,4096]{1,0:T(8,128)(2,1)S(1)}, u32[]{:S(2)}, u32[]{:S(2)}) collective-permute-start(bf16[192,4096]{1,0:T(8,128)(2,1)S(1)} %slice.163), channel_id=1, source_target_pairs={{0,4},{4,0},{8,12},{12,8},{1,5},{5,1},{9,13},{13,9},{2,6},{6,2},{1... | collective-permute-start | bytes 4718600 | tf_op jit(solution)/shard_map/ppermute | solution.py:26
  264.7 28.1 %collective-permute-start.15 = (bf16[48,4096]{1,0:T(8,128)(2,1)S(1)}, bf16[48,4096]{1,0:T(8,128)(2,1)S(1)}, u32[]{:S(2)}, u32[]{:S(2)}) collective-permute-start(bf16[48,4096]{1,0:T(8,128)(2,1)S(1)} %get-tuple-element.29), channel_id=1, source_target_pairs={{0,8},{4,12},{8,0},{12,4},{1,9},{5,13},{9,1},{13,5},{2,10},{6,14},... | collective-permute-start | bytes 1179656 | tf_op jit(solution)/shard_map/ppermute | solution.py:26
  265.3 28.1 %collective-permute-start.19 = (bf16[48,4096]{1,0:T(8,128)(2,1)S(1)}, bf16[48,4096]{1,0:T(8,128)(2,1)S(1)}, u32[]{:S(2)}, u32[]{:S(2)}) collective-permute-start(bf16[48,4096]{1,0:T(8,128)(2,1)S(1)} %get-tuple-element.31), channel_id=1, source_target_pairs={{0,8},{4,12},{8,0},{12,4},{1,9},{5,13},{9,1},{13,5},{2,10},{6,14},... | collective-permute-start | bytes 1179656 | tf_op jit(solution)/shard_map/ppermute | solution.py:26
  266.8 28.0 %collective-permute-start.17 = (bf16[48,4096]{1,0:T(8,128)(2,1)S(1)}, bf16[48,4096]{1,0:T(8,128)(2,1)S(1)}, u32[]{:S(2)}, u32[]{:S(2)}) collective-permute-start(bf16[48,4096]{1,0:T(8,128)(2,1)S(1)} %get-tuple-element.32), channel_id=1, source_target_pairs={{0,8},{4,12},{8,0},{12,4},{1,9},{5,13},{9,1},{13,5},{2,10},{6,14},... | collective-permute-start | bytes 1179656 | tf_op jit(solution)/shard_map/ppermute | solution.py:26
  291.2 50.5 %collective-permute-start.21 = (bf16[48,4096]{1,0:T(8,128)(2,1)S(1)}, bf16[48,4096]{1,0:T(8,128)(2,1)S(1)}, u32[]{:S(2)}, u32[]{:S(2)}) collective-permute-start(bf16[48,4096]{1,0:T(8,128)(2,1)S(1)} %get-tuple-element.30), channel_id=1, source_target_pairs={{0,8},{4,12},{8,0},{12,4},{1,9},{5,13},{9,1},{13,5},{2,10},{6,14},... | collective-permute-start | bytes 1179656 | tf_op jit(solution)/shard_map/ppermute | solution.py:26
  292.8 19.0 %collective-permute-start.35 = (bf16[48,4096]{1,0:T(8,128)(2,1)S(1)}, bf16[48,4096]{1,0:T(8,128)(2,1)S(1)}, u32[]{:S(2)}, u32[]{:S(2)}) collective-permute-start(bf16[48,4096]{1,0:T(8,128)(2,1)S(1)} %get-tuple-element.22), channel_id=1, source_target_pairs={{0,8},{4,12},{8,0},{12,4},{1,9},{5,13},{9,1},{13,5},{2,10},{6,14},... | collective-permute-start | bytes 1179656 | tf_op jit(solution)/shard_map/ppermute | solution.py:26
  293.4 26.8 %collective-permute-start.39 = (bf16[48,4096]{1,0:T(8,128)(2,1)S(1)}, bf16[48,4096]{1,0:T(8,128)(2,1)S(1)}, u32[]{:S(2)}, u32[]{:S(2)}) collective-permute-start(bf16[48,4096]{1,0:T(8,128)(2,1)S(1)} %get-tuple-element.24), channel_id=1, source_target_pairs={{0,8},{4,12},{8,0},{12,4},{1,9},{5,13},{9,1},{13,5},{2,10},{6,14},... | collective-permute-start | bytes 1179656 | tf_op jit(solution)/shard_map/ppermute | solution.py:26
  294.9 33.8 %collective-permute-start.37 = (bf16[48,4096]{1,0:T(8,128)(2,1)S(1)}, bf16[48,4096]{1,0:T(8,128)(2,1)S(1)}, u32[]{:S(2)}, u32[]{:S(2)}) collective-permute-start(bf16[48,4096]{1,0:T(8,128)(2,1)S(1)} %get-tuple-element.25), channel_id=1, source_target_pairs={{0,8},{4,12},{8,0},{12,4},{1,9},{5,13},{9,1},{13,5},{2,10},{6,14},... | collective-permute-start | bytes 1179656 | tf_op jit(solution)/shard_map/ppermute | solution.py:26
  297.2 63.4 %collective-permute-start.41 = (bf16[48,4096]{1,0:T(8,128)(2,1)S(1)}, bf16[48,4096]{1,0:T(8,128)(2,1)S(1)}, u32[]{:S(2)}, u32[]{:S(2)}) collective-permute-start(bf16[48,4096]{1,0:T(8,128)(2,1)S(1)} %get-tuple-element.23), channel_id=1, source_target_pairs={{0,8},{4,12},{8,0},{12,4},{1,9},{5,13},{9,1},{13,5},{2,10},{6,14},... | collective-permute-start | bytes 1179656 | tf_op jit(solution)/shard_map/ppermute | solution.py:26
  311.8 29.9 %collective-permute-start.16 = (bf16[48,4096]{1,0:T(8,128)(2,1)S(1)}, bf16[48,4096]{1,0:T(8,128)(2,1)S(1)}, u32[]{:S(2)}, u32[]{:S(2)}) collective-permute-start(bf16[48,4096]{1,0:T(8,128)(2,1)S(1)} %get-tuple-element.26), channel_id=1, source_target_pairs={{0,1},{1,2},{2,3},{3,0},{4,5},{5,6},{6,7},{7,4},{8,9},{9,10},{10,1... | collective-permute-start | bytes 1179656 | tf_op jit(solution)/shard_map/ppermute | solution.py:21
  320.2 25.3 %collective-permute-start.20 = (bf16[48,4096]{1,0:T(8,128)(2,1)S(1)}, bf16[48,4096]{1,0:T(8,128)(2,1)S(1)}, u32[]{:S(2)}, u32[]{:S(2)}) collective-permute-start(bf16[48,4096]{1,0:T(8,128)(2,1)S(1)} %get-tuple-element.27), channel_id=1, source_target_pairs={{0,3},{1,0},{2,1},{3,2},{4,7},{5,4},{6,5},{7,6},{8,11},{9,8},{10,9... | collective-permute-start | bytes 1179656 | tf_op jit(solution)/shard_map/ppermute | solution.py:21
  328.6 29.8 %collective-permute-start.18 = (bf16[48,4096]{1,0:T(8,128)(2,1)S(1)}, bf16[48,4096]{1,0:T(8,128)(2,1)S(1)}, u32[]{:S(2)}, u32[]{:S(2)}) collective-permute-start(bf16[48,4096]{1,0:T(8,128)(2,1)S(1)} %get-tuple-element.28), channel_id=1, source_target_pairs={{0,2},{1,3},{2,0},{3,1},{4,6},{5,7},{6,4},{7,5},{8,10},{9,11},{10,... | collective-permute-start | bytes 1179656 | tf_op jit(solution)/shard_map/ppermute | solution.py:21
  341.7 18.9 %collective-permute-start.36 = (bf16[48,4096]{1,0:T(8,128)(2,1)S(1)}, bf16[48,4096]{1,0:T(8,128)(2,1)S(1)}, u32[]{:S(2)}, u32[]{:S(2)}) collective-permute-start(bf16[48,4096]{1,0:T(8,128)(2,1)S(1)} %get-tuple-element.19), channel_id=1, source_target_pairs={{0,1},{1,2},{2,3},{3,0},{4,5},{5,6},{6,7},{7,4},{8,9},{9,10},{10,1... | collective-permute-start | bytes 1179656 | tf_op jit(solution)/shard_map/ppermute | solution.py:21
  341.7 21.8 %collective-permute-start.40 = (bf16[48,4096]{1,0:T(8,128)(2,1)S(1)}, bf16[48,4096]{1,0:T(8,128)(2,1)S(1)}, u32[]{:S(2)}, u32[]{:S(2)}) collective-permute-start(bf16[48,4096]{1,0:T(8,128)(2,1)S(1)} %get-tuple-element.20), channel_id=1, source_target_pairs={{0,3},{1,0},{2,1},{3,2},{4,7},{5,4},{6,5},{7,6},{8,11},{9,8},{10,9... | collective-permute-start | bytes 1179656 | tf_op jit(solution)/shard_map/ppermute | solution.py:21
  345.5 34.8 %collective-permute-start.38 = (bf16[48,4096]{1,0:T(8,128)(2,1)S(1)}, bf16[48,4096]{1,0:T(8,128)(2,1)S(1)}, u32[]{:S(2)}, u32[]{:S(2)}) collective-permute-start(bf16[48,4096]{1,0:T(8,128)(2,1)S(1)} %get-tuple-element.21), channel_id=1, source_target_pairs={{0,2},{1,3},{2,0},{3,1},{4,6},{5,7},{6,4},{7,5},{8,10},{9,11},{10,... | collective-permute-start | bytes 1179656 | tf_op jit(solution)/shard_map/ppermute | solution.py:21
  (8 other events, 21.4 us)

commit v3 on v1

v3 whole, which is shorter than its diff:
```python
import functools

import jax
import jax.numpy as jnp
from jax import lax
from jax.experimental import pallas as pl
from jax.experimental.pallas import tpu as pltpu
from jax.sharding import PartitionSpec as P

CORE, CHIP = 1, 2
PARTS = 3
VMEM_BYTES = 56 * 1024 * 1024


def dot(left, right, left_dim, right_dim):
    return lax.dot_general(
        left, right, (((left_dim,), (right_dim,)), ((), ())), preferred_element_type=jnp.float32
    )


def after(array, *others):
    return lax.optimization_barrier((array, *others))[0]


def wide(block):
    return block.astype(jnp.float32)


def narrow(block):
    return block.astype(jnp.bfloat16)


def contract_kernel(n_pieces, n_weights, right_dim, *refs):
    pieces, weights = refs[:n_pieces], refs[n_pieces : n_pieces + n_weights]
    outs, total = refs[n_pieces + n_weights : -1], refs[-1]
    step = pl.program_id(0)

    @pl.when(step == 0)
    def _():
        total[...] = jnp.zeros_like(total)

    rows = jnp.concatenate([piece[...] for piece in pieces], axis=0)
    for i, weight in enumerate(weights):
        total[i] += dot(rows, weight[...], 1, right_dim)

    @pl.when(step == pl.num_programs(0) - 1)
    def _():
        size = outs[0].shape[0]
        for i, out in enumerate(outs):
            group, weight = divmod(i, n_weights)
            out[...] = narrow(total[weight, group * size : (group + 1) * size])


def contract(groups, weights, right_dim):
    pieces = sum(groups, [])
    arrays = [array for array, _ in pieces]
    size, width = arrays[0].shape[1:]
    units = weights[0].shape[1 - right_dim]
    block = min(1024, width)
    if right_dim == 0:
        weight_spec = pl.BlockSpec((block, units), lambda k: (k, 0))
    else:
        weight_spec = pl.BlockSpec((units, block), lambda k: (0, k))
    shape = (size * len(groups[0]), units)
    n_outs = len(groups) * len(weights)
    return pl.pallas_call(
        functools.partial(contract_kernel, len(pieces), len(weights), right_dim),
        grid=(width // block,),
        in_specs=[
            pl.BlockSpec((None, size, block), lambda k, index=index: (index, 0, k))
            for _, index in pieces
        ]
        + [weight_spec] * len(weights),
        out_specs=[pl.BlockSpec(shape, lambda k: (0, 0))] * n_outs,
        out_shape=[jax.ShapeDtypeStruct(shape, jnp.bfloat16)] * n_outs,
        scratch_shapes=[pltpu.VMEM((len(weights), size * len(pieces), units), jnp.float32)],
        compiler_params=pltpu.CompilerParams(vmem_limit_bytes=VMEM_BYTES),
        cost_estimate=pl.CostEstimate(flops=1000, bytes_accessed=1000, transcendentals=0),
    )(*arrays, *weights)


def expand_kernel(n, right_dim, *refs):
    lefts, weights, outs = refs[:n], refs[n : 2 * n], refs[2 * n :]
    total = sum(dot(left[...], weight[...], 1, right_dim) for left, weight in zip(lefts, weights))
    half = total.shape[0] // 2
    outs[0][...] = narrow(total[:half])
    outs[1][...] = narrow(total[half:])


def expand(lefts, weights, right_dim):
    rows, units = lefts[0].shape
    width = weights[0].shape[1 - right_dim]
    block = min(512, width)
    if right_dim == 0:
        weight_spec = pl.BlockSpec((units, block), lambda j: (0, j))
    else:
        weight_spec = pl.BlockSpec((block, units), lambda j: (j, 0))
    out = jax.ShapeDtypeStruct((rows // 2, width), jnp.bfloat16)
    halves = pl.pallas_call(
        functools.partial(expand_kernel, len(lefts), right_dim),
        grid=(width // block,),
        in_specs=[pl.BlockSpec((rows, units), lambda j: (0, 0))] * len(lefts)
        + [weight_spec] * len(weights),
        out_specs=[pl.BlockSpec((rows // 2, block), lambda j: (0, j))] * 2,
        out_shape=[out, out],
        compiler_params=pltpu.CompilerParams(vmem_limit_bytes=VMEM_BYTES),
        cost_estimate=pl.CostEstimate(flops=1000, bytes_accessed=1000, transcendentals=0),
    )(*lefts, *weights)
    return list(halves)


def swap(block, bit):
    n = lax.axis_size("col")
    return lax.ppermute(block, "col", [(i, i ^ bit) for i in range(n)])


def row_moves(partial):
    n = lax.axis_size("row")
    return [
        lax.ppermute(partial, "row", [(i, (i + step) % n) for i in range(n)])
        for step in range(1, n)
    ]


def row_sum(partial, moved, *others):
    return sum([wide(after(block, *others)) for block in moved], wide(partial))


def line_gather(*shards):
    return lax.all_gather(jnp.stack(shards), "depth", axis=1, tiled=True)


def line_scatter(line):
    return wide(lax.psum_scatter(line, "depth", scatter_dimension=0, tiled=True))


def cut(array, part):
    tiles = array.shape[1] // 128
    first, last = (128 * (tiles * i // PARTS) for i in (part, part + 1))
    return array[:, first:last]


def add(*blocks):
    return narrow(sum(wide(block) for block in blocks))


def grads_of(gate, up, hidden_grad):
    sigma = jax.nn.sigmoid(gate)
    gate_grad = narrow(hidden_grad * up * sigma * (1.0 + gate * (1.0 - sigma)))
    return gate_grad, narrow(hidden_grad * (gate * sigma))


def hidden_of(gate, up):
    return narrow(gate * jax.nn.sigmoid(gate) * up)


def body(tokens, gate_weight, up_weight, down_weight, cotangent):
    cotangent_next = swap(cotangent, CHIP)
    token_near = after(line_gather(tokens), cotangent_next)
    cotangents = line_gather(after(cotangent, token_near), after(cotangent_next, token_near))
    token_far = swap(token_near, CHIP)
    token_near = [token_near, swap(token_near, CORE)]

    pieces = [(array, 0) for array in token_near]
    (gate_near,) = contract([pieces], [gate_weight], 0)
    gate_moved = row_moves(gate_near)
    pieces[0] = (after(token_near[0], gate_near), 0)
    (up_near,) = contract([pieces], [up_weight], 0)
    up_moved = row_moves(after(up_near, *gate_moved))

    token_far = after(token_far, *up_moved)
    token_far = [token_far, swap(token_far, CORE)]
    gate_near, up_near = row_sum(gate_near, gate_moved), row_sum(up_near, up_moved)
    hidden_near = hidden_of(gate_near, up_near)
    pieces = [(after(token_far[0], hidden_near), 0), (token_far[1], 0)]
    gate_far, up_far = contract([pieces], [gate_weight, up_weight], 0)
    gate_moved = row_moves(gate_far)

    mixed_near = expand([after(hidden_near, up_far)], [down_weight], 0)
    mixed_near[1] = swap(mixed_near[1], CORE)
    cotangents = after(cotangents, up_far)
    cotangents = [cotangents, swap(cotangents, CORE)]
    first = after(cotangents[0], *gate_moved, *mixed_near[:1])
    up_moved = row_moves(after(up_far, *gate_moved))
    groups = [[(first, i), (cotangents[1], i)] for i in (1, 0)]
    grad_far, grad_near = contract(groups, [down_weight], 1)
    mixed_near = add(mixed_near[0], after(mixed_near[1], grad_far))

    gate_far = row_sum(gate_far, gate_moved)
    up_far = row_sum(up_far, up_moved, grad_far, mixed_near)
    mixed_near = line_scatter(mixed_near)
    grad_far_moved = row_moves(after(grad_far, *up_moved))
    hidden_far = hidden_of(gate_far, up_far)
    mixed_far = expand([hidden_far], [down_weight], 0)
    mixed_far[1] = swap(mixed_far[1], CORE)
    grad_far = row_sum(grad_far, grad_far_moved, mixed_far[0])
    grad_near_moved = row_moves(after(grad_near, *grad_far_moved))
    far_grads = grads_of(gate_far, up_far, grad_far)
    mine, other = expand(far_grads, [gate_weight, up_weight], 1)
    mixed_far = add(mixed_far[0], after(mixed_far[1], mine))
    other = swap(after(other, mixed_far, *grad_near_moved), CORE)
    mixed_far = line_scatter(mixed_far)

    far_sums = [add(cut(mine, 0), cut(other, 0))]
    grad_near = row_sum(grad_near, grad_near_moved, *far_sums)
    near_grads = grads_of(gate_near, up_near, grad_near)
    for part in range(1, PARTS):
        far_sums.append(add(cut(mine, part), cut(after(other, *near_grads), part)))
    token_all = jnp.concatenate([array[0] for array in token_near + token_far], axis=0)
    cotangent_all = jnp.concatenate([array[i] for i in (0, 1) for array in cotangents], axis=0)
    gate_grad, up_grad = (jnp.concatenate(pair, axis=0) for pair in zip(near_grads, far_grads))
    hidden = jnp.concatenate([hidden_near, hidden_far], axis=0)

    moved = swap(far_sums[0], CHIP)
    mine, other = expand(near_grads, [gate_weight, up_weight], 1)
    other = swap(other, CORE)
    lines = [add(cut(mine, 0), cut(other, 0), after(moved, mine))]
    moved = swap(after(far_sums[1], moved), CHIP)
    gate_total = dot(token_all, after(gate_grad, *lines), 0, 0)
    lines.append(add(cut(mine, 1), cut(other, 1), after(moved, gate_total)))
    moved = swap(after(far_sums[2], moved, gate_total), CHIP)
    up_total = dot(token_all, after(up_grad, *lines), 0, 0)
    lines.append(add(cut(mine, 2), cut(other, 2), after(moved, up_total)))
    down_total = dot(after(hidden, *lines), cotangent_all, 0, 0)
    mixed = mixed_near + wide(swap(after(narrow(mixed_far), *lines), CHIP))
    token_grad = jnp.concatenate([line_scatter(line) for line in lines], axis=1)
    return (mixed, token_grad, gate_total, up_total, down_total)


def solution(mesh):
    activations = P(("depth", "col"), "row")
    wide_weight = P("row", ("col", "depth"))
    tall_weight = P(("col", "depth"), "row")
    return jax.shard_map(
        body,
        mesh=mesh,
        in_specs=(activations, wide_weight, wide_weight, tall_weight, activations),
        out_specs=(activations, activations, wide_weight, wide_weight, tall_weight),
        check_vma=False,
    )
```

time: 392 us -> 353 us (0.901)
  Pallas kernels: 0 us -> 81.9 us
  waiting for transfers between devices: 229 us -> 156 us
  matrix products: 104 us -> 35.1 us
  other arithmetic: 8.32 us -> 34.6 us
  local copies, waits for them, and re-layouts: 32.4 us -> 10.3 us
  starting transfers between devices: 3.7 us -> 18.7 us
    pallas_call x0 -> x8, Pallas kernels: none -> 81.9 us  [the longest x4 43.8 us: expand(): pl.pallas_call(functools.partial(expand_kernel, len(lefts), right_dim), g...]
    all_gather x2, waiting for transfers between devices: 104 us -> 29.1 us  [line_gather(): return lax.all_gather(jnp.stack(shards), 'depth', axis=1, tiled=True)]
    dot_general x9 -> x3, matrix products: 104 us -> 35.1 us  [dot(): lax.dot_general(left, right, (((left_dim,), (right_dim,)), ((), ())), pre...]
    ppermute x3 -> x19, waiting for transfers between devices: 30.9 us -> 93.5 us  [the longest x6 68.1 us: row_moves(): lax.ppermute(partial, 'row', [(i, (i + step) % n) for i in range(n)])]
    reduce_scatter x2 -> x5, waiting for transfers between devices: 92.5 us -> 33 us  [line_scatter(): lax.psum_scatter(line, 'depth', scatter_dimension=0, tiled=True)]
    unnamed x14 -> x62, local copies, waits for them, and re-layouts: 32.4 us -> 6.42 us
    convert_element_type x3 -> x11, other arithmetic: 8.32 us -> 25.6 us  [narrow(): return block.astype(jnp.bfloat16)]
    ppermute x3 -> x19, starting transfers between devices: 3.55 us -> 18 us  [the longest x13 10.1 us: swap(): return lax.ppermute(block, 'col', [(i, i ^ bit) for i in range(n)])]
  transfers between devices with their start and end apart: 7 -> 26, of which waited for: 5 -> 14; matrix products, arithmetic and copies ran while one was open for 29% -> 19% of each run, Pallas kernels for 0% -> 21%
where the time goes in v3:
time: 353 us; the launch traced here: 351 us
  waiting for transfers between devices  156 us (44%)
  Pallas kernels  81.9 us (23%)
  matrix products  35.1 us (10%)
  other arithmetic  34.6 us (10%)
  starting transfers between devices  18.7 us (5%)
  between operations  14.3 us (4%)
  local copies, waits for them, and re-layouts  10.3 us (3%)
    ppermute x6, waiting for transfers between devices, row_moves(): lax.ppermute(partial, 'row', [(i, (i + step) % n) for i in range(n)])  68.1 us
    pallas_call x4, Pallas kernels, expand(): pl.pallas_call(functools.partial(expand_kernel, len(lefts), right_dim), g...  43.8 us
    pallas_call x4, Pallas kernels, contract(): pl.pallas_call(functools.partial(contract_kernel, len(pieces), len(weight...  38.1 us
    dot_general x3, matrix products, dot(): lax.dot_general(left, right, (((left_dim,), (right_dim,)), ((), ())), pre...  35.1 us
    reduce_scatter x5, waiting for transfers between devices, line_scatter(): lax.psum_scatter(line, 'depth', scatter_dimension=0, tiled=True)  33 us
    all_gather x2, waiting for transfers between devices, line_gather(): return lax.all_gather(jnp.stack(shards), 'depth', axis=1, tiled=True)  29.1 us
    convert_element_type x11, other arithmetic, narrow(): return block.astype(jnp.bfloat16)  25.6 us
    ppermute x13, waiting for transfers between devices, swap(): return lax.ppermute(block, 'col', [(i, i ^ bit) for i in range(n)])  25.4 us
  transfers between devices with their start and end apart: 26, of which 14 were waited for; matrix products, arithmetic and copies ran while one was open for 19% of the time, Pallas kernels for 21%

profile of v3, /device:TPU:0, one launch (start us, length us, event | category | flops | bytes accessed | tf_op | source)
XLA Modules:
  0.0 351.3 jit_solution(7540443036184502244)
XLA Ops:
  7.9 3.0 collective-permute-start
  11.0 9.3 %collective-permute-done = bf16[48,4096]{1,0:T(8,128)(2,1)S(1)} collective-permute-done((bf16[48,4096]{1,0:T(8,128)(2,1)}, bf16[48,4096]{1,0:T(8,128)(2,1)S(1)}, u32[]{:S(2)}, u32[]{:S(2)}) %collective-permute-start) | collective-permute-done | bytes 393248 | tf_op jit(solution)/shard_map/ppermute | solution.py:114
  20.3 29.1 %all-gather.6.cloned.1.call-done = bf16[192,4096]{1,0:T(8,128)(2,1)} async-done(((bf16[48,4096]{1,0:T(8,128)(2,1)}), bf16[192,4096]{1,0:T(8,128)(2,1)}) %all-gather.6.cloned.1.call-update) | async-done | bytes 1572880 | tf_op jit(solution)/shard_map/all_gather | solution.py:130
  49.4 2.1 pad_maximum_fusion.6
  51.6 1.5 collective-permute-start.4
  53.2 1.9 collective-permute-done.1.refs_1_
  56.2 7.9 %shard_map.92 = bf16[384,896]{1,0:T(8,128)(2,1)} custom-call(bf16[1,192,4096]{2,1,0:T(8,128)(2,1)} %bitcast.18, bf16[1,192,4096]{2,1,0:T(8,128)(2,1)} %copy-done.5, bf16[4096,896]{1,0:T(8,128)(2,1)} %refs_2_.9), custom_call_target="tpu_custom_call" | custom-call | flops 1000 | bytes 1000 | tf_op jit(solution)/shard_map/pallas_call | solution.py:66
  64.0 1.5 collective-permute-start.2
  65.6 7.7 %shard_map.93 = bf16[384,896]{1,0:T(8,128)(2,1)} custom-call(bf16[1,192,4096]{2,1,0:T(8,128)(2,1)} %bitcast.19, bf16[1,192,4096]{2,1,0:T(8,128)(2,1)} %copy-done.5, bf16[4096,896]{1,0:T(8,128)(2,1)} %refs_3_.5), custom_call_target="tpu_custom_call" | custom-call | flops 1000 | bytes 1000 | tf_op jit(solution)/shard_map/pallas_call | solution.py:66
  73.2 8.5 %collective-permute-done.2 = bf16[384,896]{1,0:T(8,128)(2,1)S(1)} collective-permute-done((bf16[384,896]{1,0:T(8,128)(2,1)}, bf16[384,896]{1,0:T(8,128)(2,1)S(1)}, u32[]{:S(2)}, u32[]{:S(2)}) %collective-permute-start.2) | collective-permute-done | bytes 688160 | tf_op jit(solution)/shard_map/ppermute | solution.py:120
  81.8 1.5 collective-permute-start.3
  83.2 5.2 %collective-permute-done.4.refs_0_ = bf16[1,192,4096]{2,1,0:T(8,128)(2,1)S(1)} collective-permute-done((bf16[1,192,4096]{2,1,0:T(8,128)(2,1)S(1)}, bf16[1,192,4096]{2,1,0:T(8,128)(2,1)S(1)}, u32[]{:S(2)}, u32[]{:S(2)}) %collective-permute-start.4) | collective-permute-done | bytes 1572896 | tf_op jit(solution)/shard_map/ppermute | solution.py:114
  88.4 10.3 %collective-permute-done.3 = bf16[384,896]{1,0:T(8,128)(2,1)S(1)} collective-permute-done((bf16[384,896]{1,0:T(8,128)(2,1)}, bf16[384,896]{1,0:T(8,128)(2,1)S(1)}, u32[]{:S(2)}, u32[]{:S(2)}) %collective-permute-start.3) | collective-permute-done | bytes 688160 | tf_op jit(solution)/shard_map/ppermute | solution.py:120
  98.8 2.8 multiply_convert_fusion.5.refs_0_
  103.3 11.6 %shard_map.94 = (bf16[384,896]{1,0:T(8,128)(2,1)}, bf16[384,896]{1,0:T(8,128)(2,1)}) custom-call(bf16[1,192,4096]{2,1,0:T(8,128)(2,1)} %copy-done.22, bf16[1,192,4096]{2,1,0:T(8,128)(2,1)} %copy-done.23, bf16[4096,896]{1,0:T(8,128)(2,1)} %refs_2_.9, bf16[4096,896]{1,0:T(8,128)(2,1)} %refs_3_.5), custom_call_target="tpu_custom_call" | custom-call | flops 1000 | bytes 1000 | tf_op jit(solution)/shard_map/pallas_call | solution.py:66
  115.1 9.1 %shard_map.95 = (bf16[192,4096]{1,0:T(8,128)(2,1)}, bf16[192,4096]{1,0:T(8,128)(2,1)}) custom-call(bf16[384,896]{1,0:T(8,128)(2,1)} %multiply_convert_fusion.5.refs_0_, bf16[896,4096]{1,0:T(8,128)(2,1)} %refs_1_.3), custom_call_target="tpu_custom_call" | custom-call | flops 1000 | bytes 1000 | tf_op jit(solution)/shard_map/pallas_call | solution.py:99
  124.5 1.4 collective-permute-start.7
  125.9 16.2 %collective-permute-done.7 = bf16[384,896]{1,0:T(8,128)(2,1)S(1)} collective-permute-done((bf16[384,896]{1,0:T(8,128)(2,1)S(1)}, bf16[384,896]{1,0:T(8,128)(2,1)S(1)}, u32[]{:S(2)}, u32[]{:S(2)}) %collective-permute-start.7) | collective-permute-done | bytes 688160 | tf_op jit(solution)/shard_map/ppermute | solution.py:120
  142.1 1.4 collective-permute-start.9
  143.5 1.7 copy-done.1
  145.2 11.0 %shard_map.96 = (bf16[384,896]{1,0:T(8,128)(2,1)}, bf16[384,896]{1,0:T(8,128)(2,1)}) custom-call(bf16[2,192,4096]{2,1,0:T(8,128)(2,1)} %all-gather.4.cloned.1.call-done.refs_0_.refs_2_, bf16[2,192,4096]{2,1,0:T(8,128)(2,1)} %copy-done.1, bf16[2,192,4096]{2,1,0:T(8,128)(2,1)} %all-gather.4.cloned.1.call-done.refs_0_.refs_2_, bf16[2,192,4096]{2,1,0:T(8,128)(2,1)} %copy-done.1, ...), custom_call_target="tpu_custom_call" | custom-call | flops 1000 | bytes 1000 | tf_op jit(solution)/shard_map/pallas_call | solution.py:66
  156.2 3.1 add_convert_fusion.1
  160.7 9.1 %shard_map.97 = (bf16[192,4096]{1,0:T(8,128)(2,1)}, bf16[192,4096]{1,0:T(8,128)(2,1)}) custom-call(bf16[384,896]{1,0:T(8,128)(2,1)} %multiply_convert_fusion.4.refs_0_, bf16[896,4096]{1,0:T(8,128)(2,1)} %refs_1_.3), custom_call_target="tpu_custom_call" | custom-call | flops 1000 | bytes 1000 | tf_op jit(solution)/shard_map/pallas_call | solution.py:99
  170.8 16.8 %collective-permute-done.11 = bf16[384,896]{1,0:T(8,128)(2,1)S(1)} collective-permute-done((bf16[384,896]{1,0:T(8,128)(2,1)S(1)}, bf16[384,896]{1,0:T(8,128)(2,1)S(1)}, u32[]{:S(2)}, u32[]{:S(2)}) %collective-permute-start.11) | collective-permute-done | bytes 688160 | tf_op jit(solution)/shard_map/ppermute | solution.py:120
  187.6 2.1 multiply_convert_fusion.2
  189.7 12.8 %shard_map.98 = (bf16[192,4096]{1,0:T(8,128)(2,1)}, bf16[192,4096]{1,0:T(8,128)(2,1)}) custom-call(bf16[384,896]{1,0:T(8,128)(2,1)} %get-tuple-element.96.refs_0_, bf16[384,896]{1,0:T(8,128)(2,1)} %get-tuple-element.95.refs_1_, bf16[4096,896]{1,0:T(8,128)(2,1)} %refs_2_.9, bf16[4096,896]{1,0:T(8,128)(2,1)} %refs_3_.5), custom_call_target="tpu_custom_call" | custom-call | flops 1000 | bytes 1000 | tf_op jit(solution)/shard_map/pallas_call | solution.py:99
  202.6 1.8 add_convert_fusion
  205.6 16.3 %collective-permute-done.12 = bf16[384,896]{1,0:T(8,128)(2,1)} collective-permute-done((bf16[384,896]{1,0:T(8,128)(2,1)}, bf16[384,896]{1,0:T(8,128)(2,1)}, u32[]{:S(2)}, u32[]{:S(2)}) %collective-permute-start.12) | collective-permute-done | bytes 688160 | tf_op jit(solution)/shard_map/ppermute | solution.py:120
  221.9 1.9 slice_bitcast_fusion.3
  226.3 2.2 add_convert_fusion.7
  228.5 3.2 multiply_convert_fusion
  231.7 12.8 %shard_map.99 = (bf16[192,4096]{1,0:T(8,128)(2,1)}, bf16[192,4096]{1,0:T(8,128)(2,1)}) custom-call(bf16[384,896]{1,0:T(8,128)(2,1)} %get-tuple-element.94.refs_0_, bf16[384,896]{1,0:T(8,128)(2,1)} %get-tuple-element.93.refs_1_, bf16[4096,896]{1,0:T(8,128)(2,1)} %refs_2_.9, bf16[4096,896]{1,0:T(8,128)(2,1)} %refs_3_.5), custom_call_target="tpu_custom_call" | custom-call | flops 1000 | bytes 1000 | tf_op jit(solution)/shard_map/pallas_call | solution.py:99
  245.2 2.0 slice_bitcast_fusion.1
  247.2 1.5 collective-permute-start.15
  248.7 1.8 pad_maximum_fusion.1
  250.4 2.6 add_convert_fusion.3
  253.0 7.5 %collective-permute-done.15 = bf16[192,1280]{1,0:T(8,128)(2,1)S(1)} collective-permute-done((bf16[192,1280]{1,0:T(8,128)(2,1)}, bf16[192,1280]{1,0:T(8,128)(2,1)S(1)}, u32[]{:S(2)}, u32[]{:S(2)}) %collective-permute-start.15) | collective-permute-done | bytes 491552 | tf_op jit(solution)/shard_map/ppermute | solution.py:114
  260.5 1.5 collective-permute-start.16
  263.1 2.0 add_convert_fusion.6
  265.2 11.9 %fusion.11 = f32[4096,896]{1,0:T(8,128)} fusion(bf16[768,896]{1,0:T(8,128)(2,1)} %get-tuple-element.80, bf16[192,4096]{1,0:T(8,128)(2,1)} %bitcast.26, bf16[192,4096]{1,0:T(8,128)(2,1)} %bitcast.24, bf16[192,4096]{1,0:T(8,128)(2,1)S(1)} %bitcast.22, bf16[192,4096]{1,0:T(8,128)(2,1)S(1)} %copy-done.4), kind=kOutput, calls=%fused_computation.39 | convolution fusion | flops 5662310400 | bytes 22347776 | tf_op jit(solution)/shard_map/dot_general | solution.py:16
  277.1 2.4 add_convert_fusion.4
  280.3 11.9 %fusion.10 = f32[4096,896]{1,0:T(8,128)} fusion(bf16[768,896]{1,0:T(8,128)(2,1)} %get-tuple-element.83, bf16[192,4096]{1,0:T(8,128)(2,1)} %bitcast.27, bf16[192,4096]{1,0:T(8,128)(2,1)} %bitcast.25, bf16[192,4096]{1,0:T(8,128)(2,1)S(1)} %bitcast.23, bf16[192,4096]{1,0:T(8,128)(2,1)S(1)} %copy-done.4), kind=kOutput, calls=%fused_computation.38 | convolution fusion | flops 5662310400 | bytes 22347776 | tf_op jit(solution)/shard_map/dot_general | solution.py:16
  293.2 2.2 add_convert_fusion.2
  296.2 11.3 %fusion = f32[896,4096]{1,0:T(8,128)} fusion(bf16[768,896]{1,0:T(8,128)(2,1)} %pad_maximum_fusion.3, bf16[192,4096]{1,0:T(8,128)(2,1)} %get-tuple-element.90, bf16[192,4096]{1,0:T(8,128)(2,1)} %get-tuple-element.88, bf16[192,4096]{1,0:T(8,128)(2,1)} %get-tuple-element.89, bf16[192,4096]{1,0:T(8,128)(2,1)S(1)} %copy-done.25), kind=kOutput, calls=%fused_computation.1 | convolution fusion | flops 5662310400 | bytes 22347776 | tf_op jit(solution)/shard_map/dot_general | solution.py:16
  307.5 2.0 convert_add_fusion.6
  309.4 10.0 %reduce-scatter.12.cloned.1.call-done = bf16[48,1408]{1,0:T(8,128)(2,1)} async-done(((bf16[192,1408]{1,0:T(8,128)(2,1)}), bf16[48,1408]{1,0:T(8,128)(2,1)}) %reduce-scatter.12.cloned.1.call-update) | async-done | bytes 135184 | tf_op jit(solution)/shard_map/reduce_scatter | solution.py:134
  319.5 23.0 %reduce-scatter.14.cloned.1.call-done = bf16[48,1408]{1,0:T(8,128)(2,1)} async-done(((bf16[192,1408]{1,0:T(8,128)(2,1)}), bf16[48,1408]{1,0:T(8,128)(2,1)}) %reduce-scatter.14.cloned.1.call-update) | async-done | bytes 135184 | tf_op jit(solution)/shard_map/reduce_scatter | solution.py:134
  342.4 2.0 maximum_convert_fusion
  (102 shorter events, 15.0 us)
Async XLA Ops:
  7.2 42.2 %all-gather.6.cloned.1.call-start = ((), (), s32[]{:S(2)}) async-start(), calls=%async_computation.11 | async-start | bytes 1966080 | tf_op jit(solution)/shard_map/all_gather | solution.py:130
  7.9 107.0 %all-gather.4.cloned.1.call-start = ((), (), s32[]{:S(2)}) async-start(), calls=%async_computation.5 | async-start | bytes 3932160 | tf_op jit(solution)/shard_map/all_gather | solution.py:130
  7.9 12.4 %collective-permute-start = (bf16[48,4096]{1,0:T(8,128)(2,1)}, bf16[48,4096]{1,0:T(8,128)(2,1)S(1)}, u32[]{:S(2)}, u32[]{:S(2)}) collective-permute-start(bf16[48,4096]{1,0:T(8,128)(2,1)} %param.9), channel_id=1, source_target_pairs={{0,8},{4,12},{8,0},{12,4},{1,9},{5,13},{9,1},{13,5},{2,10},{6,14},... | collective-permute-start | bytes 1179656 | tf_op jit(solution)/shard_map/ppermute | solution.py:114
  51.5 243.9 %reduce-scatter.8.cloned.1.call-start = ((), (), s32[]{:S(2)}) async-start(), calls=%async_computation.7 | async-start | bytes 1966080 | tf_op jit(solution)/shard_map/reduce_scatter | solution.py:134
  51.5 3.5 collective-permute-start.1
  51.6 36.8 %collective-permute-start.4 = (bf16[1,192,4096]{2,1,0:T(8,128)(2,1)S(1)}, bf16[1,192,4096]{2,1,0:T(8,128)(2,1)S(1)}, u32[]{:S(2)}, u32[]{:S(2)}) collective-permute-start(bf16[1,192,4096]{2,1,0:T(8,128)(2,1)S(1)} %bitcast.21), channel_id=1, source_target_pairs={{0,8},{4,12},{8,0},{12,4},{1,9},{5,13},{9,1},{13,5},{2,10},{6,14},... | collective-permute-start | bytes 4718600 | tf_op jit(solution)/shard_map/ppermute | solution.py:114
  64.0 34.7 %copy-start.13 = (bf16[384,896]{1,0:T(8,128)(2,1)S(1)}, bf16[384,896]{1,0:T(8,128)(2,1)}, u32[]{:S(2)}) copy-start(bf16[384,896]{1,0:T(8,128)(2,1)} %shard_map.92) | copy-start | bytes 2064388
  64.0 17.7 %collective-permute-start.2 = (bf16[384,896]{1,0:T(8,128)(2,1)}, bf16[384,896]{1,0:T(8,128)(2,1)S(1)}, u32[]{:S(2)}, u32[]{:S(2)}) collective-permute-start(bf16[384,896]{1,0:T(8,128)(2,1)} %shard_map.92), channel_id=1, source_target_pairs={{0,16},{16,0},{1,17},{17,1},{2,18},{18,2},{3,19},{19,3},{4,20},{20... | collective-permute-start | bytes 2064392 | tf_op jit(solution)/shard_map/ppermute | solution.py:120
  81.8 19.8 %copy-start.16 = (bf16[384,896]{1,0:T(8,128)(2,1)}, bf16[384,896]{1,0:T(8,128)(2,1)S(1)}, u32[]{:S(2)}) copy-start(bf16[384,896]{1,0:T(8,128)(2,1)S(1)} %collective-permute-done.2) | copy-start | bytes 2064388
  81.8 17.0 %collective-permute-start.3 = (bf16[384,896]{1,0:T(8,128)(2,1)}, bf16[384,896]{1,0:T(8,128)(2,1)S(1)}, u32[]{:S(2)}, u32[]{:S(2)}) collective-permute-start(bf16[384,896]{1,0:T(8,128)(2,1)} %shard_map.93), channel_id=1, source_target_pairs={{0,16},{16,0},{1,17},{17,1},{2,18},{18,2},{3,19},{19,3},{4,20},{20... | collective-permute-start | bytes 2064392 | tf_op jit(solution)/shard_map/ppermute | solution.py:120
  88.4 13.1 %copy-start.22 = (bf16[1,192,4096]{2,1,0:T(8,128)(2,1)}, bf16[1,192,4096]{2,1,0:T(8,128)(2,1)S(1)}, u32[]{:S(2)}) copy-start(bf16[1,192,4096]{2,1,0:T(8,128)(2,1)S(1)} %collective-permute-done.4.refs_0_) | copy-start | bytes 4718596
  98.8 3.4 collective-permute-start.5
  114.9 9.6 %copy-start.20 = (bf16[384,896]{1,0:T(8,128)(2,1)S(1)}, bf16[384,896]{1,0:T(8,128)(2,1)}, u32[]{:S(2)}) copy-start(bf16[384,896]{1,0:T(8,128)(2,1)} %get-tuple-element.58) | copy-start | bytes 2064388
  114.9 27.2 %copy-start.21 = (bf16[384,896]{1,0:T(8,128)(2,1)S(1)}, bf16[384,896]{1,0:T(8,128)(2,1)}, u32[]{:S(2)}) copy-start(bf16[384,896]{1,0:T(8,128)(2,1)} %get-tuple-element.62) | copy-start | bytes 2064388
  114.9 28.6 %collective-permute-start.8 = (bf16[2,192,4096]{2,1,0:T(8,128)(2,1)}, bf16[2,192,4096]{2,1,0:T(8,128)(2,1)S(1)}, u32[]{:S(2)}, u32[]{:S(2)}) collective-permute-start(bf16[2,192,4096]{2,1,0:T(8,128)(2,1)} %all-gather.4.cloned.1.call-done.refs_0_.refs_2_), channel_id=1, source_target_pairs={{0,4},{4,0},{8,12},{12,8},{1,5},{5,1},{9,13},{13,9},{2,6},{6,2},{1... | collective-permute-start | bytes 9437192 | tf_op jit(solution)/shard_map/ppermute | solution.py:114
  124.2 31.9 %collective-permute-start.6 = (bf16[192,4096]{1,0:T(8,128)(2,1)}, bf16[192,4096]{1,0:T(8,128)(2,1)}, u32[]{:S(2)}, u32[]{:S(2)}) collective-permute-start(bf16[192,4096]{1,0:T(8,128)(2,1)} %get-tuple-element.54), channel_id=1, source_target_pairs={{0,4},{4,0},{8,12},{12,8},{1,5},{5,1},{9,13},{13,9},{2,6},{6,2},{1... | collective-permute-start | bytes 4718600 | tf_op jit(solution)/shard_map/ppermute | solution.py:114
  124.5 17.6 %collective-permute-start.7 = (bf16[384,896]{1,0:T(8,128)(2,1)S(1)}, bf16[384,896]{1,0:T(8,128)(2,1)S(1)}, u32[]{:S(2)}, u32[]{:S(2)}) collective-permute-start(bf16[384,896]{1,0:T(8,128)(2,1)S(1)} %copy-done.20), channel_id=1, source_target_pairs={{0,16},{16,0},{1,17},{17,1},{2,18},{18,2},{3,19},{19,3},{4,20},{20... | collective-permute-start | bytes 2064392 | tf_op jit(solution)/shard_map/ppermute | solution.py:120
  142.1 17.2 %collective-permute-start.9 = (bf16[384,896]{1,0:T(8,128)(2,1)S(1)}, bf16[384,896]{1,0:T(8,128)(2,1)S(1)}, u32[]{:S(2)}, u32[]{:S(2)}) collective-permute-start(bf16[384,896]{1,0:T(8,128)(2,1)S(1)} %copy-done.21), channel_id=1, source_target_pairs={{0,16},{16,0},{1,17},{17,1},{2,18},{18,2},{3,19},{19,3},{4,20},{20... | collective-permute-start | bytes 2064392 | tf_op jit(solution)/shard_map/ppermute | solution.py:120
  143.5 12.7 %copy-start.27 = (bf16[192,4096]{1,0:T(8,128)(2,1)S(1)}, bf16[192,4096]{1,0:T(8,128)(2,1)}, u32[]{:S(2)}) copy-start(bf16[192,4096]{1,0:T(8,128)(2,1)} %get-tuple-element.53) | copy-start | bytes 4718596
  160.7 9.1 %copy-start.30 = (bf16[384,896]{1,0:T(8,128)(2,1)S(1)}, bf16[384,896]{1,0:T(8,128)(2,1)}, u32[]{:S(2)}) copy-start(bf16[384,896]{1,0:T(8,128)(2,1)} %get-tuple-element.66) | copy-start | bytes 2064388
  169.8 32.7 %collective-permute-start.10 = (bf16[192,4096]{1,0:T(8,128)(2,1)}, bf16[192,4096]{1,0:T(8,128)(2,1)S(1)}, u32[]{:S(2)}, u32[]{:S(2)}) collective-permute-start(bf16[192,4096]{1,0:T(8,128)(2,1)} %get-tuple-element.65), channel_id=1, source_target_pairs={{0,4},{4,0},{8,12},{12,8},{1,5},{5,1},{9,13},{13,9},{2,6},{6,2},{1... | collective-permute-start | bytes 4718600 | tf_op jit(solution)/shard_map/ppermute | solution.py:114
  169.8 17.8 %collective-permute-start.11 = (bf16[384,896]{1,0:T(8,128)(2,1)S(1)}, bf16[384,896]{1,0:T(8,128)(2,1)S(1)}, u32[]{:S(2)}, u32[]{:S(2)}) collective-permute-start(bf16[384,896]{1,0:T(8,128)(2,1)S(1)} %copy-done.30), channel_id=1, source_target_pairs={{0,16},{16,0},{1,17},{17,1},{2,18},{18,2},{3,19},{19,3},{4,20},{20... | collective-permute-start | bytes 2064392 | tf_op jit(solution)/shard_map/ppermute | solution.py:120
  189.7 12.8 %copy-start.26 = (bf16[192,4096]{1,0:T(8,128)(2,1)S(1)}, bf16[192,4096]{1,0:T(8,128)(2,1)}, u32[]{:S(2)}) copy-start(bf16[192,4096]{1,0:T(8,128)(2,1)} %get-tuple-element.64) | copy-start | bytes 4718596
  202.5 19.4 %copy-start = (bf16[2,192,4096]{2,1,0:T(8,128)(2,1)S(1)}, bf16[2,192,4096]{2,1,0:T(8,128)(2,1)}, u32[]{:S(2)}) copy-start(bf16[2,192,4096]{2,1,0:T(8,128)(2,1)} %all-gather.4.cloned.1.call-done.refs_0_.refs_2_) | copy-start | bytes 9437188
  204.3 103.1 %reduce-scatter.6.cloned.1.call-start = ((), (), s32[]{:S(2)}) async-start(), calls=%async_computation.6 | async-start | bytes 1966080 | tf_op jit(solution)/shard_map/reduce_scatter | solution.py:134
  204.6 17.4 %collective-permute-start.12 = (bf16[384,896]{1,0:T(8,128)(2,1)}, bf16[384,896]{1,0:T(8,128)(2,1)}, u32[]{:S(2)}, u32[]{:S(2)}) collective-permute-start(bf16[384,896]{1,0:T(8,128)(2,1)} %get-tuple-element.71), channel_id=1, source_target_pairs={{0,16},{16,0},{1,17},{17,1},{2,18},{18,2},{3,19},{19,3},{4,20},{20... | collective-permute-start | bytes 2064392 | tf_op jit(solution)/shard_map/ppermute | solution.py:120
  221.9 4.4 %collective-permute-start.13 = (bf16[192,4096]{1,0:T(8,128)(2,1)}, bf16[192,4096]{1,0:T(8,128)(2,1)}, u32[]{:S(2)}, u32[]{:S(2)}) collective-permute-start(bf16[192,4096]{1,0:T(8,128)(2,1)} %get-tuple-element.73), channel_id=1, source_target_pairs={{0,4},{4,0},{8,12},{12,8},{1,5},{5,1},{9,13},{13,9},{2,6},{6,2},{1... | collective-permute-start | bytes 4718600 | tf_op jit(solution)/shard_map/ppermute | solution.py:114
  223.8 4.7 %copy-start.14 = (bf16[384,896]{1,0:T(8,128)(2,1)S(1)}, bf16[384,896]{1,0:T(8,128)(2,1)}, u32[]{:S(2)}) copy-start(bf16[384,896]{1,0:T(8,128)(2,1)} %shard_map.92) | copy-start | bytes 2064388
  223.8 4.7 %copy-start.15 = (bf16[384,896]{1,0:T(8,128)(2,1)S(1)}, bf16[384,896]{1,0:T(8,128)(2,1)}, u32[]{:S(2)}) copy-start(bf16[384,896]{1,0:T(8,128)(2,1)} %shard_map.93) | copy-start | bytes 2064388
  223.8 4.7 %copy-start.17 = (bf16[384,896]{1,0:T(8,128)(2,1)S(1)}, bf16[384,896]{1,0:T(8,128)(2,1)}, u32[]{:S(2)}) copy-start(bf16[384,896]{1,0:T(8,128)(2,1)} %copy-done.16) | copy-start | bytes 2064388
  223.9 85.6 %reduce-scatter.10.cloned.1.call-start = ((), (), s32[]{:S(2)}) async-start(), calls=%async_computation.8 | async-start | bytes 614400 | tf_op jit(solution)/shard_map/reduce_scatter | solution.py:134
  225.1 3.4 copy-start.19
  225.1 3.4 copy-start.29
  231.7 13.5 %copy-start.2 = (bf16[2,192,4096]{2,1,0:T(8,128)(2,1)S(1)}, bf16[2,192,4096]{2,1,0:T(8,128)(2,1)}, u32[]{:S(2)}) copy-start(bf16[2,192,4096]{2,1,0:T(8,128)(2,1)} %copy-done.1) | copy-start | bytes 9437188
  244.5 4.1 %copy-start.7 = (bf16[384,896]{1,0:T(8,128)(2,1)S(1)}, bf16[384,896]{1,0:T(8,128)(2,1)}, u32[]{:S(2)}) copy-start(bf16[384,896]{1,0:T(8,128)(2,1)} %get-tuple-element.95.refs_1_) | copy-start | bytes 2064388
  244.5 4.1 %copy-start.8 = (bf16[384,896]{1,0:T(8,128)(2,1)S(1)}, bf16[384,896]{1,0:T(8,128)(2,1)}, u32[]{:S(2)}) copy-start(bf16[384,896]{1,0:T(8,128)(2,1)} %get-tuple-element.96.refs_0_) | copy-start | bytes 2064388
  244.5 4.1 %copy-start.9 = (bf16[384,896]{1,0:T(8,128)(2,1)S(1)}, bf16[384,896]{1,0:T(8,128)(2,1)}, u32[]{:S(2)}) copy-start(bf16[384,896]{1,0:T(8,128)(2,1)} %get-tuple-element.93.refs_1_) | copy-start | bytes 2064388
  244.5 4.1 %copy-start.10 = (bf16[384,896]{1,0:T(8,128)(2,1)S(1)}, bf16[384,896]{1,0:T(8,128)(2,1)}, u32[]{:S(2)}) copy-start(bf16[384,896]{1,0:T(8,128)(2,1)} %get-tuple-element.94.refs_0_) | copy-start | bytes 2064388
  244.5 17.4 %collective-permute-start.14 = (bf16[192,4096]{1,0:T(8,128)(2,1)}, bf16[192,4096]{1,0:T(8,128)(2,1)S(1)}, u32[]{:S(2)}, u32[]{:S(2)}) collective-permute-start(bf16[192,4096]{1,0:T(8,128)(2,1)} %get-tuple-element.76), channel_id=1, source_target_pairs={{0,4},{4,0},{8,12},{12,8},{1,5},{5,1},{9,13},{13,9},{2,6},{6,2},{1... | collective-permute-start | bytes 4718600 | tf_op jit(solution)/shard_map/ppermute | solution.py:114
  247.2 13.3 %collective-permute-start.15 = (bf16[192,1280]{1,0:T(8,128)(2,1)}, bf16[192,1280]{1,0:T(8,128)(2,1)S(1)}, u32[]{:S(2)}, u32[]{:S(2)}) collective-permute-start(bf16[192,1280]{1,0:T(8,128)(2,1)} %add_convert_fusion.7), channel_id=1, source_target_pairs={{0,8},{4,12},{8,0},{12,4},{1,9},{5,13},{9,1},{13,5},{2,10},{6,14},... | collective-permute-start | bytes 1474568 | tf_op jit(solution)/shard_map/ppermute | solution.py:114
  250.4 14.8 %copy-start.6 = (bf16[1,192,4096]{2,1,0:T(8,128)(2,1)S(1)}, bf16[1,192,4096]{2,1,0:T(8,128)(2,1)}, u32[]{:S(2)}) copy-start(bf16[1,192,4096]{2,1,0:T(8,128)(2,1)} %copy-done.5) | copy-start | bytes 4718596
  253.0 12.2 %copy-start.4 = (bf16[192,4096]{1,0:T(8,128)(2,1)S(1)}, bf16[192,4096]{1,0:T(8,128)(2,1)}, u32[]{:S(2)}) copy-start(bf16[192,4096]{1,0:T(8,128)(2,1)} %all-gather.6.cloned.1.call-done) | copy-start | bytes 4718596
  260.5 16.6 %collective-permute-start.16 = (bf16[192,1408]{1,0:T(8,128)(2,1)}, bf16[192,1408]{1,0:T(8,128)(2,1)}, u32[]{:S(2)}, u32[]{:S(2)}) collective-permute-start(bf16[192,1408]{1,0:T(8,128)(2,1)} %get-tuple-element.79), channel_id=1, source_target_pairs={{0,8},{4,12},{8,0},{12,4},{1,9},{5,13},{9,1},{13,5},{2,10},{6,14},... | collective-permute-start | bytes 1622024 | tf_op jit(solution)/shard_map/ppermute | solution.py:114
  265.1 54.4 %reduce-scatter.12.cloned.1.call-start = ((), (), s32[]{:S(2)}) async-start(), calls=%async_computation.9 | async-start | bytes 675840 | tf_op jit(solution)/shard_map/reduce_scatter | solution.py:134
  279.5 63.0 %reduce-scatter.14.cloned.1.call-start = ((), (), s32[]{:S(2)}) async-start(), calls=%async_computation.10 | async-start | bytes 675840 | tf_op jit(solution)/shard_map/reduce_scatter | solution.py:134
  279.7 13.4 %collective-permute-start.17 = (bf16[192,1408]{1,0:T(8,128)(2,1)}, bf16[192,1408]{1,0:T(8,128)(2,1)S(1)}, u32[]{:S(2)}, u32[]{:S(2)}) collective-permute-start(bf16[192,1408]{1,0:T(8,128)(2,1)} %get-tuple-element.82), channel_id=1, source_target_pairs={{0,8},{4,12},{8,0},{12,4},{1,9},{5,13},{9,1},{13,5},{2,10},{6,14},... | collective-permute-start | bytes 1622024 | tf_op jit(solution)/shard_map/ppermute | solution.py:114
  292.3 3.9 %copy-start.25 = (bf16[192,4096]{1,0:T(8,128)(2,1)S(1)}, bf16[192,4096]{1,0:T(8,128)(2,1)}, u32[]{:S(2)}) copy-start(bf16[192,4096]{1,0:T(8,128)(2,1)} %get-tuple-element.87) | copy-start | bytes 4718596
  295.4 12.1 %collective-permute-start.18 = (bf16[48,4096]{1,0:T(8,128)(2,1)}, bf16[48,4096]{1,0:T(8,128)(2,1)S(1)}, u32[]{:S(2)}, u32[]{:S(2)}) collective-permute-start(bf16[48,4096]{1,0:T(8,128)(2,1)} %reduce-scatter.8.cloned.1.call-done), channel_id=1, source_target_pairs={{0,8},{4,12},{8,0},{12,4},{1,9},{5,13},{9,1},{13,5},{2,10},{6,14},... | collective-permute-start | bytes 1179656 | tf_op jit(solution)/shard_map/ppermute | solution.py:114
  (9 other events, 15.7 us)
Sparse Core Ops, SparseCore 0:
  9.6 39.7 all-gather.5
  51.6 62.3 all-gather.3
  204.5 33.5 reduce-scatter.7
  240.3 34.2 reduce-scatter.5
  276.7 20.2 reduce-scatter.9
  299.2 20.2 reduce-scatter.11
  322.3 20.0 reduce-scatter.13

commit v4 on v3

v4 whole, which is shorter than its diff:
```python
import functools

import jax
import jax.numpy as jnp
from jax import lax
from jax.experimental import pallas as pl
from jax.experimental.pallas import tpu as pltpu
from jax.sharding import PartitionSpec as P

CORE, CHIP = 1, 2
VMEM_BYTES = 56 * 1024 * 1024


def dot(left, right, left_dim, right_dim):
    return lax.dot_general(
        left, right, (((left_dim,), (right_dim,)), ((), ())), preferred_element_type=jnp.float32
    )


def after(array, *others):
    return lax.optimization_barrier((array, *others))[0]


def wide(block):
    return block.astype(jnp.float32)


def narrow(block):
    return block.astype(jnp.bfloat16)


def cost(flops, *arrays):
    moved = sum(array.size * array.dtype.itemsize for array in arrays)
    return pl.CostEstimate(flops=flops, bytes_accessed=moved, transcendentals=0)


def contract_kernel(n_pieces, n_weights, right_dim, *refs):
    pieces, weights = refs[:n_pieces], refs[n_pieces : n_pieces + n_weights]
    outs, total = refs[n_pieces + n_weights : -1], refs[-1]
    step = pl.program_id(0)

    @pl.when(step == 0)
    def _():
        total[...] = jnp.zeros_like(total)

    rows = jnp.concatenate([piece[...] for piece in pieces], axis=0)
    for i, weight in enumerate(weights):
        total[i] += dot(rows, weight[...], 1, right_dim)

    @pl.when(step == pl.num_programs(0) - 1)
    def _():
        size = outs[0].shape[0]
        for i, out in enumerate(outs):
            part, weight = divmod(i, n_weights)
            out[...] = narrow(total[weight, part * size : (part + 1) * size])


def contract(pieces, weights, right_dim, parts=1):
    width = pieces[0].shape[1]
    units = weights[0].shape[1 - right_dim]
    block = min(1024, width)
    if right_dim == 0:
        weight_spec = pl.BlockSpec((block, units), lambda k: (k, 0))
    else:
        weight_spec = pl.BlockSpec((units, block), lambda k: (0, k))
    rows = sum(piece.shape[0] for piece in pieces)
    out = jax.ShapeDtypeStruct((rows // parts, units), jnp.bfloat16)
    n_outs = parts * len(weights)
    return pl.pallas_call(
        functools.partial(contract_kernel, len(pieces), len(weights), right_dim),
        grid=(width // block,),
        in_specs=[pl.BlockSpec((piece.shape[0], block), lambda k: (0, k)) for piece in pieces]
        + [weight_spec] * len(weights),
        out_specs=[pl.BlockSpec(out.shape, lambda k: (0, 0))] * n_outs,
        out_shape=[out] * n_outs,
        scratch_shapes=[pltpu.VMEM((len(weights), rows, units), jnp.float32)],
        compiler_params=pltpu.CompilerParams(vmem_limit_bytes=VMEM_BYTES),
        cost_estimate=cost(2 * len(weights) * rows * width * units, *pieces, *weights),
    )(*pieces, *weights)


def expand_kernel(n, right_dim, *refs):
    lefts, weights, outs = refs[:n], refs[n : 2 * n], refs[2 * n :]
    total = sum(dot(left[...], weight[...], 1, right_dim) for left, weight in zip(lefts, weights))
    half = total.shape[0] // 2
    outs[0][...] = narrow(total[:half])
    outs[1][...] = narrow(total[half:])


def expand(lefts, weights, right_dim):
    rows, units = lefts[0].shape
    width = weights[0].shape[1 - right_dim]
    block = min(512, width)
    if right_dim == 0:
        weight_spec = pl.BlockSpec((units, block), lambda j: (0, j))
    else:
        weight_spec = pl.BlockSpec((block, units), lambda j: (j, 0))
    out = jax.ShapeDtypeStruct((rows // 2, width), jnp.bfloat16)
    return pl.pallas_call(
        functools.partial(expand_kernel, len(lefts), right_dim),
        grid=(width // block,),
        in_specs=[pl.BlockSpec((rows, units), lambda j: (0, 0))] * len(lefts)
        + [weight_spec] * len(weights),
        out_specs=[pl.BlockSpec((rows // 2, block), lambda j: (0, j))] * 2,
        out_shape=[out, out],
        compiler_params=pltpu.CompilerParams(vmem_limit_bytes=VMEM_BYTES),
        cost_estimate=cost(2 * len(lefts) * rows * width * units, *lefts, *weights, out, out),
    )(*lefts, *weights)


def wide_grad_kernel(n_pieces, *refs):
    pieces, grads, outs = refs[:n_pieces], refs[n_pieces:-2], refs[-2:]
    rows = jnp.concatenate([piece[...] for piece in pieces], axis=0)
    half = len(grads) // 2
    for i, out in enumerate(outs):
        grad = jnp.concatenate([grad[...] for grad in grads[i * half : (i + 1) * half]], axis=0)
        out[...] = dot(rows, grad, 0, 0)


def wide_grads(pieces, gate_grads, up_grads):
    grads = [*gate_grads, *up_grads]
    width, units = pieces[0].shape[1], grads[0].shape[1]
    block = min(512, width)
    rows = sum(piece.shape[0] for piece in pieces)
    out = jax.ShapeDtypeStruct((width, units), jnp.float32)
    return pl.pallas_call(
        functools.partial(wide_grad_kernel, len(pieces)),
        grid=(width // block,),
        in_specs=[pl.BlockSpec((piece.shape[0], block), lambda j: (0, j)) for piece in pieces]
        + [pl.BlockSpec(grad.shape, lambda j: (0, 0)) for grad in grads],
        out_specs=[pl.BlockSpec((block, units), lambda j: (j, 0))] * 2,
        out_shape=[out, out],
        compiler_params=pltpu.CompilerParams(vmem_limit_bytes=VMEM_BYTES),
        cost_estimate=cost(4 * rows * width * units, *pieces, *grads, out, out),
    )(*pieces, *grads)


def tall_grad_kernel(n_pieces, *refs):
    pieces, hiddens, out = refs[:n_pieces], refs[n_pieces:-1], refs[-1]
    rows = jnp.concatenate([piece[...] for piece in pieces], axis=0)
    hidden = jnp.concatenate([hidden[...] for hidden in hiddens], axis=0)
    out[...] = dot(hidden, rows, 0, 0)


def tall_grad(pieces, hiddens):
    width, units = pieces[0].shape[1], hiddens[0].shape[1]
    block = min(512, width)
    rows = sum(piece.shape[0] for piece in pieces)
    out = jax.ShapeDtypeStruct((units, width), jnp.float32)
    return pl.pallas_call(
        functools.partial(tall_grad_kernel, len(pieces)),
        grid=(width // block,),
        in_specs=[pl.BlockSpec((piece.shape[0], block), lambda j: (0, j)) for piece in pieces]
        + [pl.BlockSpec(hidden.shape, lambda j: (0, 0)) for hidden in hiddens],
        out_specs=pl.BlockSpec((units, block), lambda j: (0, j)),
        out_shape=out,
        compiler_params=pltpu.CompilerParams(vmem_limit_bytes=VMEM_BYTES),
        cost_estimate=cost(2 * rows * width * units, *pieces, *hiddens, out),
    )(*pieces, *hiddens)


def shift(block, step):
    n = lax.axis_size("depth")
    return lax.ppermute(block, "depth", [(i, (i + step) % n) for i in range(n)])


def swap(block, bit):
    n = lax.axis_size("col")
    return lax.ppermute(block, "col", [(i, i ^ bit) for i in range(n)])


def row_moves(partial):
    n = lax.axis_size("row")
    return [
        lax.ppermute(partial, "row", [(i, (i + step) % n) for i in range(n)])
        for step in range(1, n)
    ]


def row_sum(partial, moved, *others):
    return sum([wide(after(block, *others)) for block in moved], wide(partial))


def add(*blocks):
    return narrow(sum(wide(block) for block in blocks))


def grads_of(gate, up, hidden_grad):
    sigma = jax.nn.sigmoid(gate)
    gate_grad = narrow(hidden_grad * up * sigma * (1.0 + gate * (1.0 - sigma)))
    return gate_grad, narrow(hidden_grad * (gate * sigma))


def hidden_of(gate, up):
    return narrow(gate * jax.nn.sigmoid(gate) * up)


def sync(*arrays):
    return lax.optimization_barrier(arrays)


def other_cores(blocks):
    return [swap(block, CORE) for block in blocks]


def chip_part(mine, moved):
    half = mine.shape[0] // 2
    return add(mine[half:], moved[half:]), (mine[:half], moved[:half])


def owner_parts(kept, moved):
    size = moved.shape[0] // 2
    rows = [slice(0, size), slice(size, 2 * size)]
    return [sum(wide(block[at]) for block in (*kept, moved)) for at in rows]


def body(tokens, gate_weight, up_weight, down_weight, cotangent):
    near1, far0, core0 = sync(shift(tokens, 1), swap(tokens, CHIP), swap(tokens, CORE))

    near3, far1, *moved = sync(
        shift(after(tokens, near1), 3), swap(near1, CHIP), *other_cores([near1, far0])
    )
    token_a = [tokens, near1, far0, far1, core0, *moved, swap(far1, CORE)]

    near2, far3 = shift(after(near1, near3), 1), swap(near3, CHIP)
    (gate_a,) = contract(token_a, [gate_weight], 0)
    near2, far3, gate_a = sync(near2, far3, gate_a)

    gate_moved = row_moves(gate_a)
    far2, cot_near1 = swap(near2, CHIP), shift(after(cotangent, near2), 1)
    (up_a,) = contract([after(tokens, gate_a), *token_a[1:]], [up_weight], 0)
    far2, cot_near1, up_a, *gate_moved = sync(far2, cot_near1, up_a, *gate_moved)
    gate_a = row_sum(gate_a, gate_moved)

    up_moved = row_moves(up_a)
    token_b = [near3, near2, far3, far2]
    token_b += other_cores(after(block, up_a) for block in token_b)
    cot = after(cotangent, cot_near1)
    cot_far0, cot_far1, cot_near3 = swap(cot, CHIP), swap(cot_near1, CHIP), shift(cot, 3)
    gate_b, up_b = contract(token_b, [gate_weight, up_weight], 0)
    cot_far0, cot_far1, cot_near3, gate_b, up_b, *up_moved = sync(
        cot_far0, cot_far1, cot_near3, gate_b, up_b, *up_moved
    )
    up_a = row_sum(up_a, up_moved)
    hidden_a = hidden_of(gate_a, up_a)

    gate_moved = row_moves(gate_b)
    cot_near2, cot_far3 = shift(after(cot_near1, cot_near3), 1), swap(cot_near3, CHIP)
    mine, other = expand([hidden_a], [down_weight], 0)
    cot_near2, cot_far3, mine, other, *gate_moved = sync(
        cot_near2, cot_far3, mine, other, *gate_moved
    )
    gate_b = row_sum(gate_b, gate_moved)

    up_moved = row_moves(after(up_b, mine))
    cot_far2 = swap(cot_near2, CHIP)
    other = swap(other, CORE)
    cots = [after(cotangent, mine), cot_near1, cot_far0, cot_far1]
    cots += other_cores(after(block, mine) for block in cots)
    cots += [cot_near3, cot_near2, cot_far3, cot_far2]
    cots += other_cores(after(block, mine) for block in cots[8:])
    grad_a, grad_b = contract(cots, [down_weight], 1, parts=2)
    other, grad_a, grad_b, *up_moved = sync(other, grad_a, grad_b, *up_moved)
    up_b = row_sum(up_b, up_moved)
    hidden_b = hidden_of(gate_b, up_b)

    grad_b_moved = row_moves(grad_b)
    sent, mixed_a = chip_part(mine, other)
    mixed_a_moved = swap(sent, CHIP)
    mine, other = expand([hidden_b], [down_weight], 0)
    mixed_a_moved, mine, other, *grad_b_moved = sync(mixed_a_moved, mine, other, *grad_b_moved)
    grad_b = row_sum(grad_b, grad_b_moved)

    grad_a_moved = row_moves(after(grad_a, mine))
    sent, mixed_b = chip_part(mine, swap(other, CORE))
    mixed_b_moved = swap(sent, CHIP)
    mixed_a = owner_parts(mixed_a, mixed_a_moved)
    part1 = shift(narrow(mixed_a[1]), -1)
    grads_b = grads_of(gate_b, up_b, grad_b)
    mine, other = expand(grads_b, [gate_weight, up_weight], 1)
    mine, other, mixed_b_moved, part1, *grad_a_moved = sync(
        mine, other, mixed_b_moved, part1, *grad_a_moved
    )
    grad_a = row_sum(grad_a, grad_a_moved)

    sent, token_grad_b = chip_part(mine, swap(other, CORE))
    token_b_moved = swap(sent, CHIP)
    mixed_b = owner_parts(mixed_b, mixed_b_moved)
    part3, part2 = (shift(narrow(part), -k) for part, k in zip(mixed_b, (3, 2)))
    grads_a = grads_of(gate_a, up_a, grad_a)
    mine, other = expand(grads_a, [gate_weight, up_weight], 1)
    mine, other, token_b_moved, part2, part3 = sync(mine, other, token_b_moved, part2, part3)
    mixed = sum((wide(part) for part in (part1, part2, part3)), mixed_a[0])

    sent, token_grad_a = chip_part(mine, swap(other, CORE))
    token_a_moved = swap(sent, CHIP)
    token_grad_b = owner_parts(token_grad_b, token_b_moved)
    part3, part2 = (shift(narrow(part), -k) for part, k in zip(token_grad_b, (3, 2)))
    gate_total, up_total = wide_grads(
        [after(token_a[0], sent), *token_a[1:], *token_b],
        [grads_a[0], grads_b[0]],
        [grads_a[1], grads_b[1]],
    )
    token_a_moved, part2, part3, gate_total, up_total = sync(
        token_a_moved, part2, part3, gate_total, up_total
    )

    token_grad_a = owner_parts(token_grad_a, token_a_moved)
    part1 = shift(narrow(token_grad_a[1]), -1)
    down_total = tall_grad(cots, [after(hidden_a, gate_total), hidden_b])
    part1, down_total = sync(part1, down_total)
    token_grad = sum((wide(part) for part in (part1, part2, part3)), token_grad_a[0])
    return (mixed, token_grad, gate_total, up_total, down_total)


def solution(mesh):
    activations = P(("depth", "col"), "row")
    wide_weight = P("row", ("col", "depth"))
    tall_weight = P(("col", "depth"), "row")
    return jax.shard_map(
        body,
        mesh=mesh,
        in_specs=(activations, wide_weight, wide_weight, tall_weight, activations),
        out_specs=(activations, activations, wide_weight, wide_weight, tall_weight),
        check_vma=False,
    )
```

time: 353 us -> 258 us (0.73)
  waiting for transfers between devices: 156 us -> 81.5 us
  matrix products: 35.1 us -> 0 us
  Pallas kernels: 81.9 us -> 114 us
  between operations: 14.3 us -> 0.96 us
  starting transfers between devices: 18.7 us -> 31.9 us
  other arithmetic: 34.6 us -> 24.8 us
  local copies, waits for them, and re-layouts: 10.3 us -> 2.9 us
    ppermute x6, waiting for transfers between devices: 68.1 us -> 15.2 us  [row_moves(): lax.ppermute(partial, 'row', [(i, (i + step) % n) for i in range(n)])]
    dot_general x3 -> x0, matrix products: 35.1 us -> none  [dot(): lax.dot_general(left, right, (((left_dim,), (right_dim,)), ((), ())), pre...]
    ppermute x0 -> x12, waiting for transfers between devices: none -> 34.4 us  [shift(): return lax.ppermute(block, 'depth', [(i, (i + step) % n) for i in range(n)])]
    reduce_scatter x5 -> x0, waiting for transfers between devices: 33 us -> none  [line_scatter(): lax.psum_scatter(line, 'depth', scatter_dimension=0, tiled=True)]
    pallas_call x0 -> x2, Pallas kernels: none -> 31.6 us  [the longest x1 18.4 us: wide_grads(): pl.pallas_call(functools.partial(wide_grad_kernel, len(pieces)), grid=(wi...]
    all_gather x2 -> x0, waiting for transfers between devices: 29.1 us -> none  [line_gather(): return lax.all_gather(jnp.stack(shards), 'depth', axis=1, tiled=True)]
    ppermute x0 -> x12, starting transfers between devices: none -> 9.22 us  [shift(): return lax.ppermute(block, 'depth', [(i, (i + step) % n) for i in range(n)])]
    ppermute x13 -> x32, waiting for transfers between devices: 25.4 us -> 31.9 us  [swap(): return lax.ppermute(block, 'col', [(i, i ^ bit) for i in range(n)])]
  transfers between devices with their start and end apart: 26 -> 50, of which waited for: 14 -> 22; matrix products, arithmetic and copies ran while one was open for 19% -> 8% of each run, Pallas kernels for 21% -> 44%
where the time goes in v4:
time: 258 us; the launch traced here: 256 us
  Pallas kernels  114 us (44%)
  waiting for transfers between devices  81.5 us (32%)
  starting transfers between devices  31.9 us (12%)
  other arithmetic  24.8 us (10%)
  local copies, waits for them, and re-layouts  2.9 us (1%)
    pallas_call x4, Pallas kernels, expand(): pl.pallas_call(functools.partial(expand_kernel, len(lefts), right_dim), g...  43.6 us
    pallas_call x4, Pallas kernels, contract(): pl.pallas_call(functools.partial(contract_kernel, len(pieces), len(weight...  38.5 us
    ppermute x12, waiting for transfers between devices, shift(): return lax.ppermute(block, 'depth', [(i, (i + step) % n) for i in range(n)])  34.4 us
    ppermute x32, waiting for transfers between devices, swap(): return lax.ppermute(block, 'col', [(i, i ^ bit) for i in range(n)])  31.9 us
    convert_element_type x12, other arithmetic, narrow(): return block.astype(jnp.bfloat16)  21.2 us
    pallas_call x1, Pallas kernels, wide_grads(): pl.pallas_call(functools.partial(wide_grad_kernel, len(pieces)), grid=(wi...  18.4 us
    ppermute x6, waiting for transfers between devices, row_moves(): lax.ppermute(partial, 'row', [(i, (i + step) % n) for i in range(n)])  15.2 us
    ppermute x32, starting transfers between devices, swap(): return lax.ppermute(block, 'col', [(i, i ^ bit) for i in range(n)])  14.3 us
  transfers between devices with their start and end apart: 50, of which 22 were waited for; matrix products, arithmetic and copies ran while one was open for 8% of the time, Pallas kernels for 44%

profile of v4, /device:TPU:0, one launch (start us, length us, event | category | flops | bytes accessed | tf_op | source)
XLA Modules:
  0.0 255.9 jit_solution(8504021193286262301)
XLA Ops:
  1.2 2.6 %collective-permute-start.1 = (bf16[48,4096]{1,0:T(8,128)(2,1)}, bf16[48,4096]{1,0:T(8,128)(2,1)S(1)}, u32[]{:S(2)}, u32[]{:S(2)}) collective-permute-start(bf16[48,4096]{1,0:T(8,128)(2,1)} %refs_0_.4), channel_id=1, source_target_pairs={{0,8},{4,12},{8,0},{12,4},{1,9},{5,13},{9,1},{13,5},{2,10},{6,14},... | collective-permute-start | bytes 1179656 | tf_op jit(solution)/shard_map/ppermute | solution.py:169
  3.8 1.6 collective-permute-start
  5.3 8.3 %collective-permute-done.1.refs_2_ = bf16[48,4096]{1,0:T(8,128)(2,1)S(1)} collective-permute-done((bf16[48,4096]{1,0:T(8,128)(2,1)}, bf16[48,4096]{1,0:T(8,128)(2,1)S(1)}, u32[]{:S(2)}, u32[]{:S(2)}) %collective-permute-start.1) | collective-permute-done | bytes 393248 | tf_op jit(solution)/shard_map/ppermute | solution.py:169
  13.7 3.4 %collective-permute-done.refs_1_ = bf16[48,4096]{1,0:T(8,128)(2,1)S(1)} collective-permute-done((bf16[48,4096]{1,0:T(8,128)(2,1)}, bf16[48,4096]{1,0:T(8,128)(2,1)S(1)}, u32[]{:S(2)}, u32[]{:S(2)}) %collective-permute-start) | collective-permute-done | bytes 393248 | tf_op jit(solution)/shard_map/ppermute | solution.py:164
  17.0 1.7 collective-permute-start.3
  19.8 7.9 %collective-permute-done.3.refs_0_.refs_8_ = bf16[48,4096]{1,0:T(8,128)(2,1)S(1)} collective-permute-done((bf16[48,4096]{1,0:T(8,128)(2,1)}, bf16[48,4096]{1,0:T(8,128)(2,1)S(1)}, u32[]{:S(2)}, u32[]{:S(2)}) %collective-permute-start.3) | collective-permute-done | bytes 393248 | tf_op jit(solution)/shard_map/ppermute | solution.py:164
  27.7 2.5 collective-permute-done.4.refs_3_
  32.8 7.8 %shard_map.92 = bf16[384,896]{1,0:T(8,128)(2,1)} custom-call(bf16[48,4096]{1,0:T(8,128)(2,1)} %refs_0_.4, bf16[48,4096]{1,0:T(8,128)(2,1)} %copy-done.6, bf16[48,4096]{1,0:T(8,128)(2,1)} %copy-done.5, bf16[48,4096]{1,0:T(8,128)(2,1)} %copy-done.9, bf16[48,4096]{1,0:T(8,128)(2,1)} %copy-done.4, bf16[48,4096]{1,0:T(8,128)(2,1)} %copy-done.8, ...), custom_call_target="tpu_custom_call" | custom-call | flops 2818572288 | bytes 10485760 | tf_op jit(solution)/shard_map/pallas_call | solution.py:69
  40.6 3.0 %collective-permute-done.7.refs_1_.refs_9_ = bf16[48,4096]{1,0:T(8,128)(2,1)S(1)} collective-permute-done((bf16[48,4096]{1,0:T(8,128)(2,1)S(1)}, bf16[48,4096]{1,0:T(8,128)(2,1)S(1)}, u32[]{:S(2)}, u32[]{:S(2)}) %collective-permute-start.7) | collective-permute-done | bytes 393248 | tf_op jit(solution)/shard_map/ppermute | solution.py:164
  43.6 1.6 collective-permute-start.12
  45.7 7.8 %shard_map.93 = bf16[384,896]{1,0:T(8,128)(2,1)} custom-call(bf16[48,4096]{1,0:T(8,128)(2,1)} %refs_0_.4, bf16[48,4096]{1,0:T(8,128)(2,1)} %copy-done.6, bf16[48,4096]{1,0:T(8,128)(2,1)} %copy-done.5, bf16[48,4096]{1,0:T(8,128)(2,1)} %copy-done.9, bf16[48,4096]{1,0:T(8,128)(2,1)} %copy-done.4, bf16[48,4096]{1,0:T(8,128)(2,1)} %copy-done.8, ...), custom_call_target="tpu_custom_call" | custom-call | flops 2818572288 | bytes 10485760 | tf_op jit(solution)/shard_map/pallas_call | solution.py:69
  53.5 3.9 %collective-permute-done.11.refs_1_ = bf16[48,4096]{1,0:T(8,128)(2,1)S(1)} collective-permute-done((bf16[48,4096]{1,0:T(8,128)(2,1)S(1)}, bf16[48,4096]{1,0:T(8,128)(2,1)S(1)}, u32[]{:S(2)}, u32[]{:S(2)}) %collective-permute-start.11) | collective-permute-done | bytes 393248 | tf_op jit(solution)/shard_map/ppermute | solution.py:164
  57.5 3.5 %collective-permute-done.12 = bf16[384,896]{1,0:T(8,128)(2,1)S(1)} collective-permute-done((bf16[384,896]{1,0:T(8,128)(2,1)}, bf16[384,896]{1,0:T(8,128)(2,1)S(1)}, u32[]{:S(2)}, u32[]{:S(2)}) %collective-permute-start.12) | collective-permute-done | bytes 688160 | tf_op jit(solution)/shard_map/ppermute | solution.py:175
  62.0 1.5 collective-permute-start.20
  63.5 1.4 collective-permute-start.15
  65.4 1.5 collective-permute-start.14
  66.9 11.7 %shard_map.94 = (bf16[384,896]{1,0:T(8,128)(2,1)}, bf16[384,896]{1,0:T(8,128)(2,1)}) custom-call(bf16[48,4096]{1,0:T(8,128)(2,1)} %copy-done.36, bf16[48,4096]{1,0:T(8,128)(2,1)} %copy-done.37, bf16[48,4096]{1,0:T(8,128)(2,1)} %copy-done.38, bf16[48,4096]{1,0:T(8,128)(2,1)} %copy-done.39, bf16[48,4096]{1,0:T(8,128)(2,1)} %copy-done.40, ...), custom_call_target="tpu_custom_call" | custom-call | flops 5637144576 | bytes 17825792 | tf_op jit(solution)/shard_map/pallas_call | solution.py:69
  78.7 5.1 %collective-permute-done.14.refs_3_ = bf16[48,4096]{1,0:T(8,128)(2,1)S(1)} collective-permute-done((bf16[48,4096]{1,0:T(8,128)(2,1)S(1)}, bf16[48,4096]{1,0:T(8,128)(2,1)S(1)}, u32[]{:S(2)}, u32[]{:S(2)}) %collective-permute-start.14) | collective-permute-done | bytes 393248 | tf_op jit(solution)/shard_map/ppermute | solution.py:169
  86.0 1.4 multiply_convert_fusion.5.refs_0_.refs_16_
  87.5 9.1 %shard_map.95 = (bf16[192,4096]{1,0:T(8,128)(2,1)}, bf16[192,4096]{1,0:T(8,128)(2,1)}) custom-call(bf16[384,896]{1,0:T(8,128)(2,1)} %multiply_convert_fusion.5.refs_0_.refs_16_, bf16[896,4096]{1,0:T(8,128)(2,1)} %refs_1_.3), custom_call_target="tpu_custom_call" | custom-call | flops 2818572288 | bytes 11173888 | tf_op jit(solution)/shard_map/pallas_call | solution.py:99
  96.6 3.3 %collective-permute-done.23 = bf16[384,896]{1,0:T(8,128)(2,1)S(1)} collective-permute-done((bf16[384,896]{1,0:T(8,128)(2,1)}, bf16[384,896]{1,0:T(8,128)(2,1)S(1)}, u32[]{:S(2)}, u32[]{:S(2)}) %collective-permute-start.23) | collective-permute-done | bytes 688160 | tf_op jit(solution)/shard_map/ppermute | solution.py:175
  101.8 9.9 %collective-permute-done.29.refs_11_ = bf16[48,4096]{1,0:T(8,128)(2,1)S(1)} collective-permute-done((bf16[48,4096]{1,0:T(8,128)(2,1)}, bf16[48,4096]{1,0:T(8,128)(2,1)S(1)}, u32[]{:S(2)}, u32[]{:S(2)}) %collective-permute-start.29) | collective-permute-done | bytes 393248 | tf_op jit(solution)/shard_map/ppermute | solution.py:169
  113.5 1.5 collective-permute-start.34
  116.2 11.2 %shard_map.96 = (bf16[384,896]{1,0:T(8,128)(2,1)}, bf16[384,896]{1,0:T(8,128)(2,1)}) custom-call(bf16[48,4096]{1,0:T(8,128)(2,1)} %refs_0_.5, bf16[48,4096]{1,0:T(8,128)(2,1)} %copy-done.23, bf16[48,4096]{1,0:T(8,128)(2,1)} %copy-done.25, bf16[48,4096]{1,0:T(8,128)(2,1)} %copy-done.26, bf16[48,4096]{1,0:T(8,128)(2,1)} %copy-done.28, ...), custom_call_target="tpu_custom_call" | custom-call | flops 5637144576 | bytes 13631488 | tf_op jit(solution)/shard_map/pallas_call | solution.py:69
  127.4 3.6 %collective-permute-done.34 = bf16[384,896]{1,0:T(8,128)(2,1)S(1)} collective-permute-done((bf16[384,896]{1,0:T(8,128)(2,1)S(1)}, bf16[384,896]{1,0:T(8,128)(2,1)S(1)}, u32[]{:S(2)}, u32[]{:S(2)}) %collective-permute-start.34) | collective-permute-done | bytes 688160 | tf_op jit(solution)/shard_map/ppermute | solution.py:175
  131.0 2.2 add_convert_fusion.3
  133.7 1.4 collective-permute-start.36
  135.2 1.5 multiply_convert_fusion.4.refs_0_.refs_17_
  136.6 9.0 %shard_map.97 = (bf16[192,4096]{1,0:T(8,128)(2,1)}, bf16[192,4096]{1,0:T(8,128)(2,1)}) custom-call(bf16[384,896]{1,0:T(8,128)(2,1)} %multiply_convert_fusion.4.refs_0_.refs_17_, bf16[896,4096]{1,0:T(8,128)(2,1)} %refs_1_.3), custom_call_target="tpu_custom_call" | custom-call | flops 2818572288 | bytes 11173888 | tf_op jit(solution)/shard_map/pallas_call | solution.py:99
  145.6 4.7 %collective-permute-done.36 = bf16[384,896]{1,0:T(8,128)(2,1)} collective-permute-done((bf16[384,896]{1,0:T(8,128)(2,1)}, bf16[384,896]{1,0:T(8,128)(2,1)}, u32[]{:S(2)}, u32[]{:S(2)}) %collective-permute-start.36) | collective-permute-done | bytes 688160 | tf_op jit(solution)/shard_map/ppermute | solution.py:175
  150.3 1.8 collective-permute-done.35
  152.1 1.4 collective-permute-start.40
  153.6 1.9 add_convert_fusion.9
  155.7 1.3 add_convert_fusion.2
  157.6 3.4 %multiply_convert_fusion.2 = (bf16[384,896]{1,0:T(8,128)(2,1)}, bf16[384,896]{1,0:T(8,128)(2,1)}) fusion(bf16[384,896]{1,0:T(8,128)(2,1)} %collective-permute-done.36, bf16[384,896]{1,0:T(8,128)(2,1)} %get-tuple-element.147, bf16[384,896]{1,0:T(8,128)(2,1)S(1)} %collective-permute-done.23, bf16[384,896]{1,0:T(8,128)(2,1)S(1)} %copy-done.2, ...), kind=kLoop, calls=%fused_computation.7 | loop fusion | flops 7569408 | bytes 5505024 | tf_op jit(solution)/shard_map/convert_element_type | solution.py:29
  161.1 1.4 collective-permute-start.39
  162.5 12.8 %shard_map.98 = (bf16[192,4096]{1,0:T(8,128)(2,1)}, bf16[192,4096]{1,0:T(8,128)(2,1)}) custom-call(bf16[384,896]{1,0:T(8,128)(2,1)} %get-tuple-element.186.refs_0_.refs_17_, bf16[384,896]{1,0:T(8,128)(2,1)} %get-tuple-element.185.refs_1_.refs_19_, bf16[4096,896]{1,0:T(8,128)(2,1)} %refs_2_.3, bf16[4096,896]{1,0:T(8,128)(2,1)} %refs_3_.3), custom_call_target="tpu_custom_call" | custom-call | flops 5637144576 | bytes 19202048 | tf_op jit(solution)/shard_map/pallas_call | solution.py:99
  175.3 1.7 collective-permute-done.38
  177.1 2.6 %add_convert_fusion.7 = (bf16[48,4096]{1,0:T(8,128)(2,1)}, bf16[48,4096]{1,0:T(8,128)(2,1)}) fusion(bf16[192,4096]{1,0:T(8,128)(2,1)} %copy-done.18, bf16[96,4096]{1,0:T(8,128)(2,1)} %collective-permute-done.38, bf16[192,4096]{1,0:T(8,128)(2,1)S(1)} %copy-done.15), kind=kLoop, calls=%fused_computation.25 | loop fusion | flops 2359296 | bytes 3145728 | tf_op jit(solution)/shard_map/convert_element_type | solution.py:29
  184.4 3.2 %multiply_convert_fusion = (bf16[384,896]{1,0:T(8,128)(2,1)}, bf16[384,896]{1,0:T(8,128)(2,1)}) fusion(bf16[384,896]{1,0:T(8,128)(2,1)} %collective-permute-done.40, bf16[384,896]{1,0:T(8,128)(2,1)S(1)} %copy-done.19, bf16[384,896]{1,0:T(8,128)(2,1)S(1)} %collective-permute-done.12, bf16[384,896]{1,0:T(8,128)(2,1)S(1)} %copy-done, ...), kind=kLoop, calls=%fused_computation.4 | loop fusion | flops 7569408 | bytes 5505024 | tf_op jit(solution)/shard_map/convert_element_type | solution.py:29
  187.6 12.8 %shard_map.99 = (bf16[192,4096]{1,0:T(8,128)(2,1)}, bf16[192,4096]{1,0:T(8,128)(2,1)}) custom-call(bf16[384,896]{1,0:T(8,128)(2,1)} %get-tuple-element.184.refs_0_.refs_16_, bf16[384,896]{1,0:T(8,128)(2,1)} %get-tuple-element.183.refs_1_.refs_18_, bf16[4096,896]{1,0:T(8,128)(2,1)} %refs_2_.3, bf16[4096,896]{1,0:T(8,128)(2,1)} %refs_3_.3), custom_call_target="tpu_custom_call" | custom-call | flops 5637144576 | bytes 19202048 | tf_op jit(solution)/shard_map/pallas_call | solution.py:99
  200.4 9.1 %collective-permute-done.43 = bf16[48,4096]{1,0:T(8,128)(2,1)} collective-permute-done((bf16[48,4096]{1,0:T(8,128)(2,1)}, bf16[48,4096]{1,0:T(8,128)(2,1)}, u32[]{:S(2)}, u32[]{:S(2)}) %collective-permute-start.43) | collective-permute-done | bytes 393248 | tf_op jit(solution)/shard_map/ppermute | solution.py:164
  209.6 2.3 add_convert_fusion.5
  212.4 2.4 convert_add_fusion.7
  215.9 18.4 %shard_map.100 = (f32[4096,896]{1,0:T(8,128)}, f32[4096,896]{1,0:T(8,128)}) custom-call(bf16[48,4096]{1,0:T(8,128)(2,1)} %refs_0_.4, bf16[48,4096]{1,0:T(8,128)(2,1)} %copy-done.6, bf16[48,4096]{1,0:T(8,128)(2,1)} %copy-done.5, bf16[48,4096]{1,0:T(8,128)(2,1)} %copy-done.9, bf16[48,4096]{1,0:T(8,128)(2,1)} %copy-done.4, bf16[48,4096]{1,0:T(8,128)(2,1)} %copy-done.8, ...), custom_call_target="tpu_custom_call" | custom-call | flops 11274289152 | bytes 38404096 | tf_op jit(solution)/shard_map/pallas_call | solution.py:126
  234.4 6.9 %collective-permute-done.47 = bf16[48,4096]{1,0:T(8,128)(2,1)S(1)} collective-permute-done((bf16[48,4096]{1,0:T(8,128)(2,1)}, bf16[48,4096]{1,0:T(8,128)(2,1)S(1)}, u32[]{:S(2)}, u32[]{:S(2)}) %collective-permute-start.47) | collective-permute-done | bytes 393248 | tf_op jit(solution)/shard_map/ppermute | solution.py:164
  241.6 13.1 %shard_map.101 = f32[896,4096]{1,0:T(8,128)} custom-call(bf16[48,4096]{1,0:T(8,128)(2,1)} %refs_0_.5, bf16[48,4096]{1,0:T(8,128)(2,1)} %copy-done.23, bf16[48,4096]{1,0:T(8,128)(2,1)} %copy-done.25, bf16[48,4096]{1,0:T(8,128)(2,1)} %copy-done.26, bf16[48,4096]{1,0:T(8,128)(2,1)} %copy-done.28, bf16[48,4096]{1,0:T(8,128)(2,1)} %copy-done.30, ...), custom_call_target="tpu_custom_call" | custom-call | flops 5637144576 | bytes 22347776 | tf_op jit(solution)/shard_map/pallas_call | solution.py:150
  254.7 1.2 convert_add_fusion.6
  (162 shorter events, 21.2 us)
Async XLA Ops:
  0.6 4.7 %collective-permute-start.2 = (bf16[48,4096]{1,0:T(8,128)(2,1)}, bf16[48,4096]{1,0:T(8,128)(2,1)S(1)}, u32[]{:S(2)}, u32[]{:S(2)}) collective-permute-start(bf16[48,4096]{1,0:T(8,128)(2,1)} %refs_0_.4), channel_id=1, source_target_pairs={{0,4},{4,0},{8,12},{12,8},{1,5},{5,1},{9,13},{13,9},{2,6},{6,2},{1... | collective-permute-start | bytes 1179656 | tf_op jit(solution)/shard_map/ppermute | solution.py:169
  1.2 12.5 %collective-permute-start.1 = (bf16[48,4096]{1,0:T(8,128)(2,1)}, bf16[48,4096]{1,0:T(8,128)(2,1)S(1)}, u32[]{:S(2)}, u32[]{:S(2)}) collective-permute-start(bf16[48,4096]{1,0:T(8,128)(2,1)} %refs_0_.4), channel_id=1, source_target_pairs={{0,8},{4,12},{8,0},{12,4},{1,9},{5,13},{9,1},{13,5},{2,10},{6,14},... | collective-permute-start | bytes 1179656 | tf_op jit(solution)/shard_map/ppermute | solution.py:169
  3.8 13.3 %collective-permute-start = (bf16[48,4096]{1,0:T(8,128)(2,1)}, bf16[48,4096]{1,0:T(8,128)(2,1)S(1)}, u32[]{:S(2)}, u32[]{:S(2)}) collective-permute-start(bf16[48,4096]{1,0:T(8,128)(2,1)} %refs_0_.4), channel_id=1, source_target_pairs={{0,1},{1,2},{2,3},{3,0},{4,5},{5,6},{6,7},{7,4},{8,9},{9,10},{10,1... | collective-permute-start | bytes 1179656 | tf_op jit(solution)/shard_map/ppermute | solution.py:164
  17.0 10.7 %collective-permute-start.3 = (bf16[48,4096]{1,0:T(8,128)(2,1)}, bf16[48,4096]{1,0:T(8,128)(2,1)S(1)}, u32[]{:S(2)}, u32[]{:S(2)}) collective-permute-start(bf16[48,4096]{1,0:T(8,128)(2,1)} %refs_0_.4), channel_id=1, source_target_pairs={{0,3},{1,0},{2,1},{3,2},{4,7},{5,4},{6,5},{7,6},{8,11},{9,8},{10,9... | collective-permute-start | bytes 1179656 | tf_op jit(solution)/shard_map/ppermute | solution.py:164
  18.8 9.0 %collective-permute-start.6 = (bf16[48,4096]{1,0:T(8,128)(2,1)S(1)}, bf16[48,4096]{1,0:T(8,128)(2,1)S(1)}, u32[]{:S(2)}, u32[]{:S(2)}) collective-permute-start(bf16[48,4096]{1,0:T(8,128)(2,1)S(1)} %collective-permute-done.1.refs_2_), channel_id=1, source_target_pairs={{0,4},{4,0},{8,12},{12,8},{1,5},{5,1},{9,13},{13,9},{2,6},{6,2},{1... | collective-permute-start | bytes 1179656 | tf_op jit(solution)/shard_map/ppermute | solution.py:169
  18.8 9.0 %collective-permute-start.5 = (bf16[48,4096]{1,0:T(8,128)(2,1)S(1)}, bf16[48,4096]{1,0:T(8,128)(2,1)S(1)}, u32[]{:S(2)}, u32[]{:S(2)}) collective-permute-start(bf16[48,4096]{1,0:T(8,128)(2,1)S(1)} %collective-permute-done.refs_1_), channel_id=1, source_target_pairs={{0,4},{4,0},{8,12},{12,8},{1,5},{5,1},{9,13},{13,9},{2,6},{6,2},{1... | collective-permute-start | bytes 1179656 | tf_op jit(solution)/shard_map/ppermute | solution.py:169
  19.3 11.0 %collective-permute-start.4 = (bf16[48,4096]{1,0:T(8,128)(2,1)S(1)}, bf16[48,4096]{1,0:T(8,128)(2,1)S(1)}, u32[]{:S(2)}, u32[]{:S(2)}) collective-permute-start(bf16[48,4096]{1,0:T(8,128)(2,1)S(1)} %collective-permute-done.refs_1_), channel_id=1, source_target_pairs={{0,8},{4,12},{8,0},{12,4},{1,9},{5,13},{9,1},{13,5},{2,10},{6,14},... | collective-permute-start | bytes 1179656 | tf_op jit(solution)/shard_map/ppermute | solution.py:169
  30.3 13.3 %collective-permute-start.7 = (bf16[48,4096]{1,0:T(8,128)(2,1)S(1)}, bf16[48,4096]{1,0:T(8,128)(2,1)S(1)}, u32[]{:S(2)}, u32[]{:S(2)}) collective-permute-start(bf16[48,4096]{1,0:T(8,128)(2,1)S(1)} %collective-permute-done.refs_1_), channel_id=1, source_target_pairs={{0,1},{1,2},{2,3},{3,0},{4,5},{5,6},{6,7},{7,4},{8,9},{9,10},{10,1... | collective-permute-start | bytes 1179656 | tf_op jit(solution)/shard_map/ppermute | solution.py:164
  30.6 13.0 %collective-permute-start.8 = (bf16[48,4096]{1,0:T(8,128)(2,1)S(1)}, bf16[48,4096]{1,0:T(8,128)(2,1)S(1)}, u32[]{:S(2)}, u32[]{:S(2)}) collective-permute-start(bf16[48,4096]{1,0:T(8,128)(2,1)S(1)} %collective-permute-done.3.refs_0_.refs_8_), channel_id=1, source_target_pairs={{0,8},{4,12},{8,0},{12,4},{1,9},{5,13},{9,1},{13,5},{2,10},{6,14},... | collective-permute-start | bytes 1179656 | tf_op jit(solution)/shard_map/ppermute | solution.py:169
  43.6 17.3 %collective-permute-start.12 = (bf16[384,896]{1,0:T(8,128)(2,1)}, bf16[384,896]{1,0:T(8,128)(2,1)S(1)}, u32[]{:S(2)}, u32[]{:S(2)}) collective-permute-start(bf16[384,896]{1,0:T(8,128)(2,1)} %shard_map.92), channel_id=1, source_target_pairs={{0,16},{16,0},{1,17},{17,1},{2,18},{18,2},{3,19},{19,3},{4,20},{20... | collective-permute-start | bytes 2064392 | tf_op jit(solution)/shard_map/ppermute | solution.py:175
  45.2 12.3 %collective-permute-start.11 = (bf16[48,4096]{1,0:T(8,128)(2,1)S(1)}, bf16[48,4096]{1,0:T(8,128)(2,1)S(1)}, u32[]{:S(2)}, u32[]{:S(2)}) collective-permute-start(bf16[48,4096]{1,0:T(8,128)(2,1)S(1)} %copy-done.22), channel_id=1, source_target_pairs={{0,1},{1,2},{2,3},{3,0},{4,5},{5,6},{6,7},{7,4},{8,9},{9,10},{10,1... | collective-permute-start | bytes 1179656 | tf_op jit(solution)/shard_map/ppermute | solution.py:164
  45.2 12.3 %collective-permute-start.10 = (bf16[48,4096]{1,0:T(8,128)(2,1)S(1)}, bf16[48,4096]{1,0:T(8,128)(2,1)S(1)}, u32[]{:S(2)}, u32[]{:S(2)}) collective-permute-start(bf16[48,4096]{1,0:T(8,128)(2,1)S(1)} %collective-permute-done.7.refs_1_.refs_9_), channel_id=1, source_target_pairs={{0,8},{4,12},{8,0},{12,4},{1,9},{5,13},{9,1},{13,5},{2,10},{6,14},... | collective-permute-start | bytes 1179656 | tf_op jit(solution)/shard_map/ppermute | solution.py:169
  61.0 2.5 collective-permute-start.16
  61.0 3.9 %collective-permute-start.17 = (bf16[48,4096]{1,0:T(8,128)(2,1)S(1)}, bf16[48,4096]{1,0:T(8,128)(2,1)S(1)}, u32[]{:S(2)}, u32[]{:S(2)}) collective-permute-start(bf16[48,4096]{1,0:T(8,128)(2,1)S(1)} %collective-permute-done.7.refs_1_.refs_9_), channel_id=1, source_target_pairs={{0,4},{4,0},{8,12},{12,8},{1,5},{5,1},{9,13},{13,9},{2,6},{6,2},{1... | collective-permute-start | bytes 1179656 | tf_op jit(solution)/shard_map/ppermute | solution.py:169
  61.5 3.9 %collective-permute-start.18 = (bf16[48,4096]{1,0:T(8,128)(2,1)S(1)}, bf16[48,4096]{1,0:T(8,128)(2,1)S(1)}, u32[]{:S(2)}, u32[]{:S(2)}) collective-permute-start(bf16[48,4096]{1,0:T(8,128)(2,1)S(1)} %collective-permute-done.8.refs_2_.refs_10_), channel_id=1, source_target_pairs={{0,4},{4,0},{8,12},{12,8},{1,5},{5,1},{9,13},{13,9},{2,6},{6,2},{1... | collective-permute-start | bytes 1179656 | tf_op jit(solution)/shard_map/ppermute | solution.py:169
  61.6 5.3 %collective-permute-start.19 = (bf16[48,4096]{1,0:T(8,128)(2,1)S(1)}, bf16[48,4096]{1,0:T(8,128)(2,1)}, u32[]{:S(2)}, u32[]{:S(2)}) collective-permute-start(bf16[48,4096]{1,0:T(8,128)(2,1)S(1)} %collective-permute-done.10.refs_3_.refs_11_), channel_id=1, source_target_pairs={{0,4},{4,0},{8,12},{12,8},{1,5},{5,1},{9,13},{13,9},{2,6},{6,2},{1... | collective-permute-start | bytes 1179656 | tf_op jit(solution)/shard_map/ppermute | solution.py:169
  62.0 21.8 %collective-permute-start.20 = (bf16[384,896]{1,0:T(8,128)(2,1)}, bf16[384,896]{1,0:T(8,128)(2,1)S(1)}, u32[]{:S(2)}, u32[]{:S(2)}) collective-permute-start(bf16[384,896]{1,0:T(8,128)(2,1)} %shard_map.93), channel_id=1, source_target_pairs={{0,16},{16,0},{1,17},{17,1},{2,18},{18,2},{3,19},{19,3},{4,20},{20... | collective-permute-start | bytes 2064392 | tf_op jit(solution)/shard_map/ppermute | solution.py:175
  63.5 15.2 %collective-permute-start.15 = (bf16[48,4096]{1,0:T(8,128)(2,1)S(1)}, bf16[48,4096]{1,0:T(8,128)(2,1)S(1)}, u32[]{:S(2)}, u32[]{:S(2)}) collective-permute-start(bf16[48,4096]{1,0:T(8,128)(2,1)S(1)} %copy-done.22), channel_id=1, source_target_pairs={{0,3},{1,0},{2,1},{3,2},{4,7},{5,4},{6,5},{7,6},{8,11},{9,8},{10,9... | collective-permute-start | bytes 1179656 | tf_op jit(solution)/shard_map/ppermute | solution.py:164
  64.9 13.8 %collective-permute-start.13 = (bf16[48,4096]{1,0:T(8,128)(2,1)S(1)}, bf16[48,4096]{1,0:T(8,128)(2,1)S(1)}, u32[]{:S(2)}, u32[]{:S(2)}) collective-permute-start(bf16[48,4096]{1,0:T(8,128)(2,1)S(1)} %copy-done.22), channel_id=1, source_target_pairs={{0,8},{4,12},{8,0},{12,4},{1,9},{5,13},{9,1},{13,5},{2,10},{6,14},... | collective-permute-start | bytes 1179656 | tf_op jit(solution)/shard_map/ppermute | solution.py:169
  65.4 18.4 %collective-permute-start.14 = (bf16[48,4096]{1,0:T(8,128)(2,1)S(1)}, bf16[48,4096]{1,0:T(8,128)(2,1)S(1)}, u32[]{:S(2)}, u32[]{:S(2)}) collective-permute-start(bf16[48,4096]{1,0:T(8,128)(2,1)S(1)} %collective-permute-done.11.refs_1_), channel_id=1, source_target_pairs={{0,8},{4,12},{8,0},{12,4},{1,9},{5,13},{9,1},{13,5},{2,10},{6,14},... | collective-permute-start | bytes 1179656 | tf_op jit(solution)/shard_map/ppermute | solution.py:169
  83.8 16.1 %collective-permute-start.23 = (bf16[384,896]{1,0:T(8,128)(2,1)}, bf16[384,896]{1,0:T(8,128)(2,1)S(1)}, u32[]{:S(2)}, u32[]{:S(2)}) collective-permute-start(bf16[384,896]{1,0:T(8,128)(2,1)} %get-tuple-element.122), channel_id=1, source_target_pairs={{0,16},{16,0},{1,17},{17,1},{2,18},{18,2},{3,19},{19,3},{4,20},{20... | collective-permute-start | bytes 2064392 | tf_op jit(solution)/shard_map/ppermute | solution.py:175
  84.9 11.8 %collective-permute-start.22 = (bf16[48,4096]{1,0:T(8,128)(2,1)S(1)}, bf16[48,4096]{1,0:T(8,128)(2,1)}, u32[]{:S(2)}, u32[]{:S(2)}) collective-permute-start(bf16[48,4096]{1,0:T(8,128)(2,1)S(1)} %collective-permute-done.15.refs_8_), channel_id=1, source_target_pairs={{0,8},{4,12},{8,0},{12,4},{1,9},{5,13},{9,1},{13,5},{2,10},{6,14},... | collective-permute-start | bytes 1179656 | tf_op jit(solution)/shard_map/ppermute | solution.py:169
  85.4 11.2 %collective-permute-start.21 = (bf16[48,4096]{1,0:T(8,128)(2,1)S(1)}, bf16[48,4096]{1,0:T(8,128)(2,1)S(1)}, u32[]{:S(2)}, u32[]{:S(2)}) collective-permute-start(bf16[48,4096]{1,0:T(8,128)(2,1)S(1)} %collective-permute-done.11.refs_1_), channel_id=1, source_target_pairs={{0,1},{1,2},{2,3},{3,0},{4,5},{5,6},{6,7},{7,4},{8,9},{9,10},{10,1... | collective-permute-start | bytes 1179656 | tf_op jit(solution)/shard_map/ppermute | solution.py:164
  100.0 1.7 collective-permute-start.25
  100.0 31.0 %collective-permute-start.24 = (bf16[192,4096]{1,0:T(8,128)(2,1)}, bf16[192,4096]{1,0:T(8,128)(2,1)}, u32[]{:S(2)}, u32[]{:S(2)}) collective-permute-start(bf16[192,4096]{1,0:T(8,128)(2,1)} %get-tuple-element.124), channel_id=1, source_target_pairs={{0,4},{4,0},{8,12},{12,8},{1,5},{5,1},{9,13},{13,9},{2,6},{6,2},{1... | collective-permute-start | bytes 4718600 | tf_op jit(solution)/shard_map/ppermute | solution.py:169
  100.5 11.3 %collective-permute-start.29 = (bf16[48,4096]{1,0:T(8,128)(2,1)}, bf16[48,4096]{1,0:T(8,128)(2,1)S(1)}, u32[]{:S(2)}, u32[]{:S(2)}) collective-permute-start(bf16[48,4096]{1,0:T(8,128)(2,1)} %copy-done.27), channel_id=1, source_target_pairs={{0,8},{4,12},{8,0},{12,4},{1,9},{5,13},{9,1},{13,5},{2,10},{6,14},... | collective-permute-start | bytes 1179656 | tf_op jit(solution)/shard_map/ppermute | solution.py:169
  101.0 10.8 %collective-permute-start.26 = (bf16[48,4096]{1,0:T(8,128)(2,1)S(1)}, bf16[48,4096]{1,0:T(8,128)(2,1)S(1)}, u32[]{:S(2)}, u32[]{:S(2)}) collective-permute-start(bf16[48,4096]{1,0:T(8,128)(2,1)S(1)} %collective-permute-done.11.refs_1_), channel_id=1, source_target_pairs={{0,4},{4,0},{8,12},{12,8},{1,5},{5,1},{9,13},{13,9},{2,6},{6,2},{1... | collective-permute-start | bytes 1179656 | tf_op jit(solution)/shard_map/ppermute | solution.py:169
  101.0 11.3 %collective-permute-start.27 = (bf16[48,4096]{1,0:T(8,128)(2,1)S(1)}, bf16[48,4096]{1,0:T(8,128)(2,1)S(1)}, u32[]{:S(2)}, u32[]{:S(2)}) collective-permute-start(bf16[48,4096]{1,0:T(8,128)(2,1)S(1)} %collective-permute-done.13.refs_2_), channel_id=1, source_target_pairs={{0,4},{4,0},{8,12},{12,8},{1,5},{5,1},{9,13},{13,9},{2,6},{6,2},{1... | collective-permute-start | bytes 1179656 | tf_op jit(solution)/shard_map/ppermute | solution.py:169
  101.7 10.7 %collective-permute-start.28 = (bf16[48,4096]{1,0:T(8,128)(2,1)S(1)}, bf16[48,4096]{1,0:T(8,128)(2,1)S(1)}, u32[]{:S(2)}, u32[]{:S(2)}) collective-permute-start(bf16[48,4096]{1,0:T(8,128)(2,1)S(1)} %collective-permute-done.14.refs_3_), channel_id=1, source_target_pairs={{0,4},{4,0},{8,12},{12,8},{1,5},{5,1},{9,13},{13,9},{2,6},{6,2},{1... | collective-permute-start | bytes 1179656 | tf_op jit(solution)/shard_map/ppermute | solution.py:169
  111.8 3.2 %collective-permute-start.31 = (bf16[48,4096]{1,0:T(8,128)(2,1)}, bf16[48,4096]{1,0:T(8,128)(2,1)S(1)}, u32[]{:S(2)}, u32[]{:S(2)}) collective-permute-start(bf16[48,4096]{1,0:T(8,128)(2,1)} %copy-done.27), channel_id=1, source_target_pairs={{0,4},{4,0},{8,12},{12,8},{1,5},{5,1},{9,13},{13,9},{2,6},{6,2},{1... | collective-permute-start | bytes 1179656 | tf_op jit(solution)/shard_map/ppermute | solution.py:169
  112.3 3.1 %collective-permute-start.32 = (bf16[48,4096]{1,0:T(8,128)(2,1)}, bf16[48,4096]{1,0:T(8,128)(2,1)S(1)}, u32[]{:S(2)}, u32[]{:S(2)}) collective-permute-start(bf16[48,4096]{1,0:T(8,128)(2,1)} %collective-permute-done.22.refs_10_), channel_id=1, source_target_pairs={{0,4},{4,0},{8,12},{12,8},{1,5},{5,1},{9,13},{13,9},{2,6},{6,2},{1... | collective-permute-start | bytes 1179656 | tf_op jit(solution)/shard_map/ppermute | solution.py:169
  112.4 3.0 %collective-permute-start.33 = (bf16[48,4096]{1,0:T(8,128)(2,1)S(1)}, bf16[48,4096]{1,0:T(8,128)(2,1)}, u32[]{:S(2)}, u32[]{:S(2)}) collective-permute-start(bf16[48,4096]{1,0:T(8,128)(2,1)S(1)} %collective-permute-done.29.refs_11_), channel_id=1, source_target_pairs={{0,4},{4,0},{8,12},{12,8},{1,5},{5,1},{9,13},{13,9},{2,6},{6,2},{1... | collective-permute-start | bytes 1179656 | tf_op jit(solution)/shard_map/ppermute | solution.py:169
  113.5 17.5 %collective-permute-start.34 = (bf16[384,896]{1,0:T(8,128)(2,1)S(1)}, bf16[384,896]{1,0:T(8,128)(2,1)S(1)}, u32[]{:S(2)}, u32[]{:S(2)}) collective-permute-start(bf16[384,896]{1,0:T(8,128)(2,1)S(1)} %copy-done.3), channel_id=1, source_target_pairs={{0,16},{16,0},{1,17},{17,1},{2,18},{18,2},{3,19},{19,3},{4,20},{20... | collective-permute-start | bytes 2064392 | tf_op jit(solution)/shard_map/ppermute | solution.py:175
  133.2 18.9 %collective-permute-start.35 = (bf16[96,4096]{1,0:T(8,128)(2,1)}, bf16[96,4096]{1,0:T(8,128)(2,1)S(1)}, u32[]{:S(2)}, u32[]{:S(2)}) collective-permute-start(bf16[96,4096]{1,0:T(8,128)(2,1)} %add_convert_fusion.3), channel_id=1, source_target_pairs={{0,8},{4,12},{8,0},{12,4},{1,9},{5,13},{9,1},{13,5},{2,10},{6,14},... | collective-permute-start | bytes 2359304 | tf_op jit(solution)/shard_map/ppermute | solution.py:169
  133.7 16.6 %collective-permute-start.36 = (bf16[384,896]{1,0:T(8,128)(2,1)}, bf16[384,896]{1,0:T(8,128)(2,1)}, u32[]{:S(2)}, u32[]{:S(2)}) collective-permute-start(bf16[384,896]{1,0:T(8,128)(2,1)} %get-tuple-element.147), channel_id=1, source_target_pairs={{0,16},{16,0},{1,17},{17,1},{2,18},{18,2},{3,19},{19,3},{4,20},{20... | collective-permute-start | bytes 2064392 | tf_op jit(solution)/shard_map/ppermute | solution.py:175
  152.1 3.6 %collective-permute-start.37 = (bf16[192,4096]{1,0:T(8,128)(2,1)}, bf16[192,4096]{1,0:T(8,128)(2,1)S(1)}, u32[]{:S(2)}, u32[]{:S(2)}) collective-permute-start(bf16[192,4096]{1,0:T(8,128)(2,1)} %get-tuple-element.153), channel_id=1, source_target_pairs={{0,4},{4,0},{8,12},{12,8},{1,5},{5,1},{9,13},{13,9},{2,6},{6,2},{1... | collective-permute-start | bytes 4718600 | tf_op jit(solution)/shard_map/ppermute | solution.py:169
  152.1 23.2 %collective-permute-start.40 = (bf16[384,896]{1,0:T(8,128)(2,1)}, bf16[384,896]{1,0:T(8,128)(2,1)}, u32[]{:S(2)}, u32[]{:S(2)}) collective-permute-start(bf16[384,896]{1,0:T(8,128)(2,1)} %get-tuple-element.155), channel_id=1, source_target_pairs={{0,16},{16,0},{1,17},{17,1},{2,18},{18,2},{3,19},{19,3},{4,20},{20... | collective-permute-start | bytes 2064392 | tf_op jit(solution)/shard_map/ppermute | solution.py:175
  157.1 19.9 %collective-permute-start.38 = (bf16[96,4096]{1,0:T(8,128)(2,1)}, bf16[96,4096]{1,0:T(8,128)(2,1)}, u32[]{:S(2)}, u32[]{:S(2)}) collective-permute-start(bf16[96,4096]{1,0:T(8,128)(2,1)} %add_convert_fusion.2), channel_id=1, source_target_pairs={{0,8},{4,12},{8,0},{12,4},{1,9},{5,13},{9,1},{13,5},{2,10},{6,14},... | collective-permute-start | bytes 2359304 | tf_op jit(solution)/shard_map/ppermute | solution.py:169
  161.1 14.2 %collective-permute-start.39 = (bf16[48,4096]{1,0:T(8,128)(2,1)}, bf16[48,4096]{1,0:T(8,128)(2,1)S(1)}, u32[]{:S(2)}, u32[]{:S(2)}) collective-permute-start(bf16[48,4096]{1,0:T(8,128)(2,1)} %add_convert_fusion.9), channel_id=1, source_target_pairs={{0,3},{1,0},{2,1},{3,2},{4,7},{5,4},{6,5},{7,6},{8,11},{9,8},{10,9... | collective-permute-start | bytes 1179656 | tf_op jit(solution)/shard_map/ppermute | solution.py:164
  177.0 4.2 %collective-permute-start.41 = (bf16[192,4096]{1,0:T(8,128)(2,1)}, bf16[192,4096]{1,0:T(8,128)(2,1)S(1)}, u32[]{:S(2)}, u32[]{:S(2)}) collective-permute-start(bf16[192,4096]{1,0:T(8,128)(2,1)} %get-tuple-element.161), channel_id=1, source_target_pairs={{0,4},{4,0},{8,12},{12,8},{1,5},{5,1},{9,13},{13,9},{2,6},{6,2},{1... | collective-permute-start | bytes 4718600 | tf_op jit(solution)/shard_map/ppermute | solution.py:169
  179.7 20.7 %collective-permute-start.44 = (bf16[48,4096]{1,0:T(8,128)(2,1)}, bf16[48,4096]{1,0:T(8,128)(2,1)}, u32[]{:S(2)}, u32[]{:S(2)}) collective-permute-start(bf16[48,4096]{1,0:T(8,128)(2,1)} %get-tuple-element.181), channel_id=1, source_target_pairs={{0,1},{1,2},{2,3},{3,0},{4,5},{5,6},{6,7},{7,4},{8,9},{9,10},{10,1... | collective-permute-start | bytes 1179656 | tf_op jit(solution)/shard_map/ppermute | solution.py:164
  180.4 29.2 %collective-permute-start.43 = (bf16[48,4096]{1,0:T(8,128)(2,1)}, bf16[48,4096]{1,0:T(8,128)(2,1)}, u32[]{:S(2)}, u32[]{:S(2)}) collective-permute-start(bf16[48,4096]{1,0:T(8,128)(2,1)} %get-tuple-element.182), channel_id=1, source_target_pairs={{0,2},{1,3},{2,0},{3,1},{4,6},{5,7},{6,4},{7,5},{8,10},{9,11},{10,... | collective-permute-start | bytes 1179656 | tf_op jit(solution)/shard_map/ppermute | solution.py:164
  183.5 26.1 %collective-permute-start.42 = (bf16[96,4096]{1,0:T(8,128)(2,1)}, bf16[96,4096]{1,0:T(8,128)(2,1)}, u32[]{:S(2)}, u32[]{:S(2)}) collective-permute-start(bf16[96,4096]{1,0:T(8,128)(2,1)} %add_convert_fusion.1), channel_id=1, source_target_pairs={{0,8},{4,12},{8,0},{12,4},{1,9},{5,13},{9,1},{13,5},{2,10},{6,14},... | collective-permute-start | bytes 2359304 | tf_op jit(solution)/shard_map/ppermute | solution.py:169
  209.5 5.3 %collective-permute-start.45 = (bf16[192,4096]{1,0:T(8,128)(2,1)}, bf16[192,4096]{1,0:T(8,128)(2,1)S(1)}, u32[]{:S(2)}, u32[]{:S(2)}) collective-permute-start(bf16[192,4096]{1,0:T(8,128)(2,1)} %get-tuple-element.166), channel_id=1, source_target_pairs={{0,4},{4,0},{8,12},{12,8},{1,5},{5,1},{9,13},{13,9},{2,6},{6,2},{1... | collective-permute-start | bytes 4718600 | tf_op jit(solution)/shard_map/ppermute | solution.py:169
  211.9 22.5 %collective-permute-start.48 = (bf16[48,4096]{1,0:T(8,128)(2,1)}, bf16[48,4096]{1,0:T(8,128)(2,1)S(1)}, u32[]{:S(2)}, u32[]{:S(2)}) collective-permute-start(bf16[48,4096]{1,0:T(8,128)(2,1)} %get-tuple-element.179), channel_id=1, source_target_pairs={{0,1},{1,2},{2,3},{3,0},{4,5},{5,6},{6,7},{7,4},{8,9},{9,10},{10,1... | collective-permute-start | bytes 1179656 | tf_op jit(solution)/shard_map/ppermute | solution.py:164
  211.9 29.5 %collective-permute-start.47 = (bf16[48,4096]{1,0:T(8,128)(2,1)}, bf16[48,4096]{1,0:T(8,128)(2,1)S(1)}, u32[]{:S(2)}, u32[]{:S(2)}) collective-permute-start(bf16[48,4096]{1,0:T(8,128)(2,1)} %get-tuple-element.180), channel_id=1, source_target_pairs={{0,2},{1,3},{2,0},{3,1},{4,6},{5,7},{6,4},{7,5},{8,10},{9,11},{10,... | collective-permute-start | bytes 1179656 | tf_op jit(solution)/shard_map/ppermute | solution.py:164
  215.1 26.3 %collective-permute-start.46 = (bf16[96,4096]{1,0:T(8,128)(2,1)S(1)}, bf16[96,4096]{1,0:T(8,128)(2,1)S(1)}, u32[]{:S(2)}, u32[]{:S(2)}) collective-permute-start(bf16[96,4096]{1,0:T(8,128)(2,1)S(1)} %add_convert_fusion), channel_id=1, source_target_pairs={{0,8},{4,12},{8,0},{12,4},{1,9},{5,13},{9,1},{13,5},{2,10},{6,14},... | collective-permute-start | bytes 2359304 | tf_op jit(solution)/shard_map/ppermute | solution.py:169
  241.5 13.2 %collective-permute-start.49 = (bf16[48,4096]{1,0:T(8,128)(2,1)S(1)}, bf16[48,4096]{1,0:T(8,128)(2,1)S(1)}, u32[]{:S(2)}, u32[]{:S(2)}) collective-permute-start(bf16[48,4096]{1,0:T(8,128)(2,1)S(1)} %add_convert_fusion.4), channel_id=1, source_target_pairs={{0,3},{1,0},{2,1},{3,2},{4,7},{5,4},{6,5},{7,6},{8,11},{9,8},{10,9... | collective-permute-start | bytes 1179656 | tf_op jit(solution)/shard_map/ppermute | solution.py:164
  (45 other events, 548.8 us)

commit v5 on v4

v5 whole, which is shorter than its diff:
```python
import functools

import jax
import jax.numpy as jnp
from jax import lax
from jax.experimental import pallas as pl
from jax.experimental.pallas import tpu as pltpu
from jax.sharding import PartitionSpec as P

CORE, CHIP = 1, 2
VMEM_BYTES = 56 * 1024 * 1024


def dot(left, right, left_dim, right_dim):
    return lax.dot_general(
        left, right, (((left_dim,), (right_dim,)), ((), ())), preferred_element_type=jnp.float32
    )


def after(array, *others):
    return lax.optimization_barrier((array, *others))[0]


def wide(block):
    return block.astype(jnp.float32)


def narrow(block):
    return block.astype(jnp.bfloat16)


def cost(flops, *arrays):
    moved = sum(array.size * array.dtype.itemsize for array in arrays)
    return pl.CostEstimate(flops=flops, bytes_accessed=moved, transcendentals=0)


def contract_kernel(n_pieces, n_weights, right_dim, *refs):
    pieces, weights = refs[:n_pieces], refs[n_pieces : n_pieces + n_weights]
    out, total = refs[-2:]
    step = pl.program_id(0)

    @pl.when(step == 0)
    def _():
        total[...] = jnp.zeros_like(total)

    rows = jnp.concatenate([piece[...] for piece in pieces], axis=0)
    for i, weight in enumerate(weights):
        total[i * rows.shape[0] : (i + 1) * rows.shape[0]] += dot(rows, weight[...], 1, right_dim)

    @pl.when(step == pl.num_programs(0) - 1)
    def _():
        out[...] = narrow(total[...])


def contract(pieces, weights, right_dim):
    width = pieces[0].shape[1]
    units = weights[0].shape[1 - right_dim]
    block = min(1024, width)
    if right_dim == 0:
        weight_spec = pl.BlockSpec((block, units), lambda k: (k, 0))
    else:
        weight_spec = pl.BlockSpec((units, block), lambda k: (0, k))
    rows = sum(piece.shape[0] for piece in pieces)
    shape = (rows * len(weights), units)
    return pl.pallas_call(
        functools.partial(contract_kernel, len(pieces), len(weights), right_dim),
        grid=(width // block,),
        in_specs=[pl.BlockSpec((piece.shape[0], block), lambda k: (0, k)) for piece in pieces]
        + [weight_spec] * len(weights),
        out_specs=pl.BlockSpec(shape, lambda k: (0, 0)),
        out_shape=jax.ShapeDtypeStruct(shape, jnp.bfloat16),
        scratch_shapes=[pltpu.VMEM(shape, jnp.float32)],
        compiler_params=pltpu.CompilerParams(vmem_limit_bytes=VMEM_BYTES),
        cost_estimate=cost(2 * len(weights) * rows * width * units, *pieces, *weights),
    )(*pieces, *weights)


def store_halves(total, outs):
    size = total.shape[0] // 8
    for i, out in enumerate(outs):
        for at, (half, block) in enumerate(((0, 0), (0, 1), (1, 0), (1, 1))):
            first = (4 * block + 2 * i + half) * size
            out[at * size : (at + 1) * size] = narrow(total[first : first + size])


def expand_kernel(n, *refs):
    lefts, weights, outs = refs[: 2 * n], refs[2 * n : 3 * n], refs[3 * n :]
    total = 0.0
    for i, weight in enumerate(weights):
        left = jnp.concatenate([block[...] for block in lefts[2 * i : 2 * i + 2]], axis=0)
        total = total + dot(left, weight[...], 1, 1)
    store_halves(total, outs)


def expand(lefts, weights):
    blocks = sum(lefts, [])
    rows, units = blocks[0].shape
    width = weights[0].shape[0]
    block = min(512, width)
    out = jax.ShapeDtypeStruct((rows, width), jnp.bfloat16)
    return pl.pallas_call(
        functools.partial(expand_kernel, len(lefts)),
        grid=(width // block,),
        in_specs=[pl.BlockSpec((rows, units), lambda j: (0, 0))] * len(blocks)
        + [pl.BlockSpec((block, units), lambda j: (j, 0))] * len(weights),
        out_specs=[pl.BlockSpec((rows, block), lambda j: (0, j))] * 2,
        out_shape=[out, out],
        compiler_params=pltpu.CompilerParams(vmem_limit_bytes=VMEM_BYTES),
        cost_estimate=cost(4 * len(lefts) * rows * width * units, *blocks, *weights, out, out),
    )(*blocks, *weights)


def down_kernel(n_pieces, *refs):
    pieces, (first, second, weight, grad, mine, other, total) = refs[:n_pieces], refs[n_pieces:]
    step = pl.program_id(0)

    @pl.when(step == 0)
    def _():
        total[...] = jnp.zeros_like(total)

    rows = jnp.concatenate([piece[...] for piece in pieces], axis=0)
    total[...] += dot(rows, weight[...], 1, 1)
    hidden = jnp.concatenate([first[...], second[...]], axis=0)
    store_halves(dot(hidden, weight[...], 1, 0), (mine, other))

    @pl.when(step == pl.num_programs(0) - 1)
    def _():
        grad[...] = narrow(total[...])


def down_products(pieces, hiddens, weight):
    units, width = weight.shape
    block = min(512, width)
    rows = sum(piece.shape[0] for piece in pieces)
    half = hiddens[0].shape[0]
    grad = jax.ShapeDtypeStruct((rows, units), jnp.bfloat16)
    out = jax.ShapeDtypeStruct((half, width), jnp.bfloat16)
    return pl.pallas_call(
        functools.partial(down_kernel, len(pieces)),
        grid=(width // block,),
        in_specs=[pl.BlockSpec((piece.shape[0], block), lambda j: (0, j)) for piece in pieces]
        + [pl.BlockSpec((half, units), lambda j: (0, 0))] * 2
        + [pl.BlockSpec((units, block), lambda j: (0, j))],
        out_specs=[pl.BlockSpec(grad.shape, lambda j: (0, 0))]
        + [pl.BlockSpec((half, block), lambda j: (0, j))] * 2,
        out_shape=[grad, out, out],
        scratch_shapes=[pltpu.VMEM(grad.shape, jnp.float32)],
        compiler_params=pltpu.CompilerParams(vmem_limit_bytes=VMEM_BYTES),
        cost_estimate=cost(4 * rows * width * units, *pieces, *hiddens, weight, out, out),
    )(*pieces, *hiddens, weight)


def wide_grad_kernel(n_pieces, *refs):
    pieces, grads, outs = refs[:n_pieces], refs[n_pieces:-2], refs[-2:]
    rows = jnp.concatenate([piece[...] for piece in pieces], axis=0)
    half = len(grads) // 2
    for i, out in enumerate(outs):
        grad = jnp.concatenate([grad[...] for grad in grads[i * half : (i + 1) * half]], axis=0)
        out[...] = dot(rows, grad, 0, 0)


def wide_grads(pieces, gate_grads, up_grads):
    grads = [*gate_grads, *up_grads]
    width, units = pieces[0].shape[1], grads[0].shape[1]
    block = min(512, width)
    rows = sum(piece.shape[0] for piece in pieces)
    out = jax.ShapeDtypeStruct((width, units), jnp.float32)
    return pl.pallas_call(
        functools.partial(wide_grad_kernel, len(pieces)),
        grid=(width // block,),
        in_specs=[pl.BlockSpec((piece.shape[0], block), lambda j: (0, j)) for piece in pieces]
        + [pl.BlockSpec(grad.shape, lambda j: (0, 0)) for grad in grads],
        out_specs=[pl.BlockSpec((block, units), lambda j: (j, 0))] * 2,
        out_shape=[out, out],
        compiler_params=pltpu.CompilerParams(vmem_limit_bytes=VMEM_BYTES),
        cost_estimate=cost(4 * rows * width * units, *pieces, *grads, out, out),
    )(*pieces, *grads)


def tall_grad_kernel(n_pieces, *refs):
    pieces, hiddens, out = refs[:n_pieces], refs[n_pieces:-1], refs[-1]
    rows = jnp.concatenate([piece[...] for piece in pieces], axis=0)
    hidden = jnp.concatenate([hidden[...] for hidden in hiddens], axis=0)
    out[...] = dot(hidden, rows, 0, 0)


def tall_grad(pieces, hiddens):
    width, units = pieces[0].shape[1], hiddens[0].shape[1]
    block = min(512, width)
    rows = sum(piece.shape[0] for piece in pieces)
    out = jax.ShapeDtypeStruct((units, width), jnp.float32)
    return pl.pallas_call(
        functools.partial(tall_grad_kernel, len(pieces)),
        grid=(width // block,),
        in_specs=[pl.BlockSpec((piece.shape[0], block), lambda j: (0, j)) for piece in pieces]
        + [pl.BlockSpec(hidden.shape, lambda j: (0, 0)) for hidden in hiddens],
        out_specs=pl.BlockSpec((units, block), lambda j: (0, j)),
        out_shape=out,
        compiler_params=pltpu.CompilerParams(vmem_limit_bytes=VMEM_BYTES),
        cost_estimate=cost(2 * rows * width * units, *pieces, *hiddens, out),
    )(*pieces, *hiddens)


def shift(block, step):
    n = lax.axis_size("depth")
    return lax.ppermute(block, "depth", [(i, (i + step) % n) for i in range(n)])


def swap(block, bit):
    n = lax.axis_size("col")
    return lax.ppermute(block, "col", [(i, i ^ bit) for i in range(n)])


def row_moves(partial):
    n = lax.axis_size("row")
    return [
        lax.ppermute(partial, "row", [(i, (i + step) % n) for i in range(n)])
        for step in range(1, n)
    ]


def row_sum(partial, moved, *others):
    return sum([wide(after(block, *others)) for block in moved], wide(partial))


def add(*blocks):
    return narrow(sum(wide(block) for block in blocks))


def grads_of(gate, up, hidden_grad):
    sigma = jax.nn.sigmoid(gate)
    gate_grad = narrow(hidden_grad * up * sigma * (1.0 + gate * (1.0 - sigma)))
    return gate_grad, narrow(hidden_grad * (gate * sigma))


def hidden_of(gate, up):
    return narrow(gate * jax.nn.sigmoid(gate) * up)


def sync(*arrays):
    return lax.optimization_barrier(arrays)


def other_cores(blocks):
    return [swap(block, CORE) for block in blocks]


def chip_part(mine, moved):
    half = mine.shape[0] // 2
    return add(mine[half:], moved[half:]), (mine[:half], moved[:half])


def owner_parts(kept, moved):
    size = moved.shape[0] // 2
    rows = [slice(0, size), slice(size, 2 * size)]
    return [sum(wide(block[at]) for block in (*kept, moved)) for at in rows]


def quad(near, far, moved):
    return [near, far, *moved]


def body(tokens, gate_weight, up_weight, down_weight, cotangent):
    pair = [gate_weight, up_weight]

    def pair_sums(partial, moved):
        half = partial.shape[0] // 2
        total = row_sum(partial, moved)
        return total[:half], total[half:]

    near1, far0, core0 = sync(shift(tokens, 1), swap(tokens, CHIP), swap(tokens, CORE))

    near3, far1 = shift(after(tokens, near1), 3), swap(near1, CHIP)
    core1, far_core0 = other_cores([near1, far0])
    token0 = quad(tokens, far0, [core0, far_core0])
    pair0 = contract(token0, pair, 0)
    near3, far1, core1, pair0 = sync(near3, far1, core1, pair0)

    pair0_moved = row_moves(pair0)
    cot = after(cotangent, pair0)
    near2, cot_near3 = shift(near1, 1), shift(cot, 3)
    far3, cot_far0 = swap(near3, CHIP), swap(cot, CHIP)
    token1 = quad(near1, far1, [core1, swap(far1, CORE)])
    pair1 = contract(token1, pair, 0)
    near2, cot_near3, far3, cot_far0, pair1, *pair0_moved = sync(
        near2, cot_near3, far3, cot_far0, pair1, *pair0_moved
    )

    gate0, up0 = pair_sums(pair0, pair0_moved)
    hidden0 = hidden_of(gate0, up0)
    pair1_moved = row_moves(pair1)
    cot = after(cotangent, pair1)
    cot_near2 = shift(cot, 2)
    far2, cot_far3 = swap(near2, CHIP), swap(cot_near3, CHIP)
    token3 = quad(near3, far3, other_cores([after(near3, pair1), far3]))
    pair3 = contract(token3, pair, 0)
    cot_near2, far2, cot_far3, pair3, *pair1_moved = sync(
        cot_near2, far2, cot_far3, pair3, *pair1_moved
    )

    gate1, up1 = pair_sums(pair1, pair1_moved)
    hidden1 = hidden_of(gate1, up1)
    pair3_moved = row_moves(pair3)
    cot = after(cotangent, pair3)
    cot_near1, cot_far2 = shift(cot, 1), swap(cot_near2, CHIP)
    token2 = quad(near2, far2, other_cores([after(near2, pair3), far2]))
    pair2 = contract(token2, pair, 0)
    cot_near1, cot_far2, pair2, *pair3_moved = sync(cot_near1, cot_far2, pair2, *pair3_moved)

    gate3, up3 = pair_sums(pair3, pair3_moved)
    hidden3 = hidden_of(gate3, up3)
    pair2_moved = row_moves(pair2)
    cot_far1 = swap(cot_near1, CHIP)
    cot3 = quad(cot_near3, cot_far3, other_cores(after(x, pair2) for x in (cot_near3, cot_far3)))
    cot2 = quad(cot_near2, cot_far2, other_cores(after(x, pair2) for x in (cot_near2, cot_far2)))
    grad_b, mine, other = down_products(cot3 + cot2, [hidden0, hidden1], down_weight)
    cot_far1, grad_b, mine, other, *pair2_moved = sync(
        cot_far1, grad_b, mine, other, *pair2_moved
    )

    gate2, up2 = pair_sums(pair2, pair2_moved)
    hidden2 = hidden_of(gate2, up2)
    grad_b_moved = row_moves(grad_b)
    sent, mixed_a = chip_part(mine, swap(other, CORE))
    mixed_a_moved = swap(sent, CHIP)
    cot = after(cotangent, grad_b)
    cot0 = quad(cot, cot_far0, other_cores([cot, after(cot_far0, grad_b)]))
    cot1 = quad(cot_near1, cot_far1, other_cores([after(cot_near1, grad_b), cot_far1]))
    grad_a, mine, other = down_products(cot0 + cot1, [hidden3, hidden2], down_weight)
    mixed_a_moved, grad_a, mine, other, *grad_b_moved = sync(
        mixed_a_moved, grad_a, mine, other, *grad_b_moved
    )

    grad_b = row_sum(grad_b, grad_b_moved)
    grad_a_moved = row_moves(grad_a)
    sent, mixed_b = chip_part(mine, swap(other, CORE))
    mixed_b_moved = swap(sent, CHIP)
    half = grad_b.shape[0] // 2
    grads3 = grads_of(gate3, up3, grad_b[:half])
    grads2 = grads_of(gate2, up2, grad_b[half:])
    mine, other = expand([[x, y] for x, y in zip(grads3, grads2)], pair)
    mixed_b_moved, mine, other, *grad_a_moved = sync(mixed_b_moved, mine, other, *grad_a_moved)

    grad_a = row_sum(grad_a, grad_a_moved)
    sent, token_grad_b = chip_part(mine, swap(other, CORE))
    token_b_moved = swap(sent, CHIP)
    mixed_b = owner_parts(mixed_b, mixed_b_moved)
    part3, part2 = shift(narrow(mixed_b[0]), 1), shift(narrow(mixed_b[1]), -1)
    grads0 = grads_of(gate0, up0, grad_a[:half])
    grads1 = grads_of(gate1, up1, grad_a[half:])
    mine, other = expand([[x, y] for x, y in zip(grads0, grads1)], pair)
    token_b_moved, mine, other, part3, part2 = sync(token_b_moved, mine, other, part3, part2)

    sent, token_grad_a = chip_part(mine, swap(other, CORE))
    token_a_moved = swap(sent, CHIP)
    mixed_a = owner_parts(mixed_a, mixed_a_moved)
    part1 = shift(narrow(mixed_a[1] + wide(part2)), -1)
    mixed = mixed_a[0] + wide(part3)
    token_grad_b = owner_parts(token_grad_b, token_b_moved)
    part3, part2 = shift(narrow(token_grad_b[0]), 1), shift(narrow(token_grad_b[1]), -1)
    gate_total, up_total = wide_grads(
        [after(tokens, sent), *token0[1:], *token1, *token3, *token2],
        [grads0[0], grads1[0], grads3[0], grads2[0]],
        [grads0[1], grads1[1], grads3[1], grads2[1]],
    )
    token_a_moved, part1, part2, part3, gate_total, up_total = sync(
        token_a_moved, part1, part2, part3, gate_total, up_total
    )
    mixed = mixed + wide(part1)

    token_grad_a = owner_parts(token_grad_a, token_a_moved)
    part1 = shift(narrow(token_grad_a[1] + wide(part2)), -1)
    down_total = tall_grad(
        cot0 + cot1 + cot3 + cot2, [after(hidden0, gate_total), hidden1, hidden3, hidden2]
    )
    token_grad = token_grad_a[0] + wide(part3) + wide(part1)
    return (mixed, token_grad, gate_total, up_total, down_total)


def solution(mesh):
    activations = P(("depth", "col"), "row")
    wide_weight = P("row", ("col", "depth"))
    tall_weight = P(("col", "depth"), "row")
    return jax.shard_map(
        body,
        mesh=mesh,
        in_specs=(activations, wide_weight, wide_weight, tall_weight, activations),
        out_specs=(activations, activations, wide_weight, wide_weight, tall_weight),
        check_vma=False,
    )
```

time: 258 us -> 241 us (0.934)
  waiting for transfers between devices: 81.5 us -> 41.6 us
  starting transfers between devices: 31.9 us -> 50.2 us
  local copies, waits for them, and re-layouts: 2.9 us -> 6.92 us
  Pallas kernels: 114 us -> 118 us
  other arithmetic: 24.8 us -> 21.4 us
    ppermute x12, waiting for transfers between devices: 34.4 us -> 17 us  [shift(): return lax.ppermute(block, 'depth', [(i, (i + step) % n) for i in range(n)])]
    ppermute x12, starting transfers between devices: 9.22 us -> 25.4 us  [shift(): return lax.ppermute(block, 'depth', [(i, (i + step) % n) for i in range(n)])]
    ppermute x6, waiting for transfers between devices: 15.2 us -> 3.38 us  [row_moves(): lax.ppermute(partial, 'row', [(i, (i + step) % n) for i in range(n)])]
    ppermute x32, waiting for transfers between devices: 31.9 us -> 21.2 us  [swap(): return lax.ppermute(block, 'col', [(i, i ^ bit) for i in range(n)])]
    pallas_call x4, Pallas kernels: 43.6 us -> 50.9 us  [the longest x2 25.8 us: expand(): pl.pallas_call(functools.partial(expand_kernel, len(lefts)), grid=(width...]
    convert_element_type x12 -> x13, other arithmetic: 21.2 us -> 14.7 us  [narrow(): return block.astype(jnp.bfloat16)]
    unnamed x86 -> x88, local copies, waits for them, and re-layouts: 2.9 us -> 6.92 us
    add x2 -> x8, other arithmetic: 3.57 us -> 6.68 us  [the longest x6 3.22 us: row_sum(): return sum([wide(after(block, *others)) for block in moved], wide(partial))]
  transfers between devices with their start and end apart: 50 -> 50, of which waited for: 22 -> 16; matrix products, arithmetic and copies ran while one was open for 8% -> 8% of each run, Pallas kernels for 44% -> 49%
where the time goes in v5:
time: 241 us; the launch traced here: 239 us
  Pallas kernels  118 us (49%)
  starting transfers between devices  50.2 us (21%)
  waiting for transfers between devices  41.6 us (17%)
  other arithmetic  21.4 us (9%)
  local copies, waits for them, and re-layouts  6.92 us (3%)
    pallas_call x4, Pallas kernels, contract(): pl.pallas_call(functools.partial(contract_kernel, len(pieces), len(weight...  35.6 us
    pallas_call x2, Pallas kernels, expand(): pl.pallas_call(functools.partial(expand_kernel, len(lefts)), grid=(width...  25.8 us
    ppermute x12, starting transfers between devices, shift(): return lax.ppermute(block, 'depth', [(i, (i + step) % n) for i in range(n)])  25.4 us
    pallas_call x2, Pallas kernels, down_products(): pl.pallas_call(functools.partial(down_kernel, len(pieces)), grid=(width /...  25.1 us
    ppermute x32, waiting for transfers between devices, swap(): return lax.ppermute(block, 'col', [(i, i ^ bit) for i in range(n)])  21.2 us
    pallas_call x1, Pallas kernels, wide_grads(): pl.pallas_call(functools.partial(wide_grad_kernel, len(pieces)), grid=(wi...  18.6 us
    ppermute x12, waiting for transfers between devices, shift(): return lax.ppermute(block, 'depth', [(i, (i + step) % n) for i in range(n)])  17 us
    ppermute x32, starting transfers between devices, swap(): return lax.ppermute(block, 'col', [(i, i ^ bit) for i in range(n)])  16.9 us
  transfers between devices with their start and end apart: 50, of which 16 were waited for; matrix products, arithmetic and copies ran while one was open for 8% of the time, Pallas kernels for 49%

profile of v5, /device:TPU:0, one launch (start us, length us, event | category | flops | bytes accessed | tf_op | source)
XLA Modules:
  0.0 239.2 jit_solution(5295099975082078787)
XLA Ops:
  1.2 2.6 %collective-permute-start.1 = (bf16[48,4096]{1,0:T(8,128)(2,1)}, bf16[48,4096]{1,0:T(8,128)(2,1)S(1)}, u32[]{:S(2)}, u32[]{:S(2)}) collective-permute-start(bf16[48,4096]{1,0:T(8,128)(2,1)} %refs_0_.3), channel_id=1, source_target_pairs={{0,8},{4,12},{8,0},{12,4},{1,9},{5,13},{9,1},{13,5},{2,10},{6,14},... | collective-permute-start | bytes 1179656 | tf_op jit(solution)/shard_map/ppermute | solution.py:211
  3.8 1.6 collective-permute-start
  5.3 8.3 %collective-permute-done.1.refs_1_ = bf16[48,4096]{1,0:T(8,128)(2,1)S(1)} collective-permute-done((bf16[48,4096]{1,0:T(8,128)(2,1)}, bf16[48,4096]{1,0:T(8,128)(2,1)S(1)}, u32[]{:S(2)}, u32[]{:S(2)}) %collective-permute-start.1) | collective-permute-done | bytes 393248 | tf_op jit(solution)/shard_map/ppermute | solution.py:211
  13.7 3.4 %collective-permute-done.refs_0_.refs_4_ = bf16[48,4096]{1,0:T(8,128)(2,1)S(1)} collective-permute-done((bf16[48,4096]{1,0:T(8,128)(2,1)}, bf16[48,4096]{1,0:T(8,128)(2,1)S(1)}, u32[]{:S(2)}, u32[]{:S(2)}) %collective-permute-start) | collective-permute-done | bytes 393248 | tf_op jit(solution)/shard_map/ppermute | solution.py:206
  17.0 1.7 collective-permute-start.4
  20.3 8.9 %shard_map.92 = bf16[384,896]{1,0:T(8,128)(2,1)} custom-call(bf16[48,4096]{1,0:T(8,128)(2,1)} %refs_0_.3, bf16[48,4096]{1,0:T(8,128)(2,1)} %copy-done.19, bf16[48,4096]{1,0:T(8,128)(2,1)} %copy-done.18, bf16[48,4096]{1,0:T(8,128)(2,1)} %copy-done.22, bf16[4096,896]{1,0:T(8,128)(2,1)} %refs_4_.11, bf16[4096,896]{1,0:T(8,128)(2,1)} %refs_5_.11), custom_call_target="tpu_custom_call" | custom-call | flops 2818572288 | bytes 16252928 | tf_op jit(solution)/shard_map/pallas_call | solution.py:65
  30.3 1.5 collective-permute-start.12
  32.7 3.5 %collective-permute-start.8 = (bf16[48,4096]{1,0:T(8,128)(2,1)S(1)}, bf16[48,4096]{1,0:T(8,128)(2,1)S(1)}, u32[]{:S(2)}, u32[]{:S(2)}) collective-permute-start(bf16[48,4096]{1,0:T(8,128)(2,1)S(1)} %copy-done.17), channel_id=1, source_target_pairs={{0,3},{1,0},{2,1},{3,2},{4,7},{5,4},{6,5},{7,6},{8,11},{9,8},{10,9... | collective-permute-start | bytes 1179656 | tf_op jit(solution)/shard_map/ppermute | solution.py:206
  36.2 1.5 collective-permute-start.9
  37.7 8.9 %shard_map.93 = bf16[384,896]{1,0:T(8,128)(2,1)} custom-call(bf16[48,4096]{1,0:T(8,128)(2,1)} %copy-done.20, bf16[48,4096]{1,0:T(8,128)(2,1)} %copy-done.25, bf16[48,4096]{1,0:T(8,128)(2,1)} %copy-done.24, bf16[48,4096]{1,0:T(8,128)(2,1)} %copy-done.26, bf16[4096,896]{1,0:T(8,128)(2,1)} %refs_4_.11, bf16[4096,896]{1,0:T(8,128)(2,1)} %refs_5_.11), custom_call_target="tpu_custom_call" | custom-call | flops 2818572288 | bytes 16252928 | tf_op jit(solution)/shard_map/pallas_call | solution.py:65
  46.6 5.2 %collective-permute-done.8.refs_0_.refs_8_ = bf16[48,4096]{1,0:T(8,128)(2,1)S(1)} collective-permute-done((bf16[48,4096]{1,0:T(8,128)(2,1)S(1)}, bf16[48,4096]{1,0:T(8,128)(2,1)S(1)}, u32[]{:S(2)}, u32[]{:S(2)}) %collective-permute-start.8) | collective-permute-done | bytes 393248 | tf_op jit(solution)/shard_map/ppermute | solution.py:206
  52.6 2.1 collective-permute-start.13
  55.2 1.5 collective-permute-start.15
  57.6 8.9 %shard_map.94 = bf16[384,896]{1,0:T(8,128)(2,1)} custom-call(bf16[48,4096]{1,0:T(8,128)(2,1)} %copy-done.23, bf16[48,4096]{1,0:T(8,128)(2,1)} %copy-done.29, bf16[48,4096]{1,0:T(8,128)(2,1)} %copy-done.30, bf16[48,4096]{1,0:T(8,128)(2,1)} %copy-done.31, bf16[4096,896]{1,0:T(8,128)(2,1)} %refs_4_.11, bf16[4096,896]{1,0:T(8,128)(2,1)} %refs_5_.11), custom_call_target="tpu_custom_call" | custom-call | flops 2818572288 | bytes 16252928 | tf_op jit(solution)/shard_map/pallas_call | solution.py:65
  66.4 6.9 %collective-permute-done.13.refs_4_.refs_12_ = bf16[48,4096]{1,0:T(8,128)(2,1)S(1)} collective-permute-done((bf16[48,4096]{1,0:T(8,128)(2,1)S(1)}, bf16[48,4096]{1,0:T(8,128)(2,1)S(1)}, u32[]{:S(2)}, u32[]{:S(2)}) %collective-permute-start.13) | collective-permute-done | bytes 393248 | tf_op jit(solution)/shard_map/ppermute | solution.py:206
  74.4 1.5 collective-permute-start.23
  76.4 1.7 collective-permute-start.19
  79.5 8.9 %shard_map.95 = bf16[384,896]{1,0:T(8,128)(2,1)} custom-call(bf16[48,4096]{1,0:T(8,128)(2,1)} %copy-done.27, bf16[48,4096]{1,0:T(8,128)(2,1)} %copy-done.35, bf16[48,4096]{1,0:T(8,128)(2,1)} %copy-done.40, bf16[48,4096]{1,0:T(8,128)(2,1)} %collective-permute-done.22.refs_3_.refs_15_, bf16[4096,896]{1,0:T(8,128)(2,1)} %refs_4_.11, bf16[4096,896]{1,0:T(8,128)(2,1)} %refs_5_.11), custom_call_target="tpu_custom_call" | custom-call | flops 2818572288 | bytes 16252928 | tf_op jit(solution)/shard_map/pallas_call | solution.py:65
  89.2 1.9 collective-permute-done.23
  92.3 1.6 collective-permute-start.29
  93.9 1.2 multiply_convert_fusion.10
  97.1 12.6 %shard_map.96 = (bf16[384,896]{1,0:T(8,128)(2,1)}, bf16[192,4096]{1,0:T(8,128)(2,1)}, bf16[192,4096]{1,0:T(8,128)(2,1)}) custom-call(bf16[48,4096]{1,0:T(8,128)(2,1)} %copy-done.21, bf16[48,4096]{1,0:T(8,128)(2,1)} %collective-permute-done.15.refs_1_.refs_9_, bf16[48,4096]{1,0:T(8,128)(2,1)} %copy-done.36, bf16[48,4096]{1,0:T(8,128)(2,1)} %copy-done.37, ...), custom_call_target="tpu_custom_call" | custom-call | flops 5637144576 | bytes 14319616 | tf_op jit(solution)/shard_map/pallas_call | solution.py:138
  111.9 1.5 collective-permute-done.30
  113.7 1.2 collective-permute-start.31
  115.0 1.3 collective-permute-start.36
  118.8 12.5 %shard_map.97 = (bf16[384,896]{1,0:T(8,128)(2,1)}, bf16[192,4096]{1,0:T(8,128)(2,1)}, bf16[192,4096]{1,0:T(8,128)(2,1)}) custom-call(bf16[48,4096]{1,0:T(8,128)(2,1)} %refs_0_.4, bf16[48,4096]{1,0:T(8,128)(2,1)} %collective-permute-done.10.refs_1_, bf16[48,4096]{1,0:T(8,128)(2,1)} %copy-done.41, bf16[48,4096]{1,0:T(8,128)(2,1)} %copy-done.42, ...), custom_call_target="tpu_custom_call" | custom-call | flops 5637144576 | bytes 14319616 | tf_op jit(solution)/shard_map/pallas_call | solution.py:138
  131.3 1.4 collective-permute-done.36
  133.4 1.4 collective-permute-start.39
  134.8 1.4 convert_add_fusion.1
  140.4 1.7 multiply_convert_fusion.4
  142.1 12.9 %shard_map.98 = (bf16[192,4096]{1,0:T(8,128)(2,1)}, bf16[192,4096]{1,0:T(8,128)(2,1)}) custom-call(bf16[192,896]{1,0:T(8,128)(2,1)} %get-tuple-element.167.refs_0_.refs_18_, bf16[192,896]{1,0:T(8,128)(2,1)} %get-tuple-element.162.refs_1_.refs_19_, bf16[192,896]{1,0:T(8,128)(2,1)} %get-tuple-element.168.refs_2_.refs_22_, ...), custom_call_target="tpu_custom_call" | custom-call | flops 5637144576 | bytes 19202048 | tf_op jit(solution)/shard_map/pallas_call | solution.py:101
  155.0 4.1 %collective-permute-done.38 = bf16[96,4096]{1,0:T(8,128)(2,1)S(1)} collective-permute-done((bf16[96,4096]{1,0:T(8,128)(2,1)}, bf16[96,4096]{1,0:T(8,128)(2,1)S(1)}, u32[]{:S(2)}, u32[]{:S(2)}) %collective-permute-start.38) | collective-permute-done | bytes 786464 | tf_op jit(solution)/shard_map/ppermute | solution.py:211
  159.1 1.2 add_convert_fusion.8
  160.3 2.8 %collective-permute-start.43 = (bf16[48,4096]{1,0:T(8,128)(2,1)}, bf16[48,4096]{1,0:T(8,128)(2,1)}, u32[]{:S(2)}, u32[]{:S(2)}) collective-permute-start(bf16[48,4096]{1,0:T(8,128)(2,1)} %get-tuple-element.155), channel_id=1, source_target_pairs={{0,3},{1,0},{2,1},{3,2},{4,7},{5,4},{6,5},{7,6},{8,11},{9,8},{10,9... | collective-permute-start | bytes 1179656 | tf_op jit(solution)/shard_map/ppermute | solution.py:206
  163.1 1.2 convert_add_fusion
  165.4 1.2 collective-permute-start.41
  166.6 1.7 multiply_convert_fusion
  168.3 12.9 %shard_map.99 = (bf16[192,4096]{1,0:T(8,128)(2,1)}, bf16[192,4096]{1,0:T(8,128)(2,1)}) custom-call(bf16[192,896]{1,0:T(8,128)(2,1)} %get-tuple-element.165.refs_0_.refs_16_, bf16[192,896]{1,0:T(8,128)(2,1)} %get-tuple-element.158.refs_1_.refs_17_, bf16[192,896]{1,0:T(8,128)(2,1)} %get-tuple-element.166.refs_2_.refs_20_, ...), custom_call_target="tpu_custom_call" | custom-call | flops 5637144576 | bytes 19202048 | tf_op jit(solution)/shard_map/pallas_call | solution.py:101
  181.6 3.7 %collective-permute-done.41 = bf16[96,4096]{1,0:T(8,128)(2,1)S(1)} collective-permute-done((bf16[96,4096]{1,0:T(8,128)(2,1)}, bf16[96,4096]{1,0:T(8,128)(2,1)S(1)}, u32[]{:S(2)}, u32[]{:S(2)}) %collective-permute-start.41) | collective-permute-done | bytes 786464 | tf_op jit(solution)/shard_map/ppermute | solution.py:211
  185.3 2.1 add_convert_fusion.7
  187.4 3.5 %collective-permute-start.46 = (bf16[48,4096]{1,0:T(8,128)(2,1)}, bf16[48,4096]{1,0:T(8,128)(2,1)}, u32[]{:S(2)}, u32[]{:S(2)}) collective-permute-start(bf16[48,4096]{1,0:T(8,128)(2,1)} %add_convert_fusion.7), channel_id=1, source_target_pairs={{0,3},{1,0},{2,1},{3,2},{4,7},{5,4},{6,5},{7,6},{8,11},{9,8},{10,9... | collective-permute-start | bytes 1179656 | tf_op jit(solution)/shard_map/ppermute | solution.py:206
  192.1 3.8 %collective-permute-start.47 = (bf16[48,4096]{1,0:T(8,128)(2,1)}, bf16[48,4096]{1,0:T(8,128)(2,1)}, u32[]{:S(2)}, u32[]{:S(2)}) collective-permute-start(bf16[48,4096]{1,0:T(8,128)(2,1)} %get-tuple-element.154), channel_id=1, source_target_pairs={{0,3},{1,0},{2,1},{3,2},{4,7},{5,4},{6,5},{7,6},{8,11},{9,8},{10,9... | collective-permute-start | bytes 1179656 | tf_op jit(solution)/shard_map/ppermute | solution.py:206
  197.1 1.2 collective-permute-start.45
  198.2 18.6 %shard_map.100 = (f32[4096,896]{1,0:T(8,128)}, f32[4096,896]{1,0:T(8,128)}) custom-call(bf16[48,4096]{1,0:T(8,128)(2,1)} %refs_0_.3, bf16[48,4096]{1,0:T(8,128)(2,1)} %copy-done.19, bf16[48,4096]{1,0:T(8,128)(2,1)} %copy-done.18, bf16[48,4096]{1,0:T(8,128)(2,1)} %copy-done.22, bf16[48,4096]{1,0:T(8,128)(2,1)} %copy-done.20, bf16[48,4096]{1,0:T(8,128)(2,1)} %copy-done.25, ...), custom_call_target="tpu_custom_call" | custom-call | flops 11274289152 | bytes 38404096 | tf_op jit(solution)/shard_map/pallas_call | solution.py:168
  217.2 1.2 add_convert_fusion.4
  218.4 4.3 %collective-permute-start.49 = (bf16[48,4096]{1,0:T(8,128)(2,1)S(1)}, bf16[48,4096]{1,0:T(8,128)(2,1)S(1)}, u32[]{:S(2)}, u32[]{:S(2)}) collective-permute-start(bf16[48,4096]{1,0:T(8,128)(2,1)S(1)} %add_convert_fusion.4), channel_id=1, source_target_pairs={{0,3},{1,0},{2,1},{3,2},{4,7},{5,4},{6,5},{7,6},{8,11},{9,8},{10,9... | collective-permute-start | bytes 1179656 | tf_op jit(solution)/shard_map/ppermute | solution.py:206
  222.7 2.3 convert_add_fusion.7
  225.1 13.0 %shard_map.101 = f32[896,4096]{1,0:T(8,128)} custom-call(bf16[48,4096]{1,0:T(8,128)(2,1)} %refs_0_.4, bf16[48,4096]{1,0:T(8,128)(2,1)} %collective-permute-done.10.refs_1_, bf16[48,4096]{1,0:T(8,128)(2,1)} %copy-done.41, bf16[48,4096]{1,0:T(8,128)(2,1)} %copy-done.42, bf16[48,4096]{1,0:T(8,128)(2,1)} %copy-done.32, ...), custom_call_target="tpu_custom_call" | custom-call | flops 5637144576 | bytes 22347776 | tf_op jit(solution)/shard_map/pallas_call | solution.py:192
  (171 shorter events, 28.1 us)
Async XLA Ops:
  0.6 4.7 %collective-permute-start.2 = (bf16[48,4096]{1,0:T(8,128)(2,1)}, bf16[48,4096]{1,0:T(8,128)(2,1)S(1)}, u32[]{:S(2)}, u32[]{:S(2)}) collective-permute-start(bf16[48,4096]{1,0:T(8,128)(2,1)} %refs_0_.3), channel_id=1, source_target_pairs={{0,4},{4,0},{8,12},{12,8},{1,5},{5,1},{9,13},{13,9},{2,6},{6,2},{1... | collective-permute-start | bytes 1179656 | tf_op jit(solution)/shard_map/ppermute | solution.py:211
  1.2 12.5 %collective-permute-start.1 = (bf16[48,4096]{1,0:T(8,128)(2,1)}, bf16[48,4096]{1,0:T(8,128)(2,1)S(1)}, u32[]{:S(2)}, u32[]{:S(2)}) collective-permute-start(bf16[48,4096]{1,0:T(8,128)(2,1)} %refs_0_.3), channel_id=1, source_target_pairs={{0,8},{4,12},{8,0},{12,4},{1,9},{5,13},{9,1},{13,5},{2,10},{6,14},... | collective-permute-start | bytes 1179656 | tf_op jit(solution)/shard_map/ppermute | solution.py:211
  3.8 13.3 %collective-permute-start = (bf16[48,4096]{1,0:T(8,128)(2,1)}, bf16[48,4096]{1,0:T(8,128)(2,1)S(1)}, u32[]{:S(2)}, u32[]{:S(2)}) collective-permute-start(bf16[48,4096]{1,0:T(8,128)(2,1)} %refs_0_.3), channel_id=1, source_target_pairs={{0,1},{1,2},{2,3},{3,0},{4,5},{5,6},{6,7},{7,4},{8,9},{9,10},{10,1... | collective-permute-start | bytes 1179656 | tf_op jit(solution)/shard_map/ppermute | solution.py:206
  17.0 12.1 %collective-permute-start.4 = (bf16[48,4096]{1,0:T(8,128)(2,1)}, bf16[48,4096]{1,0:T(8,128)(2,1)S(1)}, u32[]{:S(2)}, u32[]{:S(2)}) collective-permute-start(bf16[48,4096]{1,0:T(8,128)(2,1)} %refs_0_.3), channel_id=1, source_target_pairs={{0,3},{1,0},{2,1},{3,2},{4,7},{5,4},{6,5},{7,6},{8,11},{9,8},{10,9... | collective-permute-start | bytes 1179656 | tf_op jit(solution)/shard_map/ppermute | solution.py:206
  18.8 10.4 %collective-permute-start.6 = (bf16[48,4096]{1,0:T(8,128)(2,1)S(1)}, bf16[48,4096]{1,0:T(8,128)(2,1)S(1)}, u32[]{:S(2)}, u32[]{:S(2)}) collective-permute-start(bf16[48,4096]{1,0:T(8,128)(2,1)S(1)} %collective-permute-done.refs_0_.refs_4_), channel_id=1, source_target_pairs={{0,4},{4,0},{8,12},{12,8},{1,5},{5,1},{9,13},{13,9},{2,6},{6,2},{1... | collective-permute-start | bytes 1179656 | tf_op jit(solution)/shard_map/ppermute | solution.py:211
  19.0 11.3 %collective-permute-start.5 = (bf16[48,4096]{1,0:T(8,128)(2,1)S(1)}, bf16[48,4096]{1,0:T(8,128)(2,1)S(1)}, u32[]{:S(2)}, u32[]{:S(2)}) collective-permute-start(bf16[48,4096]{1,0:T(8,128)(2,1)S(1)} %collective-permute-done.refs_0_.refs_4_), channel_id=1, source_target_pairs={{0,8},{4,12},{8,0},{12,4},{1,9},{5,13},{9,1},{13,5},{2,10},{6,14},... | collective-permute-start | bytes 1179656 | tf_op jit(solution)/shard_map/ppermute | solution.py:211
  30.3 5.9 %collective-permute-start.11 = (bf16[48,4096]{1,0:T(8,128)(2,1)S(1)}, bf16[48,4096]{1,0:T(8,128)(2,1)S(1)}, u32[]{:S(2)}, u32[]{:S(2)}) collective-permute-start(bf16[48,4096]{1,0:T(8,128)(2,1)S(1)} %collective-permute-done.5.refs_1_.refs_5_), channel_id=1, source_target_pairs={{0,4},{4,0},{8,12},{12,8},{1,5},{5,1},{9,13},{13,9},{2,6},{6,2},{1... | collective-permute-start | bytes 1179656 | tf_op jit(solution)/shard_map/ppermute | solution.py:211
  30.3 21.5 %collective-permute-start.12 = (bf16[384,896]{1,0:T(8,128)(2,1)}, bf16[384,896]{1,0:T(8,128)(2,1)S(1)}, u32[]{:S(2)}, u32[]{:S(2)}) collective-permute-start(bf16[384,896]{1,0:T(8,128)(2,1)} %shard_map.92), channel_id=1, source_target_pairs={{0,16},{16,0},{1,17},{17,1},{2,18},{18,2},{3,19},{19,3},{4,20},{20... | collective-permute-start | bytes 2064392 | tf_op jit(solution)/shard_map/ppermute | solution.py:217
  31.8 14.8 %collective-permute-start.3 = (bf16[48,4096]{1,0:T(8,128)(2,1)S(1)}, bf16[48,4096]{1,0:T(8,128)(2,1)S(1)}, u32[]{:S(2)}, u32[]{:S(2)}) collective-permute-start(bf16[48,4096]{1,0:T(8,128)(2,1)S(1)} %collective-permute-done.refs_0_.refs_4_), channel_id=1, source_target_pairs={{0,1},{1,2},{2,3},{3,0},{4,5},{5,6},{6,7},{7,4},{8,9},{9,10},{10,1... | collective-permute-start | bytes 1179656 | tf_op jit(solution)/shard_map/ppermute | solution.py:206
  32.1 14.5 %collective-permute-start.10 = (bf16[48,4096]{1,0:T(8,128)(2,1)S(1)}, bf16[48,4096]{1,0:T(8,128)(2,1)}, u32[]{:S(2)}, u32[]{:S(2)}) collective-permute-start(bf16[48,4096]{1,0:T(8,128)(2,1)S(1)} %copy-done.17), channel_id=1, source_target_pairs={{0,8},{4,12},{8,0},{12,4},{1,9},{5,13},{9,1},{13,5},{2,10},{6,14},... | collective-permute-start | bytes 1179656 | tf_op jit(solution)/shard_map/ppermute | solution.py:211
  32.7 19.1 %collective-permute-start.8 = (bf16[48,4096]{1,0:T(8,128)(2,1)S(1)}, bf16[48,4096]{1,0:T(8,128)(2,1)S(1)}, u32[]{:S(2)}, u32[]{:S(2)}) collective-permute-start(bf16[48,4096]{1,0:T(8,128)(2,1)S(1)} %copy-done.17), channel_id=1, source_target_pairs={{0,3},{1,0},{2,1},{3,2},{4,7},{5,4},{6,5},{7,6},{8,11},{9,8},{10,9... | collective-permute-start | bytes 1179656 | tf_op jit(solution)/shard_map/ppermute | solution.py:206
  36.2 15.6 %collective-permute-start.9 = (bf16[48,4096]{1,0:T(8,128)(2,1)S(1)}, bf16[48,4096]{1,0:T(8,128)(2,1)S(1)}, u32[]{:S(2)}, u32[]{:S(2)}) collective-permute-start(bf16[48,4096]{1,0:T(8,128)(2,1)S(1)} %collective-permute-done.4.refs_0_.refs_8_), channel_id=1, source_target_pairs={{0,8},{4,12},{8,0},{12,4},{1,9},{5,13},{9,1},{13,5},{2,10},{6,14},... | collective-permute-start | bytes 1179656 | tf_op jit(solution)/shard_map/ppermute | solution.py:211
  51.8 3.5 %collective-permute-start.16 = (bf16[48,4096]{1,0:T(8,128)(2,1)S(1)}, bf16[48,4096]{1,0:T(8,128)(2,1)S(1)}, u32[]{:S(2)}, u32[]{:S(2)}) collective-permute-start(bf16[48,4096]{1,0:T(8,128)(2,1)S(1)} %collective-permute-done.4.refs_0_.refs_8_), channel_id=1, source_target_pairs={{0,4},{4,0},{8,12},{12,8},{1,5},{5,1},{9,13},{13,9},{2,6},{6,2},{1... | collective-permute-start | bytes 1179656 | tf_op jit(solution)/shard_map/ppermute | solution.py:211
  51.9 22.5 %collective-permute-start.18 = (bf16[384,896]{1,0:T(8,128)(2,1)}, bf16[384,896]{1,0:T(8,128)(2,1)S(1)}, u32[]{:S(2)}, u32[]{:S(2)}) collective-permute-start(bf16[384,896]{1,0:T(8,128)(2,1)} %shard_map.93), channel_id=1, source_target_pairs={{0,16},{16,0},{1,17},{17,1},{2,18},{18,2},{3,19},{19,3},{4,20},{20... | collective-permute-start | bytes 2064392 | tf_op jit(solution)/shard_map/ppermute | solution.py:217
  52.5 4.3 %collective-permute-start.17 = (bf16[48,4096]{1,0:T(8,128)(2,1)S(1)}, bf16[48,4096]{1,0:T(8,128)(2,1)S(1)}, u32[]{:S(2)}, u32[]{:S(2)}) collective-permute-start(bf16[48,4096]{1,0:T(8,128)(2,1)S(1)} %collective-permute-done.9.refs_1_.refs_9_), channel_id=1, source_target_pairs={{0,4},{4,0},{8,12},{12,8},{1,5},{5,1},{9,13},{13,9},{2,6},{6,2},{1... | collective-permute-start | bytes 1179656 | tf_op jit(solution)/shard_map/ppermute | solution.py:211
  52.6 20.7 %collective-permute-start.13 = (bf16[48,4096]{1,0:T(8,128)(2,1)S(1)}, bf16[48,4096]{1,0:T(8,128)(2,1)S(1)}, u32[]{:S(2)}, u32[]{:S(2)}) collective-permute-start(bf16[48,4096]{1,0:T(8,128)(2,1)S(1)} %copy-done.17), channel_id=1, source_target_pairs={{0,2},{1,3},{2,0},{3,1},{4,6},{5,7},{6,4},{7,5},{8,10},{9,11},{10,... | collective-permute-start | bytes 1179656 | tf_op jit(solution)/shard_map/ppermute | solution.py:206
  54.7 18.6 %collective-permute-start.14 = (bf16[48,4096]{1,0:T(8,128)(2,1)S(1)}, bf16[48,4096]{1,0:T(8,128)(2,1)S(1)}, u32[]{:S(2)}, u32[]{:S(2)}) collective-permute-start(bf16[48,4096]{1,0:T(8,128)(2,1)S(1)} %collective-permute-done.3.refs_0_.refs_12_), channel_id=1, source_target_pairs={{0,8},{4,12},{8,0},{12,4},{1,9},{5,13},{9,1},{13,5},{2,10},{6,14},... | collective-permute-start | bytes 1179656 | tf_op jit(solution)/shard_map/ppermute | solution.py:211
  55.2 19.1 %collective-permute-start.15 = (bf16[48,4096]{1,0:T(8,128)(2,1)S(1)}, bf16[48,4096]{1,0:T(8,128)(2,1)}, u32[]{:S(2)}, u32[]{:S(2)}) collective-permute-start(bf16[48,4096]{1,0:T(8,128)(2,1)S(1)} %collective-permute-done.8.refs_0_.refs_8_), channel_id=1, source_target_pairs={{0,8},{4,12},{8,0},{12,4},{1,9},{5,13},{9,1},{13,5},{2,10},{6,14},... | collective-permute-start | bytes 1179656 | tf_op jit(solution)/shard_map/ppermute | solution.py:211
  74.4 16.8 %collective-permute-start.23 = (bf16[384,896]{1,0:T(8,128)(2,1)}, bf16[384,896]{1,0:T(8,128)(2,1)S(1)}, u32[]{:S(2)}, u32[]{:S(2)}) collective-permute-start(bf16[384,896]{1,0:T(8,128)(2,1)} %shard_map.94), channel_id=1, source_target_pairs={{0,16},{16,0},{1,17},{17,1},{2,18},{18,2},{3,19},{19,3},{4,20},{20... | collective-permute-start | bytes 2064392 | tf_op jit(solution)/shard_map/ppermute | solution.py:217
  75.9 3.6 %collective-permute-start.22 = (bf16[48,4096]{1,0:T(8,128)(2,1)S(1)}, bf16[48,4096]{1,0:T(8,128)(2,1)}, u32[]{:S(2)}, u32[]{:S(2)}) collective-permute-start(bf16[48,4096]{1,0:T(8,128)(2,1)S(1)} %collective-permute-done.14.refs_1_.refs_13_), channel_id=1, source_target_pairs={{0,4},{4,0},{8,12},{12,8},{1,5},{5,1},{9,13},{13,9},{2,6},{6,2},{1... | collective-permute-start | bytes 1179656 | tf_op jit(solution)/shard_map/ppermute | solution.py:211
  76.4 12.8 %collective-permute-start.19 = (bf16[48,4096]{1,0:T(8,128)(2,1)S(1)}, bf16[48,4096]{1,0:T(8,128)(2,1)S(1)}, u32[]{:S(2)}, u32[]{:S(2)}) collective-permute-start(bf16[48,4096]{1,0:T(8,128)(2,1)S(1)} %copy-done.17), channel_id=1, source_target_pairs={{0,1},{1,2},{2,3},{3,0},{4,5},{5,6},{6,7},{7,4},{8,9},{9,10},{10,1... | collective-permute-start | bytes 1179656 | tf_op jit(solution)/shard_map/ppermute | solution.py:206
  78.1 11.1 %collective-permute-start.20 = (bf16[48,4096]{1,0:T(8,128)(2,1)S(1)}, bf16[48,4096]{1,0:T(8,128)(2,1)}, u32[]{:S(2)}, u32[]{:S(2)}) collective-permute-start(bf16[48,4096]{1,0:T(8,128)(2,1)S(1)} %collective-permute-done.13.refs_4_.refs_12_), channel_id=1, source_target_pairs={{0,8},{4,12},{8,0},{12,4},{1,9},{5,13},{9,1},{13,5},{2,10},{6,14},... | collective-permute-start | bytes 1179656 | tf_op jit(solution)/shard_map/ppermute | solution.py:211
  91.1 4.0 %collective-permute-start.25 = (bf16[48,4096]{1,0:T(8,128)(2,1)S(1)}, bf16[48,4096]{1,0:T(8,128)(2,1)S(1)}, u32[]{:S(2)}, u32[]{:S(2)}) collective-permute-start(bf16[48,4096]{1,0:T(8,128)(2,1)S(1)} %collective-permute-done.8.refs_0_.refs_8_), channel_id=1, source_target_pairs={{0,4},{4,0},{8,12},{12,8},{1,5},{5,1},{9,13},{13,9},{2,6},{6,2},{1... | collective-permute-start | bytes 1179656 | tf_op jit(solution)/shard_map/ppermute | solution.py:211
  91.1 5.0 %collective-permute-start.26 = (bf16[48,4096]{1,0:T(8,128)(2,1)}, bf16[48,4096]{1,0:T(8,128)(2,1)S(1)}, u32[]{:S(2)}, u32[]{:S(2)}) collective-permute-start(bf16[48,4096]{1,0:T(8,128)(2,1)} %collective-permute-done.15.refs_1_.refs_9_), channel_id=1, source_target_pairs={{0,4},{4,0},{8,12},{12,8},{1,5},{5,1},{9,13},{13,9},{2,6},{6,2},{1... | collective-permute-start | bytes 1179656 | tf_op jit(solution)/shard_map/ppermute | solution.py:211
  91.7 4.5 %collective-permute-start.27 = (bf16[48,4096]{1,0:T(8,128)(2,1)S(1)}, bf16[48,4096]{1,0:T(8,128)(2,1)S(1)}, u32[]{:S(2)}, u32[]{:S(2)}) collective-permute-start(bf16[48,4096]{1,0:T(8,128)(2,1)S(1)} %collective-permute-done.13.refs_4_.refs_12_), channel_id=1, source_target_pairs={{0,4},{4,0},{8,12},{12,8},{1,5},{5,1},{9,13},{13,9},{2,6},{6,2},{1... | collective-permute-start | bytes 1179656 | tf_op jit(solution)/shard_map/ppermute | solution.py:211
  91.7 4.5 %collective-permute-start.28 = (bf16[48,4096]{1,0:T(8,128)(2,1)}, bf16[48,4096]{1,0:T(8,128)(2,1)S(1)}, u32[]{:S(2)}, u32[]{:S(2)}) collective-permute-start(bf16[48,4096]{1,0:T(8,128)(2,1)} %collective-permute-done.20.refs_5_.refs_13_), channel_id=1, source_target_pairs={{0,4},{4,0},{8,12},{12,8},{1,5},{5,1},{9,13},{13,9},{2,6},{6,2},{1... | collective-permute-start | bytes 1179656 | tf_op jit(solution)/shard_map/ppermute | solution.py:211
  92.3 17.4 %collective-permute-start.29 = (bf16[384,896]{1,0:T(8,128)(2,1)S(1)}, bf16[384,896]{1,0:T(8,128)(2,1)S(1)}, u32[]{:S(2)}, u32[]{:S(2)}) collective-permute-start(bf16[384,896]{1,0:T(8,128)(2,1)S(1)} %copy-done.3), channel_id=1, source_target_pairs={{0,16},{16,0},{1,17},{17,1},{2,18},{18,2},{3,19},{19,3},{4,20},{20... | collective-permute-start | bytes 2064392 | tf_op jit(solution)/shard_map/ppermute | solution.py:217
  95.1 14.6 %collective-permute-start.24 = (bf16[48,4096]{1,0:T(8,128)(2,1)S(1)}, bf16[48,4096]{1,0:T(8,128)(2,1)}, u32[]{:S(2)}, u32[]{:S(2)}) collective-permute-start(bf16[48,4096]{1,0:T(8,128)(2,1)S(1)} %copy-done.33), channel_id=1, source_target_pairs={{0,8},{4,12},{8,0},{12,4},{1,9},{5,13},{9,1},{13,5},{2,10},{6,14},... | collective-permute-start | bytes 1179656 | tf_op jit(solution)/shard_map/ppermute | solution.py:211
  109.8 3.7 %collective-permute-start.30 = (bf16[192,4096]{1,0:T(8,128)(2,1)}, bf16[192,4096]{1,0:T(8,128)(2,1)S(1)}, u32[]{:S(2)}, u32[]{:S(2)}) collective-permute-start(bf16[192,4096]{1,0:T(8,128)(2,1)} %get-tuple-element.113), channel_id=1, source_target_pairs={{0,4},{4,0},{8,12},{12,8},{1,5},{5,1},{9,13},{13,9},{2,6},{6,2},{1... | collective-permute-start | bytes 4718600 | tf_op jit(solution)/shard_map/ppermute | solution.py:211
  110.9 4.1 %collective-permute-start.32 = (bf16[48,4096]{1,0:T(8,128)(2,1)S(1)}, bf16[48,4096]{1,0:T(8,128)(2,1)S(1)}, u32[]{:S(2)}, u32[]{:S(2)}) collective-permute-start(bf16[48,4096]{1,0:T(8,128)(2,1)S(1)} %copy-done.17), channel_id=1, source_target_pairs={{0,4},{4,0},{8,12},{12,8},{1,5},{5,1},{9,13},{13,9},{2,6},{6,2},{1... | collective-permute-start | bytes 1179656 | tf_op jit(solution)/shard_map/ppermute | solution.py:211
  111.4 5.9 %collective-permute-start.33 = (bf16[48,4096]{1,0:T(8,128)(2,1)}, bf16[48,4096]{1,0:T(8,128)(2,1)S(1)}, u32[]{:S(2)}, u32[]{:S(2)}) collective-permute-start(bf16[48,4096]{1,0:T(8,128)(2,1)} %collective-permute-done.10.refs_1_), channel_id=1, source_target_pairs={{0,4},{4,0},{8,12},{12,8},{1,5},{5,1},{9,13},{13,9},{2,6},{6,2},{1... | collective-permute-start | bytes 1179656 | tf_op jit(solution)/shard_map/ppermute | solution.py:211
  111.4 5.8 %collective-permute-start.34 = (bf16[48,4096]{1,0:T(8,128)(2,1)S(1)}, bf16[48,4096]{1,0:T(8,128)(2,1)S(1)}, u32[]{:S(2)}, u32[]{:S(2)}) collective-permute-start(bf16[48,4096]{1,0:T(8,128)(2,1)S(1)} %copy-done.34), channel_id=1, source_target_pairs={{0,4},{4,0},{8,12},{12,8},{1,5},{5,1},{9,13},{13,9},{2,6},{6,2},{1... | collective-permute-start | bytes 1179656 | tf_op jit(solution)/shard_map/ppermute | solution.py:211
  111.9 6.8 %collective-permute-start.35 = (bf16[48,4096]{1,0:T(8,128)(2,1)}, bf16[48,4096]{1,0:T(8,128)(2,1)}, u32[]{:S(2)}, u32[]{:S(2)}) collective-permute-start(bf16[48,4096]{1,0:T(8,128)(2,1)} %collective-permute-done.24.refs_5_), channel_id=1, source_target_pairs={{0,4},{4,0},{8,12},{12,8},{1,5},{5,1},{9,13},{13,9},{2,6},{6,2},{1... | collective-permute-start | bytes 1179656 | tf_op jit(solution)/shard_map/ppermute | solution.py:211
  113.7 19.8 %collective-permute-start.31 = (bf16[96,4096]{1,0:T(8,128)(2,1)S(1)}, bf16[96,4096]{1,0:T(8,128)(2,1)}, u32[]{:S(2)}, u32[]{:S(2)}) collective-permute-start(bf16[96,4096]{1,0:T(8,128)(2,1)S(1)} %add_convert_fusion.3), channel_id=1, source_target_pairs={{0,8},{4,12},{8,0},{12,4},{1,9},{5,13},{9,1},{13,5},{2,10},{6,14},... | collective-permute-start | bytes 2359304 | tf_op jit(solution)/shard_map/ppermute | solution.py:211
  115.0 17.7 %collective-permute-start.36 = (bf16[384,896]{1,0:T(8,128)(2,1)}, bf16[384,896]{1,0:T(8,128)(2,1)}, u32[]{:S(2)}, u32[]{:S(2)}) collective-permute-start(bf16[384,896]{1,0:T(8,128)(2,1)} %get-tuple-element.114), channel_id=1, source_target_pairs={{0,16},{16,0},{1,17},{17,1},{2,18},{18,2},{3,19},{19,3},{4,20},{20... | collective-permute-start | bytes 2064392 | tf_op jit(solution)/shard_map/ppermute | solution.py:217
  133.4 3.6 %collective-permute-start.37 = (bf16[192,4096]{1,0:T(8,128)(2,1)}, bf16[192,4096]{1,0:T(8,128)(2,1)S(1)}, u32[]{:S(2)}, u32[]{:S(2)}) collective-permute-start(bf16[192,4096]{1,0:T(8,128)(2,1)} %get-tuple-element.127), channel_id=1, source_target_pairs={{0,4},{4,0},{8,12},{12,8},{1,5},{5,1},{9,13},{13,9},{2,6},{6,2},{1... | collective-permute-start | bytes 4718600 | tf_op jit(solution)/shard_map/ppermute | solution.py:211
  133.4 21.6 %collective-permute-start.39 = (bf16[384,896]{1,0:T(8,128)(2,1)}, bf16[384,896]{1,0:T(8,128)(2,1)}, u32[]{:S(2)}, u32[]{:S(2)}) collective-permute-start(bf16[384,896]{1,0:T(8,128)(2,1)} %get-tuple-element.131), channel_id=1, source_target_pairs={{0,16},{16,0},{1,17},{17,1},{2,18},{18,2},{3,19},{19,3},{4,20},{20... | collective-permute-start | bytes 2064392 | tf_op jit(solution)/shard_map/ppermute | solution.py:217
  139.3 19.8 %collective-permute-start.38 = (bf16[96,4096]{1,0:T(8,128)(2,1)}, bf16[96,4096]{1,0:T(8,128)(2,1)S(1)}, u32[]{:S(2)}, u32[]{:S(2)}) collective-permute-start(bf16[96,4096]{1,0:T(8,128)(2,1)} %add_convert_fusion.2), channel_id=1, source_target_pairs={{0,8},{4,12},{8,0},{12,4},{1,9},{5,13},{9,1},{13,5},{2,10},{6,14},... | collective-permute-start | bytes 2359304 | tf_op jit(solution)/shard_map/ppermute | solution.py:211
  159.1 5.3 %collective-permute-start.40 = (bf16[192,4096]{1,0:T(8,128)(2,1)}, bf16[192,4096]{1,0:T(8,128)(2,1)S(1)}, u32[]{:S(2)}, u32[]{:S(2)}) collective-permute-start(bf16[192,4096]{1,0:T(8,128)(2,1)} %get-tuple-element.133), channel_id=1, source_target_pairs={{0,4},{4,0},{8,12},{12,8},{1,5},{5,1},{9,13},{13,9},{2,6},{6,2},{1... | collective-permute-start | bytes 4718600 | tf_op jit(solution)/shard_map/ppermute | solution.py:211
  160.3 20.9 %collective-permute-start.43 = (bf16[48,4096]{1,0:T(8,128)(2,1)}, bf16[48,4096]{1,0:T(8,128)(2,1)}, u32[]{:S(2)}, u32[]{:S(2)}) collective-permute-start(bf16[48,4096]{1,0:T(8,128)(2,1)} %get-tuple-element.155), channel_id=1, source_target_pairs={{0,3},{1,0},{2,1},{3,2},{4,7},{5,4},{6,5},{7,6},{8,11},{9,8},{10,9... | collective-permute-start | bytes 1179656 | tf_op jit(solution)/shard_map/ppermute | solution.py:206
  163.1 18.5 %collective-permute-start.42 = (bf16[48,4096]{1,0:T(8,128)(2,1)}, bf16[48,4096]{1,0:T(8,128)(2,1)}, u32[]{:S(2)}, u32[]{:S(2)}) collective-permute-start(bf16[48,4096]{1,0:T(8,128)(2,1)} %get-tuple-element.156), channel_id=1, source_target_pairs={{0,1},{1,2},{2,3},{3,0},{4,5},{5,6},{6,7},{7,4},{8,9},{9,10},{10,1... | collective-permute-start | bytes 1179656 | tf_op jit(solution)/shard_map/ppermute | solution.py:206
  165.4 19.9 %collective-permute-start.41 = (bf16[96,4096]{1,0:T(8,128)(2,1)}, bf16[96,4096]{1,0:T(8,128)(2,1)S(1)}, u32[]{:S(2)}, u32[]{:S(2)}) collective-permute-start(bf16[96,4096]{1,0:T(8,128)(2,1)} %add_convert_fusion.1), channel_id=1, source_target_pairs={{0,8},{4,12},{8,0},{12,4},{1,9},{5,13},{9,1},{13,5},{2,10},{6,14},... | collective-permute-start | bytes 2359304 | tf_op jit(solution)/shard_map/ppermute | solution.py:211
  185.3 10.6 %collective-permute-start.44 = (bf16[192,4096]{1,0:T(8,128)(2,1)}, bf16[192,4096]{1,0:T(8,128)(2,1)S(1)}, u32[]{:S(2)}, u32[]{:S(2)}) collective-permute-start(bf16[192,4096]{1,0:T(8,128)(2,1)} %get-tuple-element.140), channel_id=1, source_target_pairs={{0,4},{4,0},{8,12},{12,8},{1,5},{5,1},{9,13},{13,9},{2,6},{6,2},{1... | collective-permute-start | bytes 4718600 | tf_op jit(solution)/shard_map/ppermute | solution.py:211
  187.4 29.4 %collective-permute-start.46 = (bf16[48,4096]{1,0:T(8,128)(2,1)}, bf16[48,4096]{1,0:T(8,128)(2,1)}, u32[]{:S(2)}, u32[]{:S(2)}) collective-permute-start(bf16[48,4096]{1,0:T(8,128)(2,1)} %add_convert_fusion.7), channel_id=1, source_target_pairs={{0,3},{1,0},{2,1},{3,2},{4,7},{5,4},{6,5},{7,6},{8,11},{9,8},{10,9... | collective-permute-start | bytes 1179656 | tf_op jit(solution)/shard_map/ppermute | solution.py:206
  192.1 24.8 %collective-permute-start.48 = (bf16[48,4096]{1,0:T(8,128)(2,1)}, bf16[48,4096]{1,0:T(8,128)(2,1)S(1)}, u32[]{:S(2)}, u32[]{:S(2)}) collective-permute-start(bf16[48,4096]{1,0:T(8,128)(2,1)} %get-tuple-element.153), channel_id=1, source_target_pairs={{0,1},{1,2},{2,3},{3,0},{4,5},{5,6},{6,7},{7,4},{8,9},{9,10},{10,1... | collective-permute-start | bytes 1179656 | tf_op jit(solution)/shard_map/ppermute | solution.py:206
  192.1 25.1 %collective-permute-start.47 = (bf16[48,4096]{1,0:T(8,128)(2,1)}, bf16[48,4096]{1,0:T(8,128)(2,1)}, u32[]{:S(2)}, u32[]{:S(2)}) collective-permute-start(bf16[48,4096]{1,0:T(8,128)(2,1)} %get-tuple-element.154), channel_id=1, source_target_pairs={{0,3},{1,0},{2,1},{3,2},{4,7},{5,4},{6,5},{7,6},{8,11},{9,8},{10,9... | collective-permute-start | bytes 1179656 | tf_op jit(solution)/shard_map/ppermute | solution.py:206
  197.1 20.1 %collective-permute-start.45 = (bf16[96,4096]{1,0:T(8,128)(2,1)S(1)}, bf16[96,4096]{1,0:T(8,128)(2,1)S(1)}, u32[]{:S(2)}, u32[]{:S(2)}) collective-permute-start(bf16[96,4096]{1,0:T(8,128)(2,1)S(1)} %add_convert_fusion), channel_id=1, source_target_pairs={{0,8},{4,12},{8,0},{12,4},{1,9},{5,13},{9,1},{13,5},{2,10},{6,14},... | collective-permute-start | bytes 2359304 | tf_op jit(solution)/shard_map/ppermute | solution.py:211
  218.4 19.7 %collective-permute-start.49 = (bf16[48,4096]{1,0:T(8,128)(2,1)S(1)}, bf16[48,4096]{1,0:T(8,128)(2,1)S(1)}, u32[]{:S(2)}, u32[]{:S(2)}) collective-permute-start(bf16[48,4096]{1,0:T(8,128)(2,1)S(1)} %add_convert_fusion.4), channel_id=1, source_target_pairs={{0,3},{1,0},{2,1},{3,2},{4,7},{5,4},{6,5},{7,6},{8,11},{9,8},{10,9... | collective-permute-start | bytes 1179656 | tf_op jit(solution)/shard_map/ppermute | solution.py:206
  (46 other events, 411.5 us)

commit v6 on v5

--- a/solution.py
+++ b/solution.py
@@ -9,6 +9,7 @@
 
 CORE, CHIP = 1, 2
 VMEM_BYTES = 56 * 1024 * 1024
+DEEP = pl.Buffered(4)
 
 
 def dot(left, right, left_dim, right_dim):
@@ -32,6 +33,38 @@
 def cost(flops, *arrays):
     moved = sum(array.size * array.dtype.itemsize for array in arrays)
     return pl.CostEstimate(flops=flops, bytes_accessed=moved, transcendentals=0)
+
+
+def streamed(kernel, steps, in_specs, out_specs, out_shape, total, flops):
+    def outer(*refs):
+        kept = refs[len(in_specs) + len(out_specs) :]
+        pipeline = pltpu.emit_pipeline(
+            lambda *blocks: kernel(*blocks, *kept),
+            grid=(steps,),
+            in_specs=in_specs,
+            out_specs=out_specs,
+        )
+        pipeline(*refs[: len(in_specs) + len(out_specs)])
+
+    def call(*operands):
+        return pl.pallas_call(
+            outer,
+            in_specs=[pl.BlockSpec(memory_space=pl.ANY)] * len(in_specs),
+            out_specs=[pl.BlockSpec(memory_space=pl.ANY)] * len(out_specs),
+            out_shape=out_shape,
+            scratch_shapes=[pltpu.VMEM(shape, jnp.float32) for shape in total],
+            compiler_params=pltpu.CompilerParams(vmem_limit_bytes=VMEM_BYTES),
+            cost_estimate=cost(flops, *operands, *out_shape),
+        )(*operands)
+
+    return call
+
+
+def piece_specs(pieces, block):
+    return [
+        pl.BlockSpec((piece.shape[0], block), lambda j: (0, j), pipeline_mode=DEEP)
+        for piece in pieces
+    ]
 
 
 def contract_kernel(n_pieces, n_weights, right_dim, *refs):
@@ -55,24 +88,23 @@
 def contract(pieces, weights, right_dim):
     width = pieces[0].shape[1]
     units = weights[0].shape[1 - right_dim]
-    block = min(1024, width)
+    block = min(512, width)
     if right_dim == 0:
-        weight_spec = pl.BlockSpec((block, units), lambda k: (k, 0))
+        weight_spec = pl.BlockSpec((block, units), lambda k: (k, 0), pipeline_mode=DEEP)
     else:
-        weight_spec = pl.BlockSpec((units, block), lambda k: (0, k))
+        weight_spec = pl.BlockSpec((units, block), lambda k: (0, k), pipeline_mode=DEEP)
     rows = sum(piece.shape[0] for piece in pieces)
     shape = (rows * len(weights), units)
-    return pl.pallas_call(
+    (out,) = streamed(
         functools.partial(contract_kernel, len(pieces), len(weights), right_dim),
-        grid=(width // block,),
-        in_specs=[pl.BlockSpec((piece.shape[0], block), lambda k: (0, k)) for piece in pieces]
-        + [weight_spec] * len(weights),
-        out_specs=pl.BlockSpec(shape, lambda k: (0, 0)),
-        out_shape=jax.ShapeDtypeStruct(shape, jnp.bfloat16),
-        scratch_shapes=[pltpu.VMEM(shape, jnp.float32)],
-        compiler_params=pltpu.CompilerParams(vmem_limit_bytes=VMEM_BYTES),
-        cost_estimate=cost(2 * len(weights) * rows * width * units, *pieces, *weights),
+        width // block,
+        piece_specs(pieces, block) + [weight_spec] * len(weights),
+        [pl.BlockSpec(shape, lambda k: (0, 0))],
+        [jax.ShapeDtypeStruct(shape, jnp.bfloat16)],
+        [shape],
+        2 * len(weights) * rows * width * units,
     )(*pieces, *weights)
+    return out
 
 
 def store_halves(total, outs):
@@ -98,15 +130,15 @@
     width = weights[0].shape[0]
     block = min(512, width)
     out = jax.ShapeDtypeStruct((rows, width), jnp.bfloat16)
-    return pl.pallas_call(
+    return streamed(
         functools.partial(expand_kernel, len(lefts)),
-        grid=(width // block,),
-        in_specs=[pl.BlockSpec((rows, units), lambda j: (0, 0))] * len(blocks)
-        + [pl.BlockSpec((block, units), lambda j: (j, 0))] * len(weights),
-        out_specs=[pl.BlockSpec((rows, block), lambda j: (0, j))] * 2,
-        out_shape=[out, out],
-        compiler_params=pltpu.CompilerParams(vmem_limit_bytes=VMEM_BYTES),
-        cost_estimate=cost(4 * len(lefts) * rows * width * units, *blocks, *weights, out, out),
+        width // block,
+        [pl.BlockSpec((rows, units), lambda j: (0, 0))] * len(blocks)
+        + [pl.BlockSpec((block, units), lambda j: (j, 0), pipeline_mode=DEEP)] * len(weights),
+        [pl.BlockSpec((rows, block), lambda j: (0, j))] * 2,
+        [out, out],
+        [],
+        4 * len(lefts) * rows * width * units,
     )(*blocks, *weights)
 
 
@@ -135,18 +167,17 @@
     half = hiddens[0].shape[0]
     grad = jax.ShapeDtypeStruct((rows, units), jnp.bfloat16)
     out = jax.ShapeDtypeStruct((half, width), jnp.bfloat16)
-    return pl.pallas_call(
+    return streamed(
         functools.partial(down_kernel, len(pieces)),
-        grid=(width // block,),
-        in_specs=[pl.BlockSpec((piece.shape[0], block), lambda j: (0, j)) for piece in pieces]
+        width // block,
+        piece_specs(pieces, block)
         + [pl.BlockSpec((half, units), lambda j: (0, 0))] * 2
-        + [pl.BlockSpec((units, block), lambda j: (0, j))],
-        out_specs=[pl.BlockSpec(grad.shape, lambda j: (0, 0))]
+        + [pl.BlockSpec((units, block), lambda j: (0, j), pipeline_mode=DEEP)],
+        [pl.BlockSpec(grad.shape, lambda j: (0, 0))]
         + [pl.BlockSpec((half, block), lambda j: (0, j))] * 2,
-        out_shape=[grad, out, out],
-        scratch_shapes=[pltpu.VMEM(grad.shape, jnp.float32)],
-        compiler_params=pltpu.CompilerParams(vmem_limit_bytes=VMEM_BYTES),
-        cost_estimate=cost(4 * rows * width * units, *pieces, *hiddens, weight, out, out),
+        [grad, out, out],
+        [grad.shape],
+        4 * rows * width * units,
     )(*pieces, *hiddens, weight)
 
 
@@ -165,15 +196,15 @@
     block = min(512, width)
     rows = sum(piece.shape[0] for piece in pieces)
     out = jax.ShapeDtypeStruct((width, units), jnp.float32)
-    return pl.pallas_call(
+    return streamed(
         functools.partial(wide_grad_kernel, len(pieces)),
-        grid=(width // block,),
-        in_specs=[pl.BlockSpec((piece.shape[0], block), lambda j: (0, j)) for piece in pieces]
+        width // block,
+        piece_specs(pieces, block)
         + [pl.BlockSpec(grad.shape, lambda j: (0, 0)) for grad in grads],
-        out_specs=[pl.BlockSpec((block, units), lambda j: (j, 0))] * 2,
-        out_shape=[out, out],
-        compiler_params=pltpu.CompilerParams(vmem_limit_bytes=VMEM_BYTES),
-        cost_estimate=cost(4 * rows * width * units, *pieces, *grads, out, out),
+        [pl.BlockSpec((block, units), lambda j: (j, 0))] * 2,
+        [out, out],
+        [],
+        4 * rows * width * units,
     )(*pieces, *grads)
 
 
@@ -189,16 +220,17 @@
     block = min(512, width)
     rows = sum(piece.shape[0] for piece in pieces)
     out = jax.ShapeDtypeStruct((units, width), jnp.float32)
-    return pl.pallas_call(
+    (out,) = streamed(
         functools.partial(tall_grad_kernel, len(pieces)),
-        grid=(width // block,),
-        in_specs=[pl.BlockSpec((piece.shape[0], block), lambda j: (0, j)) for piece in pieces]
+        width // block,
+        piece_specs(pieces, block)
         + [pl.BlockSpec(hidden.shape, lambda j: (0, 0)) for hidden in hiddens],
-        out_specs=pl.BlockSpec((units, block), lambda j: (0, j)),
-        out_shape=out,
-        compiler_params=pltpu.CompilerParams(vmem_limit_bytes=VMEM_BYTES),
-        cost_estimate=cost(2 * rows * width * units, *pieces, *hiddens, out),
+        [pl.BlockSpec((units, block), lambda j: (0, j))],
+        [out],
+        [],
+        2 * rows * width * units,
     )(*pieces, *hiddens)
+    return out
 
 
 def shift(block, step):
@@ -305,7 +337,10 @@
     cot_near1, cot_far2 = shift(cot, 1), swap(cot_near2, CHIP)
     token2 = quad(near2, far2, other_cores([after(near2, pair3), far2]))
     pair2 = contract(token2, pair, 0)
-    cot_near1, cot_far2, pair2, *pair3_moved = sync(cot_near1, cot_far2, pair2, *pair3_moved)
+    cot0 = quad(cot, cot_far0, other_cores([cot, after(cot_far0, pair3)]))
+    cot_near1, cot_far2, pair2, cot0[2], cot0[3], *pair3_moved = sync(
+        cot_near1, cot_far2, pair2, cot0[2], cot0[3], *pair3_moved
+    )
 
     gate3, up3 = pair_sums(pair3, pair3_moved)
     hidden3 = hidden_of(gate3, up3)
@@ -323,17 +358,15 @@
     grad_b_moved = row_moves(grad_b)
     sent, mixed_a = chip_part(mine, swap(other, CORE))
     mixed_a_moved = swap(sent, CHIP)
-    cot = after(cotangent, grad_b)
-    cot0 = quad(cot, cot_far0, other_cores([cot, after(cot_far0, grad_b)]))
     cot1 = quad(cot_near1, cot_far1, other_cores([after(cot_near1, grad_b), cot_far1]))
     grad_a, mine, other = down_products(cot0 + cot1, [hidden3, hidden2], down_weight)
     mixed_a_moved, grad_a, mine, other, *grad_b_moved = sync(
         mixed_a_moved, grad_a, mine, other, *grad_b_moved
     )
 
-    grad_b = row_sum(grad_b, grad_b_moved)
     grad_a_moved = row_moves(grad_a)
     sent, mixed_b = chip_part(mine, swap(other, CORE))
+    grad_b = row_sum(grad_b, grad_b_moved, sent)
     mixed_b_moved = swap(sent, CHIP)
     half = grad_b.shape[0] // 2
     grads3 = grads_of(gate3, up3, grad_b[:half])
@@ -341,10 +374,10 @@
     mine, other = expand([[x, y] for x, y in zip(grads3, grads2)], pair)
     mixed_b_moved, mine, other, *grad_a_moved = sync(mixed_b_moved, mine, other, *grad_a_moved)
 
-    grad_a = row_sum(grad_a, grad_a_moved)
     sent, token_grad_b = chip_part(mine, swap(other, CORE))
     token_b_moved = swap(sent, CHIP)
-    mixed_b = owner_parts(mixed_b, mixed_b_moved)
+    grad_a = row_sum(grad_a, grad_a_moved, sent)
+    mixed_b = owner_parts(mixed_b, after(mixed_b_moved, sent))
     part3, part2 = shift(narrow(mixed_b[0]), 1), shift(narrow(mixed_b[1]), -1)
     grads0 = grads_of(gate0, up0, grad_a[:half])
     grads1 = grads_of(gate1, up1, grad_a[half:])
@@ -353,10 +386,10 @@
 
     sent, token_grad_a = chip_part(mine, swap(other, CORE))
     token_a_moved = swap(sent, CHIP)
-    mixed_a = owner_parts(mixed_a, mixed_a_moved)
+    mixed_a = owner_parts(mixed_a, after(mixed_a_moved, sent))
     part1 = shift(narrow(mixed_a[1] + wide(part2)), -1)
     mixed = mixed_a[0] + wide(part3)
-    token_grad_b = owner_parts(token_grad_b, token_b_moved)
+    token_grad_b = owner_parts(token_grad_b, after(token_b_moved, sent))
     part3, part2 = shift(narrow(token_grad_b[0]), 1), shift(narrow(token_grad_b[1]), -1)
     gate_total, up_total = wide_grads(
         [after(tokens, sent), *token0[1:], *token1, *token3, *token2],

time: 241 us -> 258 us (1.071)
  Pallas kernels: 118 us -> 129 us
  waiting for transfers between devices: 41.6 us -> 50.3 us
  starting transfers between devices: 50.2 us -> 42.1 us
  other arithmetic: 21.4 us -> 27.1 us
    pallas_call x10, Pallas kernels: 118 us -> 129 us  [call(): pl.pallas_call(outer, in_specs=[pl.BlockSpec(memory_space=pl.ANY)] * len(...]
    ppermute x12, starting transfers between devices: 25.4 us -> 18.7 us  [shift(): return lax.ppermute(block, 'depth', [(i, (i + step) % n) for i in range(n)])]
    ppermute x12, waiting for transfers between devices: 17 us -> 22.1 us  [shift(): return lax.ppermute(block, 'depth', [(i, (i + step) % n) for i in range(n)])]
    ppermute x32, waiting for transfers between devices: 21.2 us -> 26.2 us  [swap(): return lax.ppermute(block, 'col', [(i, i ^ bit) for i in range(n)])]
    convert_element_type x13, other arithmetic: 14.7 us -> 19.6 us  [narrow(): return block.astype(jnp.bfloat16)]
    unnamed x88 -> x94, local copies, waits for them, and re-layouts: 6.92 us -> 6.66 us
  transfers between devices with their start and end apart: 50 -> 50, of which waited for: 16 -> 18; matrix products, arithmetic and copies ran while one was open for 8% -> 7% of each run, Pallas kernels for 49% -> 50%
where the time goes in v6:
time: 258 us; the launch traced here: 257 us
  Pallas kernels  129 us (50%)
  waiting for transfers between devices  50.3 us (19%)
  starting transfers between devices  42.1 us (16%)
  other arithmetic  27.1 us (11%)
  local copies, waits for them, and re-layouts  6.66 us (3%)
    pallas_call x10, Pallas kernels, call(): pl.pallas_call(outer, in_specs=[pl.BlockSpec(memory_space=pl.ANY)] * len(...  129 us
    ppermute x32, waiting for transfers between devices, swap(): return lax.ppermute(block, 'col', [(i, i ^ bit) for i in range(n)])  26.2 us
    ppermute x12, waiting for transfers between devices, shift(): return lax.ppermute(block, 'depth', [(i, (i + step) % n) for i in range(n)])  22.1 us
    convert_element_type x13, other arithmetic, narrow(): return block.astype(jnp.bfloat16)  19.6 us
    ppermute x12, starting transfers between devices, shift(): return lax.ppermute(block, 'depth', [(i, (i + step) % n) for i in range(n)])  18.7 us
    ppermute x32, starting transfers between devices, swap(): return lax.ppermute(block, 'col', [(i, i ^ bit) for i in range(n)])  17.2 us
    unnamed x94, local copies, waits for them, and re-layouts  6.66 us
    ppermute x6, starting transfers between devices, row_moves(): lax.ppermute(partial, 'row', [(i, (i + step) % n) for i in range(n)])  6.21 us
  transfers between devices with their start and end apart: 50, of which 18 were waited for; matrix products, arithmetic and copies ran while one was open for 7% of the time, Pallas kernels for 50%

profile of v6, /device:TPU:0, one launch (start us, length us, event | category | flops | bytes accessed | tf_op | source)
XLA Modules:
  0.0 256.5 jit_solution(18046174123996545426)
XLA Ops:
  1.2 2.6 %collective-permute-start.1 = (bf16[48,4096]{1,0:T(8,128)(2,1)}, bf16[48,4096]{1,0:T(8,128)(2,1)S(1)}, u32[]{:S(2)}, u32[]{:S(2)}) collective-permute-start(bf16[48,4096]{1,0:T(8,128)(2,1)} %refs_0_.3), channel_id=1, source_target_pairs={{0,8},{4,12},{8,0},{12,4},{1,9},{5,13},{9,1},{13,5},{2,10},{6,14},... | collective-permute-start | bytes 1179656 | tf_op jit(solution)/shard_map/ppermute | solution.py:243
  3.8 1.6 collective-permute-start
  5.3 8.3 %collective-permute-done.1.refs_1_ = bf16[48,4096]{1,0:T(8,128)(2,1)S(1)} collective-permute-done((bf16[48,4096]{1,0:T(8,128)(2,1)}, bf16[48,4096]{1,0:T(8,128)(2,1)S(1)}, u32[]{:S(2)}, u32[]{:S(2)}) %collective-permute-start.1) | collective-permute-done | bytes 393248 | tf_op jit(solution)/shard_map/ppermute | solution.py:243
  13.7 3.4 %collective-permute-done.refs_0_.refs_4_ = bf16[48,4096]{1,0:T(8,128)(2,1)S(1)} collective-permute-done((bf16[48,4096]{1,0:T(8,128)(2,1)}, bf16[48,4096]{1,0:T(8,128)(2,1)S(1)}, u32[]{:S(2)}, u32[]{:S(2)}) %collective-permute-start) | collective-permute-done | bytes 393248 | tf_op jit(solution)/shard_map/ppermute | solution.py:238
  17.0 1.7 collective-permute-start.4
  20.3 7.8 %shard_map.92 = bf16[384,896]{1,0:T(8,128)(2,1)} custom-call(bf16[48,4096]{1,0:T(8,128)(2,1)} %refs_0_.3, bf16[48,4096]{1,0:T(8,128)(2,1)} %copy-done.23, bf16[48,4096]{1,0:T(8,128)(2,1)} %copy-done.22, bf16[48,4096]{1,0:T(8,128)(2,1)} %copy-done.27, bf16[4096,896]{1,0:T(8,128)(2,1)} %refs_4_.11, bf16[4096,896]{1,0:T(8,128)(2,1)} %refs_5_.11), custom_call_target="tpu_custom_call" | custom-call | flops 2818572288 | bytes 16941056 | tf_op jit(solution)/shard_map/pallas_call | solution.py:50
  28.8 1.5 collective-permute-done.5.refs_1_.refs_5_
  30.3 1.5 collective-permute-start.12
  32.6 3.5 %collective-permute-start.8 = (bf16[48,4096]{1,0:T(8,128)(2,1)S(1)}, bf16[48,4096]{1,0:T(8,128)(2,1)S(1)}, u32[]{:S(2)}, u32[]{:S(2)}) collective-permute-start(bf16[48,4096]{1,0:T(8,128)(2,1)S(1)} %copy-done.21), channel_id=1, source_target_pairs={{0,3},{1,0},{2,1},{3,2},{4,7},{5,4},{6,5},{7,6},{8,11},{9,8},{10,9... | collective-permute-start | bytes 1179656 | tf_op jit(solution)/shard_map/ppermute | solution.py:238
  36.1 1.5 collective-permute-start.9
  37.7 7.8 %shard_map.93 = bf16[384,896]{1,0:T(8,128)(2,1)} custom-call(bf16[48,4096]{1,0:T(8,128)(2,1)} %copy-done.24, bf16[48,4096]{1,0:T(8,128)(2,1)} %copy-done.30, bf16[48,4096]{1,0:T(8,128)(2,1)} %copy-done.29, bf16[48,4096]{1,0:T(8,128)(2,1)} %copy-done.31, bf16[4096,896]{1,0:T(8,128)(2,1)} %refs_4_.11, bf16[4096,896]{1,0:T(8,128)(2,1)} %refs_5_.11), custom_call_target="tpu_custom_call" | custom-call | flops 2818572288 | bytes 16941056 | tf_op jit(solution)/shard_map/pallas_call | solution.py:50
  45.6 6.2 %collective-permute-done.8.refs_0_.refs_8_ = bf16[48,4096]{1,0:T(8,128)(2,1)S(1)} collective-permute-done((bf16[48,4096]{1,0:T(8,128)(2,1)S(1)}, bf16[48,4096]{1,0:T(8,128)(2,1)S(1)}, u32[]{:S(2)}, u32[]{:S(2)}) %collective-permute-start.8) | collective-permute-done | bytes 393248 | tf_op jit(solution)/shard_map/ppermute | solution.py:238
  52.6 2.1 collective-permute-start.13
  55.2 1.5 collective-permute-start.15
  57.6 7.8 %shard_map.94 = bf16[384,896]{1,0:T(8,128)(2,1)} custom-call(bf16[48,4096]{1,0:T(8,128)(2,1)} %copy-done.28, bf16[48,4096]{1,0:T(8,128)(2,1)} %copy-done.35, bf16[48,4096]{1,0:T(8,128)(2,1)} %copy-done.36, bf16[48,4096]{1,0:T(8,128)(2,1)} %copy-done.37, bf16[4096,896]{1,0:T(8,128)(2,1)} %refs_4_.11, bf16[4096,896]{1,0:T(8,128)(2,1)} %refs_5_.11), custom_call_target="tpu_custom_call" | custom-call | flops 2818572288 | bytes 16941056 | tf_op jit(solution)/shard_map/pallas_call | solution.py:50
  65.3 8.0 %collective-permute-done.13.refs_4_.refs_12_ = bf16[48,4096]{1,0:T(8,128)(2,1)S(1)} collective-permute-done((bf16[48,4096]{1,0:T(8,128)(2,1)S(1)}, bf16[48,4096]{1,0:T(8,128)(2,1)S(1)}, u32[]{:S(2)}, u32[]{:S(2)}) %collective-permute-start.13) | collective-permute-done | bytes 393248 | tf_op jit(solution)/shard_map/ppermute | solution.py:238
  74.8 1.5 collective-permute-start.25
  76.3 1.7 collective-permute-start.19
  79.8 7.8 %shard_map.95 = bf16[384,896]{1,0:T(8,128)(2,1)} custom-call(bf16[48,4096]{1,0:T(8,128)(2,1)} %copy-done.32, bf16[48,4096]{1,0:T(8,128)(2,1)} %copy-done.39, bf16[48,4096]{1,0:T(8,128)(2,1)} %copy-done.40, bf16[48,4096]{1,0:T(8,128)(2,1)} %copy-done.41, bf16[4096,896]{1,0:T(8,128)(2,1)} %refs_4_.11, bf16[4096,896]{1,0:T(8,128)(2,1)} %refs_5_.11), custom_call_target="tpu_custom_call" | custom-call | flops 2818572288 | bytes 16941056 | tf_op jit(solution)/shard_map/pallas_call | solution.py:50
  87.6 2.2 collective-permute-done.19.refs_4_
  90.5 2.0 collective-permute-done.25
  93.7 1.6 collective-permute-start.31
  98.2 14.2 %shard_map.96 = (bf16[384,896]{1,0:T(8,128)(2,1)}, bf16[192,4096]{1,0:T(8,128)(2,1)}, bf16[192,4096]{1,0:T(8,128)(2,1)}) custom-call(bf16[48,4096]{1,0:T(8,128)(2,1)} %copy-done.26, bf16[48,4096]{1,0:T(8,128)(2,1)} %copy-done.34, bf16[48,4096]{1,0:T(8,128)(2,1)} %copy-done.42, bf16[48,4096]{1,0:T(8,128)(2,1)} %copy-done.43, bf16[48,4096]{1,0:T(8,128)(2,1)} %copy-done.33, ...), custom_call_target="tpu_custom_call" | custom-call | flops 5637144576 | bytes 15007744 | tf_op jit(solution)/shard_map/pallas_call | solution.py:50
  115.4 1.5 collective-permute-done.32
  117.0 1.5 collective-permute-start.33
  120.4 14.1 %shard_map.97 = (bf16[384,896]{1,0:T(8,128)(2,1)}, bf16[192,4096]{1,0:T(8,128)(2,1)}, bf16[192,4096]{1,0:T(8,128)(2,1)}) custom-call(bf16[48,4096]{1,0:T(8,128)(2,1)} %refs_0_.4, bf16[48,4096]{1,0:T(8,128)(2,1)} %copy-done.25, bf16[48,4096]{1,0:T(8,128)(2,1)} %copy-done.38, bf16[48,4096]{1,0:T(8,128)(2,1)} %collective-permute-done.24.refs_3_, ...), custom_call_target="tpu_custom_call" | custom-call | flops 5637144576 | bytes 15007744 | tf_op jit(solution)/shard_map/pallas_call | solution.py:50
  134.5 2.2 collective-permute-done.33
  138.1 3.1 %collective-permute-done.37 = bf16[192,4096]{1,0:T(8,128)(2,1)S(1)} collective-permute-done((bf16[192,4096]{1,0:T(8,128)(2,1)}, bf16[192,4096]{1,0:T(8,128)(2,1)S(1)}, u32[]{:S(2)}, u32[]{:S(2)}) %collective-permute-start.37) | collective-permute-done | bytes 1572896 | tf_op jit(solution)/shard_map/ppermute | solution.py:243
  141.2 2.2 add_convert_fusion.2
  144.8 1.4 convert_add_fusion.1
  146.2 1.7 multiply_convert_fusion.4
  148.0 14.6 %shard_map.98 = (bf16[192,4096]{1,0:T(8,128)(2,1)}, bf16[192,4096]{1,0:T(8,128)(2,1)}) custom-call(bf16[192,896]{1,0:T(8,128)(2,1)} %get-tuple-element.179.refs_0_.refs_18_, bf16[192,896]{1,0:T(8,128)(2,1)} %get-tuple-element.174.refs_1_.refs_19_, bf16[192,896]{1,0:T(8,128)(2,1)} %get-tuple-element.180.refs_2_.refs_22_, ...), custom_call_target="tpu_custom_call" | custom-call | flops 5637144576 | bytes 19202048 | tf_op jit(solution)/shard_map/pallas_call | solution.py:50
  163.2 3.6 %collective-permute-done.40 = bf16[192,4096]{1,0:T(8,128)(2,1)S(1)} collective-permute-done((bf16[192,4096]{1,0:T(8,128)(2,1)}, bf16[192,4096]{1,0:T(8,128)(2,1)S(1)}, u32[]{:S(2)}, u32[]{:S(2)}) %collective-permute-start.40) | collective-permute-done | bytes 1572896 | tf_op jit(solution)/shard_map/ppermute | solution.py:243
  166.8 2.2 add_convert_fusion.1
  172.8 2.1 collective-permute-start.43
  174.9 1.8 multiply_convert_fusion
  176.7 14.7 %shard_map.99 = (bf16[192,4096]{1,0:T(8,128)(2,1)}, bf16[192,4096]{1,0:T(8,128)(2,1)}) custom-call(bf16[192,896]{1,0:T(8,128)(2,1)} %get-tuple-element.177.refs_0_.refs_16_, bf16[192,896]{1,0:T(8,128)(2,1)} %get-tuple-element.170.refs_1_.refs_17_, bf16[192,896]{1,0:T(8,128)(2,1)} %get-tuple-element.178.refs_2_.refs_20_, ...), custom_call_target="tpu_custom_call" | custom-call | flops 5637144576 | bytes 19202048 | tf_op jit(solution)/shard_map/pallas_call | solution.py:50
  191.3 1.6 collective-permute-done.42
  193.7 3.6 %collective-permute-done.44 = bf16[192,4096]{1,0:T(8,128)(2,1)S(1)} collective-permute-done((bf16[192,4096]{1,0:T(8,128)(2,1)}, bf16[192,4096]{1,0:T(8,128)(2,1)S(1)}, u32[]{:S(2)}, u32[]{:S(2)}) %collective-permute-start.44) | collective-permute-done | bytes 1572896 | tf_op jit(solution)/shard_map/ppermute | solution.py:243
  197.4 2.2 add_convert_fusion
  200.8 2.0 add_convert_fusion.7
  202.7 1.7 collective-permute-start.46
  205.9 3.5 %collective-permute-start.47 = (bf16[48,4096]{1,0:T(8,128)(2,1)}, bf16[48,4096]{1,0:T(8,128)(2,1)S(1)}, u32[]{:S(2)}, u32[]{:S(2)}) collective-permute-start(bf16[48,4096]{1,0:T(8,128)(2,1)} %get-tuple-element.166), channel_id=1, source_target_pairs={{0,3},{1,0},{2,1},{3,2},{4,7},{5,4},{6,5},{7,6},{8,11},{9,8},{10,9... | collective-permute-start | bytes 1179656 | tf_op jit(solution)/shard_map/ppermute | solution.py:238
  209.4 25.9 %shard_map.100 = (f32[4096,896]{1,0:T(8,128)}, f32[4096,896]{1,0:T(8,128)}) custom-call(bf16[48,4096]{1,0:T(8,128)(2,1)} %refs_0_.3, bf16[48,4096]{1,0:T(8,128)(2,1)} %copy-done.23, bf16[48,4096]{1,0:T(8,128)(2,1)} %copy-done.22, bf16[48,4096]{1,0:T(8,128)(2,1)} %copy-done.27, bf16[48,4096]{1,0:T(8,128)(2,1)} %copy-done.24, bf16[48,4096]{1,0:T(8,128)(2,1)} %copy-done.30, ...), custom_call_target="tpu_custom_call" | custom-call | flops 11274289152 | bytes 38404096 | tf_op jit(solution)/shard_map/pallas_call | solution.py:50
  235.4 2.0 add_convert_fusion.4
  237.6 2.1 convert_add_fusion.7
  239.7 14.7 %shard_map.101 = f32[896,4096]{1,0:T(8,128)} custom-call(bf16[48,4096]{1,0:T(8,128)(2,1)} %refs_0_.4, bf16[48,4096]{1,0:T(8,128)(2,1)} %copy-done.25, bf16[48,4096]{1,0:T(8,128)(2,1)} %copy-done.38, bf16[48,4096]{1,0:T(8,128)(2,1)} %collective-permute-done.24.refs_3_, bf16[48,4096]{1,0:T(8,128)(2,1)} %collective-permute-done.19.refs_4_, ...), custom_call_target="tpu_custom_call" | custom-call | flops 5637144576 | bytes 22347776 | tf_op jit(solution)/shard_map/pallas_call | solution.py:50
  254.4 2.1 convert_add_fusion.6
  (177 shorter events, 29.7 us)
Async XLA Ops:
  0.6 4.7 %collective-permute-start.2 = (bf16[48,4096]{1,0:T(8,128)(2,1)}, bf16[48,4096]{1,0:T(8,128)(2,1)S(1)}, u32[]{:S(2)}, u32[]{:S(2)}) collective-permute-start(bf16[48,4096]{1,0:T(8,128)(2,1)} %refs_0_.3), channel_id=1, source_target_pairs={{0,4},{4,0},{8,12},{12,8},{1,5},{5,1},{9,13},{13,9},{2,6},{6,2},{1... | collective-permute-start | bytes 1179656 | tf_op jit(solution)/shard_map/ppermute | solution.py:243
  1.2 12.5 %collective-permute-start.1 = (bf16[48,4096]{1,0:T(8,128)(2,1)}, bf16[48,4096]{1,0:T(8,128)(2,1)S(1)}, u32[]{:S(2)}, u32[]{:S(2)}) collective-permute-start(bf16[48,4096]{1,0:T(8,128)(2,1)} %refs_0_.3), channel_id=1, source_target_pairs={{0,8},{4,12},{8,0},{12,4},{1,9},{5,13},{9,1},{13,5},{2,10},{6,14},... | collective-permute-start | bytes 1179656 | tf_op jit(solution)/shard_map/ppermute | solution.py:243
  3.8 13.3 %collective-permute-start = (bf16[48,4096]{1,0:T(8,128)(2,1)}, bf16[48,4096]{1,0:T(8,128)(2,1)S(1)}, u32[]{:S(2)}, u32[]{:S(2)}) collective-permute-start(bf16[48,4096]{1,0:T(8,128)(2,1)} %refs_0_.3), channel_id=1, source_target_pairs={{0,1},{1,2},{2,3},{3,0},{4,5},{5,6},{6,7},{7,4},{8,9},{9,10},{10,1... | collective-permute-start | bytes 1179656 | tf_op jit(solution)/shard_map/ppermute | solution.py:238
  17.0 11.7 %collective-permute-start.4 = (bf16[48,4096]{1,0:T(8,128)(2,1)}, bf16[48,4096]{1,0:T(8,128)(2,1)S(1)}, u32[]{:S(2)}, u32[]{:S(2)}) collective-permute-start(bf16[48,4096]{1,0:T(8,128)(2,1)} %refs_0_.3), channel_id=1, source_target_pairs={{0,3},{1,0},{2,1},{3,2},{4,7},{5,4},{6,5},{7,6},{8,11},{9,8},{10,9... | collective-permute-start | bytes 1179656 | tf_op jit(solution)/shard_map/ppermute | solution.py:238
  18.8 10.0 %collective-permute-start.6 = (bf16[48,4096]{1,0:T(8,128)(2,1)S(1)}, bf16[48,4096]{1,0:T(8,128)(2,1)S(1)}, u32[]{:S(2)}, u32[]{:S(2)}) collective-permute-start(bf16[48,4096]{1,0:T(8,128)(2,1)S(1)} %collective-permute-done.refs_0_.refs_4_), channel_id=1, source_target_pairs={{0,4},{4,0},{8,12},{12,8},{1,5},{5,1},{9,13},{13,9},{2,6},{6,2},{1... | collective-permute-start | bytes 1179656 | tf_op jit(solution)/shard_map/ppermute | solution.py:243
  19.0 11.3 %collective-permute-start.5 = (bf16[48,4096]{1,0:T(8,128)(2,1)S(1)}, bf16[48,4096]{1,0:T(8,128)(2,1)S(1)}, u32[]{:S(2)}, u32[]{:S(2)}) collective-permute-start(bf16[48,4096]{1,0:T(8,128)(2,1)S(1)} %collective-permute-done.refs_0_.refs_4_), channel_id=1, source_target_pairs={{0,8},{4,12},{8,0},{12,4},{1,9},{5,13},{9,1},{13,5},{2,10},{6,14},... | collective-permute-start | bytes 1179656 | tf_op jit(solution)/shard_map/ppermute | solution.py:243
  30.3 5.8 %collective-permute-start.11 = (bf16[48,4096]{1,0:T(8,128)(2,1)S(1)}, bf16[48,4096]{1,0:T(8,128)(2,1)S(1)}, u32[]{:S(2)}, u32[]{:S(2)}) collective-permute-start(bf16[48,4096]{1,0:T(8,128)(2,1)S(1)} %collective-permute-done.5.refs_1_.refs_5_), channel_id=1, source_target_pairs={{0,4},{4,0},{8,12},{12,8},{1,5},{5,1},{9,13},{13,9},{2,6},{6,2},{1... | collective-permute-start | bytes 1179656 | tf_op jit(solution)/shard_map/ppermute | solution.py:243
  30.3 21.5 %collective-permute-start.12 = (bf16[384,896]{1,0:T(8,128)(2,1)}, bf16[384,896]{1,0:T(8,128)(2,1)S(1)}, u32[]{:S(2)}, u32[]{:S(2)}) collective-permute-start(bf16[384,896]{1,0:T(8,128)(2,1)} %shard_map.92), channel_id=1, source_target_pairs={{0,16},{16,0},{1,17},{17,1},{2,18},{18,2},{3,19},{19,3},{4,20},{20... | collective-permute-start | bytes 2064392 | tf_op jit(solution)/shard_map/ppermute | solution.py:249
  31.8 13.8 %collective-permute-start.3 = (bf16[48,4096]{1,0:T(8,128)(2,1)S(1)}, bf16[48,4096]{1,0:T(8,128)(2,1)S(1)}, u32[]{:S(2)}, u32[]{:S(2)}) collective-permute-start(bf16[48,4096]{1,0:T(8,128)(2,1)S(1)} %collective-permute-done.refs_0_.refs_4_), channel_id=1, source_target_pairs={{0,1},{1,2},{2,3},{3,0},{4,5},{5,6},{6,7},{7,4},{8,9},{9,10},{10,1... | collective-permute-start | bytes 1179656 | tf_op jit(solution)/shard_map/ppermute | solution.py:238
  32.1 13.5 %collective-permute-start.10 = (bf16[48,4096]{1,0:T(8,128)(2,1)S(1)}, bf16[48,4096]{1,0:T(8,128)(2,1)S(1)}, u32[]{:S(2)}, u32[]{:S(2)}) collective-permute-start(bf16[48,4096]{1,0:T(8,128)(2,1)S(1)} %copy-done.21), channel_id=1, source_target_pairs={{0,8},{4,12},{8,0},{12,4},{1,9},{5,13},{9,1},{13,5},{2,10},{6,14},... | collective-permute-start | bytes 1179656 | tf_op jit(solution)/shard_map/ppermute | solution.py:243
  32.6 19.1 %collective-permute-start.8 = (bf16[48,4096]{1,0:T(8,128)(2,1)S(1)}, bf16[48,4096]{1,0:T(8,128)(2,1)S(1)}, u32[]{:S(2)}, u32[]{:S(2)}) collective-permute-start(bf16[48,4096]{1,0:T(8,128)(2,1)S(1)} %copy-done.21), channel_id=1, source_target_pairs={{0,3},{1,0},{2,1},{3,2},{4,7},{5,4},{6,5},{7,6},{8,11},{9,8},{10,9... | collective-permute-start | bytes 1179656 | tf_op jit(solution)/shard_map/ppermute | solution.py:238
  36.1 15.6 %collective-permute-start.9 = (bf16[48,4096]{1,0:T(8,128)(2,1)S(1)}, bf16[48,4096]{1,0:T(8,128)(2,1)S(1)}, u32[]{:S(2)}, u32[]{:S(2)}) collective-permute-start(bf16[48,4096]{1,0:T(8,128)(2,1)S(1)} %collective-permute-done.4.refs_0_.refs_8_), channel_id=1, source_target_pairs={{0,8},{4,12},{8,0},{12,4},{1,9},{5,13},{9,1},{13,5},{2,10},{6,14},... | collective-permute-start | bytes 1179656 | tf_op jit(solution)/shard_map/ppermute | solution.py:243
  51.9 22.4 %collective-permute-start.18 = (bf16[384,896]{1,0:T(8,128)(2,1)}, bf16[384,896]{1,0:T(8,128)(2,1)S(1)}, u32[]{:S(2)}, u32[]{:S(2)}) collective-permute-start(bf16[384,896]{1,0:T(8,128)(2,1)} %shard_map.93), channel_id=1, source_target_pairs={{0,16},{16,0},{1,17},{17,1},{2,18},{18,2},{3,19},{19,3},{4,20},{20... | collective-permute-start | bytes 2064392 | tf_op jit(solution)/shard_map/ppermute | solution.py:249
  52.5 4.3 %collective-permute-start.17 = (bf16[48,4096]{1,0:T(8,128)(2,1)S(1)}, bf16[48,4096]{1,0:T(8,128)(2,1)S(1)}, u32[]{:S(2)}, u32[]{:S(2)}) collective-permute-start(bf16[48,4096]{1,0:T(8,128)(2,1)S(1)} %collective-permute-done.9.refs_1_.refs_9_), channel_id=1, source_target_pairs={{0,4},{4,0},{8,12},{12,8},{1,5},{5,1},{9,13},{13,9},{2,6},{6,2},{1... | collective-permute-start | bytes 1179656 | tf_op jit(solution)/shard_map/ppermute | solution.py:243
  52.6 20.7 %collective-permute-start.13 = (bf16[48,4096]{1,0:T(8,128)(2,1)S(1)}, bf16[48,4096]{1,0:T(8,128)(2,1)S(1)}, u32[]{:S(2)}, u32[]{:S(2)}) collective-permute-start(bf16[48,4096]{1,0:T(8,128)(2,1)S(1)} %copy-done.21), channel_id=1, source_target_pairs={{0,2},{1,3},{2,0},{3,1},{4,6},{5,7},{6,4},{7,5},{8,10},{9,11},{10,... | collective-permute-start | bytes 1179656 | tf_op jit(solution)/shard_map/ppermute | solution.py:238
  54.7 18.6 %collective-permute-start.14 = (bf16[48,4096]{1,0:T(8,128)(2,1)S(1)}, bf16[48,4096]{1,0:T(8,128)(2,1)S(1)}, u32[]{:S(2)}, u32[]{:S(2)}) collective-permute-start(bf16[48,4096]{1,0:T(8,128)(2,1)S(1)} %collective-permute-done.3.refs_0_.refs_12_), channel_id=1, source_target_pairs={{0,8},{4,12},{8,0},{12,4},{1,9},{5,13},{9,1},{13,5},{2,10},{6,14},... | collective-permute-start | bytes 1179656 | tf_op jit(solution)/shard_map/ppermute | solution.py:243
  55.2 19.0 %collective-permute-start.15 = (bf16[48,4096]{1,0:T(8,128)(2,1)S(1)}, bf16[48,4096]{1,0:T(8,128)(2,1)S(1)}, u32[]{:S(2)}, u32[]{:S(2)}) collective-permute-start(bf16[48,4096]{1,0:T(8,128)(2,1)S(1)} %collective-permute-done.8.refs_0_.refs_8_), channel_id=1, source_target_pairs={{0,8},{4,12},{8,0},{12,4},{1,9},{5,13},{9,1},{13,5},{2,10},{6,14},... | collective-permute-start | bytes 1179656 | tf_op jit(solution)/shard_map/ppermute | solution.py:243
  74.3 3.8 %collective-permute-start.21 = (bf16[48,4096]{1,0:T(8,128)(2,1)S(1)}, bf16[48,4096]{1,0:T(8,128)(2,1)S(1)}, u32[]{:S(2)}, u32[]{:S(2)}) collective-permute-start(bf16[48,4096]{1,0:T(8,128)(2,1)S(1)} %collective-permute-done.3.refs_0_.refs_12_), channel_id=1, source_target_pairs={{0,4},{4,0},{8,12},{12,8},{1,5},{5,1},{9,13},{13,9},{2,6},{6,2},{1... | collective-permute-start | bytes 1179656 | tf_op jit(solution)/shard_map/ppermute | solution.py:243
  74.3 4.0 %collective-permute-start.22 = (bf16[48,4096]{1,0:T(8,128)(2,1)S(1)}, bf16[48,4096]{1,0:T(8,128)(2,1)S(1)}, u32[]{:S(2)}, u32[]{:S(2)}) collective-permute-start(bf16[48,4096]{1,0:T(8,128)(2,1)S(1)} %collective-permute-done.14.refs_1_.refs_13_), channel_id=1, source_target_pairs={{0,4},{4,0},{8,12},{12,8},{1,5},{5,1},{9,13},{13,9},{2,6},{6,2},{1... | collective-permute-start | bytes 1179656 | tf_op jit(solution)/shard_map/ppermute | solution.py:243
  74.8 17.6 %collective-permute-start.25 = (bf16[384,896]{1,0:T(8,128)(2,1)}, bf16[384,896]{1,0:T(8,128)(2,1)S(1)}, u32[]{:S(2)}, u32[]{:S(2)}) collective-permute-start(bf16[384,896]{1,0:T(8,128)(2,1)} %shard_map.94), channel_id=1, source_target_pairs={{0,16},{16,0},{1,17},{17,1},{2,18},{18,2},{3,19},{19,3},{4,20},{20... | collective-permute-start | bytes 2064392 | tf_op jit(solution)/shard_map/ppermute | solution.py:249
  76.3 11.3 %collective-permute-start.23 = (bf16[48,4096]{1,0:T(8,128)(2,1)S(1)}, bf16[48,4096]{1,0:T(8,128)(2,1)S(1)}, u32[]{:S(2)}, u32[]{:S(2)}) collective-permute-start(bf16[48,4096]{1,0:T(8,128)(2,1)S(1)} %copy-done.21), channel_id=1, source_target_pairs={{0,4},{4,0},{8,12},{12,8},{1,5},{5,1},{9,13},{13,9},{2,6},{6,2},{1... | collective-permute-start | bytes 1179656 | tf_op jit(solution)/shard_map/ppermute | solution.py:243
  76.3 13.4 %collective-permute-start.19 = (bf16[48,4096]{1,0:T(8,128)(2,1)S(1)}, bf16[48,4096]{1,0:T(8,128)(2,1)}, u32[]{:S(2)}, u32[]{:S(2)}) collective-permute-start(bf16[48,4096]{1,0:T(8,128)(2,1)S(1)} %copy-done.21), channel_id=1, source_target_pairs={{0,1},{1,2},{2,3},{3,0},{4,5},{5,6},{6,7},{7,4},{8,9},{9,10},{10,1... | collective-permute-start | bytes 1179656 | tf_op jit(solution)/shard_map/ppermute | solution.py:238
  78.0 11.7 %collective-permute-start.24 = (bf16[48,4096]{1,0:T(8,128)(2,1)S(1)}, bf16[48,4096]{1,0:T(8,128)(2,1)}, u32[]{:S(2)}, u32[]{:S(2)}) collective-permute-start(bf16[48,4096]{1,0:T(8,128)(2,1)S(1)} %collective-permute-done.10.refs_1_), channel_id=1, source_target_pairs={{0,4},{4,0},{8,12},{12,8},{1,5},{5,1},{9,13},{13,9},{2,6},{6,2},{1... | collective-permute-start | bytes 1179656 | tf_op jit(solution)/shard_map/ppermute | solution.py:243
  79.1 11.4 %collective-permute-start.20 = (bf16[48,4096]{1,0:T(8,128)(2,1)S(1)}, bf16[48,4096]{1,0:T(8,128)(2,1)}, u32[]{:S(2)}, u32[]{:S(2)}) collective-permute-start(bf16[48,4096]{1,0:T(8,128)(2,1)S(1)} %collective-permute-done.13.refs_4_.refs_12_), channel_id=1, source_target_pairs={{0,8},{4,12},{8,0},{12,4},{1,9},{5,13},{9,1},{13,5},{2,10},{6,14},... | collective-permute-start | bytes 1179656 | tf_op jit(solution)/shard_map/ppermute | solution.py:243
  92.5 4.0 %collective-permute-start.27 = (bf16[48,4096]{1,0:T(8,128)(2,1)S(1)}, bf16[48,4096]{1,0:T(8,128)(2,1)S(1)}, u32[]{:S(2)}, u32[]{:S(2)}) collective-permute-start(bf16[48,4096]{1,0:T(8,128)(2,1)S(1)} %collective-permute-done.8.refs_0_.refs_8_), channel_id=1, source_target_pairs={{0,4},{4,0},{8,12},{12,8},{1,5},{5,1},{9,13},{13,9},{2,6},{6,2},{1... | collective-permute-start | bytes 1179656 | tf_op jit(solution)/shard_map/ppermute | solution.py:243
  92.5 4.7 %collective-permute-start.28 = (bf16[48,4096]{1,0:T(8,128)(2,1)S(1)}, bf16[48,4096]{1,0:T(8,128)(2,1)S(1)}, u32[]{:S(2)}, u32[]{:S(2)}) collective-permute-start(bf16[48,4096]{1,0:T(8,128)(2,1)S(1)} %collective-permute-done.15.refs_1_.refs_9_), channel_id=1, source_target_pairs={{0,4},{4,0},{8,12},{12,8},{1,5},{5,1},{9,13},{13,9},{2,6},{6,2},{1... | collective-permute-start | bytes 1179656 | tf_op jit(solution)/shard_map/ppermute | solution.py:243
  93.0 4.2 %collective-permute-start.29 = (bf16[48,4096]{1,0:T(8,128)(2,1)S(1)}, bf16[48,4096]{1,0:T(8,128)(2,1)S(1)}, u32[]{:S(2)}, u32[]{:S(2)}) collective-permute-start(bf16[48,4096]{1,0:T(8,128)(2,1)S(1)} %collective-permute-done.13.refs_4_.refs_12_), channel_id=1, source_target_pairs={{0,4},{4,0},{8,12},{12,8},{1,5},{5,1},{9,13},{13,9},{2,6},{6,2},{1... | collective-permute-start | bytes 1179656 | tf_op jit(solution)/shard_map/ppermute | solution.py:243
  93.1 4.1 %collective-permute-start.30 = (bf16[48,4096]{1,0:T(8,128)(2,1)}, bf16[48,4096]{1,0:T(8,128)(2,1)S(1)}, u32[]{:S(2)}, u32[]{:S(2)}) collective-permute-start(bf16[48,4096]{1,0:T(8,128)(2,1)} %collective-permute-done.20.refs_5_.refs_13_), channel_id=1, source_target_pairs={{0,4},{4,0},{8,12},{12,8},{1,5},{5,1},{9,13},{13,9},{2,6},{6,2},{1... | collective-permute-start | bytes 1179656 | tf_op jit(solution)/shard_map/ppermute | solution.py:243
  93.7 18.7 %collective-permute-start.31 = (bf16[384,896]{1,0:T(8,128)(2,1)S(1)}, bf16[384,896]{1,0:T(8,128)(2,1)S(1)}, u32[]{:S(2)}, u32[]{:S(2)}) collective-permute-start(bf16[384,896]{1,0:T(8,128)(2,1)S(1)} %copy-done.3), channel_id=1, source_target_pairs={{0,16},{16,0},{1,17},{17,1},{2,18},{18,2},{3,19},{19,3},{4,20},{20... | collective-permute-start | bytes 2064392 | tf_op jit(solution)/shard_map/ppermute | solution.py:249
  96.5 15.9 %collective-permute-start.26 = (bf16[48,4096]{1,0:T(8,128)(2,1)}, bf16[48,4096]{1,0:T(8,128)(2,1)}, u32[]{:S(2)}, u32[]{:S(2)}) collective-permute-start(bf16[48,4096]{1,0:T(8,128)(2,1)} %collective-permute-done.19.refs_4_), channel_id=1, source_target_pairs={{0,8},{4,12},{8,0},{12,4},{1,9},{5,13},{9,1},{13,5},{2,10},{6,14},... | collective-permute-start | bytes 1179656 | tf_op jit(solution)/shard_map/ppermute | solution.py:243
  113.2 3.6 %collective-permute-start.32 = (bf16[192,4096]{1,0:T(8,128)(2,1)}, bf16[192,4096]{1,0:T(8,128)(2,1)S(1)}, u32[]{:S(2)}, u32[]{:S(2)}) collective-permute-start(bf16[192,4096]{1,0:T(8,128)(2,1)} %get-tuple-element.121), channel_id=1, source_target_pairs={{0,4},{4,0},{8,12},{12,8},{1,5},{5,1},{9,13},{13,9},{2,6},{6,2},{1... | collective-permute-start | bytes 4718600 | tf_op jit(solution)/shard_map/ppermute | solution.py:243
  114.3 20.2 %collective-permute-start.36 = (bf16[384,896]{1,0:T(8,128)(2,1)}, bf16[384,896]{1,0:T(8,128)(2,1)}, u32[]{:S(2)}, u32[]{:S(2)}) collective-permute-start(bf16[384,896]{1,0:T(8,128)(2,1)} %get-tuple-element.125), channel_id=1, source_target_pairs={{0,16},{16,0},{1,17},{17,1},{2,18},{18,2},{3,19},{19,3},{4,20},{20... | collective-permute-start | bytes 2064392 | tf_op jit(solution)/shard_map/ppermute | solution.py:249
  114.8 4.8 %collective-permute-start.34 = (bf16[48,4096]{1,0:T(8,128)(2,1)}, bf16[48,4096]{1,0:T(8,128)(2,1)S(1)}, u32[]{:S(2)}, u32[]{:S(2)}) collective-permute-start(bf16[48,4096]{1,0:T(8,128)(2,1)} %collective-permute-done.19.refs_4_), channel_id=1, source_target_pairs={{0,4},{4,0},{8,12},{12,8},{1,5},{5,1},{9,13},{13,9},{2,6},{6,2},{1... | collective-permute-start | bytes 1179656 | tf_op jit(solution)/shard_map/ppermute | solution.py:243
  115.1 4.5 %collective-permute-start.35 = (bf16[48,4096]{1,0:T(8,128)(2,1)}, bf16[48,4096]{1,0:T(8,128)(2,1)}, u32[]{:S(2)}, u32[]{:S(2)}) collective-permute-start(bf16[48,4096]{1,0:T(8,128)(2,1)} %collective-permute-done.26.refs_5_), channel_id=1, source_target_pairs={{0,4},{4,0},{8,12},{12,8},{1,5},{5,1},{9,13},{13,9},{2,6},{6,2},{1... | collective-permute-start | bytes 1179656 | tf_op jit(solution)/shard_map/ppermute | solution.py:243
  117.0 19.6 %collective-permute-start.33 = (bf16[96,4096]{1,0:T(8,128)(2,1)S(1)}, bf16[96,4096]{1,0:T(8,128)(2,1)S(1)}, u32[]{:S(2)}, u32[]{:S(2)}) collective-permute-start(bf16[96,4096]{1,0:T(8,128)(2,1)S(1)} %add_convert_fusion.3), channel_id=1, source_target_pairs={{0,8},{4,12},{8,0},{12,4},{1,9},{5,13},{9,1},{13,5},{2,10},{6,14},... | collective-permute-start | bytes 2359304 | tf_op jit(solution)/shard_map/ppermute | solution.py:243
  137.6 3.6 %collective-permute-start.37 = (bf16[192,4096]{1,0:T(8,128)(2,1)}, bf16[192,4096]{1,0:T(8,128)(2,1)S(1)}, u32[]{:S(2)}, u32[]{:S(2)}) collective-permute-start(bf16[192,4096]{1,0:T(8,128)(2,1)} %get-tuple-element.134), channel_id=1, source_target_pairs={{0,4},{4,0},{8,12},{12,8},{1,5},{5,1},{9,13},{13,9},{2,6},{6,2},{1... | collective-permute-start | bytes 4718600 | tf_op jit(solution)/shard_map/ppermute | solution.py:243
  137.6 24.9 %collective-permute-start.39 = (bf16[384,896]{1,0:T(8,128)(2,1)}, bf16[384,896]{1,0:T(8,128)(2,1)}, u32[]{:S(2)}, u32[]{:S(2)}) collective-permute-start(bf16[384,896]{1,0:T(8,128)(2,1)} %get-tuple-element.139), channel_id=1, source_target_pairs={{0,16},{16,0},{1,17},{17,1},{2,18},{18,2},{3,19},{19,3},{4,20},{20... | collective-permute-start | bytes 2064392 | tf_op jit(solution)/shard_map/ppermute | solution.py:249
  143.4 19.8 %collective-permute-start.38 = (bf16[96,4096]{1,0:T(8,128)(2,1)}, bf16[96,4096]{1,0:T(8,128)(2,1)S(1)}, u32[]{:S(2)}, u32[]{:S(2)}) collective-permute-start(bf16[96,4096]{1,0:T(8,128)(2,1)} %add_convert_fusion.2), channel_id=1, source_target_pairs={{0,8},{4,12},{8,0},{12,4},{1,9},{5,13},{9,1},{13,5},{2,10},{6,14},... | collective-permute-start | bytes 2359304 | tf_op jit(solution)/shard_map/ppermute | solution.py:243
  163.2 3.6 %collective-permute-start.40 = (bf16[192,4096]{1,0:T(8,128)(2,1)}, bf16[192,4096]{1,0:T(8,128)(2,1)S(1)}, u32[]{:S(2)}, u32[]{:S(2)}) collective-permute-start(bf16[192,4096]{1,0:T(8,128)(2,1)} %get-tuple-element.141), channel_id=1, source_target_pairs={{0,4},{4,0},{8,12},{12,8},{1,5},{5,1},{9,13},{13,9},{2,6},{6,2},{1... | collective-permute-start | bytes 4718600 | tf_op jit(solution)/shard_map/ppermute | solution.py:243
  169.1 23.9 %collective-permute-start.41 = (bf16[96,4096]{1,0:T(8,128)(2,1)}, bf16[96,4096]{1,0:T(8,128)(2,1)S(1)}, u32[]{:S(2)}, u32[]{:S(2)}) collective-permute-start(bf16[96,4096]{1,0:T(8,128)(2,1)} %add_convert_fusion.1), channel_id=1, source_target_pairs={{0,8},{4,12},{8,0},{12,4},{1,9},{5,13},{9,1},{13,5},{2,10},{6,14},... | collective-permute-start | bytes 2359304 | tf_op jit(solution)/shard_map/ppermute | solution.py:243
  172.8 18.6 %collective-permute-start.43 = (bf16[48,4096]{1,0:T(8,128)(2,1)}, bf16[48,4096]{1,0:T(8,128)(2,1)}, u32[]{:S(2)}, u32[]{:S(2)}) collective-permute-start(bf16[48,4096]{1,0:T(8,128)(2,1)} %get-tuple-element.167), channel_id=1, source_target_pairs={{0,3},{1,0},{2,1},{3,2},{4,7},{5,4},{6,5},{7,6},{8,11},{9,8},{10,9... | collective-permute-start | bytes 1179656 | tf_op jit(solution)/shard_map/ppermute | solution.py:238
  174.9 18.1 %collective-permute-start.42 = (bf16[48,4096]{1,0:T(8,128)(2,1)S(1)}, bf16[48,4096]{1,0:T(8,128)(2,1)S(1)}, u32[]{:S(2)}, u32[]{:S(2)}) collective-permute-start(bf16[48,4096]{1,0:T(8,128)(2,1)S(1)} %get-tuple-element.168), channel_id=1, source_target_pairs={{0,1},{1,2},{2,3},{3,0},{4,5},{5,6},{6,7},{7,4},{8,9},{9,10},{10,1... | collective-permute-start | bytes 1179656 | tf_op jit(solution)/shard_map/ppermute | solution.py:238
  193.7 3.6 %collective-permute-start.44 = (bf16[192,4096]{1,0:T(8,128)(2,1)}, bf16[192,4096]{1,0:T(8,128)(2,1)S(1)}, u32[]{:S(2)}, u32[]{:S(2)}) collective-permute-start(bf16[192,4096]{1,0:T(8,128)(2,1)} %get-tuple-element.149), channel_id=1, source_target_pairs={{0,4},{4,0},{8,12},{12,8},{1,5},{5,1},{9,13},{13,9},{2,6},{6,2},{1... | collective-permute-start | bytes 4718600 | tf_op jit(solution)/shard_map/ppermute | solution.py:243
  199.6 35.8 %collective-permute-start.45 = (bf16[96,4096]{1,0:T(8,128)(2,1)}, bf16[96,4096]{1,0:T(8,128)(2,1)}, u32[]{:S(2)}, u32[]{:S(2)}) collective-permute-start(bf16[96,4096]{1,0:T(8,128)(2,1)} %add_convert_fusion), channel_id=1, source_target_pairs={{0,8},{4,12},{8,0},{12,4},{1,9},{5,13},{9,1},{13,5},{2,10},{6,14},... | collective-permute-start | bytes 2359304 | tf_op jit(solution)/shard_map/ppermute | solution.py:243
  202.7 32.6 %collective-permute-start.46 = (bf16[48,4096]{1,0:T(8,128)(2,1)}, bf16[48,4096]{1,0:T(8,128)(2,1)}, u32[]{:S(2)}, u32[]{:S(2)}) collective-permute-start(bf16[48,4096]{1,0:T(8,128)(2,1)} %add_convert_fusion.7), channel_id=1, source_target_pairs={{0,3},{1,0},{2,1},{3,2},{4,7},{5,4},{6,5},{7,6},{8,11},{9,8},{10,9... | collective-permute-start | bytes 1179656 | tf_op jit(solution)/shard_map/ppermute | solution.py:238
  205.6 29.8 %collective-permute-start.48 = (bf16[48,4096]{1,0:T(8,128)(2,1)}, bf16[48,4096]{1,0:T(8,128)(2,1)S(1)}, u32[]{:S(2)}, u32[]{:S(2)}) collective-permute-start(bf16[48,4096]{1,0:T(8,128)(2,1)} %get-tuple-element.165), channel_id=1, source_target_pairs={{0,1},{1,2},{2,3},{3,0},{4,5},{5,6},{6,7},{7,4},{8,9},{9,10},{10,1... | collective-permute-start | bytes 1179656 | tf_op jit(solution)/shard_map/ppermute | solution.py:238
  205.9 29.5 %collective-permute-start.47 = (bf16[48,4096]{1,0:T(8,128)(2,1)}, bf16[48,4096]{1,0:T(8,128)(2,1)S(1)}, u32[]{:S(2)}, u32[]{:S(2)}) collective-permute-start(bf16[48,4096]{1,0:T(8,128)(2,1)} %get-tuple-element.166), channel_id=1, source_target_pairs={{0,3},{1,0},{2,1},{3,2},{4,7},{5,4},{6,5},{7,6},{8,11},{9,8},{10,9... | collective-permute-start | bytes 1179656 | tf_op jit(solution)/shard_map/ppermute | solution.py:238
  237.4 17.0 %collective-permute-start.49 = (bf16[48,4096]{1,0:T(8,128)(2,1)}, bf16[48,4096]{1,0:T(8,128)(2,1)S(1)}, u32[]{:S(2)}, u32[]{:S(2)}) collective-permute-start(bf16[48,4096]{1,0:T(8,128)(2,1)} %add_convert_fusion.4), channel_id=1, source_target_pairs={{0,3},{1,0},{2,1},{3,2},{4,7},{5,4},{6,5},{7,6},{8,11},{9,8},{10,9... | collective-permute-start | bytes 1179656 | tf_op jit(solution)/shard_map/ppermute | solution.py:238
  (49 other events, 467.5 us)

commit v7 on v5

--- a/solution.py
+++ b/solution.py
@@ -34,7 +34,7 @@
     return pl.CostEstimate(flops=flops, bytes_accessed=moved, transcendentals=0)
 
 
-def contract_kernel(n_pieces, n_weights, right_dim, *refs):
+def contract_kernel(n_pieces, n_weights, *refs):
     pieces, weights = refs[:n_pieces], refs[n_pieces : n_pieces + n_weights]
     out, total = refs[-2:]
     step = pl.program_id(0)
@@ -44,32 +44,31 @@
         total[...] = jnp.zeros_like(total)
 
     rows = jnp.concatenate([piece[...] for piece in pieces], axis=0)
-    for i, weight in enumerate(weights):
-        total[i * rows.shape[0] : (i + 1) * rows.shape[0]] += dot(rows, weight[...], 1, right_dim)
+    weight = jnp.concatenate([weight[...] for weight in weights], axis=1)
+    total[...] += dot(rows, weight, 1, 0)
 
     @pl.when(step == pl.num_programs(0) - 1)
     def _():
-        out[...] = narrow(total[...])
-
-
-def contract(pieces, weights, right_dim):
+        size, units = rows.shape[0], total.shape[1] // n_weights
+        for i in range(n_weights):
+            out[i * size : (i + 1) * size] = narrow(total[:, i * units : (i + 1) * units])
+
+
+def contract(pieces, weights):
     width = pieces[0].shape[1]
-    units = weights[0].shape[1 - right_dim]
+    units = weights[0].shape[1]
     block = min(1024, width)
-    if right_dim == 0:
-        weight_spec = pl.BlockSpec((block, units), lambda k: (k, 0))
-    else:
-        weight_spec = pl.BlockSpec((units, block), lambda k: (0, k))
+    weight_spec = pl.BlockSpec((block, units), lambda k: (k, 0))
     rows = sum(piece.shape[0] for piece in pieces)
     shape = (rows * len(weights), units)
     return pl.pallas_call(
-        functools.partial(contract_kernel, len(pieces), len(weights), right_dim),
+        functools.partial(contract_kernel, len(pieces), len(weights)),
         grid=(width // block,),
         in_specs=[pl.BlockSpec((piece.shape[0], block), lambda k: (0, k)) for piece in pieces]
         + [weight_spec] * len(weights),
         out_specs=pl.BlockSpec(shape, lambda k: (0, 0)),
         out_shape=jax.ShapeDtypeStruct(shape, jnp.bfloat16),
-        scratch_shapes=[pltpu.VMEM(shape, jnp.float32)],
+        scratch_shapes=[pltpu.VMEM((rows, units * len(weights)), jnp.float32)],
         compiler_params=pltpu.CompilerParams(vmem_limit_bytes=VMEM_BYTES),
         cost_estimate=cost(2 * len(weights) * rows * width * units, *pieces, *weights),
     )(*pieces, *weights)
@@ -85,11 +84,12 @@
 
 def expand_kernel(n, *refs):
     lefts, weights, outs = refs[: 2 * n], refs[2 * n : 3 * n], refs[3 * n :]
-    total = 0.0
-    for i, weight in enumerate(weights):
-        left = jnp.concatenate([block[...] for block in lefts[2 * i : 2 * i + 2]], axis=0)
-        total = total + dot(left, weight[...], 1, 1)
-    store_halves(total, outs)
+    left = [
+        jnp.concatenate([block[...] for block in lefts[2 * i : 2 * i + 2]], axis=0)
+        for i in range(n)
+    ]
+    weight = jnp.concatenate([weight[...] for weight in weights], axis=1)
+    store_halves(dot(jnp.concatenate(left, axis=1), weight, 1, 1), outs)
 
 
 def expand(lefts, weights):
@@ -154,9 +154,14 @@
     pieces, grads, outs = refs[:n_pieces], refs[n_pieces:-2], refs[-2:]
     rows = jnp.concatenate([piece[...] for piece in pieces], axis=0)
     half = len(grads) // 2
+    grad = [
+        jnp.concatenate([grad[...] for grad in grads[i * half : (i + 1) * half]], axis=0)
+        for i in range(2)
+    ]
+    both = dot(rows, jnp.concatenate(grad, axis=1), 0, 0)
+    units = both.shape[1] // 2
     for i, out in enumerate(outs):
-        grad = jnp.concatenate([grad[...] for grad in grads[i * half : (i + 1) * half]], axis=0)
-        out[...] = dot(rows, grad, 0, 0)
+        out[...] = both[:, i * units : (i + 1) * units]
 
 
 def wide_grads(pieces, gate_grads, up_grads):
@@ -273,7 +278,7 @@
     near3, far1 = shift(after(tokens, near1), 3), swap(near1, CHIP)
     core1, far_core0 = other_cores([near1, far0])
     token0 = quad(tokens, far0, [core0, far_core0])
-    pair0 = contract(token0, pair, 0)
+    pair0 = contract(token0, pair)
     near3, far1, core1, pair0 = sync(near3, far1, core1, pair0)
 
     pair0_moved = row_moves(pair0)
@@ -281,7 +286,7 @@
     near2, cot_near3 = shift(near1, 1), shift(cot, 3)
     far3, cot_far0 = swap(near3, CHIP), swap(cot, CHIP)
     token1 = quad(near1, far1, [core1, swap(far1, CORE)])
-    pair1 = contract(token1, pair, 0)
+    pair1 = contract(token1, pair)
     near2, cot_near3, far3, cot_far0, pair1, *pair0_moved = sync(
         near2, cot_near3, far3, cot_far0, pair1, *pair0_moved
     )
@@ -293,7 +298,7 @@
     cot_near2 = shift(cot, 2)
     far2, cot_far3 = swap(near2, CHIP), swap(cot_near3, CHIP)
     token3 = quad(near3, far3, other_cores([after(near3, pair1), far3]))
-    pair3 = contract(token3, pair, 0)
+    pair3 = contract(token3, pair)
     cot_near2, far2, cot_far3, pair3, *pair1_moved = sync(
         cot_near2, far2, cot_far3, pair3, *pair1_moved
     )
@@ -304,8 +309,11 @@
     cot = after(cotangent, pair3)
     cot_near1, cot_far2 = shift(cot, 1), swap(cot_near2, CHIP)
     token2 = quad(near2, far2, other_cores([after(near2, pair3), far2]))
-    pair2 = contract(token2, pair, 0)
-    cot_near1, cot_far2, pair2, *pair3_moved = sync(cot_near1, cot_far2, pair2, *pair3_moved)
+    pair2 = contract(token2, pair)
+    cot0 = quad(cot, cot_far0, other_cores([cot, after(cot_far0, pair3)]))
+    cot_near1, cot_far2, pair2, cot0[2], cot0[3], *pair3_moved = sync(
+        cot_near1, cot_far2, pair2, cot0[2], cot0[3], *pair3_moved
+    )
 
     gate3, up3 = pair_sums(pair3, pair3_moved)
     hidden3 = hidden_of(gate3, up3)
@@ -323,8 +331,6 @@
     grad_b_moved = row_moves(grad_b)
     sent, mixed_a = chip_part(mine, swap(other, CORE))
     mixed_a_moved = swap(sent, CHIP)
-    cot = after(cotangent, grad_b)
-    cot0 = quad(cot, cot_far0, other_cores([cot, after(cot_far0, grad_b)]))
     cot1 = quad(cot_near1, cot_far1, other_cores([after(cot_near1, grad_b), cot_far1]))
     grad_a, mine, other = down_products(cot0 + cot1, [hidden3, hidden2], down_weight)
     mixed_a_moved, grad_a, mine, other, *grad_b_moved = sync(
@@ -341,10 +347,10 @@
     mine, other = expand([[x, y] for x, y in zip(grads3, grads2)], pair)
     mixed_b_moved, mine, other, *grad_a_moved = sync(mixed_b_moved, mine, other, *grad_a_moved)
 
-    grad_a = row_sum(grad_a, grad_a_moved)
     sent, token_grad_b = chip_part(mine, swap(other, CORE))
     token_b_moved = swap(sent, CHIP)
-    mixed_b = owner_parts(mixed_b, mixed_b_moved)
+    grad_a = row_sum(grad_a, grad_a_moved)
+    mixed_b = owner_parts(mixed_b, after(mixed_b_moved, sent))
     part3, part2 = shift(narrow(mixed_b[0]), 1), shift(narrow(mixed_b[1]), -1)
     grads0 = grads_of(gate0, up0, grad_a[:half])
     grads1 = grads_of(gate1, up1, grad_a[half:])
@@ -354,25 +360,27 @@
     sent, token_grad_a = chip_part(mine, swap(other, CORE))
     token_a_moved = swap(sent, CHIP)
     mixed_a = owner_parts(mixed_a, mixed_a_moved)
-    part1 = shift(narrow(mixed_a[1] + wide(part2)), -1)
-    mixed = mixed_a[0] + wide(part3)
-    token_grad_b = owner_parts(token_grad_b, token_b_moved)
-    part3, part2 = shift(narrow(token_grad_b[0]), 1), shift(narrow(token_grad_b[1]), -1)
+    token_grad_b = owner_parts(token_grad_b, after(token_b_moved, sent))
+    mixed_part3, part3 = part3, shift(narrow(token_grad_b[0]), 1)
+    back = [narrow(mixed_a[1] + wide(part2)), narrow(token_grad_b[1])]
+    back = shift(jnp.concatenate(back, axis=0), -1)
     gate_total, up_total = wide_grads(
         [after(tokens, sent), *token0[1:], *token1, *token3, *token2],
         [grads0[0], grads1[0], grads3[0], grads2[0]],
         [grads0[1], grads1[1], grads3[1], grads2[1]],
     )
-    token_a_moved, part1, part2, part3, gate_total, up_total = sync(
-        token_a_moved, part1, part2, part3, gate_total, up_total
-    )
-    mixed = mixed + wide(part1)
+    token_a_moved, back, part3, gate_total, up_total = sync(
+        token_a_moved, back, part3, gate_total, up_total
+    )
 
     token_grad_a = owner_parts(token_grad_a, token_a_moved)
-    part1 = shift(narrow(token_grad_a[1] + wide(part2)), -1)
+    size = back.shape[0] // 2
+    part1 = shift(narrow(token_grad_a[1] + wide(back[size:])), -1)
     down_total = tall_grad(
         cot0 + cot1 + cot3 + cot2, [after(hidden0, gate_total), hidden1, hidden3, hidden2]
     )
+    part1, mixed_part3, back, part3, down_total = sync(part1, mixed_part3, back, part3, down_total)
+    mixed = mixed_a[0] + wide(mixed_part3) + wide(back[:size])
     token_grad = token_grad_a[0] + wide(part3) + wide(part1)
     return (mixed, token_grad, gate_total, up_total, down_total)
 

time: 241 us -> 245 us (1.017)
  waiting for transfers between devices: 41.6 us -> 55.5 us
  starting transfers between devices: 50.2 us -> 42.1 us
    ppermute x12 -> x11, waiting for transfers between devices: 17 us -> 36.5 us  [shift(): return lax.ppermute(block, 'depth', [(i, (i + step) % n) for i in range(n)])]
    ppermute x12 -> x11, starting transfers between devices: 25.4 us -> 19.6 us  [shift(): return lax.ppermute(block, 'depth', [(i, (i + step) % n) for i in range(n)])]
    ppermute x32, waiting for transfers between devices: 21.2 us -> 16.7 us  [swap(): return lax.ppermute(block, 'col', [(i, i ^ bit) for i in range(n)])]
    unnamed x88 -> x96, local copies, waits for them, and re-layouts: 6.92 us -> 7.5 us
  transfers between devices with their start and end apart: 50 -> 49, of which waited for: 16 -> 16; matrix products, arithmetic and copies ran while one was open for 8% -> 6% of each run, Pallas kernels for 49% -> 48%
where the time goes in v7:
time: 245 us; the launch traced here: 243 us
  Pallas kernels  116 us (47%)
  waiting for transfers between devices  55.5 us (23%)
  starting transfers between devices  42.1 us (17%)
  other arithmetic  20.9 us (9%)
  local copies, waits for them, and re-layouts  7.5 us (3%)
    ppermute x11, waiting for transfers between devices, shift(): return lax.ppermute(block, 'depth', [(i, (i + step) % n) for i in range(n)])  36.5 us
    pallas_call x4, Pallas kernels, contract(): pl.pallas_call(functools.partial(contract_kernel, len(pieces), len(weight...  34.7 us
    pallas_call x2, Pallas kernels, down_products(): pl.pallas_call(functools.partial(down_kernel, len(pieces)), grid=(width /...  25.1 us
    pallas_call x2, Pallas kernels, expand(): pl.pallas_call(functools.partial(expand_kernel, len(lefts)), grid=(width...  24.9 us
    ppermute x11, starting transfers between devices, shift(): return lax.ppermute(block, 'depth', [(i, (i + step) % n) for i in range(n)])  19.6 us
    pallas_call x1, Pallas kernels, wide_grads(): pl.pallas_call(functools.partial(wide_grad_kernel, len(pieces)), grid=(wi...  17.9 us
    ppermute x32, waiting for transfers between devices, swap(): return lax.ppermute(block, 'col', [(i, i ^ bit) for i in range(n)])  16.7 us
    ppermute x32, starting transfers between devices, swap(): return lax.ppermute(block, 'col', [(i, i ^ bit) for i in range(n)])  16.3 us
  transfers between devices with their start and end apart: 49, of which 16 were waited for; matrix products, arithmetic and copies ran while one was open for 6% of the time, Pallas kernels for 48%

profile of v7, /device:TPU:0, one launch (start us, length us, event | category | flops | bytes accessed | tf_op | source)
XLA Modules:
  0.0 242.7 jit_solution(15204650500587763962)
XLA Ops:
  0.6 3.1 %collective-permute-start = (bf16[48,4096]{1,0:T(8,128)(2,1)}, bf16[48,4096]{1,0:T(8,128)(2,1)S(1)}, u32[]{:S(2)}, u32[]{:S(2)}) collective-permute-start(bf16[48,4096]{1,0:T(8,128)(2,1)} %refs_0_.3), channel_id=1, source_target_pairs={{0,1},{1,2},{2,3},{3,0},{4,5},{5,6},{6,7},{7,4},{8,9},{9,10},{10,1... | collective-permute-start | bytes 1179656 | tf_op jit(solution)/shard_map/ppermute | solution.py:211
  3.7 1.5 collective-permute-start.1
  5.2 9.8 %collective-permute-done.refs_0_.refs_4_ = bf16[48,4096]{1,0:T(8,128)(2,1)S(1)} collective-permute-done((bf16[48,4096]{1,0:T(8,128)(2,1)}, bf16[48,4096]{1,0:T(8,128)(2,1)S(1)}, u32[]{:S(2)}, u32[]{:S(2)}) %collective-permute-start) | collective-permute-done | bytes 393248 | tf_op jit(solution)/shard_map/ppermute | solution.py:211
  15.2 1.9 collective-permute-start.4
  17.0 1.5 collective-permute-start.5
  19.3 8.7 %shard_map.92 = bf16[384,896]{1,0:T(8,128)(2,1)} custom-call(bf16[48,4096]{1,0:T(8,128)(2,1)} %refs_0_.3, bf16[48,4096]{1,0:T(8,128)(2,1)} %copy-done.22, bf16[48,4096]{1,0:T(8,128)(2,1)} %copy-done.23, bf16[48,4096]{1,0:T(8,128)(2,1)} %copy-done.24, bf16[4096,896]{1,0:T(8,128)(2,1)} %refs_4_.11, bf16[4096,896]{1,0:T(8,128)(2,1)} %refs_5_.11), custom_call_target="tpu_custom_call" | custom-call | flops 2818572288 | bytes 16252928 | tf_op jit(solution)/shard_map/pallas_call | solution.py:64
  28.6 1.5 collective-permute-start.12
  30.3 1.3 collective-permute-start.10
  31.6 3.6 %collective-permute-start.8 = (bf16[48,4096]{1,0:T(8,128)(2,1)S(1)}, bf16[48,4096]{1,0:T(8,128)(2,1)S(1)}, u32[]{:S(2)}, u32[]{:S(2)}) collective-permute-start(bf16[48,4096]{1,0:T(8,128)(2,1)S(1)} %copy-done.20), channel_id=1, source_target_pairs={{0,3},{1,0},{2,1},{3,2},{4,7},{5,4},{6,5},{7,6},{8,11},{9,8},{10,9... | collective-permute-start | bytes 1179656 | tf_op jit(solution)/shard_map/ppermute | solution.py:211
  36.0 8.7 %shard_map.93 = bf16[384,896]{1,0:T(8,128)(2,1)} custom-call(bf16[48,4096]{1,0:T(8,128)(2,1)} %copy-done.21, bf16[48,4096]{1,0:T(8,128)(2,1)} %copy-done.28, bf16[48,4096]{1,0:T(8,128)(2,1)} %copy-done.29, bf16[48,4096]{1,0:T(8,128)(2,1)} %copy-done.30, bf16[4096,896]{1,0:T(8,128)(2,1)} %refs_4_.11, bf16[4096,896]{1,0:T(8,128)(2,1)} %refs_5_.11), custom_call_target="tpu_custom_call" | custom-call | flops 2818572288 | bytes 16252928 | tf_op jit(solution)/shard_map/pallas_call | solution.py:64
  44.7 6.1 %collective-permute-done.8.refs_0_.refs_8_ = bf16[48,4096]{1,0:T(8,128)(2,1)S(1)} collective-permute-done((bf16[48,4096]{1,0:T(8,128)(2,1)S(1)}, bf16[48,4096]{1,0:T(8,128)(2,1)S(1)}, u32[]{:S(2)}, u32[]{:S(2)}) %collective-permute-start.8) | collective-permute-done | bytes 393248 | tf_op jit(solution)/shard_map/ppermute | solution.py:211
  51.6 1.3 collective-permute-start.13
  52.9 1.5 collective-permute-start.14
  55.9 8.7 %shard_map.94 = bf16[384,896]{1,0:T(8,128)(2,1)} custom-call(bf16[48,4096]{1,0:T(8,128)(2,1)} %copy-done.26, bf16[48,4096]{1,0:T(8,128)(2,1)} %copy-done.33, bf16[48,4096]{1,0:T(8,128)(2,1)} %copy-done.34, bf16[48,4096]{1,0:T(8,128)(2,1)} %copy-done.35, bf16[4096,896]{1,0:T(8,128)(2,1)} %refs_4_.11, bf16[4096,896]{1,0:T(8,128)(2,1)} %refs_5_.11), custom_call_target="tpu_custom_call" | custom-call | flops 2818572288 | bytes 16252928 | tf_op jit(solution)/shard_map/pallas_call | solution.py:64
  64.6 7.8 %collective-permute-done.13.refs_4_.refs_12_ = bf16[48,4096]{1,0:T(8,128)(2,1)S(1)} collective-permute-done((bf16[48,4096]{1,0:T(8,128)(2,1)S(1)}, bf16[48,4096]{1,0:T(8,128)(2,1)S(1)}, u32[]{:S(2)}, u32[]{:S(2)}) %collective-permute-start.13) | collective-permute-done | bytes 393248 | tf_op jit(solution)/shard_map/ppermute | solution.py:211
  73.1 1.5 collective-permute-start.25
  74.5 1.5 collective-permute-start.19
  77.4 1.5 collective-permute-start.20
  79.1 8.7 %shard_map.95 = bf16[384,896]{1,0:T(8,128)(2,1)} custom-call(bf16[48,4096]{1,0:T(8,128)(2,1)} %copy-done.31, bf16[48,4096]{1,0:T(8,128)(2,1)} %copy-done.36, bf16[48,4096]{1,0:T(8,128)(2,1)} %copy-done.39, bf16[48,4096]{1,0:T(8,128)(2,1)} %copy-done.40, bf16[4096,896]{1,0:T(8,128)(2,1)} %refs_4_.11, bf16[4096,896]{1,0:T(8,128)(2,1)} %refs_5_.11), custom_call_target="tpu_custom_call" | custom-call | flops 2818572288 | bytes 16252928 | tf_op jit(solution)/shard_map/pallas_call | solution.py:64
  88.6 2.1 collective-permute-done.25
  91.9 1.6 collective-permute-start.31
  94.7 1.6 collective-permute-start.26
  97.3 12.6 %shard_map.96 = (bf16[384,896]{1,0:T(8,128)(2,1)}, bf16[192,4096]{1,0:T(8,128)(2,1)}, bf16[192,4096]{1,0:T(8,128)(2,1)}) custom-call(bf16[48,4096]{1,0:T(8,128)(2,1)} %copy-done.27, bf16[48,4096]{1,0:T(8,128)(2,1)} %collective-permute-done.15.refs_1_.refs_9_, bf16[48,4096]{1,0:T(8,128)(2,1)} %copy-done.44, bf16[48,4096]{1,0:T(8,128)(2,1)} %copy-done.43, ...), custom_call_target="tpu_custom_call" | custom-call | flops 5637144576 | bytes 14319616 | tf_op jit(solution)/shard_map/pallas_call | solution.py:138
  112.8 1.5 collective-permute-done.32
  117.1 12.5 %shard_map.97 = (bf16[384,896]{1,0:T(8,128)(2,1)}, bf16[192,4096]{1,0:T(8,128)(2,1)}, bf16[192,4096]{1,0:T(8,128)(2,1)}) custom-call(bf16[48,4096]{1,0:T(8,128)(2,1)} %refs_0_.4, bf16[48,4096]{1,0:T(8,128)(2,1)} %copy-done.25, bf16[48,4096]{1,0:T(8,128)(2,1)} %collective-permute-done.23.refs_2_, bf16[48,4096]{1,0:T(8,128)(2,1)} %collective-permute-done.24.refs_3_, ...), custom_call_target="tpu_custom_call" | custom-call | flops 5637144576 | bytes 14319616 | tf_op jit(solution)/shard_map/pallas_call | solution.py:138
  129.9 4.3 %collective-permute-done.33 = bf16[96,4096]{1,0:T(8,128)(2,1)} collective-permute-done((bf16[96,4096]{1,0:T(8,128)(2,1)S(1)}, bf16[96,4096]{1,0:T(8,128)(2,1)}, u32[]{:S(2)}, u32[]{:S(2)}) %collective-permute-start.33) | collective-permute-done | bytes 786464 | tf_op jit(solution)/shard_map/ppermute | solution.py:216
  134.8 1.4 convert_add_fusion.1
  136.2 1.6 collective-permute-done.37
  140.6 1.7 multiply_convert_fusion.4
  142.3 12.4 %shard_map.98 = (bf16[192,4096]{1,0:T(8,128)(2,1)}, bf16[192,4096]{1,0:T(8,128)(2,1)}) custom-call(bf16[192,896]{1,0:T(8,128)(2,1)} %get-tuple-element.181.refs_0_.refs_18_, bf16[192,896]{1,0:T(8,128)(2,1)} %get-tuple-element.176.refs_1_.refs_19_, bf16[192,896]{1,0:T(8,128)(2,1)} %get-tuple-element.182.refs_2_.refs_22_, ...), custom_call_target="tpu_custom_call" | custom-call | flops 5637144576 | bytes 19202048 | tf_op jit(solution)/shard_map/pallas_call | solution.py:101
  154.7 5.2 %collective-permute-done.38 = bf16[96,4096]{1,0:T(8,128)(2,1)S(1)} collective-permute-done((bf16[96,4096]{1,0:T(8,128)(2,1)}, bf16[96,4096]{1,0:T(8,128)(2,1)S(1)}, u32[]{:S(2)}, u32[]{:S(2)}) %collective-permute-start.38) | collective-permute-done | bytes 786464 | tf_op jit(solution)/shard_map/ppermute | solution.py:216
  161.1 1.7 multiply_convert_fusion
  163.5 1.2 add_convert_fusion.1
  165.5 1.6 collective-permute-start.42
  167.1 2.3 collective-permute-start.43
  169.4 12.5 %shard_map.99 = (bf16[192,4096]{1,0:T(8,128)(2,1)}, bf16[192,4096]{1,0:T(8,128)(2,1)}) custom-call(bf16[192,896]{1,0:T(8,128)(2,1)} %get-tuple-element.179.refs_0_.refs_16_, bf16[192,896]{1,0:T(8,128)(2,1)} %get-tuple-element.172.refs_1_.refs_17_, bf16[192,896]{1,0:T(8,128)(2,1)} %get-tuple-element.180.refs_2_.refs_20_, ...), custom_call_target="tpu_custom_call" | custom-call | flops 5637144576 | bytes 19202048 | tf_op jit(solution)/shard_map/pallas_call | solution.py:101
  181.9 4.4 %collective-permute-done.43 = bf16[48,4096]{1,0:T(8,128)(2,1)} collective-permute-done((bf16[48,4096]{1,0:T(8,128)(2,1)S(1)}, bf16[48,4096]{1,0:T(8,128)(2,1)}, u32[]{:S(2)}, u32[]{:S(2)}) %collective-permute-start.43) | collective-permute-done | bytes 393248 | tf_op jit(solution)/shard_map/ppermute | solution.py:211
  186.4 1.3 add_convert_fusion.7
  187.7 2.3 collective-permute-done.44
  191.1 1.2 collective-permute-start.45
  193.5 2.1 collective-permute-start.46
  195.6 17.9 %shard_map.100 = (f32[4096,896]{1,0:T(8,128)}, f32[4096,896]{1,0:T(8,128)}) custom-call(bf16[48,4096]{1,0:T(8,128)(2,1)} %refs_0_.3, bf16[48,4096]{1,0:T(8,128)(2,1)} %copy-done.22, bf16[48,4096]{1,0:T(8,128)(2,1)} %copy-done.23, bf16[48,4096]{1,0:T(8,128)(2,1)} %copy-done.24, bf16[48,4096]{1,0:T(8,128)(2,1)} %copy-done.21, bf16[48,4096]{1,0:T(8,128)(2,1)} %copy-done.28, ...), custom_call_target="tpu_custom_call" | custom-call | flops 11274289152 | bytes 38404096 | tf_op jit(solution)/shard_map/pallas_call | solution.py:173
  213.5 8.4 %collective-permute-done.47 = bf16[48,4096]{1,0:T(8,128)(2,1)S(1)} collective-permute-done((bf16[48,4096]{1,0:T(8,128)(2,1)}, bf16[48,4096]{1,0:T(8,128)(2,1)S(1)}, u32[]{:S(2)}, u32[]{:S(2)}) %collective-permute-start.47) | collective-permute-done | bytes 393248 | tf_op jit(solution)/shard_map/ppermute | solution.py:211
  221.9 1.3 add_convert_fusion.4
  223.2 2.0 collective-permute-start.48
  225.2 13.0 %shard_map.101 = f32[896,4096]{1,0:T(8,128)} custom-call(bf16[48,4096]{1,0:T(8,128)(2,1)} %refs_0_.4, bf16[48,4096]{1,0:T(8,128)(2,1)} %copy-done.25, bf16[48,4096]{1,0:T(8,128)(2,1)} %collective-permute-done.23.refs_2_, bf16[48,4096]{1,0:T(8,128)(2,1)} %collective-permute-done.24.refs_3_, bf16[48,4096]{1,0:T(8,128)(2,1)} %copy-done.37, ...), custom_call_target="tpu_custom_call" | custom-call | flops 5637144576 | bytes 22347776 | tf_op jit(solution)/shard_map/pallas_call | solution.py:197
  238.3 2.2 convert_add_fusion.6
  240.5 2.2 convert_add_fusion.7
  (178 shorter events, 25.4 us)
Async XLA Ops:
  0.6 14.4 %collective-permute-start = (bf16[48,4096]{1,0:T(8,128)(2,1)}, bf16[48,4096]{1,0:T(8,128)(2,1)S(1)}, u32[]{:S(2)}, u32[]{:S(2)}) collective-permute-start(bf16[48,4096]{1,0:T(8,128)(2,1)} %refs_0_.3), channel_id=1, source_target_pairs={{0,1},{1,2},{2,3},{3,0},{4,5},{5,6},{6,7},{7,4},{8,9},{9,10},{10,1... | collective-permute-start | bytes 1179656 | tf_op jit(solution)/shard_map/ppermute | solution.py:211
  3.7 11.4 %collective-permute-start.1 = (bf16[48,4096]{1,0:T(8,128)(2,1)}, bf16[48,4096]{1,0:T(8,128)(2,1)S(1)}, u32[]{:S(2)}, u32[]{:S(2)}) collective-permute-start(bf16[48,4096]{1,0:T(8,128)(2,1)} %refs_0_.3), channel_id=1, source_target_pairs={{0,8},{4,12},{8,0},{12,4},{1,9},{5,13},{9,1},{13,5},{2,10},{6,14},... | collective-permute-start | bytes 1179656 | tf_op jit(solution)/shard_map/ppermute | solution.py:216
  5.2 9.8 %collective-permute-start.2 = (bf16[48,4096]{1,0:T(8,128)(2,1)}, bf16[48,4096]{1,0:T(8,128)(2,1)S(1)}, u32[]{:S(2)}, u32[]{:S(2)}) collective-permute-start(bf16[48,4096]{1,0:T(8,128)(2,1)} %refs_0_.3), channel_id=1, source_target_pairs={{0,4},{4,0},{8,12},{12,8},{1,5},{5,1},{9,13},{13,9},{2,6},{6,2},{1... | collective-permute-start | bytes 1179656 | tf_op jit(solution)/shard_map/ppermute | solution.py:216
  15.2 12.8 %collective-permute-start.4 = (bf16[48,4096]{1,0:T(8,128)(2,1)}, bf16[48,4096]{1,0:T(8,128)(2,1)S(1)}, u32[]{:S(2)}, u32[]{:S(2)}) collective-permute-start(bf16[48,4096]{1,0:T(8,128)(2,1)} %refs_0_.3), channel_id=1, source_target_pairs={{0,3},{1,0},{2,1},{3,2},{4,7},{5,4},{6,5},{7,6},{8,11},{9,8},{10,9... | collective-permute-start | bytes 1179656 | tf_op jit(solution)/shard_map/ppermute | solution.py:211
  17.0 11.2 %collective-permute-start.5 = (bf16[48,4096]{1,0:T(8,128)(2,1)S(1)}, bf16[48,4096]{1,0:T(8,128)(2,1)S(1)}, u32[]{:S(2)}, u32[]{:S(2)}) collective-permute-start(bf16[48,4096]{1,0:T(8,128)(2,1)S(1)} %collective-permute-done.refs_0_.refs_4_), channel_id=1, source_target_pairs={{0,8},{4,12},{8,0},{12,4},{1,9},{5,13},{9,1},{13,5},{2,10},{6,14},... | collective-permute-start | bytes 1179656 | tf_op jit(solution)/shard_map/ppermute | solution.py:216
  18.5 9.7 %collective-permute-start.6 = (bf16[48,4096]{1,0:T(8,128)(2,1)S(1)}, bf16[48,4096]{1,0:T(8,128)(2,1)S(1)}, u32[]{:S(2)}, u32[]{:S(2)}) collective-permute-start(bf16[48,4096]{1,0:T(8,128)(2,1)S(1)} %collective-permute-done.refs_0_.refs_4_), channel_id=1, source_target_pairs={{0,4},{4,0},{8,12},{12,8},{1,5},{5,1},{9,13},{13,9},{2,6},{6,2},{1... | collective-permute-start | bytes 1179656 | tf_op jit(solution)/shard_map/ppermute | solution.py:216
  28.2 7.0 %collective-permute-start.11 = (bf16[48,4096]{1,0:T(8,128)(2,1)S(1)}, bf16[48,4096]{1,0:T(8,128)(2,1)S(1)}, u32[]{:S(2)}, u32[]{:S(2)}) collective-permute-start(bf16[48,4096]{1,0:T(8,128)(2,1)S(1)} %collective-permute-done.5.refs_1_.refs_5_), channel_id=1, source_target_pairs={{0,4},{4,0},{8,12},{12,8},{1,5},{5,1},{9,13},{13,9},{2,6},{6,2},{1... | collective-permute-start | bytes 1179656 | tf_op jit(solution)/shard_map/ppermute | solution.py:216
  28.6 22.2 %collective-permute-start.12 = (bf16[384,896]{1,0:T(8,128)(2,1)}, bf16[384,896]{1,0:T(8,128)(2,1)S(1)}, u32[]{:S(2)}, u32[]{:S(2)}) collective-permute-start(bf16[384,896]{1,0:T(8,128)(2,1)} %shard_map.92), channel_id=1, source_target_pairs={{0,16},{16,0},{1,17},{17,1},{2,18},{18,2},{3,19},{19,3},{4,20},{20... | collective-permute-start | bytes 2064392 | tf_op jit(solution)/shard_map/ppermute | solution.py:222
  30.1 14.5 %collective-permute-start.3 = (bf16[48,4096]{1,0:T(8,128)(2,1)S(1)}, bf16[48,4096]{1,0:T(8,128)(2,1)S(1)}, u32[]{:S(2)}, u32[]{:S(2)}) collective-permute-start(bf16[48,4096]{1,0:T(8,128)(2,1)S(1)} %collective-permute-done.refs_0_.refs_4_), channel_id=1, source_target_pairs={{0,1},{1,2},{2,3},{3,0},{4,5},{5,6},{6,7},{7,4},{8,9},{9,10},{10,1... | collective-permute-start | bytes 1179656 | tf_op jit(solution)/shard_map/ppermute | solution.py:211
  30.3 14.3 %collective-permute-start.10 = (bf16[48,4096]{1,0:T(8,128)(2,1)S(1)}, bf16[48,4096]{1,0:T(8,128)(2,1)S(1)}, u32[]{:S(2)}, u32[]{:S(2)}) collective-permute-start(bf16[48,4096]{1,0:T(8,128)(2,1)S(1)} %copy-done.20), channel_id=1, source_target_pairs={{0,8},{4,12},{8,0},{12,4},{1,9},{5,13},{9,1},{13,5},{2,10},{6,14},... | collective-permute-start | bytes 1179656 | tf_op jit(solution)/shard_map/ppermute | solution.py:216
  31.6 19.2 %collective-permute-start.8 = (bf16[48,4096]{1,0:T(8,128)(2,1)S(1)}, bf16[48,4096]{1,0:T(8,128)(2,1)S(1)}, u32[]{:S(2)}, u32[]{:S(2)}) collective-permute-start(bf16[48,4096]{1,0:T(8,128)(2,1)S(1)} %copy-done.20), channel_id=1, source_target_pairs={{0,3},{1,0},{2,1},{3,2},{4,7},{5,4},{6,5},{7,6},{8,11},{9,8},{10,9... | collective-permute-start | bytes 1179656 | tf_op jit(solution)/shard_map/ppermute | solution.py:211
  35.2 15.6 %collective-permute-start.9 = (bf16[48,4096]{1,0:T(8,128)(2,1)S(1)}, bf16[48,4096]{1,0:T(8,128)(2,1)S(1)}, u32[]{:S(2)}, u32[]{:S(2)}) collective-permute-start(bf16[48,4096]{1,0:T(8,128)(2,1)S(1)} %collective-permute-done.4.refs_0_.refs_8_), channel_id=1, source_target_pairs={{0,8},{4,12},{8,0},{12,4},{1,9},{5,13},{9,1},{13,5},{2,10},{6,14},... | collective-permute-start | bytes 1179656 | tf_op jit(solution)/shard_map/ppermute | solution.py:216
  50.8 3.6 %collective-permute-start.16 = (bf16[48,4096]{1,0:T(8,128)(2,1)S(1)}, bf16[48,4096]{1,0:T(8,128)(2,1)S(1)}, u32[]{:S(2)}, u32[]{:S(2)}) collective-permute-start(bf16[48,4096]{1,0:T(8,128)(2,1)S(1)} %collective-permute-done.4.refs_0_.refs_8_), channel_id=1, source_target_pairs={{0,4},{4,0},{8,12},{12,8},{1,5},{5,1},{9,13},{13,9},{2,6},{6,2},{1... | collective-permute-start | bytes 1179656 | tf_op jit(solution)/shard_map/ppermute | solution.py:216
  50.9 21.7 %collective-permute-start.18 = (bf16[384,896]{1,0:T(8,128)(2,1)}, bf16[384,896]{1,0:T(8,128)(2,1)S(1)}, u32[]{:S(2)}, u32[]{:S(2)}) collective-permute-start(bf16[384,896]{1,0:T(8,128)(2,1)} %shard_map.93), channel_id=1, source_target_pairs={{0,16},{16,0},{1,17},{17,1},{2,18},{18,2},{3,19},{19,3},{4,20},{20... | collective-permute-start | bytes 2064392 | tf_op jit(solution)/shard_map/ppermute | solution.py:222
  51.5 3.5 %collective-permute-start.17 = (bf16[48,4096]{1,0:T(8,128)(2,1)S(1)}, bf16[48,4096]{1,0:T(8,128)(2,1)S(1)}, u32[]{:S(2)}, u32[]{:S(2)}) collective-permute-start(bf16[48,4096]{1,0:T(8,128)(2,1)S(1)} %collective-permute-done.9.refs_1_.refs_9_), channel_id=1, source_target_pairs={{0,4},{4,0},{8,12},{12,8},{1,5},{5,1},{9,13},{13,9},{2,6},{6,2},{1... | collective-permute-start | bytes 1179656 | tf_op jit(solution)/shard_map/ppermute | solution.py:216
  51.6 20.7 %collective-permute-start.13 = (bf16[48,4096]{1,0:T(8,128)(2,1)S(1)}, bf16[48,4096]{1,0:T(8,128)(2,1)S(1)}, u32[]{:S(2)}, u32[]{:S(2)}) collective-permute-start(bf16[48,4096]{1,0:T(8,128)(2,1)S(1)} %copy-done.20), channel_id=1, source_target_pairs={{0,2},{1,3},{2,0},{3,1},{4,6},{5,7},{6,4},{7,5},{8,10},{9,11},{10,... | collective-permute-start | bytes 1179656 | tf_op jit(solution)/shard_map/ppermute | solution.py:211
  52.9 19.4 %collective-permute-start.14 = (bf16[48,4096]{1,0:T(8,128)(2,1)S(1)}, bf16[48,4096]{1,0:T(8,128)(2,1)S(1)}, u32[]{:S(2)}, u32[]{:S(2)}) collective-permute-start(bf16[48,4096]{1,0:T(8,128)(2,1)S(1)} %collective-permute-done.3.refs_0_.refs_12_), channel_id=1, source_target_pairs={{0,8},{4,12},{8,0},{12,4},{1,9},{5,13},{9,1},{13,5},{2,10},{6,14},... | collective-permute-start | bytes 1179656 | tf_op jit(solution)/shard_map/ppermute | solution.py:216
  54.4 18.1 %collective-permute-start.15 = (bf16[48,4096]{1,0:T(8,128)(2,1)S(1)}, bf16[48,4096]{1,0:T(8,128)(2,1)}, u32[]{:S(2)}, u32[]{:S(2)}) collective-permute-start(bf16[48,4096]{1,0:T(8,128)(2,1)S(1)} %collective-permute-done.8.refs_0_.refs_8_), channel_id=1, source_target_pairs={{0,8},{4,12},{8,0},{12,4},{1,9},{5,13},{9,1},{13,5},{2,10},{6,14},... | collective-permute-start | bytes 1179656 | tf_op jit(solution)/shard_map/ppermute | solution.py:216
  72.5 3.5 %collective-permute-start.21 = (bf16[48,4096]{1,0:T(8,128)(2,1)S(1)}, bf16[48,4096]{1,0:T(8,128)(2,1)S(1)}, u32[]{:S(2)}, u32[]{:S(2)}) collective-permute-start(bf16[48,4096]{1,0:T(8,128)(2,1)S(1)} %collective-permute-done.3.refs_0_.refs_12_), channel_id=1, source_target_pairs={{0,4},{4,0},{8,12},{12,8},{1,5},{5,1},{9,13},{13,9},{2,6},{6,2},{1... | collective-permute-start | bytes 1179656 | tf_op jit(solution)/shard_map/ppermute | solution.py:216
  72.5 4.1 %collective-permute-start.22 = (bf16[48,4096]{1,0:T(8,128)(2,1)S(1)}, bf16[48,4096]{1,0:T(8,128)(2,1)S(1)}, u32[]{:S(2)}, u32[]{:S(2)}) collective-permute-start(bf16[48,4096]{1,0:T(8,128)(2,1)S(1)} %collective-permute-done.14.refs_1_.refs_13_), channel_id=1, source_target_pairs={{0,4},{4,0},{8,12},{12,8},{1,5},{5,1},{9,13},{13,9},{2,6},{6,2},{1... | collective-permute-start | bytes 1179656 | tf_op jit(solution)/shard_map/ppermute | solution.py:216
  73.1 17.6 %collective-permute-start.25 = (bf16[384,896]{1,0:T(8,128)(2,1)}, bf16[384,896]{1,0:T(8,128)(2,1)S(1)}, u32[]{:S(2)}, u32[]{:S(2)}) collective-permute-start(bf16[384,896]{1,0:T(8,128)(2,1)} %shard_map.94), channel_id=1, source_target_pairs={{0,16},{16,0},{1,17},{17,1},{2,18},{18,2},{3,19},{19,3},{4,20},{20... | collective-permute-start | bytes 2064392 | tf_op jit(solution)/shard_map/ppermute | solution.py:222
  74.5 13.3 %collective-permute-start.19 = (bf16[48,4096]{1,0:T(8,128)(2,1)S(1)}, bf16[48,4096]{1,0:T(8,128)(2,1)S(1)}, u32[]{:S(2)}, u32[]{:S(2)}) collective-permute-start(bf16[48,4096]{1,0:T(8,128)(2,1)S(1)} %copy-done.20), channel_id=1, source_target_pairs={{0,1},{1,2},{2,3},{3,0},{4,5},{5,6},{6,7},{7,4},{8,9},{9,10},{10,1... | collective-permute-start | bytes 1179656 | tf_op jit(solution)/shard_map/ppermute | solution.py:211
  76.0 11.8 %collective-permute-start.23 = (bf16[48,4096]{1,0:T(8,128)(2,1)S(1)}, bf16[48,4096]{1,0:T(8,128)(2,1)}, u32[]{:S(2)}, u32[]{:S(2)}) collective-permute-start(bf16[48,4096]{1,0:T(8,128)(2,1)S(1)} %copy-done.20), channel_id=1, source_target_pairs={{0,4},{4,0},{8,12},{12,8},{1,5},{5,1},{9,13},{13,9},{2,6},{6,2},{1... | collective-permute-start | bytes 1179656 | tf_op jit(solution)/shard_map/ppermute | solution.py:216
  76.1 11.8 %collective-permute-start.24 = (bf16[48,4096]{1,0:T(8,128)(2,1)S(1)}, bf16[48,4096]{1,0:T(8,128)(2,1)}, u32[]{:S(2)}, u32[]{:S(2)}) collective-permute-start(bf16[48,4096]{1,0:T(8,128)(2,1)S(1)} %collective-permute-done.10.refs_1_), channel_id=1, source_target_pairs={{0,4},{4,0},{8,12},{12,8},{1,5},{5,1},{9,13},{13,9},{2,6},{6,2},{1... | collective-permute-start | bytes 1179656 | tf_op jit(solution)/shard_map/ppermute | solution.py:216
  77.4 11.2 %collective-permute-start.20 = (bf16[48,4096]{1,0:T(8,128)(2,1)S(1)}, bf16[48,4096]{1,0:T(8,128)(2,1)}, u32[]{:S(2)}, u32[]{:S(2)}) collective-permute-start(bf16[48,4096]{1,0:T(8,128)(2,1)S(1)} %collective-permute-done.13.refs_4_.refs_12_), channel_id=1, source_target_pairs={{0,8},{4,12},{8,0},{12,4},{1,9},{5,13},{9,1},{13,5},{2,10},{6,14},... | collective-permute-start | bytes 1179656 | tf_op jit(solution)/shard_map/ppermute | solution.py:216
  90.7 4.0 %collective-permute-start.30 = (bf16[48,4096]{1,0:T(8,128)(2,1)}, bf16[48,4096]{1,0:T(8,128)(2,1)S(1)}, u32[]{:S(2)}, u32[]{:S(2)}) collective-permute-start(bf16[48,4096]{1,0:T(8,128)(2,1)} %collective-permute-done.20.refs_5_.refs_13_), channel_id=1, source_target_pairs={{0,4},{4,0},{8,12},{12,8},{1,5},{5,1},{9,13},{13,9},{2,6},{6,2},{1... | collective-permute-start | bytes 1179656 | tf_op jit(solution)/shard_map/ppermute | solution.py:216
  90.7 5.6 %collective-permute-start.29 = (bf16[48,4096]{1,0:T(8,128)(2,1)S(1)}, bf16[48,4096]{1,0:T(8,128)(2,1)S(1)}, u32[]{:S(2)}, u32[]{:S(2)}) collective-permute-start(bf16[48,4096]{1,0:T(8,128)(2,1)S(1)} %collective-permute-done.13.refs_4_.refs_12_), channel_id=1, source_target_pairs={{0,4},{4,0},{8,12},{12,8},{1,5},{5,1},{9,13},{13,9},{2,6},{6,2},{1... | collective-permute-start | bytes 1179656 | tf_op jit(solution)/shard_map/ppermute | solution.py:216
  91.2 5.1 %collective-permute-start.28 = (bf16[48,4096]{1,0:T(8,128)(2,1)}, bf16[48,4096]{1,0:T(8,128)(2,1)S(1)}, u32[]{:S(2)}, u32[]{:S(2)}) collective-permute-start(bf16[48,4096]{1,0:T(8,128)(2,1)} %collective-permute-done.15.refs_1_.refs_9_), channel_id=1, source_target_pairs={{0,4},{4,0},{8,12},{12,8},{1,5},{5,1},{9,13},{13,9},{2,6},{6,2},{1... | collective-permute-start | bytes 1179656 | tf_op jit(solution)/shard_map/ppermute | solution.py:216
  91.2 5.1 %collective-permute-start.27 = (bf16[48,4096]{1,0:T(8,128)(2,1)S(1)}, bf16[48,4096]{1,0:T(8,128)(2,1)S(1)}, u32[]{:S(2)}, u32[]{:S(2)}) collective-permute-start(bf16[48,4096]{1,0:T(8,128)(2,1)S(1)} %collective-permute-done.8.refs_0_.refs_8_), channel_id=1, source_target_pairs={{0,4},{4,0},{8,12},{12,8},{1,5},{5,1},{9,13},{13,9},{2,6},{6,2},{1... | collective-permute-start | bytes 1179656 | tf_op jit(solution)/shard_map/ppermute | solution.py:216
  91.9 18.0 %collective-permute-start.31 = (bf16[384,896]{1,0:T(8,128)(2,1)S(1)}, bf16[384,896]{1,0:T(8,128)(2,1)S(1)}, u32[]{:S(2)}, u32[]{:S(2)}) collective-permute-start(bf16[384,896]{1,0:T(8,128)(2,1)S(1)} %copy-done.3), channel_id=1, source_target_pairs={{0,16},{16,0},{1,17},{17,1},{2,18},{18,2},{3,19},{19,3},{4,20},{20... | collective-permute-start | bytes 2064392 | tf_op jit(solution)/shard_map/ppermute | solution.py:222
  94.7 15.2 %collective-permute-start.26 = (bf16[48,4096]{1,0:T(8,128)(2,1)S(1)}, bf16[48,4096]{1,0:T(8,128)(2,1)S(1)}, u32[]{:S(2)}, u32[]{:S(2)}) collective-permute-start(bf16[48,4096]{1,0:T(8,128)(2,1)S(1)} %copy-done.38), channel_id=1, source_target_pairs={{0,8},{4,12},{8,0},{12,4},{1,9},{5,13},{9,1},{13,5},{2,10},{6,14},... | collective-permute-start | bytes 1179656 | tf_op jit(solution)/shard_map/ppermute | solution.py:216
  110.7 3.6 %collective-permute-start.32 = (bf16[192,4096]{1,0:T(8,128)(2,1)}, bf16[192,4096]{1,0:T(8,128)(2,1)S(1)}, u32[]{:S(2)}, u32[]{:S(2)}) collective-permute-start(bf16[192,4096]{1,0:T(8,128)(2,1)} %get-tuple-element.122), channel_id=1, source_target_pairs={{0,4},{4,0},{8,12},{12,8},{1,5},{5,1},{9,13},{13,9},{2,6},{6,2},{1... | collective-permute-start | bytes 4718600 | tf_op jit(solution)/shard_map/ppermute | solution.py:216
  111.8 18.2 %collective-permute-start.36 = (bf16[384,896]{1,0:T(8,128)(2,1)}, bf16[384,896]{1,0:T(8,128)(2,1)}, u32[]{:S(2)}, u32[]{:S(2)}) collective-permute-start(bf16[384,896]{1,0:T(8,128)(2,1)} %get-tuple-element.126), channel_id=1, source_target_pairs={{0,16},{16,0},{1,17},{17,1},{2,18},{18,2},{3,19},{19,3},{4,20},{20... | collective-permute-start | bytes 2064392 | tf_op jit(solution)/shard_map/ppermute | solution.py:222
  112.3 4.1 %collective-permute-start.34 = (bf16[48,4096]{1,0:T(8,128)(2,1)S(1)}, bf16[48,4096]{1,0:T(8,128)(2,1)S(1)}, u32[]{:S(2)}, u32[]{:S(2)}) collective-permute-start(bf16[48,4096]{1,0:T(8,128)(2,1)S(1)} %copy-done.38), channel_id=1, source_target_pairs={{0,4},{4,0},{8,12},{12,8},{1,5},{5,1},{9,13},{13,9},{2,6},{6,2},{1... | collective-permute-start | bytes 1179656 | tf_op jit(solution)/shard_map/ppermute | solution.py:216
  112.5 4.6 %collective-permute-start.35 = (bf16[48,4096]{1,0:T(8,128)(2,1)S(1)}, bf16[48,4096]{1,0:T(8,128)(2,1)}, u32[]{:S(2)}, u32[]{:S(2)}) collective-permute-start(bf16[48,4096]{1,0:T(8,128)(2,1)S(1)} %copy-done.46), channel_id=1, source_target_pairs={{0,4},{4,0},{8,12},{12,8},{1,5},{5,1},{9,13},{13,9},{2,6},{6,2},{1... | collective-permute-start | bytes 1179656 | tf_op jit(solution)/shard_map/ppermute | solution.py:216
  114.5 19.8 %collective-permute-start.33 = (bf16[96,4096]{1,0:T(8,128)(2,1)S(1)}, bf16[96,4096]{1,0:T(8,128)(2,1)}, u32[]{:S(2)}, u32[]{:S(2)}) collective-permute-start(bf16[96,4096]{1,0:T(8,128)(2,1)S(1)} %add_convert_fusion.3), channel_id=1, source_target_pairs={{0,8},{4,12},{8,0},{12,4},{1,9},{5,13},{9,1},{13,5},{2,10},{6,14},... | collective-permute-start | bytes 2359304 | tf_op jit(solution)/shard_map/ppermute | solution.py:216
  134.2 3.6 %collective-permute-start.37 = (bf16[192,4096]{1,0:T(8,128)(2,1)}, bf16[192,4096]{1,0:T(8,128)(2,1)S(1)}, u32[]{:S(2)}, u32[]{:S(2)}) collective-permute-start(bf16[192,4096]{1,0:T(8,128)(2,1)} %get-tuple-element.135), channel_id=1, source_target_pairs={{0,4},{4,0},{8,12},{12,8},{1,5},{5,1},{9,13},{13,9},{2,6},{6,2},{1... | collective-permute-start | bytes 4718600 | tf_op jit(solution)/shard_map/ppermute | solution.py:216
  134.2 20.5 %collective-permute-start.39 = (bf16[384,896]{1,0:T(8,128)(2,1)}, bf16[384,896]{1,0:T(8,128)(2,1)}, u32[]{:S(2)}, u32[]{:S(2)}) collective-permute-start(bf16[384,896]{1,0:T(8,128)(2,1)} %get-tuple-element.139), channel_id=1, source_target_pairs={{0,16},{16,0},{1,17},{17,1},{2,18},{18,2},{3,19},{19,3},{4,20},{20... | collective-permute-start | bytes 2064392 | tf_op jit(solution)/shard_map/ppermute | solution.py:222
  140.1 19.8 %collective-permute-start.38 = (bf16[96,4096]{1,0:T(8,128)(2,1)}, bf16[96,4096]{1,0:T(8,128)(2,1)S(1)}, u32[]{:S(2)}, u32[]{:S(2)}) collective-permute-start(bf16[96,4096]{1,0:T(8,128)(2,1)} %add_convert_fusion.2), channel_id=1, source_target_pairs={{0,8},{4,12},{8,0},{12,4},{1,9},{5,13},{9,1},{13,5},{2,10},{6,14},... | collective-permute-start | bytes 2359304 | tf_op jit(solution)/shard_map/ppermute | solution.py:216
  159.9 3.6 %collective-permute-start.40 = (bf16[192,4096]{1,0:T(8,128)(2,1)}, bf16[192,4096]{1,0:T(8,128)(2,1)S(1)}, u32[]{:S(2)}, u32[]{:S(2)}) collective-permute-start(bf16[192,4096]{1,0:T(8,128)(2,1)} %get-tuple-element.141), channel_id=1, source_target_pairs={{0,4},{4,0},{8,12},{12,8},{1,5},{5,1},{9,13},{13,9},{2,6},{6,2},{1... | collective-permute-start | bytes 4718600 | tf_op jit(solution)/shard_map/ppermute | solution.py:216
  164.7 21.6 %collective-permute-start.41 = (bf16[96,4096]{1,0:T(8,128)(2,1)}, bf16[96,4096]{1,0:T(8,128)(2,1)S(1)}, u32[]{:S(2)}, u32[]{:S(2)}) collective-permute-start(bf16[96,4096]{1,0:T(8,128)(2,1)} %add_convert_fusion.1), channel_id=1, source_target_pairs={{0,8},{4,12},{8,0},{12,4},{1,9},{5,13},{9,1},{13,5},{2,10},{6,14},... | collective-permute-start | bytes 2359304 | tf_op jit(solution)/shard_map/ppermute | solution.py:216
  165.5 16.4 %collective-permute-start.42 = (bf16[48,4096]{1,0:T(8,128)(2,1)S(1)}, bf16[48,4096]{1,0:T(8,128)(2,1)S(1)}, u32[]{:S(2)}, u32[]{:S(2)}) collective-permute-start(bf16[48,4096]{1,0:T(8,128)(2,1)S(1)} %get-tuple-element.170), channel_id=1, source_target_pairs={{0,1},{1,2},{2,3},{3,0},{4,5},{5,6},{6,7},{7,4},{8,9},{9,10},{10,1... | collective-permute-start | bytes 1179656 | tf_op jit(solution)/shard_map/ppermute | solution.py:211
  167.1 19.3 %collective-permute-start.43 = (bf16[48,4096]{1,0:T(8,128)(2,1)S(1)}, bf16[48,4096]{1,0:T(8,128)(2,1)}, u32[]{:S(2)}, u32[]{:S(2)}) collective-permute-start(bf16[48,4096]{1,0:T(8,128)(2,1)S(1)} %get-tuple-element.169), channel_id=1, source_target_pairs={{0,3},{1,0},{2,1},{3,2},{4,7},{5,4},{6,5},{7,6},{8,11},{9,8},{10,9... | collective-permute-start | bytes 1179656 | tf_op jit(solution)/shard_map/ppermute | solution.py:211
  186.4 3.6 %collective-permute-start.44 = (bf16[192,4096]{1,0:T(8,128)(2,1)}, bf16[192,4096]{1,0:T(8,128)(2,1)S(1)}, u32[]{:S(2)}, u32[]{:S(2)}) collective-permute-start(bf16[192,4096]{1,0:T(8,128)(2,1)} %get-tuple-element.148), channel_id=1, source_target_pairs={{0,4},{4,0},{8,12},{12,8},{1,5},{5,1},{9,13},{13,9},{2,6},{6,2},{1... | collective-permute-start | bytes 4718600 | tf_op jit(solution)/shard_map/ppermute | solution.py:216
  191.1 30.7 %collective-permute-start.45 = (bf16[96,4096]{1,0:T(8,128)(2,1)S(1)}, bf16[96,4096]{1,0:T(8,128)(2,1)}, u32[]{:S(2)}, u32[]{:S(2)}) collective-permute-start(bf16[96,4096]{1,0:T(8,128)(2,1)S(1)} %add_convert_fusion), channel_id=1, source_target_pairs={{0,8},{4,12},{8,0},{12,4},{1,9},{5,13},{9,1},{13,5},{2,10},{6,14},... | collective-permute-start | bytes 2359304 | tf_op jit(solution)/shard_map/ppermute | solution.py:216
  193.5 28.4 %collective-permute-start.46 = (bf16[96,4096]{1,0:T(8,128)(2,1)S(1)}, bf16[96,4096]{1,0:T(8,128)(2,1)}, u32[]{:S(2)}, u32[]{:S(2)}) collective-permute-start(bf16[96,4096]{1,0:T(8,128)(2,1)S(1)} %pad_maximum_fusion), channel_id=1, source_target_pairs={{0,3},{1,0},{2,1},{3,2},{4,7},{5,4},{6,5},{7,6},{8,11},{9,8},{10,9... | collective-permute-start | bytes 2359304 | tf_op jit(solution)/shard_map/ppermute | solution.py:211
  195.6 26.3 %collective-permute-start.47 = (bf16[48,4096]{1,0:T(8,128)(2,1)}, bf16[48,4096]{1,0:T(8,128)(2,1)S(1)}, u32[]{:S(2)}, u32[]{:S(2)}) collective-permute-start(bf16[48,4096]{1,0:T(8,128)(2,1)} %get-tuple-element.167), channel_id=1, source_target_pairs={{0,1},{1,2},{2,3},{3,0},{4,5},{5,6},{6,7},{7,4},{8,9},{9,10},{10,1... | collective-permute-start | bytes 1179656 | tf_op jit(solution)/shard_map/ppermute | solution.py:211
  223.2 15.1 %collective-permute-start.48 = (bf16[48,4096]{1,0:T(8,128)(2,1)S(1)}, bf16[48,4096]{1,0:T(8,128)(2,1)S(1)}, u32[]{:S(2)}, u32[]{:S(2)}) collective-permute-start(bf16[48,4096]{1,0:T(8,128)(2,1)S(1)} %add_convert_fusion.4), channel_id=1, source_target_pairs={{0,3},{1,0},{2,1},{3,2},{4,7},{5,4},{6,5},{7,6},{8,11},{9,8},{10,9... | collective-permute-start | bytes 1179656 | tf_op jit(solution)/shard_map/ppermute | solution.py:211
  (49 other events, 429.4 us)

commit v8 on v7

--- a/solution.py
+++ b/solution.py
@@ -74,12 +74,12 @@
     )(*pieces, *weights)
 
 
-def store_halves(total, outs):
+def store_parts(total, outs):
     size = total.shape[0] // 8
     for i, out in enumerate(outs):
-        for at, (half, block) in enumerate(((0, 0), (0, 1), (1, 0), (1, 1))):
-            first = (4 * block + 2 * i + half) * size
-            out[at * size : (at + 1) * size] = narrow(total[first : first + size])
+        for block in range(2):
+            first = (4 * block + i) * size
+            out[block * size : (block + 1) * size] = narrow(total[first : first + size])
 
 
 def expand_kernel(n, *refs):
@@ -89,7 +89,7 @@
         for i in range(n)
     ]
     weight = jnp.concatenate([weight[...] for weight in weights], axis=1)
-    store_halves(dot(jnp.concatenate(left, axis=1), weight, 1, 1), outs)
+    store_parts(dot(jnp.concatenate(left, axis=1), weight, 1, 1), outs)
 
 
 def expand(lefts, weights):
@@ -97,21 +97,21 @@
     rows, units = blocks[0].shape
     width = weights[0].shape[0]
     block = min(512, width)
-    out = jax.ShapeDtypeStruct((rows, width), jnp.bfloat16)
+    out = jax.ShapeDtypeStruct((rows // 2, width), jnp.bfloat16)
     return pl.pallas_call(
         functools.partial(expand_kernel, len(lefts)),
         grid=(width // block,),
         in_specs=[pl.BlockSpec((rows, units), lambda j: (0, 0))] * len(blocks)
         + [pl.BlockSpec((block, units), lambda j: (j, 0))] * len(weights),
-        out_specs=[pl.BlockSpec((rows, block), lambda j: (0, j))] * 2,
-        out_shape=[out, out],
+        out_specs=[pl.BlockSpec(out.shape[:1] + (block,), lambda j: (0, j))] * 4,
+        out_shape=[out] * 4,
         compiler_params=pltpu.CompilerParams(vmem_limit_bytes=VMEM_BYTES),
-        cost_estimate=cost(4 * len(lefts) * rows * width * units, *blocks, *weights, out, out),
+        cost_estimate=cost(4 * len(lefts) * rows * width * units, *blocks, *weights, *[out] * 4),
     )(*blocks, *weights)
 
 
 def down_kernel(n_pieces, *refs):
-    pieces, (first, second, weight, grad, mine, other, total) = refs[:n_pieces], refs[n_pieces:]
+    pieces, (first, second, weight, grad, *outs, total) = refs[:n_pieces], refs[n_pieces:]
     step = pl.program_id(0)
 
     @pl.when(step == 0)
@@ -121,7 +121,7 @@
     rows = jnp.concatenate([piece[...] for piece in pieces], axis=0)
     total[...] += dot(rows, weight[...], 1, 1)
     hidden = jnp.concatenate([first[...], second[...]], axis=0)
-    store_halves(dot(hidden, weight[...], 1, 0), (mine, other))
+    store_parts(dot(hidden, weight[...], 1, 0), outs)
 
     @pl.when(step == pl.num_programs(0) - 1)
     def _():
@@ -134,7 +134,7 @@
     rows = sum(piece.shape[0] for piece in pieces)
     half = hiddens[0].shape[0]
     grad = jax.ShapeDtypeStruct((rows, units), jnp.bfloat16)
-    out = jax.ShapeDtypeStruct((half, width), jnp.bfloat16)
+    out = jax.ShapeDtypeStruct((half // 2, width), jnp.bfloat16)
     return pl.pallas_call(
         functools.partial(down_kernel, len(pieces)),
         grid=(width // block,),
@@ -142,11 +142,11 @@
         + [pl.BlockSpec((half, units), lambda j: (0, 0))] * 2
         + [pl.BlockSpec((units, block), lambda j: (0, j))],
         out_specs=[pl.BlockSpec(grad.shape, lambda j: (0, 0))]
-        + [pl.BlockSpec((half, block), lambda j: (0, j))] * 2,
-        out_shape=[grad, out, out],
+        + [pl.BlockSpec((half // 2, block), lambda j: (0, j))] * 4,
+        out_shape=[grad] + [out] * 4,
         scratch_shapes=[pltpu.VMEM(grad.shape, jnp.float32)],
         compiler_params=pltpu.CompilerParams(vmem_limit_bytes=VMEM_BYTES),
-        cost_estimate=cost(4 * rows * width * units, *pieces, *hiddens, weight, out, out),
+        cost_estimate=cost(4 * rows * width * units, *pieces, *hiddens, weight, *[out] * 4),
     )(*pieces, *hiddens, weight)
 
 
@@ -250,9 +250,10 @@
     return [swap(block, CORE) for block in blocks]
 
 
-def chip_part(mine, moved):
-    half = mine.shape[0] // 2
-    return add(mine[half:], moved[half:]), (mine[:half], moved[:half])
+def chip_part(parts):
+    near, far, other_near, other_far = parts
+    sent = add(far, swap(other_far, CORE))
+    return sent, [near, swap(after(other_near, sent), CORE)]
 
 
 def owner_parts(kept, moved):
@@ -321,67 +322,69 @@
     cot_far1 = swap(cot_near1, CHIP)
     cot3 = quad(cot_near3, cot_far3, other_cores(after(x, pair2) for x in (cot_near3, cot_far3)))
     cot2 = quad(cot_near2, cot_far2, other_cores(after(x, pair2) for x in (cot_near2, cot_far2)))
-    grad_b, mine, other = down_products(cot3 + cot2, [hidden0, hidden1], down_weight)
-    cot_far1, grad_b, mine, other, *pair2_moved = sync(
-        cot_far1, grad_b, mine, other, *pair2_moved
-    )
+    products = down_products(cot3 + cot2, [hidden0, hidden1], down_weight)
+    cot_far1, grad_b, *rest = sync(cot_far1, *products, *pair2_moved)
+    parts, pair2_moved = rest[:4], rest[4:]
 
     gate2, up2 = pair_sums(pair2, pair2_moved)
     hidden2 = hidden_of(gate2, up2)
     grad_b_moved = row_moves(grad_b)
-    sent, mixed_a = chip_part(mine, swap(other, CORE))
+    sent, mixed_a = chip_part(parts)
     mixed_a_moved = swap(sent, CHIP)
     cot1 = quad(cot_near1, cot_far1, other_cores([after(cot_near1, grad_b), cot_far1]))
-    grad_a, mine, other = down_products(cot0 + cot1, [hidden3, hidden2], down_weight)
-    mixed_a_moved, grad_a, mine, other, *grad_b_moved = sync(
-        mixed_a_moved, grad_a, mine, other, *grad_b_moved
-    )
+    products = down_products(cot0 + cot1, [hidden3, hidden2], down_weight)
+    mixed_a_moved, mixed_a[1], grad_a, *rest = sync(
+        mixed_a_moved, mixed_a[1], *products, *grad_b_moved
+    )
+    parts, grad_b_moved = rest[:4], rest[4:]
 
     grad_b = row_sum(grad_b, grad_b_moved)
     grad_a_moved = row_moves(grad_a)
-    sent, mixed_b = chip_part(mine, swap(other, CORE))
+    sent, mixed_b = chip_part(parts)
     mixed_b_moved = swap(sent, CHIP)
     half = grad_b.shape[0] // 2
     grads3 = grads_of(gate3, up3, grad_b[:half])
     grads2 = grads_of(gate2, up2, grad_b[half:])
-    mine, other = expand([[x, y] for x, y in zip(grads3, grads2)], pair)
-    mixed_b_moved, mine, other, *grad_a_moved = sync(mixed_b_moved, mine, other, *grad_a_moved)
-
-    sent, token_grad_b = chip_part(mine, swap(other, CORE))
+    parts = expand([[x, y] for x, y in zip(grads3, grads2)], pair)
+    mixed_b_moved, mixed_b[1], *rest = sync(mixed_b_moved, mixed_b[1], *parts, *grad_a_moved)
+    parts, grad_a_moved = rest[:4], rest[4:]
+
+    sent, token_grad_b = chip_part(parts)
     token_b_moved = swap(sent, CHIP)
     grad_a = row_sum(grad_a, grad_a_moved)
     mixed_b = owner_parts(mixed_b, after(mixed_b_moved, sent))
     part3, part2 = shift(narrow(mixed_b[0]), 1), shift(narrow(mixed_b[1]), -1)
     grads0 = grads_of(gate0, up0, grad_a[:half])
     grads1 = grads_of(gate1, up1, grad_a[half:])
-    mine, other = expand([[x, y] for x, y in zip(grads0, grads1)], pair)
-    token_b_moved, mine, other, part3, part2 = sync(token_b_moved, mine, other, part3, part2)
-
-    sent, token_grad_a = chip_part(mine, swap(other, CORE))
+    parts = expand([[x, y] for x, y in zip(grads0, grads1)], pair)
+    token_b_moved, token_grad_b[1], mixed_part3, mixed_part2, *parts = sync(
+        token_b_moved, token_grad_b[1], part3, part2, *parts
+    )
+
+    sent, token_grad_a = chip_part(parts)
     token_a_moved = swap(sent, CHIP)
     mixed_a = owner_parts(mixed_a, mixed_a_moved)
     token_grad_b = owner_parts(token_grad_b, after(token_b_moved, sent))
-    mixed_part3, part3 = part3, shift(narrow(token_grad_b[0]), 1)
-    back = [narrow(mixed_a[1] + wide(part2)), narrow(token_grad_b[1])]
-    back = shift(jnp.concatenate(back, axis=0), -1)
+    part3, part2 = shift(narrow(token_grad_b[0]), 1), shift(narrow(token_grad_b[1]), -1)
+    down_total = tall_grad(
+        cot0 + cot1 + cot3 + cot2, [after(hidden0, sent), hidden1, hidden3, hidden2]
+    )
+    token_a_moved, token_grad_a[1], part2, part3, down_total = sync(
+        token_a_moved, token_grad_a[1], part2, part3, down_total
+    )
+
+    token_grad_a = owner_parts(token_grad_a, token_a_moved)
+    back = [mixed_a[1] + wide(mixed_part2), token_grad_a[1] + wide(part2)]
+    back = shift(narrow(jnp.concatenate(back, axis=0)), -1)
     gate_total, up_total = wide_grads(
-        [after(tokens, sent), *token0[1:], *token1, *token3, *token2],
+        [after(tokens, down_total), *token0[1:], *token1, *token3, *token2],
         [grads0[0], grads1[0], grads3[0], grads2[0]],
         [grads0[1], grads1[1], grads3[1], grads2[1]],
     )
-    token_a_moved, back, part3, gate_total, up_total = sync(
-        token_a_moved, back, part3, gate_total, up_total
-    )
-
-    token_grad_a = owner_parts(token_grad_a, token_a_moved)
+    back, mixed_part3, part3, gate_total = sync(back, mixed_part3, part3, gate_total)
     size = back.shape[0] // 2
-    part1 = shift(narrow(token_grad_a[1] + wide(back[size:])), -1)
-    down_total = tall_grad(
-        cot0 + cot1 + cot3 + cot2, [after(hidden0, gate_total), hidden1, hidden3, hidden2]
-    )
-    part1, mixed_part3, back, part3, down_total = sync(part1, mixed_part3, back, part3, down_total)
     mixed = mixed_a[0] + wide(mixed_part3) + wide(back[:size])
-    token_grad = token_grad_a[0] + wide(part3) + wide(part1)
+    token_grad = token_grad_a[0] + wide(part3) + wide(back[size:])
     return (mixed, token_grad, gate_total, up_total, down_total)
 
 

time: 245 us -> 233 us (0.951)
  other arithmetic: 20.9 us -> 15.3 us
  local copies, waits for them, and re-layouts: 7.5 us -> 4.25 us
    ppermute x11, waiting for transfers between devices: 36.5 us -> 28.7 us  [shift(): return lax.ppermute(block, 'depth', [(i, (i + step) % n) for i in range(n)])]
    convert_element_type x13 -> x11, other arithmetic: 13.2 us -> 7.95 us  [narrow(): return block.astype(jnp.bfloat16)]
    ppermute x32 -> x36, waiting for transfers between devices: 16.7 us -> 20.2 us  [swap(): return lax.ppermute(block, 'col', [(i, i ^ bit) for i in range(n)])]
    unnamed x96 -> x84, local copies, waits for them, and re-layouts: 7.5 us -> 4.25 us
    ppermute x32 -> x36, starting transfers between devices: 16.3 us -> 15.3 us  [swap(): return lax.ppermute(block, 'col', [(i, i ^ bit) for i in range(n)])]
  transfers between devices with their start and end apart: 49 -> 53, of which waited for: 16 -> 18; matrix products, arithmetic and copies ran while one was open for 6% -> 5% of each run, Pallas kernels for 48% -> 50%
where the time goes in v8:
time: 233 us; the launch traced here: 231 us
  Pallas kernels  115 us (49%)
  waiting for transfers between devices  53.1 us (23%)
  starting transfers between devices  41.9 us (18%)
  other arithmetic  15.3 us (7%)
  local copies, waits for them, and re-layouts  4.25 us (2%)
    pallas_call x4, Pallas kernels, contract(): pl.pallas_call(functools.partial(contract_kernel, len(pieces), len(weight...  34.8 us
    ppermute x11, waiting for transfers between devices, shift(): return lax.ppermute(block, 'depth', [(i, (i + step) % n) for i in range(n)])  28.7 us
    pallas_call x2, Pallas kernels, down_products(): pl.pallas_call(functools.partial(down_kernel, len(pieces)), grid=(width /...  25.1 us
    pallas_call x2, Pallas kernels, expand(): pl.pallas_call(functools.partial(expand_kernel, len(lefts)), grid=(width...  24.6 us
    ppermute x36, waiting for transfers between devices, swap(): return lax.ppermute(block, 'col', [(i, i ^ bit) for i in range(n)])  20.2 us
    ppermute x11, starting transfers between devices, shift(): return lax.ppermute(block, 'depth', [(i, (i + step) % n) for i in range(n)])  19.1 us
    pallas_call x1, Pallas kernels, wide_grads(): pl.pallas_call(functools.partial(wide_grad_kernel, len(pieces)), grid=(wi...  17.8 us
    ppermute x36, starting transfers between devices, swap(): return lax.ppermute(block, 'col', [(i, i ^ bit) for i in range(n)])  15.3 us
  transfers between devices with their start and end apart: 53, of which 18 were waited for; matrix products, arithmetic and copies ran while one was open for 5% of the time, Pallas kernels for 50%

profile of v8, /device:TPU:0, one launch (start us, length us, event | category | flops | bytes accessed | tf_op | source)
XLA Modules:
  0.0 231.0 jit_solution(3838132700076998356)
XLA Ops:
  1.2 2.6 %collective-permute-start.1 = (bf16[48,4096]{1,0:T(8,128)(2,1)}, bf16[48,4096]{1,0:T(8,128)(2,1)S(1)}, u32[]{:S(2)}, u32[]{:S(2)}) collective-permute-start(bf16[48,4096]{1,0:T(8,128)(2,1)} %refs_0_.4), channel_id=1, source_target_pairs={{0,8},{4,12},{8,0},{12,4},{1,9},{5,13},{9,1},{13,5},{2,10},{6,14},... | collective-permute-start | bytes 1179656 | tf_op jit(solution)/shard_map/ppermute | solution.py:216
  3.8 1.6 collective-permute-start
  5.3 8.3 %collective-permute-done.1.refs_1_ = bf16[48,4096]{1,0:T(8,128)(2,1)S(1)} collective-permute-done((bf16[48,4096]{1,0:T(8,128)(2,1)}, bf16[48,4096]{1,0:T(8,128)(2,1)S(1)}, u32[]{:S(2)}, u32[]{:S(2)}) %collective-permute-start.1) | collective-permute-done | bytes 393248 | tf_op jit(solution)/shard_map/ppermute | solution.py:216
  13.7 3.4 %collective-permute-done.refs_0_.refs_4_ = bf16[48,4096]{1,0:T(8,128)(2,1)S(1)} collective-permute-done((bf16[48,4096]{1,0:T(8,128)(2,1)}, bf16[48,4096]{1,0:T(8,128)(2,1)S(1)}, u32[]{:S(2)}, u32[]{:S(2)}) %collective-permute-start) | collective-permute-done | bytes 393248 | tf_op jit(solution)/shard_map/ppermute | solution.py:211
  17.0 1.7 collective-permute-start.4
  20.3 8.7 %shard_map.92 = bf16[384,896]{1,0:T(8,128)(2,1)} custom-call(bf16[48,4096]{1,0:T(8,128)(2,1)} %refs_0_.4, bf16[48,4096]{1,0:T(8,128)(2,1)} %copy-done.19, bf16[48,4096]{1,0:T(8,128)(2,1)} %copy-done.18, bf16[48,4096]{1,0:T(8,128)(2,1)} %copy-done.21, bf16[4096,896]{1,0:T(8,128)(2,1)} %refs_4_.11, bf16[4096,896]{1,0:T(8,128)(2,1)} %refs_5_.11), custom_call_target="tpu_custom_call" | custom-call | flops 2818572288 | bytes 16252928 | tf_op jit(solution)/shard_map/pallas_call | solution.py:64
  29.0 1.3 collective-permute-done.5.refs_1_.refs_5_
  30.3 1.5 collective-permute-start.12
  32.6 3.5 %collective-permute-start.8 = (bf16[48,4096]{1,0:T(8,128)(2,1)S(1)}, bf16[48,4096]{1,0:T(8,128)(2,1)S(1)}, u32[]{:S(2)}, u32[]{:S(2)}) collective-permute-start(bf16[48,4096]{1,0:T(8,128)(2,1)S(1)} %copy-done.17), channel_id=1, source_target_pairs={{0,3},{1,0},{2,1},{3,2},{4,7},{5,4},{6,5},{7,6},{8,11},{9,8},{10,9... | collective-permute-start | bytes 1179656 | tf_op jit(solution)/shard_map/ppermute | solution.py:211
  36.1 1.5 collective-permute-start.9
  37.7 8.7 %shard_map.93 = bf16[384,896]{1,0:T(8,128)(2,1)} custom-call(bf16[48,4096]{1,0:T(8,128)(2,1)} %copy-done.20, bf16[48,4096]{1,0:T(8,128)(2,1)} %copy-done.24, bf16[48,4096]{1,0:T(8,128)(2,1)} %copy-done.23, bf16[48,4096]{1,0:T(8,128)(2,1)} %copy-done.25, bf16[4096,896]{1,0:T(8,128)(2,1)} %refs_4_.11, bf16[4096,896]{1,0:T(8,128)(2,1)} %refs_5_.11), custom_call_target="tpu_custom_call" | custom-call | flops 2818572288 | bytes 16252928 | tf_op jit(solution)/shard_map/pallas_call | solution.py:64
  46.4 5.4 %collective-permute-done.8.refs_0_.refs_8_ = bf16[48,4096]{1,0:T(8,128)(2,1)S(1)} collective-permute-done((bf16[48,4096]{1,0:T(8,128)(2,1)S(1)}, bf16[48,4096]{1,0:T(8,128)(2,1)S(1)}, u32[]{:S(2)}, u32[]{:S(2)}) %collective-permute-start.8) | collective-permute-done | bytes 393248 | tf_op jit(solution)/shard_map/ppermute | solution.py:211
  52.6 2.1 collective-permute-start.13
  55.2 1.5 collective-permute-start.15
  57.5 8.7 %shard_map.94 = bf16[384,896]{1,0:T(8,128)(2,1)} custom-call(bf16[48,4096]{1,0:T(8,128)(2,1)} %copy-done.22, bf16[48,4096]{1,0:T(8,128)(2,1)} %copy-done.27, bf16[48,4096]{1,0:T(8,128)(2,1)} %copy-done.28, bf16[48,4096]{1,0:T(8,128)(2,1)} %copy-done.29, bf16[4096,896]{1,0:T(8,128)(2,1)} %refs_4_.11, bf16[4096,896]{1,0:T(8,128)(2,1)} %refs_5_.11), custom_call_target="tpu_custom_call" | custom-call | flops 2818572288 | bytes 16252928 | tf_op jit(solution)/shard_map/pallas_call | solution.py:64
  66.2 7.2 %collective-permute-done.13.refs_4_.refs_12_ = bf16[48,4096]{1,0:T(8,128)(2,1)} collective-permute-done((bf16[48,4096]{1,0:T(8,128)(2,1)S(1)}, bf16[48,4096]{1,0:T(8,128)(2,1)}, u32[]{:S(2)}, u32[]{:S(2)}) %collective-permute-start.13) | collective-permute-done | bytes 393248 | tf_op jit(solution)/shard_map/ppermute | solution.py:211
  74.8 1.5 collective-permute-start.25
  76.3 1.7 collective-permute-start.19
  79.1 8.7 %shard_map.95 = bf16[384,896]{1,0:T(8,128)(2,1)} custom-call(bf16[48,4096]{1,0:T(8,128)(2,1)} %copy-done.26, bf16[48,4096]{1,0:T(8,128)(2,1)} %copy-done.30, bf16[48,4096]{1,0:T(8,128)(2,1)} %copy-done.33, bf16[48,4096]{1,0:T(8,128)(2,1)} %copy-done.34, bf16[4096,896]{1,0:T(8,128)(2,1)} %refs_4_.11, bf16[4096,896]{1,0:T(8,128)(2,1)} %refs_5_.11), custom_call_target="tpu_custom_call" | custom-call | flops 2818572288 | bytes 16252928 | tf_op jit(solution)/shard_map/pallas_call | solution.py:64
  87.8 1.9 collective-permute-done.19.refs_4_
  89.9 2.5 %collective-permute-done.25 = bf16[384,896]{1,0:T(8,128)(2,1)S(1)} collective-permute-done((bf16[384,896]{1,0:T(8,128)(2,1)}, bf16[384,896]{1,0:T(8,128)(2,1)S(1)}, u32[]{:S(2)}, u32[]{:S(2)}) %collective-permute-start.25) | collective-permute-done | bytes 688160 | tf_op jit(solution)/shard_map/ppermute | solution.py:222
  93.7 1.6 collective-permute-start.31
  95.2 1.3 multiply_convert_fusion.10
  98.2 12.6 %shard_map.96 = (bf16[384,896]{1,0:T(8,128)(2,1)}, bf16[96,4096]{1,0:T(8,128)(2,1)}, bf16[96,4096]{1,0:T(8,128)(2,1)}, bf16[96,4096]{1,0:T(8,128)(2,1)}, bf16[96,4096]{1,0:T(8,128)(2,1)}) custom-call(bf16[48,4096]{1,0:T(8,128)(2,1)} %copy-done.32, bf16[48,4096]{1,0:T(8,128)(2,1)} %copy-done.35, bf16[48,4096]{1,0:T(8,128)(2,1)} %copy-done.37, ...), custom_call_target="tpu_custom_call" | custom-call | flops 5637144576 | bytes 14319616 | tf_op jit(solution)/shard_map/pallas_call | solution.py:138
  112.1 0.9 multiply_convert_fusion.9.refs_8_.refs_18_
  113.1 1.5 collective-permute-start.37
  116.2 0.9 multiply_convert_fusion.8.refs_9_.refs_19_
  117.9 12.5 %shard_map.97 = (bf16[384,896]{1,0:T(8,128)(2,1)}, bf16[96,4096]{1,0:T(8,128)(2,1)}, bf16[96,4096]{1,0:T(8,128)(2,1)}, bf16[96,4096]{1,0:T(8,128)(2,1)}, bf16[96,4096]{1,0:T(8,128)(2,1)}) custom-call(bf16[48,4096]{1,0:T(8,128)(2,1)} %refs_0_.3, bf16[48,4096]{1,0:T(8,128)(2,1)} %copy-done.31, bf16[48,4096]{1,0:T(8,128)(2,1)} %collective-permute-done.23.refs_2_, ...), custom_call_target="tpu_custom_call" | custom-call | flops 5637144576 | bytes 14319616 | tf_op jit(solution)/shard_map/pallas_call | solution.py:138
  131.2 3.8 %collective-permute-done.33 = bf16[96,4096]{1,0:T(8,128)(2,1)S(1)} collective-permute-done((bf16[96,4096]{1,0:T(8,128)(2,1)S(1)}, bf16[96,4096]{1,0:T(8,128)(2,1)S(1)}, u32[]{:S(2)}, u32[]{:S(2)}) %collective-permute-start.33) | collective-permute-done | bytes 786464 | tf_op jit(solution)/shard_map/ppermute | solution.py:216
  135.9 1.4 convert_add_fusion.1
  138.5 1.7 multiply_convert_fusion.4
  140.3 12.3 %shard_map.98 = (bf16[96,4096]{1,0:T(8,128)(2,1)}, bf16[96,4096]{1,0:T(8,128)(2,1)}, bf16[96,4096]{1,0:T(8,128)(2,1)}, bf16[96,4096]{1,0:T(8,128)(2,1)}) custom-call(bf16[192,896]{1,0:T(8,128)(2,1)} %get-tuple-element.225.refs_0_.refs_18_, bf16[192,896]{1,0:T(8,128)(2,1)} %get-tuple-element.216.refs_1_.refs_19_, ...), custom_call_target="tpu_custom_call" | custom-call | flops 5637144576 | bytes 19202048 | tf_op jit(solution)/shard_map/pallas_call | solution.py:101
  153.2 4.2 %collective-permute-done.39 = bf16[96,4096]{1,0:T(8,128)(2,1)S(1)} collective-permute-done((bf16[96,4096]{1,0:T(8,128)(2,1)S(1)}, bf16[96,4096]{1,0:T(8,128)(2,1)S(1)}, u32[]{:S(2)}, u32[]{:S(2)}) %collective-permute-start.39) | collective-permute-done | bytes 786464 | tf_op jit(solution)/shard_map/ppermute | solution.py:216
  157.4 1.2 convert_add_fusion
  158.6 1.7 multiply_convert_fusion
  161.9 2.2 collective-permute-start.46
  164.1 12.3 %shard_map.99 = (bf16[96,4096]{1,0:T(8,128)(2,1)}, bf16[96,4096]{1,0:T(8,128)(2,1)}, bf16[96,4096]{1,0:T(8,128)(2,1)}, bf16[96,4096]{1,0:T(8,128)(2,1)}) custom-call(bf16[192,896]{1,0:T(8,128)(2,1)} %get-tuple-element.223.refs_0_.refs_16_, bf16[192,896]{1,0:T(8,128)(2,1)} %get-tuple-element.212.refs_1_.refs_17_, ...), custom_call_target="tpu_custom_call" | custom-call | flops 5637144576 | bytes 19202048 | tf_op jit(solution)/shard_map/pallas_call | solution.py:101
  176.5 6.4 %collective-permute-done.45 = bf16[48,4096]{1,0:T(8,128)(2,1)S(1)} collective-permute-done((bf16[48,4096]{1,0:T(8,128)(2,1)S(1)}, bf16[48,4096]{1,0:T(8,128)(2,1)S(1)}, u32[]{:S(2)}, u32[]{:S(2)}) %collective-permute-start.45) | collective-permute-done | bytes 393248 | tf_op jit(solution)/shard_map/ppermute | solution.py:211
  182.9 1.2 add_convert_fusion.7
  184.1 1.3 collective-permute-done.47
  185.6 0.9 collective-permute-start.48
  186.8 1.6 collective-permute-start.51
  188.4 2.3 collective-permute-start.50
  190.7 13.0 %shard_map.100 = f32[896,4096]{1,0:T(8,128)} custom-call(bf16[48,4096]{1,0:T(8,128)(2,1)} %refs_0_.3, bf16[48,4096]{1,0:T(8,128)(2,1)} %copy-done.31, bf16[48,4096]{1,0:T(8,128)(2,1)} %collective-permute-done.23.refs_2_, bf16[48,4096]{1,0:T(8,128)(2,1)} %collective-permute-done.24.refs_3_, bf16[48,4096]{1,0:T(8,128)(2,1)} %collective-permute-done.19.refs_4_, ...), custom_call_target="tpu_custom_call" | custom-call | flops 5637144576 | bytes 22347776 | tf_op jit(solution)/shard_map/pallas_call | solution.py:197
  203.7 4.4 %collective-permute-done.50 = bf16[48,4096]{1,0:T(8,128)(2,1)S(1)} collective-permute-done((bf16[48,4096]{1,0:T(8,128)(2,1)S(1)}, bf16[48,4096]{1,0:T(8,128)(2,1)S(1)}, u32[]{:S(2)}, u32[]{:S(2)}) %collective-permute-start.50) | collective-permute-done | bytes 393248 | tf_op jit(solution)/shard_map/ppermute | solution.py:211
  208.3 2.1 collective-permute-start.52
  210.5 17.8 %shard_map.101 = (f32[4096,896]{1,0:T(8,128)}, f32[4096,896]{1,0:T(8,128)}) custom-call(bf16[48,4096]{1,0:T(8,128)(2,1)} %refs_0_.4, bf16[48,4096]{1,0:T(8,128)(2,1)} %copy-done.19, bf16[48,4096]{1,0:T(8,128)(2,1)} %copy-done.18, bf16[48,4096]{1,0:T(8,128)(2,1)} %copy-done.21, bf16[48,4096]{1,0:T(8,128)(2,1)} %copy-done.20, bf16[48,4096]{1,0:T(8,128)(2,1)} %copy-done.24, ...), custom_call_target="tpu_custom_call" | custom-call | flops 11274289152 | bytes 38404096 | tf_op jit(solution)/shard_map/pallas_call | solution.py:173
  228.3 2.7 %convert_add_fusion.6 = (f32[48,4096]{1,0:T(8,128)}, f32[48,4096]{1,0:T(8,128)}) fusion(bf16[48,4096]{1,0:T(8,128)(2,1)S(1)} %collective-permute-done.51, bf16[96,4096]{1,0:T(8,128)(2,1)S(1)} %collective-permute-done.52, bf16[96,4096]{1,0:T(8,128)(2,1)S(1)} %collective-permute-done.48, bf16[96,4096]{1,0:T(8,128)(2,1)S(1)} %collective-permute-done.49, ...), kind=kLoop, calls=%fused_computation.11 | loop fusion | flops 3538944 | bytes 5505024 | tf_op jit(solution)/shard_map/add | solution.py:387
  (173 shorter events, 20.0 us)
Async XLA Ops:
  0.6 4.7 %collective-permute-start.2 = (bf16[48,4096]{1,0:T(8,128)(2,1)}, bf16[48,4096]{1,0:T(8,128)(2,1)S(1)}, u32[]{:S(2)}, u32[]{:S(2)}) collective-permute-start(bf16[48,4096]{1,0:T(8,128)(2,1)} %refs_0_.4), channel_id=1, source_target_pairs={{0,4},{4,0},{8,12},{12,8},{1,5},{5,1},{9,13},{13,9},{2,6},{6,2},{1... | collective-permute-start | bytes 1179656 | tf_op jit(solution)/shard_map/ppermute | solution.py:216
  1.2 12.5 %collective-permute-start.1 = (bf16[48,4096]{1,0:T(8,128)(2,1)}, bf16[48,4096]{1,0:T(8,128)(2,1)S(1)}, u32[]{:S(2)}, u32[]{:S(2)}) collective-permute-start(bf16[48,4096]{1,0:T(8,128)(2,1)} %refs_0_.4), channel_id=1, source_target_pairs={{0,8},{4,12},{8,0},{12,4},{1,9},{5,13},{9,1},{13,5},{2,10},{6,14},... | collective-permute-start | bytes 1179656 | tf_op jit(solution)/shard_map/ppermute | solution.py:216
  3.8 13.3 %collective-permute-start = (bf16[48,4096]{1,0:T(8,128)(2,1)}, bf16[48,4096]{1,0:T(8,128)(2,1)S(1)}, u32[]{:S(2)}, u32[]{:S(2)}) collective-permute-start(bf16[48,4096]{1,0:T(8,128)(2,1)} %refs_0_.4), channel_id=1, source_target_pairs={{0,1},{1,2},{2,3},{3,0},{4,5},{5,6},{6,7},{7,4},{8,9},{9,10},{10,1... | collective-permute-start | bytes 1179656 | tf_op jit(solution)/shard_map/ppermute | solution.py:211
  17.0 11.9 %collective-permute-start.4 = (bf16[48,4096]{1,0:T(8,128)(2,1)}, bf16[48,4096]{1,0:T(8,128)(2,1)S(1)}, u32[]{:S(2)}, u32[]{:S(2)}) collective-permute-start(bf16[48,4096]{1,0:T(8,128)(2,1)} %refs_0_.4), channel_id=1, source_target_pairs={{0,3},{1,0},{2,1},{3,2},{4,7},{5,4},{6,5},{7,6},{8,11},{9,8},{10,9... | collective-permute-start | bytes 1179656 | tf_op jit(solution)/shard_map/ppermute | solution.py:211
  18.8 10.2 %collective-permute-start.6 = (bf16[48,4096]{1,0:T(8,128)(2,1)S(1)}, bf16[48,4096]{1,0:T(8,128)(2,1)S(1)}, u32[]{:S(2)}, u32[]{:S(2)}) collective-permute-start(bf16[48,4096]{1,0:T(8,128)(2,1)S(1)} %collective-permute-done.refs_0_.refs_4_), channel_id=1, source_target_pairs={{0,4},{4,0},{8,12},{12,8},{1,5},{5,1},{9,13},{13,9},{2,6},{6,2},{1... | collective-permute-start | bytes 1179656 | tf_op jit(solution)/shard_map/ppermute | solution.py:216
  19.0 11.3 %collective-permute-start.5 = (bf16[48,4096]{1,0:T(8,128)(2,1)S(1)}, bf16[48,4096]{1,0:T(8,128)(2,1)S(1)}, u32[]{:S(2)}, u32[]{:S(2)}) collective-permute-start(bf16[48,4096]{1,0:T(8,128)(2,1)S(1)} %collective-permute-done.refs_0_.refs_4_), channel_id=1, source_target_pairs={{0,8},{4,12},{8,0},{12,4},{1,9},{5,13},{9,1},{13,5},{2,10},{6,14},... | collective-permute-start | bytes 1179656 | tf_op jit(solution)/shard_map/ppermute | solution.py:216
  30.3 5.8 %collective-permute-start.11 = (bf16[48,4096]{1,0:T(8,128)(2,1)S(1)}, bf16[48,4096]{1,0:T(8,128)(2,1)S(1)}, u32[]{:S(2)}, u32[]{:S(2)}) collective-permute-start(bf16[48,4096]{1,0:T(8,128)(2,1)S(1)} %collective-permute-done.5.refs_1_.refs_5_), channel_id=1, source_target_pairs={{0,4},{4,0},{8,12},{12,8},{1,5},{5,1},{9,13},{13,9},{2,6},{6,2},{1... | collective-permute-start | bytes 1179656 | tf_op jit(solution)/shard_map/ppermute | solution.py:216
  30.3 21.5 %collective-permute-start.12 = (bf16[384,896]{1,0:T(8,128)(2,1)}, bf16[384,896]{1,0:T(8,128)(2,1)S(1)}, u32[]{:S(2)}, u32[]{:S(2)}) collective-permute-start(bf16[384,896]{1,0:T(8,128)(2,1)} %shard_map.92), channel_id=1, source_target_pairs={{0,16},{16,0},{1,17},{17,1},{2,18},{18,2},{3,19},{19,3},{4,20},{20... | collective-permute-start | bytes 2064392 | tf_op jit(solution)/shard_map/ppermute | solution.py:222
  31.8 14.5 %collective-permute-start.3 = (bf16[48,4096]{1,0:T(8,128)(2,1)S(1)}, bf16[48,4096]{1,0:T(8,128)(2,1)S(1)}, u32[]{:S(2)}, u32[]{:S(2)}) collective-permute-start(bf16[48,4096]{1,0:T(8,128)(2,1)S(1)} %collective-permute-done.refs_0_.refs_4_), channel_id=1, source_target_pairs={{0,1},{1,2},{2,3},{3,0},{4,5},{5,6},{6,7},{7,4},{8,9},{9,10},{10,1... | collective-permute-start | bytes 1179656 | tf_op jit(solution)/shard_map/ppermute | solution.py:211
  32.1 14.2 %collective-permute-start.10 = (bf16[48,4096]{1,0:T(8,128)(2,1)S(1)}, bf16[48,4096]{1,0:T(8,128)(2,1)S(1)}, u32[]{:S(2)}, u32[]{:S(2)}) collective-permute-start(bf16[48,4096]{1,0:T(8,128)(2,1)S(1)} %copy-done.17), channel_id=1, source_target_pairs={{0,8},{4,12},{8,0},{12,4},{1,9},{5,13},{9,1},{13,5},{2,10},{6,14},... | collective-permute-start | bytes 1179656 | tf_op jit(solution)/shard_map/ppermute | solution.py:216
  32.6 19.1 %collective-permute-start.8 = (bf16[48,4096]{1,0:T(8,128)(2,1)S(1)}, bf16[48,4096]{1,0:T(8,128)(2,1)S(1)}, u32[]{:S(2)}, u32[]{:S(2)}) collective-permute-start(bf16[48,4096]{1,0:T(8,128)(2,1)S(1)} %copy-done.17), channel_id=1, source_target_pairs={{0,3},{1,0},{2,1},{3,2},{4,7},{5,4},{6,5},{7,6},{8,11},{9,8},{10,9... | collective-permute-start | bytes 1179656 | tf_op jit(solution)/shard_map/ppermute | solution.py:211
  36.1 15.6 %collective-permute-start.9 = (bf16[48,4096]{1,0:T(8,128)(2,1)S(1)}, bf16[48,4096]{1,0:T(8,128)(2,1)S(1)}, u32[]{:S(2)}, u32[]{:S(2)}) collective-permute-start(bf16[48,4096]{1,0:T(8,128)(2,1)S(1)} %collective-permute-done.4.refs_0_.refs_8_), channel_id=1, source_target_pairs={{0,8},{4,12},{8,0},{12,4},{1,9},{5,13},{9,1},{13,5},{2,10},{6,14},... | collective-permute-start | bytes 1179656 | tf_op jit(solution)/shard_map/ppermute | solution.py:216
  51.8 3.5 %collective-permute-start.16 = (bf16[48,4096]{1,0:T(8,128)(2,1)S(1)}, bf16[48,4096]{1,0:T(8,128)(2,1)S(1)}, u32[]{:S(2)}, u32[]{:S(2)}) collective-permute-start(bf16[48,4096]{1,0:T(8,128)(2,1)S(1)} %collective-permute-done.4.refs_0_.refs_8_), channel_id=1, source_target_pairs={{0,4},{4,0},{8,12},{12,8},{1,5},{5,1},{9,13},{13,9},{2,6},{6,2},{1... | collective-permute-start | bytes 1179656 | tf_op jit(solution)/shard_map/ppermute | solution.py:216
  51.9 22.4 %collective-permute-start.18 = (bf16[384,896]{1,0:T(8,128)(2,1)}, bf16[384,896]{1,0:T(8,128)(2,1)S(1)}, u32[]{:S(2)}, u32[]{:S(2)}) collective-permute-start(bf16[384,896]{1,0:T(8,128)(2,1)} %shard_map.93), channel_id=1, source_target_pairs={{0,16},{16,0},{1,17},{17,1},{2,18},{18,2},{3,19},{19,3},{4,20},{20... | collective-permute-start | bytes 2064392 | tf_op jit(solution)/shard_map/ppermute | solution.py:222
  52.5 4.3 %collective-permute-start.17 = (bf16[48,4096]{1,0:T(8,128)(2,1)S(1)}, bf16[48,4096]{1,0:T(8,128)(2,1)S(1)}, u32[]{:S(2)}, u32[]{:S(2)}) collective-permute-start(bf16[48,4096]{1,0:T(8,128)(2,1)S(1)} %collective-permute-done.9.refs_1_.refs_9_), channel_id=1, source_target_pairs={{0,4},{4,0},{8,12},{12,8},{1,5},{5,1},{9,13},{13,9},{2,6},{6,2},{1... | collective-permute-start | bytes 1179656 | tf_op jit(solution)/shard_map/ppermute | solution.py:216
  52.6 20.8 %collective-permute-start.13 = (bf16[48,4096]{1,0:T(8,128)(2,1)S(1)}, bf16[48,4096]{1,0:T(8,128)(2,1)}, u32[]{:S(2)}, u32[]{:S(2)}) collective-permute-start(bf16[48,4096]{1,0:T(8,128)(2,1)S(1)} %copy-done.17), channel_id=1, source_target_pairs={{0,2},{1,3},{2,0},{3,1},{4,6},{5,7},{6,4},{7,5},{8,10},{9,11},{10,... | collective-permute-start | bytes 1179656 | tf_op jit(solution)/shard_map/ppermute | solution.py:211
  54.7 18.7 %collective-permute-start.14 = (bf16[48,4096]{1,0:T(8,128)(2,1)S(1)}, bf16[48,4096]{1,0:T(8,128)(2,1)S(1)}, u32[]{:S(2)}, u32[]{:S(2)}) collective-permute-start(bf16[48,4096]{1,0:T(8,128)(2,1)S(1)} %collective-permute-done.3.refs_0_.refs_12_), channel_id=1, source_target_pairs={{0,8},{4,12},{8,0},{12,4},{1,9},{5,13},{9,1},{13,5},{2,10},{6,14},... | collective-permute-start | bytes 1179656 | tf_op jit(solution)/shard_map/ppermute | solution.py:216
  55.2 19.0 %collective-permute-start.15 = (bf16[48,4096]{1,0:T(8,128)(2,1)S(1)}, bf16[48,4096]{1,0:T(8,128)(2,1)S(1)}, u32[]{:S(2)}, u32[]{:S(2)}) collective-permute-start(bf16[48,4096]{1,0:T(8,128)(2,1)S(1)} %collective-permute-done.8.refs_0_.refs_8_), channel_id=1, source_target_pairs={{0,8},{4,12},{8,0},{12,4},{1,9},{5,13},{9,1},{13,5},{2,10},{6,14},... | collective-permute-start | bytes 1179656 | tf_op jit(solution)/shard_map/ppermute | solution.py:216
  74.3 3.8 %collective-permute-start.21 = (bf16[48,4096]{1,0:T(8,128)(2,1)S(1)}, bf16[48,4096]{1,0:T(8,128)(2,1)S(1)}, u32[]{:S(2)}, u32[]{:S(2)}) collective-permute-start(bf16[48,4096]{1,0:T(8,128)(2,1)S(1)} %collective-permute-done.3.refs_0_.refs_12_), channel_id=1, source_target_pairs={{0,4},{4,0},{8,12},{12,8},{1,5},{5,1},{9,13},{13,9},{2,6},{6,2},{1... | collective-permute-start | bytes 1179656 | tf_op jit(solution)/shard_map/ppermute | solution.py:216
  74.3 4.0 %collective-permute-start.22 = (bf16[48,4096]{1,0:T(8,128)(2,1)S(1)}, bf16[48,4096]{1,0:T(8,128)(2,1)S(1)}, u32[]{:S(2)}, u32[]{:S(2)}) collective-permute-start(bf16[48,4096]{1,0:T(8,128)(2,1)S(1)} %collective-permute-done.14.refs_1_.refs_13_), channel_id=1, source_target_pairs={{0,4},{4,0},{8,12},{12,8},{1,5},{5,1},{9,13},{13,9},{2,6},{6,2},{1... | collective-permute-start | bytes 1179656 | tf_op jit(solution)/shard_map/ppermute | solution.py:216
  74.8 17.6 %collective-permute-start.25 = (bf16[384,896]{1,0:T(8,128)(2,1)}, bf16[384,896]{1,0:T(8,128)(2,1)S(1)}, u32[]{:S(2)}, u32[]{:S(2)}) collective-permute-start(bf16[384,896]{1,0:T(8,128)(2,1)} %shard_map.94), channel_id=1, source_target_pairs={{0,16},{16,0},{1,17},{17,1},{2,18},{18,2},{3,19},{19,3},{4,20},{20... | collective-permute-start | bytes 2064392 | tf_op jit(solution)/shard_map/ppermute | solution.py:222
  76.3 11.5 %collective-permute-start.23 = (bf16[48,4096]{1,0:T(8,128)(2,1)S(1)}, bf16[48,4096]{1,0:T(8,128)(2,1)}, u32[]{:S(2)}, u32[]{:S(2)}) collective-permute-start(bf16[48,4096]{1,0:T(8,128)(2,1)S(1)} %copy-done.17), channel_id=1, source_target_pairs={{0,4},{4,0},{8,12},{12,8},{1,5},{5,1},{9,13},{13,9},{2,6},{6,2},{1... | collective-permute-start | bytes 1179656 | tf_op jit(solution)/shard_map/ppermute | solution.py:216
  76.3 13.4 %collective-permute-start.19 = (bf16[48,4096]{1,0:T(8,128)(2,1)S(1)}, bf16[48,4096]{1,0:T(8,128)(2,1)}, u32[]{:S(2)}, u32[]{:S(2)}) collective-permute-start(bf16[48,4096]{1,0:T(8,128)(2,1)S(1)} %copy-done.17), channel_id=1, source_target_pairs={{0,1},{1,2},{2,3},{3,0},{4,5},{5,6},{6,7},{7,4},{8,9},{9,10},{10,1... | collective-permute-start | bytes 1179656 | tf_op jit(solution)/shard_map/ppermute | solution.py:211
  78.0 11.7 %collective-permute-start.24 = (bf16[48,4096]{1,0:T(8,128)(2,1)S(1)}, bf16[48,4096]{1,0:T(8,128)(2,1)}, u32[]{:S(2)}, u32[]{:S(2)}) collective-permute-start(bf16[48,4096]{1,0:T(8,128)(2,1)S(1)} %collective-permute-done.10.refs_1_), channel_id=1, source_target_pairs={{0,4},{4,0},{8,12},{12,8},{1,5},{5,1},{9,13},{13,9},{2,6},{6,2},{1... | collective-permute-start | bytes 1179656 | tf_op jit(solution)/shard_map/ppermute | solution.py:216
  78.3 11.6 %collective-permute-start.20 = (bf16[48,4096]{1,0:T(8,128)(2,1)}, bf16[48,4096]{1,0:T(8,128)(2,1)}, u32[]{:S(2)}, u32[]{:S(2)}) collective-permute-start(bf16[48,4096]{1,0:T(8,128)(2,1)} %collective-permute-done.13.refs_4_.refs_12_), channel_id=1, source_target_pairs={{0,8},{4,12},{8,0},{12,4},{1,9},{5,13},{9,1},{13,5},{2,10},{6,14},... | collective-permute-start | bytes 1179656 | tf_op jit(solution)/shard_map/ppermute | solution.py:216
  92.5 4.0 %collective-permute-start.27 = (bf16[48,4096]{1,0:T(8,128)(2,1)S(1)}, bf16[48,4096]{1,0:T(8,128)(2,1)S(1)}, u32[]{:S(2)}, u32[]{:S(2)}) collective-permute-start(bf16[48,4096]{1,0:T(8,128)(2,1)S(1)} %collective-permute-done.8.refs_0_.refs_8_), channel_id=1, source_target_pairs={{0,4},{4,0},{8,12},{12,8},{1,5},{5,1},{9,13},{13,9},{2,6},{6,2},{1... | collective-permute-start | bytes 1179656 | tf_op jit(solution)/shard_map/ppermute | solution.py:216
  92.5 4.7 %collective-permute-start.28 = (bf16[48,4096]{1,0:T(8,128)(2,1)S(1)}, bf16[48,4096]{1,0:T(8,128)(2,1)S(1)}, u32[]{:S(2)}, u32[]{:S(2)}) collective-permute-start(bf16[48,4096]{1,0:T(8,128)(2,1)S(1)} %copy-done.36), channel_id=1, source_target_pairs={{0,4},{4,0},{8,12},{12,8},{1,5},{5,1},{9,13},{13,9},{2,6},{6,2},{1... | collective-permute-start | bytes 1179656 | tf_op jit(solution)/shard_map/ppermute | solution.py:216
  93.0 4.2 %collective-permute-start.29 = (bf16[48,4096]{1,0:T(8,128)(2,1)}, bf16[48,4096]{1,0:T(8,128)(2,1)S(1)}, u32[]{:S(2)}, u32[]{:S(2)}) collective-permute-start(bf16[48,4096]{1,0:T(8,128)(2,1)} %collective-permute-done.13.refs_4_.refs_12_), channel_id=1, source_target_pairs={{0,4},{4,0},{8,12},{12,8},{1,5},{5,1},{9,13},{13,9},{2,6},{6,2},{1... | collective-permute-start | bytes 1179656 | tf_op jit(solution)/shard_map/ppermute | solution.py:216
  93.1 4.2 %collective-permute-start.30 = (bf16[48,4096]{1,0:T(8,128)(2,1)}, bf16[48,4096]{1,0:T(8,128)(2,1)S(1)}, u32[]{:S(2)}, u32[]{:S(2)}) collective-permute-start(bf16[48,4096]{1,0:T(8,128)(2,1)} %collective-permute-done.20.refs_5_.refs_13_), channel_id=1, source_target_pairs={{0,4},{4,0},{8,12},{12,8},{1,5},{5,1},{9,13},{13,9},{2,6},{6,2},{1... | collective-permute-start | bytes 1179656 | tf_op jit(solution)/shard_map/ppermute | solution.py:216
  93.7 17.5 %collective-permute-start.31 = (bf16[384,896]{1,0:T(8,128)(2,1)S(1)}, bf16[384,896]{1,0:T(8,128)(2,1)S(1)}, u32[]{:S(2)}, u32[]{:S(2)}) collective-permute-start(bf16[384,896]{1,0:T(8,128)(2,1)S(1)} %copy-done.3), channel_id=1, source_target_pairs={{0,16},{16,0},{1,17},{17,1},{2,18},{18,2},{3,19},{19,3},{4,20},{20... | collective-permute-start | bytes 2064392 | tf_op jit(solution)/shard_map/ppermute | solution.py:222
  96.5 14.3 %collective-permute-start.26 = (bf16[48,4096]{1,0:T(8,128)(2,1)}, bf16[48,4096]{1,0:T(8,128)(2,1)}, u32[]{:S(2)}, u32[]{:S(2)}) collective-permute-start(bf16[48,4096]{1,0:T(8,128)(2,1)} %collective-permute-done.19.refs_4_), channel_id=1, source_target_pairs={{0,8},{4,12},{8,0},{12,4},{1,9},{5,13},{9,1},{13,5},{2,10},{6,14},... | collective-permute-start | bytes 1179656 | tf_op jit(solution)/shard_map/ppermute | solution.py:216
  112.0 3.1 %collective-permute-start.32 = (bf16[96,4096]{1,0:T(8,128)(2,1)}, bf16[96,4096]{1,0:T(8,128)(2,1)S(1)}, u32[]{:S(2)}, u32[]{:S(2)}) collective-permute-start(bf16[96,4096]{1,0:T(8,128)(2,1)} %get-tuple-element.147), channel_id=1, source_target_pairs={{0,4},{4,0},{8,12},{12,8},{1,5},{5,1},{9,13},{13,9},{2,6},{6,2},{1... | collective-permute-start | bytes 2359304 | tf_op jit(solution)/shard_map/ppermute | solution.py:216
  113.1 18.2 %collective-permute-start.37 = (bf16[384,896]{1,0:T(8,128)(2,1)}, bf16[384,896]{1,0:T(8,128)(2,1)}, u32[]{:S(2)}, u32[]{:S(2)}) collective-permute-start(bf16[384,896]{1,0:T(8,128)(2,1)} %get-tuple-element.153), channel_id=1, source_target_pairs={{0,16},{16,0},{1,17},{17,1},{2,18},{18,2},{3,19},{19,3},{4,20},{20... | collective-permute-start | bytes 2064392 | tf_op jit(solution)/shard_map/ppermute | solution.py:222
  115.3 19.7 %collective-permute-start.33 = (bf16[96,4096]{1,0:T(8,128)(2,1)S(1)}, bf16[96,4096]{1,0:T(8,128)(2,1)S(1)}, u32[]{:S(2)}, u32[]{:S(2)}) collective-permute-start(bf16[96,4096]{1,0:T(8,128)(2,1)S(1)} %add_convert_fusion.3), channel_id=1, source_target_pairs={{0,8},{4,12},{8,0},{12,4},{1,9},{5,13},{9,1},{13,5},{2,10},{6,14},... | collective-permute-start | bytes 2359304 | tf_op jit(solution)/shard_map/ppermute | solution.py:216
  116.1 15.2 %collective-permute-start.34 = (bf16[96,4096]{1,0:T(8,128)(2,1)}, bf16[96,4096]{1,0:T(8,128)(2,1)}, u32[]{:S(2)}, u32[]{:S(2)}) collective-permute-start(bf16[96,4096]{1,0:T(8,128)(2,1)} %get-tuple-element.149), channel_id=1, source_target_pairs={{0,4},{4,0},{8,12},{12,8},{1,5},{5,1},{9,13},{13,9},{2,6},{6,2},{1... | collective-permute-start | bytes 2359304 | tf_op jit(solution)/shard_map/ppermute | solution.py:216
  135.0 18.2 %collective-permute-start.41 = (bf16[384,896]{1,0:T(8,128)(2,1)}, bf16[384,896]{1,0:T(8,128)(2,1)}, u32[]{:S(2)}, u32[]{:S(2)}) collective-permute-start(bf16[384,896]{1,0:T(8,128)(2,1)} %get-tuple-element.173), channel_id=1, source_target_pairs={{0,16},{16,0},{1,17},{17,1},{2,18},{18,2},{3,19},{19,3},{4,20},{20... | collective-permute-start | bytes 2064392 | tf_op jit(solution)/shard_map/ppermute | solution.py:222
  137.7 19.6 %collective-permute-start.39 = (bf16[96,4096]{1,0:T(8,128)(2,1)S(1)}, bf16[96,4096]{1,0:T(8,128)(2,1)S(1)}, u32[]{:S(2)}, u32[]{:S(2)}) collective-permute-start(bf16[96,4096]{1,0:T(8,128)(2,1)S(1)} %add_convert_fusion.2), channel_id=1, source_target_pairs={{0,8},{4,12},{8,0},{12,4},{1,9},{5,13},{9,1},{13,5},{2,10},{6,14},... | collective-permute-start | bytes 2359304 | tf_op jit(solution)/shard_map/ppermute | solution.py:216
  138.5 14.7 %collective-permute-start.40 = (bf16[96,4096]{1,0:T(8,128)(2,1)}, bf16[96,4096]{1,0:T(8,128)(2,1)S(1)}, u32[]{:S(2)}, u32[]{:S(2)}) collective-permute-start(bf16[96,4096]{1,0:T(8,128)(2,1)} %get-tuple-element.167), channel_id=1, source_target_pairs={{0,4},{4,0},{8,12},{12,8},{1,5},{5,1},{9,13},{13,9},{2,6},{6,2},{1... | collective-permute-start | bytes 2359304 | tf_op jit(solution)/shard_map/ppermute | solution.py:216
  157.4 3.0 %collective-permute-start.42 = (bf16[96,4096]{1,0:T(8,128)(2,1)}, bf16[96,4096]{1,0:T(8,128)(2,1)S(1)}, u32[]{:S(2)}, u32[]{:S(2)}) collective-permute-start(bf16[96,4096]{1,0:T(8,128)(2,1)} %get-tuple-element.175), channel_id=1, source_target_pairs={{0,4},{4,0},{8,12},{12,8},{1,5},{5,1},{9,13},{13,9},{2,6},{6,2},{1... | collective-permute-start | bytes 2359304 | tf_op jit(solution)/shard_map/ppermute | solution.py:216
  160.6 22.3 %collective-permute-start.43 = (bf16[96,4096]{1,0:T(8,128)(2,1)S(1)}, bf16[96,4096]{1,0:T(8,128)(2,1)S(1)}, u32[]{:S(2)}, u32[]{:S(2)}) collective-permute-start(bf16[96,4096]{1,0:T(8,128)(2,1)S(1)} %add_convert_fusion.1), channel_id=1, source_target_pairs={{0,8},{4,12},{8,0},{12,4},{1,9},{5,13},{9,1},{13,5},{2,10},{6,14},... | collective-permute-start | bytes 2359304 | tf_op jit(solution)/shard_map/ppermute | solution.py:216
  161.4 21.5 %collective-permute-start.44 = (bf16[96,4096]{1,0:T(8,128)(2,1)}, bf16[96,4096]{1,0:T(8,128)(2,1)S(1)}, u32[]{:S(2)}, u32[]{:S(2)}) collective-permute-start(bf16[96,4096]{1,0:T(8,128)(2,1)} %get-tuple-element.177), channel_id=1, source_target_pairs={{0,4},{4,0},{8,12},{12,8},{1,5},{5,1},{9,13},{13,9},{2,6},{6,2},{1... | collective-permute-start | bytes 2359304 | tf_op jit(solution)/shard_map/ppermute | solution.py:216
  161.9 14.5 %collective-permute-start.46 = (bf16[48,4096]{1,0:T(8,128)(2,1)S(1)}, bf16[48,4096]{1,0:T(8,128)(2,1)S(1)}, u32[]{:S(2)}, u32[]{:S(2)}) collective-permute-start(bf16[48,4096]{1,0:T(8,128)(2,1)S(1)} %get-tuple-element.221), channel_id=1, source_target_pairs={{0,3},{1,0},{2,1},{3,2},{4,7},{5,4},{6,5},{7,6},{8,11},{9,8},{10,9... | collective-permute-start | bytes 1179656 | tf_op jit(solution)/shard_map/ppermute | solution.py:211
  164.1 18.8 %collective-permute-start.45 = (bf16[48,4096]{1,0:T(8,128)(2,1)S(1)}, bf16[48,4096]{1,0:T(8,128)(2,1)S(1)}, u32[]{:S(2)}, u32[]{:S(2)}) collective-permute-start(bf16[48,4096]{1,0:T(8,128)(2,1)S(1)} %get-tuple-element.222), channel_id=1, source_target_pairs={{0,1},{1,2},{2,3},{3,0},{4,5},{5,6},{6,7},{7,4},{8,9},{9,10},{10,1... | collective-permute-start | bytes 1179656 | tf_op jit(solution)/shard_map/ppermute | solution.py:211
  185.6 22.5 %collective-permute-start.48 = (bf16[96,4096]{1,0:T(8,128)(2,1)S(1)}, bf16[96,4096]{1,0:T(8,128)(2,1)S(1)}, u32[]{:S(2)}, u32[]{:S(2)}) collective-permute-start(bf16[96,4096]{1,0:T(8,128)(2,1)S(1)} %add_convert_fusion), channel_id=1, source_target_pairs={{0,8},{4,12},{8,0},{12,4},{1,9},{5,13},{9,1},{13,5},{2,10},{6,14},... | collective-permute-start | bytes 2359304 | tf_op jit(solution)/shard_map/ppermute | solution.py:216
  186.5 21.6 %collective-permute-start.49 = (bf16[96,4096]{1,0:T(8,128)(2,1)}, bf16[96,4096]{1,0:T(8,128)(2,1)S(1)}, u32[]{:S(2)}, u32[]{:S(2)}) collective-permute-start(bf16[96,4096]{1,0:T(8,128)(2,1)} %get-tuple-element.192), channel_id=1, source_target_pairs={{0,4},{4,0},{8,12},{12,8},{1,5},{5,1},{9,13},{13,9},{2,6},{6,2},{1... | collective-permute-start | bytes 2359304 | tf_op jit(solution)/shard_map/ppermute | solution.py:216
  186.8 16.9 %collective-permute-start.51 = (bf16[48,4096]{1,0:T(8,128)(2,1)S(1)}, bf16[48,4096]{1,0:T(8,128)(2,1)S(1)}, u32[]{:S(2)}, u32[]{:S(2)}) collective-permute-start(bf16[48,4096]{1,0:T(8,128)(2,1)S(1)} %get-tuple-element.219), channel_id=1, source_target_pairs={{0,1},{1,2},{2,3},{3,0},{4,5},{5,6},{6,7},{7,4},{8,9},{9,10},{10,1... | collective-permute-start | bytes 1179656 | tf_op jit(solution)/shard_map/ppermute | solution.py:211
  188.4 19.7 %collective-permute-start.50 = (bf16[48,4096]{1,0:T(8,128)(2,1)S(1)}, bf16[48,4096]{1,0:T(8,128)(2,1)S(1)}, u32[]{:S(2)}, u32[]{:S(2)}) collective-permute-start(bf16[48,4096]{1,0:T(8,128)(2,1)S(1)} %get-tuple-element.220), channel_id=1, source_target_pairs={{0,3},{1,0},{2,1},{3,2},{4,7},{5,4},{6,5},{7,6},{8,11},{9,8},{10,9... | collective-permute-start | bytes 1179656 | tf_op jit(solution)/shard_map/ppermute | solution.py:211
  208.3 19.9 %collective-permute-start.52 = (bf16[96,4096]{1,0:T(8,128)(2,1)S(1)}, bf16[96,4096]{1,0:T(8,128)(2,1)S(1)}, u32[]{:S(2)}, u32[]{:S(2)}) collective-permute-start(bf16[96,4096]{1,0:T(8,128)(2,1)S(1)} %pad_maximum_fusion), channel_id=1, source_target_pairs={{0,3},{1,0},{2,1},{3,2},{4,7},{5,4},{6,5},{7,6},{8,11},{9,8},{10,9... | collective-permute-start | bytes 2359304 | tf_op jit(solution)/shard_map/ppermute | solution.py:211
  (47 other events, 423.7 us)

commit v9 on v8

--- a/solution.py
+++ b/solution.py
@@ -252,18 +252,20 @@
 
 def chip_part(parts):
     near, far, other_near, other_far = parts
-    sent = add(far, swap(other_far, CORE))
-    return sent, [near, swap(after(other_near, sent), CORE)]
-
-
-def owner_parts(kept, moved):
-    size = moved.shape[0] // 2
-    rows = [slice(0, size), slice(size, 2 * size)]
-    return [sum(wide(block[at]) for block in (*kept, moved)) for at in rows]
+    moved = swap(other_far, CORE)
+    size = far.shape[0] // 2
+    sent = [add(x, y) for x, y in ((far[:size], moved[:size]), (far[size:], moved[size:]))]
+    return sent, [near, swap(after(other_near, *sent), CORE)]
+
+
+def block_sum(kept, block, *moved):
+    size = kept[0].shape[0] // 2
+    rows = slice(block * size, (block + 1) * size)
+    return sum(wide(x) for x in (*(x[rows] for x in kept), *moved))
 
 
 def quad(near, far, moved):
-    return [near, far, *moved]
+    return [*near, *far, *moved]
 
 
 def body(tokens, gate_weight, up_weight, down_weight, cotangent):
@@ -274,74 +276,82 @@
         total = row_sum(partial, moved)
         return total[:half], total[half:]
 
-    near1, far0, core0 = sync(shift(tokens, 1), swap(tokens, CHIP), swap(tokens, CORE))
-
-    near3, far1 = shift(after(tokens, near1), 3), swap(near1, CHIP)
-    core1, far_core0 = other_cores([near1, far0])
-    token0 = quad(tokens, far0, [core0, far_core0])
+    far0, near1, cot_core0 = sync(
+        swap(tokens, CHIP), shift(tokens, 1), swap(cotangent, CORE)
+    )
+    head = 16 * (cotangent.shape[0] // 48)
+    cot_head, cot_tail = cotangent[:head], cotangent[head:]
+
+    far1, near3 = swap(near1, CHIP), shift(after(tokens, near1), 3)
+    head3 = shift(after(cot_head, near1), 3)
+    core0, far_core0, core1 = other_cores([after(tokens, near1), far0, near1])
+    token0 = quad([tokens], [far0], [core0, far_core0])
     pair0 = contract(token0, pair)
-    near3, far1, core1, pair0 = sync(near3, far1, core1, pair0)
+    far1, near3, head3, core1, pair0 = sync(far1, near3, head3, core1, pair0)
 
     pair0_moved = row_moves(pair0)
-    cot = after(cotangent, pair0)
-    near2, cot_near3 = shift(near1, 1), shift(cot, 3)
-    far3, cot_far0 = swap(near3, CHIP), swap(cot, CHIP)
-    token1 = quad(near1, far1, [core1, swap(far1, CORE)])
+    near2, tail3 = (shift(after(x, pair0), k) for x, k in ((near1, 1), (cot_tail, 3)))
+    far3, far_head0 = swap(near3, CHIP), swap(after(cot_head, pair0), CHIP)
+    token1 = quad([near1], [far1], [core1, swap(far1, CORE)])
     pair1 = contract(token1, pair)
-    near2, cot_near3, far3, cot_far0, pair1, *pair0_moved = sync(
-        near2, cot_near3, far3, cot_far0, pair1, *pair0_moved
+    near2, tail3, far3, far_head0, pair1, *pair0_moved = sync(
+        near2, tail3, far3, far_head0, pair1, *pair0_moved
     )
 
     gate0, up0 = pair_sums(pair0, pair0_moved)
     hidden0 = hidden_of(gate0, up0)
     pair1_moved = row_moves(pair1)
-    cot = after(cotangent, pair1)
-    cot_near2 = shift(cot, 2)
-    far2, cot_far3 = swap(near2, CHIP), swap(cot_near3, CHIP)
-    token3 = quad(near3, far3, other_cores([after(near3, pair1), far3]))
+    cot_near3 = jnp.concatenate([head3, tail3], axis=0)
+    cot_near2 = shift(cot_near3, 3)
+    far2, far_head3 = swap(near2, CHIP), swap(after(head3, pair1), CHIP)
+    token3 = quad([near3], [far3], other_cores([after(near3, pair1), far3]))
     pair3 = contract(token3, pair)
-    cot_near2, far2, cot_far3, pair3, *pair1_moved = sync(
-        cot_near2, far2, cot_far3, pair3, *pair1_moved
+    cot_near2, far2, far_head3, pair3, *pair1_moved = sync(
+        cot_near2, far2, far_head3, pair3, *pair1_moved
     )
 
     gate1, up1 = pair_sums(pair1, pair1_moved)
     hidden1 = hidden_of(gate1, up1)
     pair3_moved = row_moves(pair3)
     cot = after(cotangent, pair3)
-    cot_near1, cot_far2 = shift(cot, 1), swap(cot_near2, CHIP)
-    token2 = quad(near2, far2, other_cores([after(near2, pair3), far2]))
+    cot_near1 = shift(cot, 1)
+    cot_far2, far_tail3 = swap(cot_near2, CHIP), swap(after(tail3, pair3), CHIP)
+    token2 = quad([near2], [far2], other_cores([after(near2, pair3), far2]))
     pair2 = contract(token2, pair)
-    cot0 = quad(cot, cot_far0, other_cores([cot, after(cot_far0, pair3)]))
-    cot_near1, cot_far2, pair2, cot0[2], cot0[3], *pair3_moved = sync(
-        cot_near1, cot_far2, pair2, cot0[2], cot0[3], *pair3_moved
+    far_head0_core = swap(after(far_head0, pair3), CORE)
+    cot_near1, cot_far2, far_tail3, pair2, far_head0_core, *pair3_moved = sync(
+        cot_near1, cot_far2, far_tail3, pair2, far_head0_core, *pair3_moved
     )
 
     gate3, up3 = pair_sums(pair3, pair3_moved)
     hidden3 = hidden_of(gate3, up3)
     pair2_moved = row_moves(pair2)
-    cot_far1 = swap(cot_near1, CHIP)
-    cot3 = quad(cot_near3, cot_far3, other_cores(after(x, pair2) for x in (cot_near3, cot_far3)))
-    cot2 = quad(cot_near2, cot_far2, other_cores(after(x, pair2) for x in (cot_near2, cot_far2)))
+    cot_far1, far_tail0 = swap(cot_near1, CHIP), swap(after(cot_tail, pair2), CHIP)
+    cot_far3 = [after(far_head3, pair2), far_tail3]
+    cot3 = quad([cot_near3], cot_far3, other_cores([after(cot_near3, pair2), *cot_far3]))
+    cot2 = quad([cot_near2], [cot_far2], other_cores([after(cot_near2, pair2), cot_far2]))
     products = down_products(cot3 + cot2, [hidden0, hidden1], down_weight)
-    cot_far1, grad_b, *rest = sync(cot_far1, *products, *pair2_moved)
+    cot_far1, far_tail0, grad_b, *rest = sync(cot_far1, far_tail0, *products, *pair2_moved)
     parts, pair2_moved = rest[:4], rest[4:]
 
     gate2, up2 = pair_sums(pair2, pair2_moved)
     hidden2 = hidden_of(gate2, up2)
     grad_b_moved = row_moves(grad_b)
-    sent, mixed_a = chip_part(parts)
+    (mixed_sent0, sent), mixed_a = chip_part(parts)
     mixed_a_moved = swap(sent, CHIP)
-    cot1 = quad(cot_near1, cot_far1, other_cores([after(cot_near1, grad_b), cot_far1]))
+    cot_far0 = [far_head0, far_tail0]
+    cot0 = quad([cotangent], cot_far0, [cot_core0, far_head0_core, swap(far_tail0, CORE)])
+    cot1 = quad([cot_near1], [cot_far1], other_cores([after(cot_near1, grad_b), cot_far1]))
     products = down_products(cot0 + cot1, [hidden3, hidden2], down_weight)
-    mixed_a_moved, mixed_a[1], grad_a, *rest = sync(
-        mixed_a_moved, mixed_a[1], *products, *grad_b_moved
+    mixed_a_moved, mixed_a[1], mixed_sent0, grad_a, *rest = sync(
+        mixed_a_moved, mixed_a[1], mixed_sent0, *products, *grad_b_moved
     )
     parts, grad_b_moved = rest[:4], rest[4:]
 
-    grad_b = row_sum(grad_b, grad_b_moved)
     grad_a_moved = row_moves(grad_a)
     sent, mixed_b = chip_part(parts)
-    mixed_b_moved = swap(sent, CHIP)
+    mixed_b_moved = swap(jnp.concatenate(sent, axis=0), CHIP)
+    grad_b = row_sum(grad_b, grad_b_moved)
     half = grad_b.shape[0] // 2
     grads3 = grads_of(gate3, up3, grad_b[:half])
     grads2 = grads_of(gate2, up2, grad_b[half:])
@@ -350,41 +360,47 @@
     parts, grad_a_moved = rest[:4], rest[4:]
 
     sent, token_grad_b = chip_part(parts)
-    token_b_moved = swap(sent, CHIP)
+    token_b_moved = swap(jnp.concatenate(sent, axis=0), CHIP)
     grad_a = row_sum(grad_a, grad_a_moved)
-    mixed_b = owner_parts(mixed_b, after(mixed_b_moved, sent))
-    part3, part2 = shift(narrow(mixed_b[0]), 1), shift(narrow(mixed_b[1]), -1)
+    size = tokens.shape[0]
+    moved = after(mixed_b_moved, *sent)
+    mixed_part3 = shift(narrow(block_sum(mixed_b, 0, moved[:size])), 1)
+    mixed_part2 = shift(narrow(block_sum(mixed_b, 1, moved[size:])), -1)
     grads0 = grads_of(gate0, up0, grad_a[:half])
     grads1 = grads_of(gate1, up1, grad_a[half:])
     parts = expand([[x, y] for x, y in zip(grads0, grads1)], pair)
     token_b_moved, token_grad_b[1], mixed_part3, mixed_part2, *parts = sync(
-        token_b_moved, token_grad_b[1], part3, part2, *parts
-    )
-
-    sent, token_grad_a = chip_part(parts)
+        token_b_moved, token_grad_b[1], mixed_part3, mixed_part2, *parts
+    )
+
+    (token_sent0, sent), token_grad_a = chip_part(parts)
     token_a_moved = swap(sent, CHIP)
-    mixed_a = owner_parts(mixed_a, mixed_a_moved)
-    token_grad_b = owner_parts(token_grad_b, after(token_b_moved, sent))
-    part3, part2 = shift(narrow(token_grad_b[0]), 1), shift(narrow(token_grad_b[1]), -1)
+    moved = after(token_b_moved, sent)
+    part3 = shift(narrow(block_sum(token_grad_b, 0, moved[:size])), 1)
+    part2 = shift(narrow(block_sum(token_grad_b, 1, moved[size:])), -1)
     down_total = tall_grad(
         cot0 + cot1 + cot3 + cot2, [after(hidden0, sent), hidden1, hidden3, hidden2]
     )
-    token_a_moved, token_grad_a[1], part2, part3, down_total = sync(
-        token_a_moved, token_grad_a[1], part2, part3, down_total
-    )
-
-    token_grad_a = owner_parts(token_grad_a, token_a_moved)
-    back = [mixed_a[1] + wide(mixed_part2), token_grad_a[1] + wide(part2)]
+    token_a_moved, token_grad_a[1], token_sent0, part2, part3, down_total = sync(
+        token_a_moved, token_grad_a[1], token_sent0, part2, part3, down_total
+    )
+
+    moved0 = swap(jnp.concatenate([mixed_sent0, token_sent0], axis=0), CHIP)
+    back = [
+        block_sum(mixed_a, 1, mixed_a_moved, mixed_part2),
+        block_sum(token_grad_a, 1, token_a_moved, part2),
+    ]
     back = shift(narrow(jnp.concatenate(back, axis=0)), -1)
     gate_total, up_total = wide_grads(
         [after(tokens, down_total), *token0[1:], *token1, *token3, *token2],
         [grads0[0], grads1[0], grads3[0], grads2[0]],
         [grads0[1], grads1[1], grads3[1], grads2[1]],
     )
-    back, mixed_part3, part3, gate_total = sync(back, mixed_part3, part3, gate_total)
-    size = back.shape[0] // 2
-    mixed = mixed_a[0] + wide(mixed_part3) + wide(back[:size])
-    token_grad = token_grad_a[0] + wide(part3) + wide(back[size:])
+    moved0, back, mixed_part3, part3, gate_total = sync(
+        moved0, back, mixed_part3, part3, gate_total
+    )
+    mixed = block_sum(mixed_a, 0, moved0[:size], mixed_part3, back[:size])
+    token_grad = block_sum(token_grad_a, 0, moved0[size:], part3, back[size:])
     return (mixed, token_grad, gate_total, up_total, down_total)
 
 

time: 233 us -> 232 us (level)
  waiting for transfers between devices: 53.1 us -> 42.8 us
  starting transfers between devices: 41.9 us -> 46.9 us
  local copies, waits for them, and re-layouts: 4.25 us -> 7.68 us
    ppermute x11 -> x12, waiting for transfers between devices: 28.7 us -> 23.3 us  [shift(): return lax.ppermute(block, 'depth', [(i, (i + step) % n) for i in range(n)])]
    ppermute x36 -> x41, starting transfers between devices: 15.3 us -> 20.4 us  [swap(): return lax.ppermute(block, 'col', [(i, i ^ bit) for i in range(n)])]
    ppermute x36 -> x41, waiting for transfers between devices: 20.2 us -> 16.7 us  [swap(): return lax.ppermute(block, 'col', [(i, i ^ bit) for i in range(n)])]
    slice x0 -> x2, local copies, waits for them, and re-layouts: none -> 2.59 us  [body(): cot_head, cot_tail = (cotangent[:head], cotangent[head:])]
    ppermute x11 -> x12, starting transfers between devices: 19.1 us -> 20.6 us  [shift(): return lax.ppermute(block, 'depth', [(i, (i + step) % n) for i in range(n)])]
    unnamed x84 -> x115, local copies, waits for them, and re-layouts: 4.25 us -> 5.08 us
  transfers between devices with their start and end apart: 53 -> 59, of which waited for: 18 -> 17; matrix products, arithmetic and copies ran while one was open for 5% -> 7% of each run, Pallas kernels for 50% -> 50%
where the time goes in v9:
time: 232 us; the launch traced here: 230 us
  Pallas kernels  116 us (50%)
  starting transfers between devices  46.9 us (20%)
  waiting for transfers between devices  42.8 us (18%)
  other arithmetic  15.1 us (7%)
  local copies, waits for them, and re-layouts  7.68 us (3%)
    pallas_call x4, Pallas kernels, contract(): pl.pallas_call(functools.partial(contract_kernel, len(pieces), len(weight...  34.7 us
    pallas_call x2, Pallas kernels, down_products(): pl.pallas_call(functools.partial(down_kernel, len(pieces)), grid=(width /...  25.3 us
    pallas_call x2, Pallas kernels, expand(): pl.pallas_call(functools.partial(expand_kernel, len(lefts)), grid=(width...  24.7 us
    ppermute x12, waiting for transfers between devices, shift(): return lax.ppermute(block, 'depth', [(i, (i + step) % n) for i in range(n)])  23.3 us
    ppermute x12, starting transfers between devices, shift(): return lax.ppermute(block, 'depth', [(i, (i + step) % n) for i in range(n)])  20.6 us
    ppermute x41, starting transfers between devices, swap(): return lax.ppermute(block, 'col', [(i, i ^ bit) for i in range(n)])  20.4 us
    pallas_call x1, Pallas kernels, wide_grads(): pl.pallas_call(functools.partial(wide_grad_kernel, len(pieces)), grid=(wi...  17.8 us
    ppermute x41, waiting for transfers between devices, swap(): return lax.ppermute(block, 'col', [(i, i ^ bit) for i in range(n)])  16.7 us
  transfers between devices with their start and end apart: 59, of which 17 were waited for; matrix products, arithmetic and copies ran while one was open for 7% of the time, Pallas kernels for 50%

profile of v9, /device:TPU:0, one launch (start us, length us, event | category | flops | bytes accessed | tf_op | source)
XLA Modules:
  0.0 229.5 jit_solution(15398583648023960390)
XLA Ops:
  0.6 3.1 %collective-permute-start.1 = (bf16[48,4096]{1,0:T(8,128)(2,1)}, bf16[48,4096]{1,0:T(8,128)(2,1)S(1)}, u32[]{:S(2)}, u32[]{:S(2)}) collective-permute-start(bf16[48,4096]{1,0:T(8,128)(2,1)} %refs_0_.6), channel_id=1, source_target_pairs={{0,1},{1,2},{2,3},{3,0},{4,5},{5,6},{6,7},{7,4},{8,9},{9,10},{10,1... | collective-permute-start | bytes 1179656 | tf_op jit(solution)/shard_map/ppermute | solution.py:211
  3.7 1.5 collective-permute-start
  5.2 9.8 %collective-permute-done.1.refs_0_.refs_4_ = bf16[48,4096]{1,0:T(8,128)(2,1)S(1)} collective-permute-done((bf16[48,4096]{1,0:T(8,128)(2,1)}, bf16[48,4096]{1,0:T(8,128)(2,1)S(1)}, u32[]{:S(2)}, u32[]{:S(2)}) %collective-permute-start.1) | collective-permute-done | bytes 393248 | tf_op jit(solution)/shard_map/ppermute | solution.py:211
  15.6 1.7 collective-permute-start.4
  17.4 1.5 collective-permute-start.3
  19.8 1.7 slice.163
  21.5 1.7 collective-permute-start.5
  24.0 8.7 %shard_map.92 = bf16[384,896]{1,0:T(8,128)(2,1)} custom-call(bf16[48,4096]{1,0:T(8,128)(2,1)} %refs_0_.6, bf16[48,4096]{1,0:T(8,128)(2,1)} %copy-done.23, bf16[48,4096]{1,0:T(8,128)(2,1)} %copy-done.24, bf16[48,4096]{1,0:T(8,128)(2,1)} %copy-done.25, bf16[4096,896]{1,0:T(8,128)(2,1)} %refs_4_.11, bf16[4096,896]{1,0:T(8,128)(2,1)} %refs_5_.11), custom_call_target="tpu_custom_call" | custom-call | flops 2818572288 | bytes 16252928 | tf_op jit(solution)/shard_map/pallas_call | solution.py:64
  32.7 1.6 collective-permute-start.14
  35.2 1.6 collective-permute-start.12
  36.8 3.5 %collective-permute-start.10 = (bf16[32,4096]{1,0:T(8,128)(2,1)}, bf16[32,4096]{1,0:T(8,128)(2,1)S(1)}, u32[]{:S(2)}, u32[]{:S(2)}) collective-permute-start(bf16[32,4096]{1,0:T(8,128)(2,1)} %slice.163), channel_id=1, source_target_pairs={{0,3},{1,0},{2,1},{3,2},{4,7},{5,4},{6,5},{7,6},{8,11},{9,8},{10,9... | collective-permute-start | bytes 786440 | tf_op jit(solution)/shard_map/ppermute | solution.py:211
  40.2 8.7 %shard_map.93 = bf16[384,896]{1,0:T(8,128)(2,1)} custom-call(bf16[48,4096]{1,0:T(8,128)(2,1)} %copy-done.22, bf16[48,4096]{1,0:T(8,128)(2,1)} %copy-done.28, bf16[48,4096]{1,0:T(8,128)(2,1)} %copy-done.27, bf16[48,4096]{1,0:T(8,128)(2,1)} %copy-done.30, bf16[4096,896]{1,0:T(8,128)(2,1)} %refs_4_.11, bf16[4096,896]{1,0:T(8,128)(2,1)} %refs_5_.11), custom_call_target="tpu_custom_call" | custom-call | flops 2818572288 | bytes 16252928 | tf_op jit(solution)/shard_map/pallas_call | solution.py:64
  49.0 3.4 %collective-permute-done.10 = bf16[32,4096]{1,0:T(8,128)(2,1)S(1)} collective-permute-done((bf16[32,4096]{1,0:T(8,128)(2,1)}, bf16[32,4096]{1,0:T(8,128)(2,1)S(1)}, u32[]{:S(2)}, u32[]{:S(2)}) %collective-permute-start.10) | collective-permute-done | bytes 262176 | tf_op jit(solution)/shard_map/ppermute | solution.py:211
  54.8 1.3 collective-permute-start.17
  56.8 8.7 %shard_map.94 = bf16[384,896]{1,0:T(8,128)(2,1)} custom-call(bf16[48,4096]{1,0:T(8,128)(2,1)} %copy-done.26, bf16[48,4096]{1,0:T(8,128)(2,1)} %copy-done.31, bf16[48,4096]{1,0:T(8,128)(2,1)} %copy-done.32, bf16[48,4096]{1,0:T(8,128)(2,1)} %copy-done.33, bf16[4096,896]{1,0:T(8,128)(2,1)} %refs_4_.11, bf16[4096,896]{1,0:T(8,128)(2,1)} %refs_5_.11), custom_call_target="tpu_custom_call" | custom-call | flops 2818572288 | bytes 16252928 | tf_op jit(solution)/shard_map/pallas_call | solution.py:64
  65.5 2.1 collective-permute-done.17.refs_1_.refs_11_
  67.6 2.5 %collective-permute-done.20 = bf16[384,896]{1,0:T(8,128)(2,1)S(1)} collective-permute-done((bf16[384,896]{1,0:T(8,128)(2,1)}, bf16[384,896]{1,0:T(8,128)(2,1)S(1)}, u32[]{:S(2)}, u32[]{:S(2)}) %collective-permute-start.20) | collective-permute-done | bytes 688160 | tf_op jit(solution)/shard_map/ppermute | solution.py:222
  72.9 1.2 collective-permute-start.23
  74.1 8.7 %shard_map.95 = bf16[384,896]{1,0:T(8,128)(2,1)} custom-call(bf16[48,4096]{1,0:T(8,128)(2,1)} %copy-done.29, bf16[48,4096]{1,0:T(8,128)(2,1)} %copy-done.34, bf16[48,4096]{1,0:T(8,128)(2,1)} %copy-done.35, bf16[48,4096]{1,0:T(8,128)(2,1)} %copy-done.36, bf16[4096,896]{1,0:T(8,128)(2,1)} %refs_4_.11, bf16[4096,896]{1,0:T(8,128)(2,1)} %refs_5_.11), custom_call_target="tpu_custom_call" | custom-call | flops 2818572288 | bytes 16252928 | tf_op jit(solution)/shard_map/pallas_call | solution.py:64
  82.8 5.3 %collective-permute-done.23.refs_2_.refs_12_ = bf16[32,4096]{1,0:T(8,128)(2,1)S(1)} collective-permute-done((bf16[32,4096]{1,0:T(8,128)(2,1)S(1)}, bf16[32,4096]{1,0:T(8,128)(2,1)S(1)}, u32[]{:S(2)}, u32[]{:S(2)}) %collective-permute-start.23) | collective-permute-done | bytes 262176 | tf_op jit(solution)/shard_map/ppermute | solution.py:216
  89.3 1.6 collective-permute-start.35
  90.9 1.2 multiply_convert_fusion.10
  93.0 1.5 collective-permute-start.28
  95.4 12.7 %shard_map.96 = (bf16[384,896]{1,0:T(8,128)(2,1)}, bf16[96,4096]{1,0:T(8,128)(2,1)}, bf16[96,4096]{1,0:T(8,128)(2,1)}, bf16[96,4096]{1,0:T(8,128)(2,1)}, bf16[96,4096]{1,0:T(8,128)(2,1)}) custom-call(bf16[48,4096]{1,0:T(8,128)(2,1)} %copy-done.15, bf16[16,4096]{1,0:T(8,128)(2,1)} %copy-done.53, bf16[32,4096]{1,0:T(8,128)(2,1)} %copy-done.45, ...), custom_call_target="tpu_custom_call" | custom-call | flops 5637144576 | bytes 14319616 | tf_op jit(solution)/shard_map/pallas_call | solution.py:138
  108.1 1.6 collective-permute-done.28.refs_7_
  116.7 12.6 %shard_map.97 = (bf16[384,896]{1,0:T(8,128)(2,1)}, bf16[96,4096]{1,0:T(8,128)(2,1)}, bf16[96,4096]{1,0:T(8,128)(2,1)}, bf16[96,4096]{1,0:T(8,128)(2,1)}, bf16[96,4096]{1,0:T(8,128)(2,1)}) custom-call(bf16[48,4096]{1,0:T(8,128)(2,1)} %refs_0_.5, bf16[16,4096]{1,0:T(8,128)(2,1)} %copy-done.52, bf16[32,4096]{1,0:T(8,128)(2,1)} %copy-done.47, ...), custom_call_target="tpu_custom_call" | custom-call | flops 5637144576 | bytes 14319616 | tf_op jit(solution)/shard_map/pallas_call | solution.py:138
  129.9 1.1 collective-permute-start.46
  131.0 1.2 convert_add_fusion.1
  132.6 1.4 collective-permute-start.44
  134.1 1.7 multiply_convert_fusion.4
  135.8 12.3 %shard_map.98 = (bf16[96,4096]{1,0:T(8,128)(2,1)}, bf16[96,4096]{1,0:T(8,128)(2,1)}, bf16[96,4096]{1,0:T(8,128)(2,1)}, bf16[96,4096]{1,0:T(8,128)(2,1)}) custom-call(bf16[192,896]{1,0:T(8,128)(2,1)} %get-tuple-element.253.refs_0_.refs_18_, bf16[192,896]{1,0:T(8,128)(2,1)} %get-tuple-element.234.refs_1_.refs_19_, ...), custom_call_target="tpu_custom_call" | custom-call | flops 5637144576 | bytes 19202048 | tf_op jit(solution)/shard_map/pallas_call | solution.py:101
  148.1 4.2 %collective-permute-done.44 = bf16[96,4096]{1,0:T(8,128)(2,1)S(1)} collective-permute-done((bf16[96,4096]{1,0:T(8,128)(2,1)S(1)}, bf16[96,4096]{1,0:T(8,128)(2,1)S(1)}, u32[]{:S(2)}, u32[]{:S(2)}) %collective-permute-start.44) | collective-permute-done | bytes 786464 | tf_op jit(solution)/shard_map/ppermute | solution.py:216
  152.3 1.2 convert_add_fusion
  153.6 1.7 multiply_convert_fusion
  155.6 1.5 collective-permute-start.48
  157.3 1.4 add_convert_fusion.6
  158.7 3.3 %collective-permute-start.51 = (bf16[48,4096]{1,0:T(8,128)(2,1)S(1)}, bf16[48,4096]{1,0:T(8,128)(2,1)S(1)}, u32[]{:S(2)}, u32[]{:S(2)}) collective-permute-start(bf16[48,4096]{1,0:T(8,128)(2,1)S(1)} %get-tuple-element.239), channel_id=1, source_target_pairs={{0,3},{1,0},{2,1},{3,2},{4,7},{5,4},{6,5},{7,6},{8,11},{9,8},{10,9... | collective-permute-start | bytes 1179656 | tf_op jit(solution)/shard_map/ppermute | solution.py:211
  162.0 12.4 %shard_map.99 = (bf16[96,4096]{1,0:T(8,128)(2,1)}, bf16[96,4096]{1,0:T(8,128)(2,1)}, bf16[96,4096]{1,0:T(8,128)(2,1)}, bf16[96,4096]{1,0:T(8,128)(2,1)}) custom-call(bf16[192,896]{1,0:T(8,128)(2,1)} %get-tuple-element.251.refs_0_.refs_16_, bf16[192,896]{1,0:T(8,128)(2,1)} %get-tuple-element.230.refs_1_.refs_17_, ...), custom_call_target="tpu_custom_call" | custom-call | flops 5637144576 | bytes 19202048 | tf_op jit(solution)/shard_map/pallas_call | solution.py:101
  174.4 5.6 %collective-permute-done.50 = bf16[48,4096]{1,0:T(8,128)(2,1)S(1)} collective-permute-done((bf16[48,4096]{1,0:T(8,128)(2,1)S(1)}, bf16[48,4096]{1,0:T(8,128)(2,1)S(1)}, u32[]{:S(2)}, u32[]{:S(2)}) %collective-permute-start.50) | collective-permute-done | bytes 393248 | tf_op jit(solution)/shard_map/ppermute | solution.py:211
  181.0 2.3 collective-permute-done.52
  184.8 1.8 collective-permute-start.56
  186.7 2.0 collective-permute-start.55
  188.7 13.2 %shard_map.100 = f32[896,4096]{1,0:T(8,128)} custom-call(bf16[48,4096]{1,0:T(8,128)(2,1)} %refs_0_.5, bf16[16,4096]{1,0:T(8,128)(2,1)} %copy-done.52, bf16[32,4096]{1,0:T(8,128)(2,1)} %copy-done.47, bf16[48,4096]{1,0:T(8,128)(2,1)} %collective-permute-done.2.refs_3_, bf16[16,4096]{1,0:T(8,128)(2,1)} %copy-done.55, bf16[32,4096]{1,0:T(8,128)(2,1)} %copy-done.49, ...), custom_call_target="tpu_custom_call" | custom-call | flops 5637144576 | bytes 22347776 | tf_op jit(solution)/shard_map/pallas_call | solution.py:197
  201.9 4.4 %collective-permute-done.55 = bf16[48,4096]{1,0:T(8,128)(2,1)S(1)} collective-permute-done((bf16[48,4096]{1,0:T(8,128)(2,1)S(1)}, bf16[48,4096]{1,0:T(8,128)(2,1)S(1)}, u32[]{:S(2)}, u32[]{:S(2)}) %collective-permute-start.55) | collective-permute-done | bytes 393248 | tf_op jit(solution)/shard_map/ppermute | solution.py:211
  206.6 2.1 collective-permute-start.58
  208.9 1.1 collective-permute-start.57
  210.0 17.8 %shard_map.101 = (f32[4096,896]{1,0:T(8,128)}, f32[4096,896]{1,0:T(8,128)}) custom-call(bf16[48,4096]{1,0:T(8,128)(2,1)} %refs_0_.6, bf16[48,4096]{1,0:T(8,128)(2,1)} %copy-done.23, bf16[48,4096]{1,0:T(8,128)(2,1)} %copy-done.24, bf16[48,4096]{1,0:T(8,128)(2,1)} %copy-done.25, bf16[48,4096]{1,0:T(8,128)(2,1)} %copy-done.22, bf16[48,4096]{1,0:T(8,128)(2,1)} %copy-done.28, ...), custom_call_target="tpu_custom_call" | custom-call | flops 11274289152 | bytes 38404096 | tf_op jit(solution)/shard_map/pallas_call | solution.py:173
  227.8 1.7 convert_add_fusion.6
  (222 shorter events, 23.4 us)
Async XLA Ops:
  0.6 14.4 %collective-permute-start.1 = (bf16[48,4096]{1,0:T(8,128)(2,1)}, bf16[48,4096]{1,0:T(8,128)(2,1)S(1)}, u32[]{:S(2)}, u32[]{:S(2)}) collective-permute-start(bf16[48,4096]{1,0:T(8,128)(2,1)} %refs_0_.6), channel_id=1, source_target_pairs={{0,1},{1,2},{2,3},{3,0},{4,5},{5,6},{6,7},{7,4},{8,9},{9,10},{10,1... | collective-permute-start | bytes 1179656 | tf_op jit(solution)/shard_map/ppermute | solution.py:211
  3.7 11.4 %collective-permute-start = (bf16[48,4096]{1,0:T(8,128)(2,1)}, bf16[48,4096]{1,0:T(8,128)(2,1)S(1)}, u32[]{:S(2)}, u32[]{:S(2)}) collective-permute-start(bf16[48,4096]{1,0:T(8,128)(2,1)} %refs_0_.6), channel_id=1, source_target_pairs={{0,8},{4,12},{8,0},{12,4},{1,9},{5,13},{9,1},{13,5},{2,10},{6,14},... | collective-permute-start | bytes 1179656 | tf_op jit(solution)/shard_map/ppermute | solution.py:216
  5.2 9.8 %collective-permute-start.2 = (bf16[48,4096]{1,0:T(8,128)(2,1)}, bf16[48,4096]{1,0:T(8,128)(2,1)}, u32[]{:S(2)}, u32[]{:S(2)}) collective-permute-start(bf16[48,4096]{1,0:T(8,128)(2,1)} %refs_0_.5), channel_id=1, source_target_pairs={{0,4},{4,0},{8,12},{12,8},{1,5},{5,1},{9,13},{13,9},{2,6},{6,2},{1... | collective-permute-start | bytes 1179656 | tf_op jit(solution)/shard_map/ppermute | solution.py:216
  15.1 6.4 %collective-permute-start.7 = (bf16[48,4096]{1,0:T(8,128)(2,1)}, bf16[48,4096]{1,0:T(8,128)(2,1)S(1)}, u32[]{:S(2)}, u32[]{:S(2)}) collective-permute-start(bf16[48,4096]{1,0:T(8,128)(2,1)} %refs_0_.6), channel_id=1, source_target_pairs={{0,4},{4,0},{8,12},{12,8},{1,5},{5,1},{9,13},{13,9},{2,6},{6,2},{1... | collective-permute-start | bytes 1179656 | tf_op jit(solution)/shard_map/ppermute | solution.py:216
  15.2 8.0 %collective-permute-start.8 = (bf16[48,4096]{1,0:T(8,128)(2,1)S(1)}, bf16[48,4096]{1,0:T(8,128)(2,1)S(1)}, u32[]{:S(2)}, u32[]{:S(2)}) collective-permute-start(bf16[48,4096]{1,0:T(8,128)(2,1)S(1)} %collective-permute-done.refs_1_), channel_id=1, source_target_pairs={{0,4},{4,0},{8,12},{12,8},{1,5},{5,1},{9,13},{13,9},{2,6},{6,2},{1... | collective-permute-start | bytes 1179656 | tf_op jit(solution)/shard_map/ppermute | solution.py:216
  15.6 17.0 %collective-permute-start.4 = (bf16[48,4096]{1,0:T(8,128)(2,1)}, bf16[48,4096]{1,0:T(8,128)(2,1)S(1)}, u32[]{:S(2)}, u32[]{:S(2)}) collective-permute-start(bf16[48,4096]{1,0:T(8,128)(2,1)} %refs_0_.6), channel_id=1, source_target_pairs={{0,3},{1,0},{2,1},{3,2},{4,7},{5,4},{6,5},{7,6},{8,11},{9,8},{10,9... | collective-permute-start | bytes 1179656 | tf_op jit(solution)/shard_map/ppermute | solution.py:211
  17.4 15.3 %collective-permute-start.6 = (bf16[48,4096]{1,0:T(8,128)(2,1)S(1)}, bf16[48,4096]{1,0:T(8,128)(2,1)S(1)}, u32[]{:S(2)}, u32[]{:S(2)}) collective-permute-start(bf16[48,4096]{1,0:T(8,128)(2,1)S(1)} %collective-permute-done.1.refs_0_.refs_4_), channel_id=1, source_target_pairs={{0,4},{4,0},{8,12},{12,8},{1,5},{5,1},{9,13},{13,9},{2,6},{6,2},{1... | collective-permute-start | bytes 1179656 | tf_op jit(solution)/shard_map/ppermute | solution.py:216
  17.4 15.3 %collective-permute-start.3 = (bf16[48,4096]{1,0:T(8,128)(2,1)S(1)}, bf16[48,4096]{1,0:T(8,128)(2,1)S(1)}, u32[]{:S(2)}, u32[]{:S(2)}) collective-permute-start(bf16[48,4096]{1,0:T(8,128)(2,1)S(1)} %collective-permute-done.1.refs_0_.refs_4_), channel_id=1, source_target_pairs={{0,8},{4,12},{8,0},{12,4},{1,9},{5,13},{9,1},{13,5},{2,10},{6,14},... | collective-permute-start | bytes 1179656 | tf_op jit(solution)/shard_map/ppermute | solution.py:216
  21.5 11.1 %collective-permute-start.5 = (bf16[16,4096]{1,0:T(8,128)(2,1)S(1)}, bf16[16,4096]{1,0:T(8,128)(2,1)S(1)}, u32[]{:S(2)}, u32[]{:S(2)}) collective-permute-start(bf16[16,4096]{1,0:T(8,128)(2,1)S(1)} %slice.162), channel_id=1, source_target_pairs={{0,3},{1,0},{2,1},{3,2},{4,7},{5,4},{6,5},{7,6},{8,11},{9,8},{10,9... | collective-permute-start | bytes 393224 | tf_op jit(solution)/shard_map/ppermute | solution.py:211
  32.7 19.7 %collective-permute-start.14 = (bf16[384,896]{1,0:T(8,128)(2,1)}, bf16[384,896]{1,0:T(8,128)(2,1)S(1)}, u32[]{:S(2)}, u32[]{:S(2)}) collective-permute-start(bf16[384,896]{1,0:T(8,128)(2,1)} %shard_map.92), channel_id=1, source_target_pairs={{0,16},{16,0},{1,17},{17,1},{2,18},{18,2},{3,19},{19,3},{4,20},{20... | collective-permute-start | bytes 2064392 | tf_op jit(solution)/shard_map/ppermute | solution.py:222
  34.3 18.1 %collective-permute-start.9 = (bf16[48,4096]{1,0:T(8,128)(2,1)S(1)}, bf16[48,4096]{1,0:T(8,128)(2,1)S(1)}, u32[]{:S(2)}, u32[]{:S(2)}) collective-permute-start(bf16[48,4096]{1,0:T(8,128)(2,1)S(1)} %collective-permute-done.1.refs_0_.refs_4_), channel_id=1, source_target_pairs={{0,1},{1,2},{2,3},{3,0},{4,5},{5,6},{6,7},{7,4},{8,9},{9,10},{10,1... | collective-permute-start | bytes 1179656 | tf_op jit(solution)/shard_map/ppermute | solution.py:211
  34.6 17.8 %collective-permute-start.11 = (bf16[48,4096]{1,0:T(8,128)(2,1)S(1)}, bf16[48,4096]{1,0:T(8,128)(2,1)S(1)}, u32[]{:S(2)}, u32[]{:S(2)}) collective-permute-start(bf16[48,4096]{1,0:T(8,128)(2,1)S(1)} %collective-permute-done.4.refs_0_.refs_8_), channel_id=1, source_target_pairs={{0,8},{4,12},{8,0},{12,4},{1,9},{5,13},{9,1},{13,5},{2,10},{6,14},... | collective-permute-start | bytes 1179656 | tf_op jit(solution)/shard_map/ppermute | solution.py:216
  35.2 13.8 %collective-permute-start.12 = (bf16[16,4096]{1,0:T(8,128)(2,1)S(1)}, bf16[16,4096]{1,0:T(8,128)(2,1)S(1)}, u32[]{:S(2)}, u32[]{:S(2)}) collective-permute-start(bf16[16,4096]{1,0:T(8,128)(2,1)S(1)} %slice.162), channel_id=1, source_target_pairs={{0,8},{4,12},{8,0},{12,4},{1,9},{5,13},{9,1},{13,5},{2,10},{6,14},... | collective-permute-start | bytes 393224 | tf_op jit(solution)/shard_map/ppermute | solution.py:216
  36.8 15.7 %collective-permute-start.10 = (bf16[32,4096]{1,0:T(8,128)(2,1)}, bf16[32,4096]{1,0:T(8,128)(2,1)S(1)}, u32[]{:S(2)}, u32[]{:S(2)}) collective-permute-start(bf16[32,4096]{1,0:T(8,128)(2,1)} %slice.163), channel_id=1, source_target_pairs={{0,3},{1,0},{2,1},{3,2},{4,7},{5,4},{6,5},{7,6},{8,11},{9,8},{10,9... | collective-permute-start | bytes 786440 | tf_op jit(solution)/shard_map/ppermute | solution.py:211
  52.4 17.6 %collective-permute-start.20 = (bf16[384,896]{1,0:T(8,128)(2,1)}, bf16[384,896]{1,0:T(8,128)(2,1)S(1)}, u32[]{:S(2)}, u32[]{:S(2)}) collective-permute-start(bf16[384,896]{1,0:T(8,128)(2,1)} %shard_map.93), channel_id=1, source_target_pairs={{0,16},{16,0},{1,17},{17,1},{2,18},{18,2},{3,19},{19,3},{4,20},{20... | collective-permute-start | bytes 2064392 | tf_op jit(solution)/shard_map/ppermute | solution.py:222
  53.6 14.0 %collective-permute-start.15 = (bf16[48,4096]{1,0:T(8,128)(2,1)S(1)}, bf16[48,4096]{1,0:T(8,128)(2,1)S(1)}, u32[]{:S(2)}, u32[]{:S(2)}) collective-permute-start(bf16[48,4096]{1,0:T(8,128)(2,1)S(1)} %constant_dynamic-update-slice_fusion.refs_0_.refs_10_), channel_id=1, source_target_pairs={{0,3},{1,0},{2,1},{3,2},{4,7},{5,4},{6,5},{7,6},{8,11},{9,8},{10,9... | collective-permute-start | bytes 1179656 | tf_op jit(solution)/shard_map/ppermute | solution.py:211
  54.0 13.6 %collective-permute-start.16 = (bf16[48,4096]{1,0:T(8,128)(2,1)S(1)}, bf16[48,4096]{1,0:T(8,128)(2,1)S(1)}, u32[]{:S(2)}, u32[]{:S(2)}) collective-permute-start(bf16[48,4096]{1,0:T(8,128)(2,1)S(1)} %collective-permute-done.9.refs_0_.refs_12_), channel_id=1, source_target_pairs={{0,8},{4,12},{8,0},{12,4},{1,9},{5,13},{9,1},{13,5},{2,10},{6,14},... | collective-permute-start | bytes 1179656 | tf_op jit(solution)/shard_map/ppermute | solution.py:216
  54.8 12.8 %collective-permute-start.17 = (bf16[16,4096]{1,0:T(8,128)(2,1)S(1)}, bf16[16,4096]{1,0:T(8,128)(2,1)S(1)}, u32[]{:S(2)}, u32[]{:S(2)}) collective-permute-start(bf16[16,4096]{1,0:T(8,128)(2,1)S(1)} %collective-permute-done.5), channel_id=1, source_target_pairs={{0,8},{4,12},{8,0},{12,4},{1,9},{5,13},{9,1},{13,5},{2,10},{6,14},... | collective-permute-start | bytes 393224 | tf_op jit(solution)/shard_map/ppermute | solution.py:216
  70.1 18.0 %collective-permute-start.27 = (bf16[384,896]{1,0:T(8,128)(2,1)}, bf16[384,896]{1,0:T(8,128)(2,1)S(1)}, u32[]{:S(2)}, u32[]{:S(2)}) collective-permute-start(bf16[384,896]{1,0:T(8,128)(2,1)} %shard_map.94), channel_id=1, source_target_pairs={{0,16},{16,0},{1,17},{17,1},{2,18},{18,2},{3,19},{19,3},{4,20},{20... | collective-permute-start | bytes 2064392 | tf_op jit(solution)/shard_map/ppermute | solution.py:222
  71.1 16.9 %collective-permute-start.21 = (bf16[48,4096]{1,0:T(8,128)(2,1)S(1)}, bf16[48,4096]{1,0:T(8,128)(2,1)}, u32[]{:S(2)}, u32[]{:S(2)}) collective-permute-start(bf16[48,4096]{1,0:T(8,128)(2,1)S(1)} %copy-done.4), channel_id=1, source_target_pairs={{0,1},{1,2},{2,3},{3,0},{4,5},{5,6},{6,7},{7,4},{8,9},{9,10},{10,1... | collective-permute-start | bytes 1179656 | tf_op jit(solution)/shard_map/ppermute | solution.py:211
  71.7 16.4 %collective-permute-start.22 = (bf16[48,4096]{1,0:T(8,128)(2,1)S(1)}, bf16[48,4096]{1,0:T(8,128)(2,1)}, u32[]{:S(2)}, u32[]{:S(2)}) collective-permute-start(bf16[48,4096]{1,0:T(8,128)(2,1)S(1)} %collective-permute-done.15.refs_6_.refs_16_), channel_id=1, source_target_pairs={{0,8},{4,12},{8,0},{12,4},{1,9},{5,13},{9,1},{13,5},{2,10},{6,14},... | collective-permute-start | bytes 1179656 | tf_op jit(solution)/shard_map/ppermute | solution.py:216
  72.4 10.3 %collective-permute-start.26 = (bf16[16,4096]{1,0:T(8,128)(2,1)S(1)}, bf16[16,4096]{1,0:T(8,128)(2,1)S(1)}, u32[]{:S(2)}, u32[]{:S(2)}) collective-permute-start(bf16[16,4096]{1,0:T(8,128)(2,1)S(1)} %collective-permute-done.12.refs_1_), channel_id=1, source_target_pairs={{0,4},{4,0},{8,12},{12,8},{1,5},{5,1},{9,13},{13,9},{2,6},{6,2},{1... | collective-permute-start | bytes 393224 | tf_op jit(solution)/shard_map/ppermute | solution.py:216
  72.9 15.1 %collective-permute-start.23 = (bf16[32,4096]{1,0:T(8,128)(2,1)S(1)}, bf16[32,4096]{1,0:T(8,128)(2,1)S(1)}, u32[]{:S(2)}, u32[]{:S(2)}) collective-permute-start(bf16[32,4096]{1,0:T(8,128)(2,1)S(1)} %copy-done.51), channel_id=1, source_target_pairs={{0,8},{4,12},{8,0},{12,4},{1,9},{5,13},{9,1},{13,5},{2,10},{6,14},... | collective-permute-start | bytes 786440 | tf_op jit(solution)/shard_map/ppermute | solution.py:216
  88.1 4.9 %collective-permute-start.30 = (bf16[48,4096]{1,0:T(8,128)(2,1)S(1)}, bf16[48,4096]{1,0:T(8,128)(2,1)S(1)}, u32[]{:S(2)}, u32[]{:S(2)}) collective-permute-start(bf16[48,4096]{1,0:T(8,128)(2,1)S(1)} %constant_dynamic-update-slice_fusion.refs_0_.refs_10_), channel_id=1, source_target_pairs={{0,4},{4,0},{8,12},{12,8},{1,5},{5,1},{9,13},{13,9},{2,6},{6,2},{1... | collective-permute-start | bytes 1179656 | tf_op jit(solution)/shard_map/ppermute | solution.py:216
  88.6 5.9 %collective-permute-start.33 = (bf16[48,4096]{1,0:T(8,128)(2,1)S(1)}, bf16[48,4096]{1,0:T(8,128)(2,1)S(1)}, u32[]{:S(2)}, u32[]{:S(2)}) collective-permute-start(bf16[48,4096]{1,0:T(8,128)(2,1)S(1)} %collective-permute-done.15.refs_6_.refs_16_), channel_id=1, source_target_pairs={{0,4},{4,0},{8,12},{12,8},{1,5},{5,1},{9,13},{13,9},{2,6},{6,2},{1... | collective-permute-start | bytes 1179656 | tf_op jit(solution)/shard_map/ppermute | solution.py:216
  88.7 5.8 %collective-permute-start.34 = (bf16[48,4096]{1,0:T(8,128)(2,1)}, bf16[48,4096]{1,0:T(8,128)(2,1)S(1)}, u32[]{:S(2)}, u32[]{:S(2)}) collective-permute-start(bf16[48,4096]{1,0:T(8,128)(2,1)} %collective-permute-done.22.refs_7_.refs_17_), channel_id=1, source_target_pairs={{0,4},{4,0},{8,12},{12,8},{1,5},{5,1},{9,13},{13,9},{2,6},{6,2},{1... | collective-permute-start | bytes 1179656 | tf_op jit(solution)/shard_map/ppermute | solution.py:216
  89.3 20.4 %collective-permute-start.35 = (bf16[384,896]{1,0:T(8,128)(2,1)S(1)}, bf16[384,896]{1,0:T(8,128)(2,1)S(1)}, u32[]{:S(2)}, u32[]{:S(2)}) collective-permute-start(bf16[384,896]{1,0:T(8,128)(2,1)S(1)} %copy-done.2), channel_id=1, source_target_pairs={{0,16},{16,0},{1,17},{17,1},{2,18},{18,2},{3,19},{19,3},{4,20},{20... | collective-permute-start | bytes 2064392 | tf_op jit(solution)/shard_map/ppermute | solution.py:222
  92.5 15.6 %collective-permute-start.29 = (bf16[32,4096]{1,0:T(8,128)(2,1)}, bf16[32,4096]{1,0:T(8,128)(2,1)S(1)}, u32[]{:S(2)}, u32[]{:S(2)}) collective-permute-start(bf16[32,4096]{1,0:T(8,128)(2,1)} %slice.163), channel_id=1, source_target_pairs={{0,8},{4,12},{8,0},{12,4},{1,9},{5,13},{9,1},{13,5},{2,10},{6,14},... | collective-permute-start | bytes 786440 | tf_op jit(solution)/shard_map/ppermute | solution.py:216
  93.0 16.7 %collective-permute-start.28 = (bf16[48,4096]{1,0:T(8,128)(2,1)}, bf16[48,4096]{1,0:T(8,128)(2,1)}, u32[]{:S(2)}, u32[]{:S(2)}) collective-permute-start(bf16[48,4096]{1,0:T(8,128)(2,1)} %collective-permute-done.21.refs_6_), channel_id=1, source_target_pairs={{0,8},{4,12},{8,0},{12,4},{1,9},{5,13},{9,1},{13,5},{2,10},{6,14},... | collective-permute-start | bytes 1179656 | tf_op jit(solution)/shard_map/ppermute | solution.py:216
  111.8 18.0 %collective-permute-start.42 = (bf16[384,896]{1,0:T(8,128)(2,1)S(1)}, bf16[384,896]{1,0:T(8,128)(2,1)}, u32[]{:S(2)}, u32[]{:S(2)}) collective-permute-start(bf16[384,896]{1,0:T(8,128)(2,1)S(1)} %copy-done.16), channel_id=1, source_target_pairs={{0,16},{16,0},{1,17},{17,1},{2,18},{18,2},{3,19},{19,3},{4,20},{20... | collective-permute-start | bytes 2064392 | tf_op jit(solution)/shard_map/ppermute | solution.py:222
  112.4 3.1 %collective-permute-start.39 = (bf16[32,4096]{1,0:T(8,128)(2,1)S(1)}, bf16[32,4096]{1,0:T(8,128)(2,1)S(1)}, u32[]{:S(2)}, u32[]{:S(2)}) collective-permute-start(bf16[32,4096]{1,0:T(8,128)(2,1)S(1)} %copy-done.48), channel_id=1, source_target_pairs={{0,4},{4,0},{8,12},{12,8},{1,5},{5,1},{9,13},{13,9},{2,6},{6,2},{1... | collective-permute-start | bytes 786440 | tf_op jit(solution)/shard_map/ppermute | solution.py:216
  112.6 4.1 %collective-permute-start.40 = (bf16[48,4096]{1,0:T(8,128)(2,1)}, bf16[48,4096]{1,0:T(8,128)(2,1)}, u32[]{:S(2)}, u32[]{:S(2)}) collective-permute-start(bf16[48,4096]{1,0:T(8,128)(2,1)} %collective-permute-done.21.refs_6_), channel_id=1, source_target_pairs={{0,4},{4,0},{8,12},{12,8},{1,5},{5,1},{9,13},{13,9},{2,6},{6,2},{1... | collective-permute-start | bytes 1179656 | tf_op jit(solution)/shard_map/ppermute | solution.py:216
  112.9 3.8 %collective-permute-start.41 = (bf16[48,4096]{1,0:T(8,128)(2,1)}, bf16[48,4096]{1,0:T(8,128)(2,1)}, u32[]{:S(2)}, u32[]{:S(2)}) collective-permute-start(bf16[48,4096]{1,0:T(8,128)(2,1)} %collective-permute-done.28.refs_7_), channel_id=1, source_target_pairs={{0,4},{4,0},{8,12},{12,8},{1,5},{5,1},{9,13},{13,9},{2,6},{6,2},{1... | collective-permute-start | bytes 1179656 | tf_op jit(solution)/shard_map/ppermute | solution.py:216
  114.1 15.7 %collective-permute-start.38 = (bf16[96,4096]{1,0:T(8,128)(2,1)}, bf16[96,4096]{1,0:T(8,128)(2,1)S(1)}, u32[]{:S(2)}, u32[]{:S(2)}) collective-permute-start(bf16[96,4096]{1,0:T(8,128)(2,1)} %get-tuple-element.163), channel_id=1, source_target_pairs={{0,4},{4,0},{8,12},{12,8},{1,5},{5,1},{9,13},{13,9},{2,6},{6,2},{1... | collective-permute-start | bytes 2359304 | tf_op jit(solution)/shard_map/ppermute | solution.py:216
  116.2 13.6 %collective-permute-start.37 = (bf16[48,4096]{1,0:T(8,128)(2,1)}, bf16[48,4096]{1,0:T(8,128)(2,1)S(1)}, u32[]{:S(2)}, u32[]{:S(2)}) collective-permute-start(bf16[48,4096]{1,0:T(8,128)(2,1)} %get-tuple-element.250), channel_id=1, source_target_pairs={{0,8},{4,12},{8,0},{12,4},{1,9},{5,13},{9,1},{13,5},{2,10},{6,14},... | collective-permute-start | bytes 1179656 | tf_op jit(solution)/shard_map/ppermute | solution.py:216
  129.9 18.2 %collective-permute-start.46 = (bf16[384,896]{1,0:T(8,128)(2,1)}, bf16[384,896]{1,0:T(8,128)(2,1)}, u32[]{:S(2)}, u32[]{:S(2)}) collective-permute-start(bf16[384,896]{1,0:T(8,128)(2,1)} %get-tuple-element.188), channel_id=1, source_target_pairs={{0,16},{16,0},{1,17},{17,1},{2,18},{18,2},{3,19},{19,3},{4,20},{20... | collective-permute-start | bytes 2064392 | tf_op jit(solution)/shard_map/ppermute | solution.py:222
  132.6 19.6 %collective-permute-start.44 = (bf16[96,4096]{1,0:T(8,128)(2,1)S(1)}, bf16[96,4096]{1,0:T(8,128)(2,1)S(1)}, u32[]{:S(2)}, u32[]{:S(2)}) collective-permute-start(bf16[96,4096]{1,0:T(8,128)(2,1)S(1)} %pad_maximum_fusion), channel_id=1, source_target_pairs={{0,8},{4,12},{8,0},{12,4},{1,9},{5,13},{9,1},{13,5},{2,10},{6,14},... | collective-permute-start | bytes 2359304 | tf_op jit(solution)/shard_map/ppermute | solution.py:216
  134.1 18.2 %collective-permute-start.45 = (bf16[96,4096]{1,0:T(8,128)(2,1)}, bf16[96,4096]{1,0:T(8,128)(2,1)}, u32[]{:S(2)}, u32[]{:S(2)}) collective-permute-start(bf16[96,4096]{1,0:T(8,128)(2,1)} %get-tuple-element.182), channel_id=1, source_target_pairs={{0,4},{4,0},{8,12},{12,8},{1,5},{5,1},{9,13},{13,9},{2,6},{6,2},{1... | collective-permute-start | bytes 2359304 | tf_op jit(solution)/shard_map/ppermute | solution.py:216
  155.6 24.5 %collective-permute-start.48 = (bf16[96,4096]{1,0:T(8,128)(2,1)S(1)}, bf16[96,4096]{1,0:T(8,128)(2,1)S(1)}, u32[]{:S(2)}, u32[]{:S(2)}) collective-permute-start(bf16[96,4096]{1,0:T(8,128)(2,1)S(1)} %pad_maximum_fusion.1), channel_id=1, source_target_pairs={{0,8},{4,12},{8,0},{12,4},{1,9},{5,13},{9,1},{13,5},{2,10},{6,14},... | collective-permute-start | bytes 2359304 | tf_op jit(solution)/shard_map/ppermute | solution.py:216
  157.1 23.0 %collective-permute-start.49 = (bf16[96,4096]{1,0:T(8,128)(2,1)}, bf16[96,4096]{1,0:T(8,128)(2,1)S(1)}, u32[]{:S(2)}, u32[]{:S(2)}) collective-permute-start(bf16[96,4096]{1,0:T(8,128)(2,1)} %get-tuple-element.192), channel_id=1, source_target_pairs={{0,4},{4,0},{8,12},{12,8},{1,5},{5,1},{9,13},{13,9},{2,6},{6,2},{1... | collective-permute-start | bytes 2359304 | tf_op jit(solution)/shard_map/ppermute | solution.py:216
  158.7 15.8 %collective-permute-start.51 = (bf16[48,4096]{1,0:T(8,128)(2,1)S(1)}, bf16[48,4096]{1,0:T(8,128)(2,1)S(1)}, u32[]{:S(2)}, u32[]{:S(2)}) collective-permute-start(bf16[48,4096]{1,0:T(8,128)(2,1)S(1)} %get-tuple-element.239), channel_id=1, source_target_pairs={{0,3},{1,0},{2,1},{3,2},{4,7},{5,4},{6,5},{7,6},{8,11},{9,8},{10,9... | collective-permute-start | bytes 1179656 | tf_op jit(solution)/shard_map/ppermute | solution.py:211
  162.0 18.0 %collective-permute-start.50 = (bf16[48,4096]{1,0:T(8,128)(2,1)S(1)}, bf16[48,4096]{1,0:T(8,128)(2,1)S(1)}, u32[]{:S(2)}, u32[]{:S(2)}) collective-permute-start(bf16[48,4096]{1,0:T(8,128)(2,1)S(1)} %get-tuple-element.240), channel_id=1, source_target_pairs={{0,1},{1,2},{2,3},{3,0},{4,5},{5,6},{6,7},{7,4},{8,9},{9,10},{10,1... | collective-permute-start | bytes 1179656 | tf_op jit(solution)/shard_map/ppermute | solution.py:211
  183.5 22.9 %collective-permute-start.53 = (bf16[48,4096]{1,0:T(8,128)(2,1)S(1)}, bf16[48,4096]{1,0:T(8,128)(2,1)S(1)}, u32[]{:S(2)}, u32[]{:S(2)}) collective-permute-start(bf16[48,4096]{1,0:T(8,128)(2,1)S(1)} %get-tuple-element.244), channel_id=1, source_target_pairs={{0,8},{4,12},{8,0},{12,4},{1,9},{5,13},{9,1},{13,5},{2,10},{6,14},... | collective-permute-start | bytes 1179656 | tf_op jit(solution)/shard_map/ppermute | solution.py:216
  184.5 21.8 %collective-permute-start.54 = (bf16[96,4096]{1,0:T(8,128)(2,1)}, bf16[96,4096]{1,0:T(8,128)(2,1)S(1)}, u32[]{:S(2)}, u32[]{:S(2)}) collective-permute-start(bf16[96,4096]{1,0:T(8,128)(2,1)} %get-tuple-element.205), channel_id=1, source_target_pairs={{0,4},{4,0},{8,12},{12,8},{1,5},{5,1},{9,13},{13,9},{2,6},{6,2},{1... | collective-permute-start | bytes 2359304 | tf_op jit(solution)/shard_map/ppermute | solution.py:216
  184.8 17.1 %collective-permute-start.56 = (bf16[48,4096]{1,0:T(8,128)(2,1)S(1)}, bf16[48,4096]{1,0:T(8,128)(2,1)S(1)}, u32[]{:S(2)}, u32[]{:S(2)}) collective-permute-start(bf16[48,4096]{1,0:T(8,128)(2,1)S(1)} %get-tuple-element.237), channel_id=1, source_target_pairs={{0,1},{1,2},{2,3},{3,0},{4,5},{5,6},{6,7},{7,4},{8,9},{9,10},{10,1... | collective-permute-start | bytes 1179656 | tf_op jit(solution)/shard_map/ppermute | solution.py:211
  186.7 19.7 %collective-permute-start.55 = (bf16[48,4096]{1,0:T(8,128)(2,1)S(1)}, bf16[48,4096]{1,0:T(8,128)(2,1)S(1)}, u32[]{:S(2)}, u32[]{:S(2)}) collective-permute-start(bf16[48,4096]{1,0:T(8,128)(2,1)S(1)} %get-tuple-element.238), channel_id=1, source_target_pairs={{0,3},{1,0},{2,1},{3,2},{4,7},{5,4},{6,5},{7,6},{8,11},{9,8},{10,9... | collective-permute-start | bytes 1179656 | tf_op jit(solution)/shard_map/ppermute | solution.py:211
  206.6 21.1 %collective-permute-start.58 = (bf16[96,4096]{1,0:T(8,128)(2,1)S(1)}, bf16[96,4096]{1,0:T(8,128)(2,1)S(1)}, u32[]{:S(2)}, u32[]{:S(2)}) collective-permute-start(bf16[96,4096]{1,0:T(8,128)(2,1)S(1)} %pad_maximum_fusion.3), channel_id=1, source_target_pairs={{0,3},{1,0},{2,1},{3,2},{4,7},{5,4},{6,5},{7,6},{8,11},{9,8},{10,9... | collective-permute-start | bytes 2359304 | tf_op jit(solution)/shard_map/ppermute | solution.py:211
  208.9 19.0 %collective-permute-start.57 = (bf16[96,4096]{1,0:T(8,128)(2,1)S(1)}, bf16[96,4096]{1,0:T(8,128)(2,1)S(1)}, u32[]{:S(2)}, u32[]{:S(2)}) collective-permute-start(bf16[96,4096]{1,0:T(8,128)(2,1)S(1)} %pad_maximum_fusion.2), channel_id=1, source_target_pairs={{0,8},{4,12},{8,0},{12,4},{1,9},{5,13},{9,1},{13,5},{2,10},{6,14},... | collective-permute-start | bytes 2359304 | tf_op jit(solution)/shard_map/ppermute | solution.py:216
  (68 other events, 504.5 us)

commit v10 on v9

--- a/solution.py
+++ b/solution.py
@@ -276,11 +276,14 @@
         total = row_sum(partial, moved)
         return total[:half], total[half:]
 
-    far0, near1, cot_core0 = sync(
-        swap(tokens, CHIP), shift(tokens, 1), swap(cotangent, CORE)
-    )
     head = 16 * (cotangent.shape[0] // 48)
-    cot_head, cot_tail = cotangent[:head], cotangent[head:]
+    far0, near1, cot_core0, cot_head, cot_tail = sync(
+        swap(tokens, CHIP),
+        shift(tokens, 1),
+        swap(cotangent, CORE),
+        cotangent[:head],
+        cotangent[head:],
+    )
 
     far1, near3 = swap(near1, CHIP), shift(after(tokens, near1), 3)
     head3 = shift(after(cot_head, near1), 3)
@@ -306,8 +309,9 @@
     far2, far_head3 = swap(near2, CHIP), swap(after(head3, pair1), CHIP)
     token3 = quad([near3], [far3], other_cores([after(near3, pair1), far3]))
     pair3 = contract(token3, pair)
-    cot_near2, far2, far_head3, pair3, *pair1_moved = sync(
-        cot_near2, far2, far_head3, pair3, *pair1_moved
+    far_head0_core = swap(after(far_head0, pair1), CORE)
+    cot_near2, far2, far_head3, pair3, far_head0_core, *pair1_moved = sync(
+        cot_near2, far2, far_head3, pair3, far_head0_core, *pair1_moved
     )
 
     gate1, up1 = pair_sums(pair1, pair1_moved)
@@ -318,17 +322,18 @@
     cot_far2, far_tail3 = swap(cot_near2, CHIP), swap(after(tail3, pair3), CHIP)
     token2 = quad([near2], [far2], other_cores([after(near2, pair3), far2]))
     pair2 = contract(token2, pair)
-    far_head0_core = swap(after(far_head0, pair3), CORE)
-    cot_near1, cot_far2, far_tail3, pair2, far_head0_core, *pair3_moved = sync(
-        cot_near1, cot_far2, far_tail3, pair2, far_head0_core, *pair3_moved
-    )
+    core3, far_head3_core = other_cores(after(x, pair3) for x in (cot_near3, far_head3))
+    cot_near1, cot_far2, far_tail3, pair2, core3, far_head3_core, hidden0, hidden1, *rest = sync(
+        cot_near1, cot_far2, far_tail3, pair2, core3, far_head3_core, hidden0, hidden1, *pair3_moved
+    )
+    pair3_moved = rest
 
     gate3, up3 = pair_sums(pair3, pair3_moved)
     hidden3 = hidden_of(gate3, up3)
     pair2_moved = row_moves(pair2)
     cot_far1, far_tail0 = swap(cot_near1, CHIP), swap(after(cot_tail, pair2), CHIP)
     cot_far3 = [after(far_head3, pair2), far_tail3]
-    cot3 = quad([cot_near3], cot_far3, other_cores([after(cot_near3, pair2), *cot_far3]))
+    cot3 = quad([cot_near3], cot_far3, [core3, far_head3_core, swap(far_tail3, CORE)])
     cot2 = quad([cot_near2], [cot_far2], other_cores([after(cot_near2, pair2), cot_far2]))
     products = down_products(cot3 + cot2, [hidden0, hidden1], down_weight)
     cot_far1, far_tail0, grad_b, *rest = sync(cot_far1, far_tail0, *products, *pair2_moved)
@@ -361,11 +366,10 @@
 
     sent, token_grad_b = chip_part(parts)
     token_b_moved = swap(jnp.concatenate(sent, axis=0), CHIP)
-    grad_a = row_sum(grad_a, grad_a_moved)
+    grad_a = row_sum(grad_a, grad_a_moved, *sent)
     size = tokens.shape[0]
-    moved = after(mixed_b_moved, *sent)
-    mixed_part3 = shift(narrow(block_sum(mixed_b, 0, moved[:size])), 1)
-    mixed_part2 = shift(narrow(block_sum(mixed_b, 1, moved[size:])), -1)
+    mixed_part3 = shift(narrow(block_sum(mixed_b, 0, mixed_b_moved[:size])), 1)
+    mixed_part2 = shift(narrow(block_sum(mixed_b, 1, mixed_b_moved[size:])), -1)
     grads0 = grads_of(gate0, up0, grad_a[:half])
     grads1 = grads_of(gate1, up1, grad_a[half:])
     parts = expand([[x, y] for x, y in zip(grads0, grads1)], pair)
@@ -375,9 +379,8 @@
 
     (token_sent0, sent), token_grad_a = chip_part(parts)
     token_a_moved = swap(sent, CHIP)
-    moved = after(token_b_moved, sent)
-    part3 = shift(narrow(block_sum(token_grad_b, 0, moved[:size])), 1)
-    part2 = shift(narrow(block_sum(token_grad_b, 1, moved[size:])), -1)
+    part3 = shift(narrow(block_sum(token_grad_b, 0, token_b_moved[:size])), 1)
+    part2 = shift(narrow(block_sum(token_grad_b, 1, token_b_moved[size:])), -1)
     down_total = tall_grad(
         cot0 + cot1 + cot3 + cot2, [after(hidden0, sent), hidden1, hidden3, hidden2]
     )

time: 232 us -> 223 us (0.961)
  waiting for transfers between devices: 42.8 us -> 30.2 us
  starting transfers between devices: 46.9 us -> 51.1 us
    ppermute x12, waiting for transfers between devices: 23.3 us -> 12.3 us  [shift(): return lax.ppermute(block, 'depth', [(i, (i + step) % n) for i in range(n)])]
    ppermute x12, starting transfers between devices: 20.6 us -> 23.4 us  [shift(): return lax.ppermute(block, 'depth', [(i, (i + step) % n) for i in range(n)])]
    unnamed x115 -> x109, local copies, waits for them, and re-layouts: 5.08 us -> 5.63 us
  transfers between devices with their start and end apart: 59 -> 59, of which waited for: 17 -> 13; matrix products, arithmetic and copies ran while one was open for 7% -> 7% of each run, Pallas kernels for 50% -> 52%
where the time goes in v10:
time: 223 us; the launch traced here: 221 us
  Pallas kernels  116 us (52%)
  starting transfers between devices  51.1 us (23%)
  waiting for transfers between devices  30.2 us (14%)
  other arithmetic  14.8 us (7%)
  local copies, waits for them, and re-layouts  7.53 us (3%)
    pallas_call x4, Pallas kernels, contract(): pl.pallas_call(functools.partial(contract_kernel, len(pieces), len(weight...  34.7 us
    pallas_call x2, Pallas kernels, down_products(): pl.pallas_call(functools.partial(down_kernel, len(pieces)), grid=(width /...  25.3 us
    pallas_call x2, Pallas kernels, expand(): pl.pallas_call(functools.partial(expand_kernel, len(lefts)), grid=(width...  24.6 us
    ppermute x12, starting transfers between devices, shift(): return lax.ppermute(block, 'depth', [(i, (i + step) % n) for i in range(n)])  23.4 us
    ppermute x41, starting transfers between devices, swap(): return lax.ppermute(block, 'col', [(i, i ^ bit) for i in range(n)])  21.4 us
    pallas_call x1, Pallas kernels, wide_grads(): pl.pallas_call(functools.partial(wide_grad_kernel, len(pieces)), grid=(wi...  17.8 us
    ppermute x41, waiting for transfers between devices, swap(): return lax.ppermute(block, 'col', [(i, i ^ bit) for i in range(n)])  16.3 us
    pallas_call x1, Pallas kernels, tall_grad(): pl.pallas_call(functools.partial(tall_grad_kernel, len(pieces)), grid=(wi...  13.2 us
  transfers between devices with their start and end apart: 59, of which 13 were waited for; matrix products, arithmetic and copies ran while one was open for 7% of the time, Pallas kernels for 52%

profile of v10, /device:TPU:0, one launch (start us, length us, event | category | flops | bytes accessed | tf_op | source)
XLA Modules:
  0.0 220.6 jit_solution(6819661865644806168)
XLA Ops:
  0.6 3.1 %collective-permute-start.1 = (bf16[48,4096]{1,0:T(8,128)(2,1)}, bf16[48,4096]{1,0:T(8,128)(2,1)S(1)}, u32[]{:S(2)}, u32[]{:S(2)}) collective-permute-start(bf16[48,4096]{1,0:T(8,128)(2,1)} %refs_0_.6), channel_id=1, source_target_pairs={{0,1},{1,2},{2,3},{3,0},{4,5},{5,6},{6,7},{7,4},{8,9},{9,10},{10,1... | collective-permute-start | bytes 1179656 | tf_op jit(solution)/shard_map/ppermute | solution.py:211
  3.7 1.5 collective-permute-start
  7.1 7.9 %collective-permute-done.1.refs_0_.refs_4_ = bf16[48,4096]{1,0:T(8,128)(2,1)S(1)} collective-permute-done((bf16[48,4096]{1,0:T(8,128)(2,1)}, bf16[48,4096]{1,0:T(8,128)(2,1)S(1)}, u32[]{:S(2)}, u32[]{:S(2)}) %collective-permute-start.1) | collective-permute-done | bytes 393248 | tf_op jit(solution)/shard_map/ppermute | solution.py:211
  15.6 1.7 collective-permute-start.4
  17.4 1.5 collective-permute-start.3
  18.9 1.7 collective-permute-start.5
  21.4 8.7 %shard_map.92 = bf16[384,896]{1,0:T(8,128)(2,1)} custom-call(bf16[48,4096]{1,0:T(8,128)(2,1)} %refs_0_.6, bf16[48,4096]{1,0:T(8,128)(2,1)} %copy-done.21, bf16[48,4096]{1,0:T(8,128)(2,1)} %copy-done.22, bf16[48,4096]{1,0:T(8,128)(2,1)} %copy-done.23, bf16[4096,896]{1,0:T(8,128)(2,1)} %refs_4_.11, bf16[4096,896]{1,0:T(8,128)(2,1)} %refs_5_.11), custom_call_target="tpu_custom_call" | custom-call | flops 2818572288 | bytes 16252928 | tf_op jit(solution)/shard_map/pallas_call | solution.py:64
  30.1 1.6 collective-permute-start.14
  32.3 1.5 collective-permute-start.11
  34.4 3.3 %collective-permute-start.10 = (bf16[32,4096]{1,0:T(8,128)(2,1)S(1)}, bf16[32,4096]{1,0:T(8,128)(2,1)S(1)}, u32[]{:S(2)}, u32[]{:S(2)}) collective-permute-start(bf16[32,4096]{1,0:T(8,128)(2,1)S(1)} %slice.163), channel_id=1, source_target_pairs={{0,3},{1,0},{2,1},{3,2},{4,7},{5,4},{6,5},{7,6},{8,11},{9,8},{10,9... | collective-permute-start | bytes 786440 | tf_op jit(solution)/shard_map/ppermute | solution.py:211
  37.7 8.7 %shard_map.93 = bf16[384,896]{1,0:T(8,128)(2,1)} custom-call(bf16[48,4096]{1,0:T(8,128)(2,1)} %copy-done.20, bf16[48,4096]{1,0:T(8,128)(2,1)} %copy-done.26, bf16[48,4096]{1,0:T(8,128)(2,1)} %copy-done.25, bf16[48,4096]{1,0:T(8,128)(2,1)} %copy-done.28, bf16[4096,896]{1,0:T(8,128)(2,1)} %refs_4_.11, bf16[4096,896]{1,0:T(8,128)(2,1)} %refs_5_.11), custom_call_target="tpu_custom_call" | custom-call | flops 2818572288 | bytes 16252928 | tf_op jit(solution)/shard_map/pallas_call | solution.py:64
  46.6 3.1 %collective-permute-done.10 = bf16[32,4096]{1,0:T(8,128)(2,1)S(1)} collective-permute-done((bf16[32,4096]{1,0:T(8,128)(2,1)S(1)}, bf16[32,4096]{1,0:T(8,128)(2,1)S(1)}, u32[]{:S(2)}, u32[]{:S(2)}) %collective-permute-start.10) | collective-permute-done | bytes 262176 | tf_op jit(solution)/shard_map/ppermute | solution.py:211
  51.0 1.3 collective-permute-start.15
  52.3 1.5 collective-permute-start.16
  55.1 8.7 %shard_map.94 = bf16[384,896]{1,0:T(8,128)(2,1)} custom-call(bf16[48,4096]{1,0:T(8,128)(2,1)} %copy-done.24, bf16[48,4096]{1,0:T(8,128)(2,1)} %copy-done.29, bf16[48,4096]{1,0:T(8,128)(2,1)} %copy-done.30, bf16[48,4096]{1,0:T(8,128)(2,1)} %copy-done.31, bf16[4096,896]{1,0:T(8,128)(2,1)} %refs_4_.11, bf16[4096,896]{1,0:T(8,128)(2,1)} %refs_5_.11), custom_call_target="tpu_custom_call" | custom-call | flops 2818572288 | bytes 16252928 | tf_op jit(solution)/shard_map/pallas_call | solution.py:64
  63.8 2.1 collective-permute-done.17.refs_1_.refs_11_
  65.9 1.6 collective-permute-done.21
  68.9 1.0 collective-permute-start.22
  71.2 1.3 multiply_convert_fusion.10
  72.5 1.5 collective-permute-start.24
  74.0 8.7 %shard_map.95 = bf16[384,896]{1,0:T(8,128)(2,1)} custom-call(bf16[48,4096]{1,0:T(8,128)(2,1)} %copy-done.27, bf16[48,4096]{1,0:T(8,128)(2,1)} %copy-done.32, bf16[48,4096]{1,0:T(8,128)(2,1)} %copy-done.33, bf16[48,4096]{1,0:T(8,128)(2,1)} %copy-done.34, bf16[4096,896]{1,0:T(8,128)(2,1)} %refs_4_.11, bf16[4096,896]{1,0:T(8,128)(2,1)} %refs_5_.11), custom_call_target="tpu_custom_call" | custom-call | flops 2818572288 | bytes 16252928 | tf_op jit(solution)/shard_map/pallas_call | solution.py:64
  82.7 4.8 %collective-permute-done.24.refs_2_.refs_12_ = bf16[32,4096]{1,0:T(8,128)(2,1)S(1)} collective-permute-done((bf16[32,4096]{1,0:T(8,128)(2,1)S(1)}, bf16[32,4096]{1,0:T(8,128)(2,1)S(1)}, u32[]{:S(2)}, u32[]{:S(2)}) %collective-permute-start.24) | collective-permute-done | bytes 262176 | tf_op jit(solution)/shard_map/ppermute | solution.py:216
  88.2 1.4 collective-permute-start.35
  90.2 1.3 collective-permute-start.30
  93.1 12.6 %shard_map.96 = (bf16[384,896]{1,0:T(8,128)(2,1)}, bf16[96,4096]{1,0:T(8,128)(2,1)}, bf16[96,4096]{1,0:T(8,128)(2,1)}, bf16[96,4096]{1,0:T(8,128)(2,1)}, bf16[96,4096]{1,0:T(8,128)(2,1)}) custom-call(bf16[48,4096]{1,0:T(8,128)(2,1)} %copy-done.15, bf16[16,4096]{1,0:T(8,128)(2,1)} %copy-done.50, bf16[32,4096]{1,0:T(8,128)(2,1)} %copy-done.41, ...), custom_call_target="tpu_custom_call" | custom-call | flops 5637144576 | bytes 14319616 | tf_op jit(solution)/shard_map/pallas_call | solution.py:138
  107.7 1.1 collective-permute-start.42
  113.2 12.6 %shard_map.97 = (bf16[384,896]{1,0:T(8,128)(2,1)}, bf16[96,4096]{1,0:T(8,128)(2,1)}, bf16[96,4096]{1,0:T(8,128)(2,1)}, bf16[96,4096]{1,0:T(8,128)(2,1)}, bf16[96,4096]{1,0:T(8,128)(2,1)}) custom-call(bf16[48,4096]{1,0:T(8,128)(2,1)} %refs_0_.5, bf16[16,4096]{1,0:T(8,128)(2,1)} %copy-done.49, bf16[32,4096]{1,0:T(8,128)(2,1)} %copy-done.43, ...), custom_call_target="tpu_custom_call" | custom-call | flops 5637144576 | bytes 14319616 | tf_op jit(solution)/shard_map/pallas_call | solution.py:138
  125.9 1.0 collective-permute-start.46
  126.9 1.2 convert_add_fusion.1
  128.7 1.5 collective-permute-start.44
  130.2 1.7 multiply_convert_fusion.4
  131.9 12.3 %shard_map.98 = (bf16[96,4096]{1,0:T(8,128)(2,1)}, bf16[96,4096]{1,0:T(8,128)(2,1)}, bf16[96,4096]{1,0:T(8,128)(2,1)}, bf16[96,4096]{1,0:T(8,128)(2,1)}) custom-call(bf16[192,896]{1,0:T(8,128)(2,1)} %get-tuple-element.265.refs_0_.refs_18_, bf16[192,896]{1,0:T(8,128)(2,1)} %get-tuple-element.246.refs_1_.refs_19_, ...), custom_call_target="tpu_custom_call" | custom-call | flops 5637144576 | bytes 19202048 | tf_op jit(solution)/shard_map/pallas_call | solution.py:101
  144.2 4.1 %collective-permute-done.44 = bf16[96,4096]{1,0:T(8,128)(2,1)S(1)} collective-permute-done((bf16[96,4096]{1,0:T(8,128)(2,1)S(1)}, bf16[96,4096]{1,0:T(8,128)(2,1)S(1)}, u32[]{:S(2)}, u32[]{:S(2)}) %collective-permute-start.44) | collective-permute-done | bytes 786464 | tf_op jit(solution)/shard_map/ppermute | solution.py:216
  148.3 1.0 add_convert_fusion.6
  149.4 3.1 %collective-permute-start.51 = (bf16[48,4096]{1,0:T(8,128)(2,1)}, bf16[48,4096]{1,0:T(8,128)(2,1)S(1)}, u32[]{:S(2)}, u32[]{:S(2)}) collective-permute-start(bf16[48,4096]{1,0:T(8,128)(2,1)} %get-tuple-element.251), channel_id=1, source_target_pairs={{0,3},{1,0},{2,1},{3,2},{4,7},{5,4},{6,5},{7,6},{8,11},{9,8},{10,9... | collective-permute-start | bytes 1179656 | tf_op jit(solution)/shard_map/ppermute | solution.py:211
  152.8 1.0 copy-done.16
  153.8 1.3 convert_add_fusion
  155.1 1.5 collective-permute-start.48
  156.6 1.7 multiply_convert_fusion
  158.4 12.3 %shard_map.99 = (bf16[96,4096]{1,0:T(8,128)(2,1)}, bf16[96,4096]{1,0:T(8,128)(2,1)}, bf16[96,4096]{1,0:T(8,128)(2,1)}, bf16[96,4096]{1,0:T(8,128)(2,1)}) custom-call(bf16[192,896]{1,0:T(8,128)(2,1)} %get-tuple-element.263.refs_0_.refs_16_, bf16[192,896]{1,0:T(8,128)(2,1)} %get-tuple-element.242.refs_1_.refs_17_, ...), custom_call_target="tpu_custom_call" | custom-call | flops 5637144576 | bytes 19202048 | tf_op jit(solution)/shard_map/pallas_call | solution.py:101
  170.9 3.9 %collective-permute-done.48 = bf16[96,4096]{1,0:T(8,128)(2,1)S(1)} collective-permute-done((bf16[96,4096]{1,0:T(8,128)(2,1)S(1)}, bf16[96,4096]{1,0:T(8,128)(2,1)S(1)}, u32[]{:S(2)}, u32[]{:S(2)}) %collective-permute-start.48) | collective-permute-done | bytes 786464 | tf_op jit(solution)/shard_map/ppermute | solution.py:216
  175.3 3.8 %collective-permute-start.55 = (bf16[48,4096]{1,0:T(8,128)(2,1)S(1)}, bf16[48,4096]{1,0:T(8,128)(2,1)S(1)}, u32[]{:S(2)}, u32[]{:S(2)}) collective-permute-start(bf16[48,4096]{1,0:T(8,128)(2,1)S(1)} %get-tuple-element.250), channel_id=1, source_target_pairs={{0,3},{1,0},{2,1},{3,2},{4,7},{5,4},{6,5},{7,6},{8,11},{9,8},{10,9... | collective-permute-start | bytes 1179656 | tf_op jit(solution)/shard_map/ppermute | solution.py:211
  179.8 1.5 collective-permute-start.53
  181.3 13.2 %shard_map.100 = f32[896,4096]{1,0:T(8,128)} custom-call(bf16[48,4096]{1,0:T(8,128)(2,1)} %refs_0_.5, bf16[16,4096]{1,0:T(8,128)(2,1)} %copy-done.49, bf16[32,4096]{1,0:T(8,128)(2,1)} %copy-done.43, bf16[48,4096]{1,0:T(8,128)(2,1)} %collective-permute-done.2.refs_3_, bf16[16,4096]{1,0:T(8,128)(2,1)} %copy-done.51, bf16[32,4096]{1,0:T(8,128)(2,1)} %copy-done.44, ...), custom_call_target="tpu_custom_call" | custom-call | flops 5637144576 | bytes 22347776 | tf_op jit(solution)/shard_map/pallas_call | solution.py:197
  195.8 3.7 %collective-permute-start.58 = (bf16[96,4096]{1,0:T(8,128)(2,1)S(1)}, bf16[96,4096]{1,0:T(8,128)(2,1)S(1)}, u32[]{:S(2)}, u32[]{:S(2)}) collective-permute-start(bf16[96,4096]{1,0:T(8,128)(2,1)S(1)} %pad_maximum_fusion.3), channel_id=1, source_target_pairs={{0,3},{1,0},{2,1},{3,2},{4,7},{5,4},{6,5},{7,6},{8,11},{9,8},{10,9... | collective-permute-start | bytes 2359304 | tf_op jit(solution)/shard_map/ppermute | solution.py:211
  199.6 1.5 collective-permute-start.57
  201.1 17.8 %shard_map.101 = (f32[4096,896]{1,0:T(8,128)}, f32[4096,896]{1,0:T(8,128)}) custom-call(bf16[48,4096]{1,0:T(8,128)(2,1)} %refs_0_.6, bf16[48,4096]{1,0:T(8,128)(2,1)} %copy-done.21, bf16[48,4096]{1,0:T(8,128)(2,1)} %copy-done.22, bf16[48,4096]{1,0:T(8,128)(2,1)} %copy-done.23, bf16[48,4096]{1,0:T(8,128)(2,1)} %copy-done.20, bf16[48,4096]{1,0:T(8,128)(2,1)} %copy-done.26, ...), custom_call_target="tpu_custom_call" | custom-call | flops 11274289152 | bytes 38404096 | tf_op jit(solution)/shard_map/pallas_call | solution.py:173
  218.9 1.7 convert_add_fusion.6
  (216 shorter events, 22.5 us)
Async XLA Ops:
  0.6 14.4 %collective-permute-start.1 = (bf16[48,4096]{1,0:T(8,128)(2,1)}, bf16[48,4096]{1,0:T(8,128)(2,1)S(1)}, u32[]{:S(2)}, u32[]{:S(2)}) collective-permute-start(bf16[48,4096]{1,0:T(8,128)(2,1)} %refs_0_.6), channel_id=1, source_target_pairs={{0,1},{1,2},{2,3},{3,0},{4,5},{5,6},{6,7},{7,4},{8,9},{9,10},{10,1... | collective-permute-start | bytes 1179656 | tf_op jit(solution)/shard_map/ppermute | solution.py:211
  3.7 11.4 %collective-permute-start = (bf16[48,4096]{1,0:T(8,128)(2,1)}, bf16[48,4096]{1,0:T(8,128)(2,1)S(1)}, u32[]{:S(2)}, u32[]{:S(2)}) collective-permute-start(bf16[48,4096]{1,0:T(8,128)(2,1)} %refs_0_.6), channel_id=1, source_target_pairs={{0,8},{4,12},{8,0},{12,4},{1,9},{5,13},{9,1},{13,5},{2,10},{6,14},... | collective-permute-start | bytes 1179656 | tf_op jit(solution)/shard_map/ppermute | solution.py:216
  5.2 9.8 %collective-permute-start.2 = (bf16[48,4096]{1,0:T(8,128)(2,1)}, bf16[48,4096]{1,0:T(8,128)(2,1)}, u32[]{:S(2)}, u32[]{:S(2)}) collective-permute-start(bf16[48,4096]{1,0:T(8,128)(2,1)} %refs_0_.5), channel_id=1, source_target_pairs={{0,4},{4,0},{8,12},{12,8},{1,5},{5,1},{9,13},{13,9},{2,6},{6,2},{1... | collective-permute-start | bytes 1179656 | tf_op jit(solution)/shard_map/ppermute | solution.py:216
  15.2 5.4 %collective-permute-start.8 = (bf16[48,4096]{1,0:T(8,128)(2,1)S(1)}, bf16[48,4096]{1,0:T(8,128)(2,1)S(1)}, u32[]{:S(2)}, u32[]{:S(2)}) collective-permute-start(bf16[48,4096]{1,0:T(8,128)(2,1)S(1)} %collective-permute-done.refs_1_), channel_id=1, source_target_pairs={{0,4},{4,0},{8,12},{12,8},{1,5},{5,1},{9,13},{13,9},{2,6},{6,2},{1... | collective-permute-start | bytes 1179656 | tf_op jit(solution)/shard_map/ppermute | solution.py:216
  15.6 14.4 %collective-permute-start.4 = (bf16[48,4096]{1,0:T(8,128)(2,1)}, bf16[48,4096]{1,0:T(8,128)(2,1)S(1)}, u32[]{:S(2)}, u32[]{:S(2)}) collective-permute-start(bf16[48,4096]{1,0:T(8,128)(2,1)} %refs_0_.6), channel_id=1, source_target_pairs={{0,3},{1,0},{2,1},{3,2},{4,7},{5,4},{6,5},{7,6},{8,11},{9,8},{10,9... | collective-permute-start | bytes 1179656 | tf_op jit(solution)/shard_map/ppermute | solution.py:211
  17.4 12.7 %collective-permute-start.6 = (bf16[48,4096]{1,0:T(8,128)(2,1)S(1)}, bf16[48,4096]{1,0:T(8,128)(2,1)S(1)}, u32[]{:S(2)}, u32[]{:S(2)}) collective-permute-start(bf16[48,4096]{1,0:T(8,128)(2,1)S(1)} %collective-permute-done.1.refs_0_.refs_4_), channel_id=1, source_target_pairs={{0,4},{4,0},{8,12},{12,8},{1,5},{5,1},{9,13},{13,9},{2,6},{6,2},{1... | collective-permute-start | bytes 1179656 | tf_op jit(solution)/shard_map/ppermute | solution.py:216
  17.4 12.7 %collective-permute-start.3 = (bf16[48,4096]{1,0:T(8,128)(2,1)S(1)}, bf16[48,4096]{1,0:T(8,128)(2,1)S(1)}, u32[]{:S(2)}, u32[]{:S(2)}) collective-permute-start(bf16[48,4096]{1,0:T(8,128)(2,1)S(1)} %collective-permute-done.1.refs_0_.refs_4_), channel_id=1, source_target_pairs={{0,8},{4,12},{8,0},{12,4},{1,9},{5,13},{9,1},{13,5},{2,10},{6,14},... | collective-permute-start | bytes 1179656 | tf_op jit(solution)/shard_map/ppermute | solution.py:216
  18.9 11.1 %collective-permute-start.5 = (bf16[16,4096]{1,0:T(8,128)(2,1)S(1)}, bf16[16,4096]{1,0:T(8,128)(2,1)S(1)}, u32[]{:S(2)}, u32[]{:S(2)}) collective-permute-start(bf16[16,4096]{1,0:T(8,128)(2,1)S(1)} %slice.162), channel_id=1, source_target_pairs={{0,3},{1,0},{2,1},{3,2},{4,7},{5,4},{6,5},{7,6},{8,11},{9,8},{10,9... | collective-permute-start | bytes 393224 | tf_op jit(solution)/shard_map/ppermute | solution.py:211
  30.1 19.7 %collective-permute-start.14 = (bf16[384,896]{1,0:T(8,128)(2,1)}, bf16[384,896]{1,0:T(8,128)(2,1)S(1)}, u32[]{:S(2)}, u32[]{:S(2)}) collective-permute-start(bf16[384,896]{1,0:T(8,128)(2,1)} %shard_map.92), channel_id=1, source_target_pairs={{0,16},{16,0},{1,17},{17,1},{2,18},{18,2},{3,19},{19,3},{4,20},{20... | collective-permute-start | bytes 2064392 | tf_op jit(solution)/shard_map/ppermute | solution.py:222
  31.7 18.1 %collective-permute-start.9 = (bf16[48,4096]{1,0:T(8,128)(2,1)S(1)}, bf16[48,4096]{1,0:T(8,128)(2,1)S(1)}, u32[]{:S(2)}, u32[]{:S(2)}) collective-permute-start(bf16[48,4096]{1,0:T(8,128)(2,1)S(1)} %collective-permute-done.1.refs_0_.refs_4_), channel_id=1, source_target_pairs={{0,1},{1,2},{2,3},{3,0},{4,5},{5,6},{6,7},{7,4},{8,9},{9,10},{10,1... | collective-permute-start | bytes 1179656 | tf_op jit(solution)/shard_map/ppermute | solution.py:211
  32.3 17.5 %collective-permute-start.11 = (bf16[48,4096]{1,0:T(8,128)(2,1)S(1)}, bf16[48,4096]{1,0:T(8,128)(2,1)S(1)}, u32[]{:S(2)}, u32[]{:S(2)}) collective-permute-start(bf16[48,4096]{1,0:T(8,128)(2,1)S(1)} %collective-permute-done.4.refs_0_.refs_8_), channel_id=1, source_target_pairs={{0,8},{4,12},{8,0},{12,4},{1,9},{5,13},{9,1},{13,5},{2,10},{6,14},... | collective-permute-start | bytes 1179656 | tf_op jit(solution)/shard_map/ppermute | solution.py:216
  33.8 12.8 %collective-permute-start.12 = (bf16[16,4096]{1,0:T(8,128)(2,1)S(1)}, bf16[16,4096]{1,0:T(8,128)(2,1)S(1)}, u32[]{:S(2)}, u32[]{:S(2)}) collective-permute-start(bf16[16,4096]{1,0:T(8,128)(2,1)S(1)} %slice.162), channel_id=1, source_target_pairs={{0,8},{4,12},{8,0},{12,4},{1,9},{5,13},{9,1},{13,5},{2,10},{6,14},... | collective-permute-start | bytes 393224 | tf_op jit(solution)/shard_map/ppermute | solution.py:216
  34.4 15.4 %collective-permute-start.10 = (bf16[32,4096]{1,0:T(8,128)(2,1)S(1)}, bf16[32,4096]{1,0:T(8,128)(2,1)S(1)}, u32[]{:S(2)}, u32[]{:S(2)}) collective-permute-start(bf16[32,4096]{1,0:T(8,128)(2,1)S(1)} %slice.163), channel_id=1, source_target_pairs={{0,3},{1,0},{2,1},{3,2},{4,7},{5,4},{6,5},{7,6},{8,11},{9,8},{10,9... | collective-permute-start | bytes 786440 | tf_op jit(solution)/shard_map/ppermute | solution.py:211
  49.8 17.6 %collective-permute-start.21 = (bf16[384,896]{1,0:T(8,128)(2,1)}, bf16[384,896]{1,0:T(8,128)(2,1)S(1)}, u32[]{:S(2)}, u32[]{:S(2)}) collective-permute-start(bf16[384,896]{1,0:T(8,128)(2,1)} %shard_map.93), channel_id=1, source_target_pairs={{0,16},{16,0},{1,17},{17,1},{2,18},{18,2},{3,19},{19,3},{4,20},{20... | collective-permute-start | bytes 2064392 | tf_op jit(solution)/shard_map/ppermute | solution.py:222
  51.0 14.9 %collective-permute-start.15 = (bf16[48,4096]{1,0:T(8,128)(2,1)S(1)}, bf16[48,4096]{1,0:T(8,128)(2,1)}, u32[]{:S(2)}, u32[]{:S(2)}) collective-permute-start(bf16[48,4096]{1,0:T(8,128)(2,1)S(1)} %constant_dynamic-update-slice_fusion.refs_0_.refs_10_), channel_id=1, source_target_pairs={{0,3},{1,0},{2,1},{3,2},{4,7},{5,4},{6,5},{7,6},{8,11},{9,8},{10,9... | collective-permute-start | bytes 1179656 | tf_op jit(solution)/shard_map/ppermute | solution.py:211
  52.3 13.6 %collective-permute-start.16 = (bf16[48,4096]{1,0:T(8,128)(2,1)S(1)}, bf16[48,4096]{1,0:T(8,128)(2,1)S(1)}, u32[]{:S(2)}, u32[]{:S(2)}) collective-permute-start(bf16[48,4096]{1,0:T(8,128)(2,1)S(1)} %collective-permute-done.9.refs_0_.refs_12_), channel_id=1, source_target_pairs={{0,8},{4,12},{8,0},{12,4},{1,9},{5,13},{9,1},{13,5},{2,10},{6,14},... | collective-permute-start | bytes 1179656 | tf_op jit(solution)/shard_map/ppermute | solution.py:216
  53.8 12.0 %collective-permute-start.17 = (bf16[16,4096]{1,0:T(8,128)(2,1)S(1)}, bf16[16,4096]{1,0:T(8,128)(2,1)S(1)}, u32[]{:S(2)}, u32[]{:S(2)}) collective-permute-start(bf16[16,4096]{1,0:T(8,128)(2,1)S(1)} %collective-permute-done.5), channel_id=1, source_target_pairs={{0,8},{4,12},{8,0},{12,4},{1,9},{5,13},{9,1},{13,5},{2,10},{6,14},... | collective-permute-start | bytes 393224 | tf_op jit(solution)/shard_map/ppermute | solution.py:216
  54.3 11.5 %collective-permute-start.20 = (bf16[16,4096]{1,0:T(8,128)(2,1)S(1)}, bf16[16,4096]{1,0:T(8,128)(2,1)S(1)}, u32[]{:S(2)}, u32[]{:S(2)}) collective-permute-start(bf16[16,4096]{1,0:T(8,128)(2,1)S(1)} %collective-permute-done.12.refs_1_), channel_id=1, source_target_pairs={{0,4},{4,0},{8,12},{12,8},{1,5},{5,1},{9,13},{13,9},{2,6},{6,2},{1... | collective-permute-start | bytes 393224 | tf_op jit(solution)/shard_map/ppermute | solution.py:216
  67.6 19.9 %collective-permute-start.29 = (bf16[384,896]{1,0:T(8,128)(2,1)S(1)}, bf16[384,896]{1,0:T(8,128)(2,1)S(1)}, u32[]{:S(2)}, u32[]{:S(2)}) collective-permute-start(bf16[384,896]{1,0:T(8,128)(2,1)S(1)} %copy-done), channel_id=1, source_target_pairs={{0,16},{16,0},{1,17},{17,1},{2,18},{18,2},{3,19},{19,3},{4,20},{20... | collective-permute-start | bytes 2064392 | tf_op jit(solution)/shard_map/ppermute | solution.py:222
  68.5 4.1 %collective-permute-start.26 = (bf16[48,4096]{1,0:T(8,128)(2,1)S(1)}, bf16[48,4096]{1,0:T(8,128)(2,1)S(1)}, u32[]{:S(2)}, u32[]{:S(2)}) collective-permute-start(bf16[48,4096]{1,0:T(8,128)(2,1)S(1)} %collective-permute-done.16.refs_1_.refs_13_), channel_id=1, source_target_pairs={{0,4},{4,0},{8,12},{12,8},{1,5},{5,1},{9,13},{13,9},{2,6},{6,2},{1... | collective-permute-start | bytes 1179656 | tf_op jit(solution)/shard_map/ppermute | solution.py:216
  68.9 18.5 %collective-permute-start.22 = (bf16[48,4096]{1,0:T(8,128)(2,1)S(1)}, bf16[48,4096]{1,0:T(8,128)(2,1)}, u32[]{:S(2)}, u32[]{:S(2)}) collective-permute-start(bf16[48,4096]{1,0:T(8,128)(2,1)S(1)} %copy-done.4), channel_id=1, source_target_pairs={{0,1},{1,2},{2,3},{3,0},{4,5},{5,6},{6,7},{7,4},{8,9},{9,10},{10,1... | collective-permute-start | bytes 1179656 | tf_op jit(solution)/shard_map/ppermute | solution.py:211
  70.0 17.5 %collective-permute-start.27 = (bf16[48,4096]{1,0:T(8,128)(2,1)S(1)}, bf16[48,4096]{1,0:T(8,128)(2,1)S(1)}, u32[]{:S(2)}, u32[]{:S(2)}) collective-permute-start(bf16[48,4096]{1,0:T(8,128)(2,1)S(1)} %constant_dynamic-update-slice_fusion.refs_0_.refs_10_), channel_id=1, source_target_pairs={{0,4},{4,0},{8,12},{12,8},{1,5},{5,1},{9,13},{13,9},{2,6},{6,2},{1... | collective-permute-start | bytes 1179656 | tf_op jit(solution)/shard_map/ppermute | solution.py:216
  70.6 16.9 %collective-permute-start.23 = (bf16[48,4096]{1,0:T(8,128)(2,1)}, bf16[48,4096]{1,0:T(8,128)(2,1)S(1)}, u32[]{:S(2)}, u32[]{:S(2)}) collective-permute-start(bf16[48,4096]{1,0:T(8,128)(2,1)} %collective-permute-done.15.refs_6_.refs_16_), channel_id=1, source_target_pairs={{0,8},{4,12},{8,0},{12,4},{1,9},{5,13},{9,1},{13,5},{2,10},{6,14},... | collective-permute-start | bytes 1179656 | tf_op jit(solution)/shard_map/ppermute | solution.py:216
  72.5 14.9 %collective-permute-start.24 = (bf16[32,4096]{1,0:T(8,128)(2,1)S(1)}, bf16[32,4096]{1,0:T(8,128)(2,1)S(1)}, u32[]{:S(2)}, u32[]{:S(2)}) collective-permute-start(bf16[32,4096]{1,0:T(8,128)(2,1)S(1)} %copy-done.48), channel_id=1, source_target_pairs={{0,8},{4,12},{8,0},{12,4},{1,9},{5,13},{9,1},{13,5},{2,10},{6,14},... | collective-permute-start | bytes 786440 | tf_op jit(solution)/shard_map/ppermute | solution.py:216
  87.5 4.0 %collective-permute-start.33 = (bf16[48,4096]{1,0:T(8,128)(2,1)}, bf16[48,4096]{1,0:T(8,128)(2,1)S(1)}, u32[]{:S(2)}, u32[]{:S(2)}) collective-permute-start(bf16[48,4096]{1,0:T(8,128)(2,1)} %collective-permute-done.15.refs_6_.refs_16_), channel_id=1, source_target_pairs={{0,4},{4,0},{8,12},{12,8},{1,5},{5,1},{9,13},{13,9},{2,6},{6,2},{1... | collective-permute-start | bytes 1179656 | tf_op jit(solution)/shard_map/ppermute | solution.py:216
  87.6 4.0 %collective-permute-start.34 = (bf16[48,4096]{1,0:T(8,128)(2,1)S(1)}, bf16[48,4096]{1,0:T(8,128)(2,1)S(1)}, u32[]{:S(2)}, u32[]{:S(2)}) collective-permute-start(bf16[48,4096]{1,0:T(8,128)(2,1)S(1)} %collective-permute-done.23.refs_7_.refs_17_), channel_id=1, source_target_pairs={{0,4},{4,0},{8,12},{12,8},{1,5},{5,1},{9,13},{13,9},{2,6},{6,2},{1... | collective-permute-start | bytes 1179656 | tf_op jit(solution)/shard_map/ppermute | solution.py:216
  88.2 18.3 %collective-permute-start.35 = (bf16[384,896]{1,0:T(8,128)(2,1)}, bf16[384,896]{1,0:T(8,128)(2,1)S(1)}, u32[]{:S(2)}, u32[]{:S(2)}) collective-permute-start(bf16[384,896]{1,0:T(8,128)(2,1)} %shard_map.95), channel_id=1, source_target_pairs={{0,16},{16,0},{1,17},{17,1},{2,18},{18,2},{3,19},{19,3},{4,20},{20... | collective-permute-start | bytes 2064392 | tf_op jit(solution)/shard_map/ppermute | solution.py:222
  89.5 16.2 %collective-permute-start.31 = (bf16[32,4096]{1,0:T(8,128)(2,1)S(1)}, bf16[32,4096]{1,0:T(8,128)(2,1)S(1)}, u32[]{:S(2)}, u32[]{:S(2)}) collective-permute-start(bf16[32,4096]{1,0:T(8,128)(2,1)S(1)} %copy-done.46), channel_id=1, source_target_pairs={{0,8},{4,12},{8,0},{12,4},{1,9},{5,13},{9,1},{13,5},{2,10},{6,14},... | collective-permute-start | bytes 786440 | tf_op jit(solution)/shard_map/ppermute | solution.py:216
  90.2 16.2 %collective-permute-start.30 = (bf16[48,4096]{1,0:T(8,128)(2,1)}, bf16[48,4096]{1,0:T(8,128)(2,1)}, u32[]{:S(2)}, u32[]{:S(2)}) collective-permute-start(bf16[48,4096]{1,0:T(8,128)(2,1)} %collective-permute-done.22.refs_6_), channel_id=1, source_target_pairs={{0,8},{4,12},{8,0},{12,4},{1,9},{5,13},{9,1},{13,5},{2,10},{6,14},... | collective-permute-start | bytes 1179656 | tf_op jit(solution)/shard_map/ppermute | solution.py:216
  107.7 18.1 %collective-permute-start.42 = (bf16[384,896]{1,0:T(8,128)(2,1)S(1)}, bf16[384,896]{1,0:T(8,128)(2,1)}, u32[]{:S(2)}, u32[]{:S(2)}) collective-permute-start(bf16[384,896]{1,0:T(8,128)(2,1)S(1)} %copy-done.17), channel_id=1, source_target_pairs={{0,16},{16,0},{1,17},{17,1},{2,18},{18,2},{3,19},{19,3},{4,20},{20... | collective-permute-start | bytes 2064392 | tf_op jit(solution)/shard_map/ppermute | solution.py:222
  109.0 4.2 %collective-permute-start.40 = (bf16[48,4096]{1,0:T(8,128)(2,1)}, bf16[48,4096]{1,0:T(8,128)(2,1)}, u32[]{:S(2)}, u32[]{:S(2)}) collective-permute-start(bf16[48,4096]{1,0:T(8,128)(2,1)} %collective-permute-done.22.refs_6_), channel_id=1, source_target_pairs={{0,4},{4,0},{8,12},{12,8},{1,5},{5,1},{9,13},{13,9},{2,6},{6,2},{1... | collective-permute-start | bytes 1179656 | tf_op jit(solution)/shard_map/ppermute | solution.py:216
  110.4 15.4 %collective-permute-start.38 = (bf16[96,4096]{1,0:T(8,128)(2,1)}, bf16[96,4096]{1,0:T(8,128)(2,1)S(1)}, u32[]{:S(2)}, u32[]{:S(2)}) collective-permute-start(bf16[96,4096]{1,0:T(8,128)(2,1)} %get-tuple-element.176), channel_id=1, source_target_pairs={{0,4},{4,0},{8,12},{12,8},{1,5},{5,1},{9,13},{13,9},{2,6},{6,2},{1... | collective-permute-start | bytes 2359304 | tf_op jit(solution)/shard_map/ppermute | solution.py:216
  112.5 13.3 %collective-permute-start.37 = (bf16[48,4096]{1,0:T(8,128)(2,1)}, bf16[48,4096]{1,0:T(8,128)(2,1)S(1)}, u32[]{:S(2)}, u32[]{:S(2)}) collective-permute-start(bf16[48,4096]{1,0:T(8,128)(2,1)} %get-tuple-element.262), channel_id=1, source_target_pairs={{0,8},{4,12},{8,0},{12,4},{1,9},{5,13},{9,1},{13,5},{2,10},{6,14},... | collective-permute-start | bytes 1179656 | tf_op jit(solution)/shard_map/ppermute | solution.py:216
  125.9 18.2 %collective-permute-start.46 = (bf16[384,896]{1,0:T(8,128)(2,1)}, bf16[384,896]{1,0:T(8,128)(2,1)}, u32[]{:S(2)}, u32[]{:S(2)}) collective-permute-start(bf16[384,896]{1,0:T(8,128)(2,1)} %get-tuple-element.201), channel_id=1, source_target_pairs={{0,16},{16,0},{1,17},{17,1},{2,18},{18,2},{3,19},{19,3},{4,20},{20... | collective-permute-start | bytes 2064392 | tf_op jit(solution)/shard_map/ppermute | solution.py:222
  128.7 19.6 %collective-permute-start.44 = (bf16[96,4096]{1,0:T(8,128)(2,1)S(1)}, bf16[96,4096]{1,0:T(8,128)(2,1)S(1)}, u32[]{:S(2)}, u32[]{:S(2)}) collective-permute-start(bf16[96,4096]{1,0:T(8,128)(2,1)S(1)} %pad_maximum_fusion), channel_id=1, source_target_pairs={{0,8},{4,12},{8,0},{12,4},{1,9},{5,13},{9,1},{13,5},{2,10},{6,14},... | collective-permute-start | bytes 2359304 | tf_op jit(solution)/shard_map/ppermute | solution.py:216
  130.2 18.2 %collective-permute-start.45 = (bf16[96,4096]{1,0:T(8,128)(2,1)}, bf16[96,4096]{1,0:T(8,128)(2,1)S(1)}, u32[]{:S(2)}, u32[]{:S(2)}) collective-permute-start(bf16[96,4096]{1,0:T(8,128)(2,1)} %get-tuple-element.195), channel_id=1, source_target_pairs={{0,4},{4,0},{8,12},{12,8},{1,5},{5,1},{9,13},{13,9},{2,6},{6,2},{1... | collective-permute-start | bytes 2359304 | tf_op jit(solution)/shard_map/ppermute | solution.py:216
  148.3 4.2 %collective-permute-start.47 = (bf16[96,4096]{1,0:T(8,128)(2,1)}, bf16[96,4096]{1,0:T(8,128)(2,1)S(1)}, u32[]{:S(2)}, u32[]{:S(2)}) collective-permute-start(bf16[96,4096]{1,0:T(8,128)(2,1)} %get-tuple-element.203), channel_id=1, source_target_pairs={{0,4},{4,0},{8,12},{12,8},{1,5},{5,1},{9,13},{13,9},{2,6},{6,2},{1... | collective-permute-start | bytes 2359304 | tf_op jit(solution)/shard_map/ppermute | solution.py:216
  149.4 21.3 %collective-permute-start.51 = (bf16[48,4096]{1,0:T(8,128)(2,1)}, bf16[48,4096]{1,0:T(8,128)(2,1)S(1)}, u32[]{:S(2)}, u32[]{:S(2)}) collective-permute-start(bf16[48,4096]{1,0:T(8,128)(2,1)} %get-tuple-element.251), channel_id=1, source_target_pairs={{0,3},{1,0},{2,1},{3,2},{4,7},{5,4},{6,5},{7,6},{8,11},{9,8},{10,9... | collective-permute-start | bytes 1179656 | tf_op jit(solution)/shard_map/ppermute | solution.py:211
  152.5 18.4 %collective-permute-start.50 = (bf16[48,4096]{1,0:T(8,128)(2,1)S(1)}, bf16[48,4096]{1,0:T(8,128)(2,1)S(1)}, u32[]{:S(2)}, u32[]{:S(2)}) collective-permute-start(bf16[48,4096]{1,0:T(8,128)(2,1)S(1)} %get-tuple-element.252), channel_id=1, source_target_pairs={{0,1},{1,2},{2,3},{3,0},{4,5},{5,6},{6,7},{7,4},{8,9},{9,10},{10,1... | collective-permute-start | bytes 1179656 | tf_op jit(solution)/shard_map/ppermute | solution.py:211
  155.1 19.7 %collective-permute-start.48 = (bf16[96,4096]{1,0:T(8,128)(2,1)S(1)}, bf16[96,4096]{1,0:T(8,128)(2,1)S(1)}, u32[]{:S(2)}, u32[]{:S(2)}) collective-permute-start(bf16[96,4096]{1,0:T(8,128)(2,1)S(1)} %pad_maximum_fusion.1), channel_id=1, source_target_pairs={{0,8},{4,12},{8,0},{12,4},{1,9},{5,13},{9,1},{13,5},{2,10},{6,14},... | collective-permute-start | bytes 2359304 | tf_op jit(solution)/shard_map/ppermute | solution.py:216
  156.6 18.2 %collective-permute-start.49 = (bf16[96,4096]{1,0:T(8,128)(2,1)S(1)}, bf16[96,4096]{1,0:T(8,128)(2,1)S(1)}, u32[]{:S(2)}, u32[]{:S(2)}) collective-permute-start(bf16[96,4096]{1,0:T(8,128)(2,1)S(1)} %copy-done.53), channel_id=1, source_target_pairs={{0,4},{4,0},{8,12},{12,8},{1,5},{5,1},{9,13},{13,9},{2,6},{6,2},{1... | collective-permute-start | bytes 2359304 | tf_op jit(solution)/shard_map/ppermute | solution.py:216
  174.9 4.2 %collective-permute-start.52 = (bf16[96,4096]{1,0:T(8,128)(2,1)}, bf16[96,4096]{1,0:T(8,128)(2,1)S(1)}, u32[]{:S(2)}, u32[]{:S(2)}) collective-permute-start(bf16[96,4096]{1,0:T(8,128)(2,1)} %get-tuple-element.216), channel_id=1, source_target_pairs={{0,4},{4,0},{8,12},{12,8},{1,5},{5,1},{9,13},{13,9},{2,6},{6,2},{1... | collective-permute-start | bytes 2359304 | tf_op jit(solution)/shard_map/ppermute | solution.py:216
  175.2 19.3 %collective-permute-start.56 = (bf16[48,4096]{1,0:T(8,128)(2,1)S(1)}, bf16[48,4096]{1,0:T(8,128)(2,1)S(1)}, u32[]{:S(2)}, u32[]{:S(2)}) collective-permute-start(bf16[48,4096]{1,0:T(8,128)(2,1)S(1)} %get-tuple-element.249), channel_id=1, source_target_pairs={{0,1},{1,2},{2,3},{3,0},{4,5},{5,6},{6,7},{7,4},{8,9},{9,10},{10,1... | collective-permute-start | bytes 1179656 | tf_op jit(solution)/shard_map/ppermute | solution.py:211
  175.3 20.2 %collective-permute-start.55 = (bf16[48,4096]{1,0:T(8,128)(2,1)S(1)}, bf16[48,4096]{1,0:T(8,128)(2,1)S(1)}, u32[]{:S(2)}, u32[]{:S(2)}) collective-permute-start(bf16[48,4096]{1,0:T(8,128)(2,1)S(1)} %get-tuple-element.250), channel_id=1, source_target_pairs={{0,3},{1,0},{2,1},{3,2},{4,7},{5,4},{6,5},{7,6},{8,11},{9,8},{10,9... | collective-permute-start | bytes 1179656 | tf_op jit(solution)/shard_map/ppermute | solution.py:211
  179.3 16.2 %collective-permute-start.54 = (bf16[96,4096]{1,0:T(8,128)(2,1)}, bf16[96,4096]{1,0:T(8,128)(2,1)S(1)}, u32[]{:S(2)}, u32[]{:S(2)}) collective-permute-start(bf16[96,4096]{1,0:T(8,128)(2,1)} %get-tuple-element.218), channel_id=1, source_target_pairs={{0,4},{4,0},{8,12},{12,8},{1,5},{5,1},{9,13},{13,9},{2,6},{6,2},{1... | collective-permute-start | bytes 2359304 | tf_op jit(solution)/shard_map/ppermute | solution.py:216
  179.8 15.7 %collective-permute-start.53 = (bf16[48,4096]{1,0:T(8,128)(2,1)S(1)}, bf16[48,4096]{1,0:T(8,128)(2,1)S(1)}, u32[]{:S(2)}, u32[]{:S(2)}) collective-permute-start(bf16[48,4096]{1,0:T(8,128)(2,1)S(1)} %get-tuple-element.256), channel_id=1, source_target_pairs={{0,8},{4,12},{8,0},{12,4},{1,9},{5,13},{9,1},{13,5},{2,10},{6,14},... | collective-permute-start | bytes 1179656 | tf_op jit(solution)/shard_map/ppermute | solution.py:216
  195.8 23.1 %collective-permute-start.58 = (bf16[96,4096]{1,0:T(8,128)(2,1)S(1)}, bf16[96,4096]{1,0:T(8,128)(2,1)S(1)}, u32[]{:S(2)}, u32[]{:S(2)}) collective-permute-start(bf16[96,4096]{1,0:T(8,128)(2,1)S(1)} %pad_maximum_fusion.3), channel_id=1, source_target_pairs={{0,3},{1,0},{2,1},{3,2},{4,7},{5,4},{6,5},{7,6},{8,11},{9,8},{10,9... | collective-permute-start | bytes 2359304 | tf_op jit(solution)/shard_map/ppermute | solution.py:211
  199.6 19.3 %collective-permute-start.57 = (bf16[96,4096]{1,0:T(8,128)(2,1)S(1)}, bf16[96,4096]{1,0:T(8,128)(2,1)S(1)}, u32[]{:S(2)}, u32[]{:S(2)}) collective-permute-start(bf16[96,4096]{1,0:T(8,128)(2,1)S(1)} %pad_maximum_fusion.2), channel_id=1, source_target_pairs={{0,8},{4,12},{8,0},{12,4},{1,9},{5,13},{9,1},{13,5},{2,10},{6,14},... | collective-permute-start | bytes 2359304 | tf_op jit(solution)/shard_map/ppermute | solution.py:216
  (65 other events, 382.8 us)

commit v11 on v10

--- a/solution.py
+++ b/solution.py
@@ -57,17 +57,29 @@
 def contract(pieces, weights):
     width = pieces[0].shape[1]
     units = weights[0].shape[1]
-    block = min(1024, width)
-    weight_spec = pl.BlockSpec((block, units), lambda k: (k, 0))
+    block = min(512, width)
+    deep = pl.Buffered(4)
     rows = sum(piece.shape[0] for piece in pieces)
-    shape = (rows * len(weights), units)
+    out = jax.ShapeDtypeStruct((rows * len(weights), units), jnp.bfloat16)
+    n_ins = len(pieces) + len(weights)
+
+    def kernel(*refs):
+        pltpu.emit_pipeline(
+            lambda *blocks: contract_kernel(len(pieces), len(weights), *blocks, refs[-1]),
+            grid=(width // block,),
+            in_specs=[
+                pl.BlockSpec((piece.shape[0], block), lambda k: (0, k), pipeline_mode=deep)
+                for piece in pieces
+            ]
+            + [pl.BlockSpec((block, units), lambda k: (k, 0), pipeline_mode=deep)] * len(weights),
+            out_specs=[pl.BlockSpec(out.shape, lambda k: (0, 0))],
+        )(*refs[:-1])
+
     return pl.pallas_call(
-        functools.partial(contract_kernel, len(pieces), len(weights)),
-        grid=(width // block,),
-        in_specs=[pl.BlockSpec((piece.shape[0], block), lambda k: (0, k)) for piece in pieces]
-        + [weight_spec] * len(weights),
-        out_specs=pl.BlockSpec(shape, lambda k: (0, 0)),
-        out_shape=jax.ShapeDtypeStruct(shape, jnp.bfloat16),
+        kernel,
+        in_specs=[pl.BlockSpec(memory_space=pl.ANY)] * n_ins,
+        out_specs=pl.BlockSpec(memory_space=pl.ANY),
+        out_shape=out,
         scratch_shapes=[pltpu.VMEM((rows, units * len(weights)), jnp.float32)],
         compiler_params=pltpu.CompilerParams(vmem_limit_bytes=VMEM_BYTES),
         cost_estimate=cost(2 * len(weights) * rows * width * units, *pieces, *weights),
@@ -130,7 +142,7 @@
 
 def down_products(pieces, hiddens, weight):
     units, width = weight.shape
-    block = min(512, width)
+    block = min(1024, width)
     rows = sum(piece.shape[0] for piece in pieces)
     half = hiddens[0].shape[0]
     grad = jax.ShapeDtypeStruct((rows, units), jnp.bfloat16)
@@ -224,8 +236,8 @@
     ]
 
 
-def row_sum(partial, moved, *others):
-    return sum([wide(after(block, *others)) for block in moved], wide(partial))
+def row_sum(partial, moved):
+    return sum([wide(block) for block in moved], wide(partial))
 
 
 def add(*blocks):
@@ -270,6 +282,14 @@
 
 def body(tokens, gate_weight, up_weight, down_weight, cotangent):
     pair = [gate_weight, up_weight]
+
+    def half_sums(partial, moved, *others):
+        half = partial.shape[0] // 2
+        moved = [after(block, *others) for block in moved]
+        return [
+            row_sum(partial[at], [block[at] for block in moved])
+            for at in (slice(0, half), slice(half, 2 * half))
+        ]
 
     def pair_sums(partial, moved):
         half = partial.shape[0] // 2
@@ -301,30 +321,30 @@
         near2, tail3, far3, far_head0, pair1, *pair0_moved
     )
 
-    gate0, up0 = pair_sums(pair0, pair0_moved)
+    gate0, up0 = half_sums(pair0, pair0_moved)
     hidden0 = hidden_of(gate0, up0)
     pair1_moved = row_moves(pair1)
     cot_near3 = jnp.concatenate([head3, tail3], axis=0)
     cot_near2 = shift(cot_near3, 3)
-    far2, far_head3 = swap(near2, CHIP), swap(after(head3, pair1), CHIP)
+    far2, far_tail3 = swap(near2, CHIP), swap(after(tail3, pair1), CHIP)
     token3 = quad([near3], [far3], other_cores([after(near3, pair1), far3]))
     pair3 = contract(token3, pair)
     far_head0_core = swap(after(far_head0, pair1), CORE)
-    cot_near2, far2, far_head3, pair3, far_head0_core, *pair1_moved = sync(
-        cot_near2, far2, far_head3, pair3, far_head0_core, *pair1_moved
-    )
-
-    gate1, up1 = pair_sums(pair1, pair1_moved)
+    cot_near2, far2, far_tail3, pair3, far_head0_core, *pair1_moved = sync(
+        cot_near2, far2, far_tail3, pair3, far_head0_core, *pair1_moved
+    )
+
+    gate1, up1 = half_sums(pair1, pair1_moved)
     hidden1 = hidden_of(gate1, up1)
     pair3_moved = row_moves(pair3)
     cot = after(cotangent, pair3)
     cot_near1 = shift(cot, 1)
-    cot_far2, far_tail3 = swap(cot_near2, CHIP), swap(after(tail3, pair3), CHIP)
+    cot_far2, far_head3 = swap(cot_near2, CHIP), swap(after(head3, pair3), CHIP)
     token2 = quad([near2], [far2], other_cores([after(near2, pair3), far2]))
     pair2 = contract(token2, pair)
-    core3, far_head3_core = other_cores(after(x, pair3) for x in (cot_near3, far_head3))
-    cot_near1, cot_far2, far_tail3, pair2, core3, far_head3_core, hidden0, hidden1, *rest = sync(
-        cot_near1, cot_far2, far_tail3, pair2, core3, far_head3_core, hidden0, hidden1, *pair3_moved
+    core3, far_tail3_core = other_cores(after(x, pair3) for x in (cot_near3, far_tail3))
+    cot_near1, cot_far2, far_head3, pair2, core3, far_tail3_core, hidden0, hidden1, *rest = sync(
+        cot_near1, cot_far2, far_head3, pair2, core3, far_tail3_core, hidden0, hidden1, *pair3_moved
     )
     pair3_moved = rest
 
@@ -332,8 +352,8 @@
     hidden3 = hidden_of(gate3, up3)
     pair2_moved = row_moves(pair2)
     cot_far1, far_tail0 = swap(cot_near1, CHIP), swap(after(cot_tail, pair2), CHIP)
-    cot_far3 = [after(far_head3, pair2), far_tail3]
-    cot3 = quad([cot_near3], cot_far3, [core3, far_head3_core, swap(far_tail3, CORE)])
+    cot_far3 = [far_head3, far_tail3]
+    cot3 = quad([cot_near3], cot_far3, [core3, swap(far_head3, CORE), far_tail3_core])
     cot2 = quad([cot_near2], [cot_far2], other_cores([after(cot_near2, pair2), cot_far2]))
     products = down_products(cot3 + cot2, [hidden0, hidden1], down_weight)
     cot_far1, far_tail0, grad_b, *rest = sync(cot_far1, far_tail0, *products, *pair2_moved)
@@ -356,22 +376,19 @@
     grad_a_moved = row_moves(grad_a)
     sent, mixed_b = chip_part(parts)
     mixed_b_moved = swap(jnp.concatenate(sent, axis=0), CHIP)
-    grad_b = row_sum(grad_b, grad_b_moved)
-    half = grad_b.shape[0] // 2
-    grads3 = grads_of(gate3, up3, grad_b[:half])
-    grads2 = grads_of(gate2, up2, grad_b[half:])
+    grad3, grad2 = half_sums(grad_b, grad_b_moved)
+    grads3, grads2 = grads_of(gate3, up3, grad3), grads_of(gate2, up2, grad2)
     parts = expand([[x, y] for x, y in zip(grads3, grads2)], pair)
     mixed_b_moved, mixed_b[1], *rest = sync(mixed_b_moved, mixed_b[1], *parts, *grad_a_moved)
     parts, grad_a_moved = rest[:4], rest[4:]
 
     sent, token_grad_b = chip_part(parts)
     token_b_moved = swap(jnp.concatenate(sent, axis=0), CHIP)
-    grad_a = row_sum(grad_a, grad_a_moved, *sent)
+    grad0, grad1 = half_sums(grad_a, grad_a_moved, *sent)
     size = tokens.shape[0]
     mixed_part3 = shift(narrow(block_sum(mixed_b, 0, mixed_b_moved[:size])), 1)
     mixed_part2 = shift(narrow(block_sum(mixed_b, 1, mixed_b_moved[size:])), -1)
-    grads0 = grads_of(gate0, up0, grad_a[:half])
-    grads1 = grads_of(gate1, up1, grad_a[half:])
+    grads0, grads1 = grads_of(gate0, up0, grad0), grads_of(gate1, up1, grad1)
     parts = expand([[x, y] for x, y in zip(grads0, grads1)], pair)
     token_b_moved, token_grad_b[1], mixed_part3, mixed_part2, *parts = sync(
         token_b_moved, token_grad_b[1], mixed_part3, mixed_part2, *parts

time: 223 us -> 223 us (level)
  Pallas kernels: 116 us -> 108 us
  other arithmetic: 14.8 us -> 19.1 us
  waiting for transfers between devices: 30.2 us -> 33.6 us
    convert_element_type x11 -> x13, other arithmetic: 9.44 us -> 15.6 us  [narrow(): return block.astype(jnp.bfloat16)]
    ppermute x41, waiting for transfers between devices: 16.3 us -> 21.3 us  [swap(): return lax.ppermute(block, 'col', [(i, i ^ bit) for i in range(n)])]
    pallas_call x4, Pallas kernels: 34.7 us -> 29.8 us  [contract(): pl.pallas_call(kernel, in_specs=[pl.BlockSpec(memory_space=pl.ANY)] * n_i...]
    pallas_call x2, Pallas kernels: 25.3 us -> 22.2 us  [down_products(): pl.pallas_call(functools.partial(down_kernel, len(pieces)), grid=(width /...]
    add x6 -> x2, other arithmetic: 3.09 us -> 0.27 us  [row_sum(): return sum([wide(block) for block in moved], wide(partial))]
    ppermute x41, starting transfers between devices: 21.4 us -> 24.1 us  [swap(): return lax.ppermute(block, 'col', [(i, i ^ bit) for i in range(n)])]
    ppermute x12, starting transfers between devices: 23.4 us -> 21 us  [shift(): return lax.ppermute(block, 'depth', [(i, (i + step) % n) for i in range(n)])]
    unnamed x109 -> x119, local copies, waits for them, and re-layouts: 5.63 us -> 4.93 us
  transfers between devices with their start and end apart: 59 -> 59, of which waited for: 13 -> 13; matrix products, arithmetic and copies ran while one was open for 7% -> 9% of each run, Pallas kernels for 52% -> 49%
where the time goes in v11:
time: 223 us; the launch traced here: 221 us
  Pallas kernels  108 us (48%)
  starting transfers between devices  51.3 us (23%)
  waiting for transfers between devices  33.6 us (15%)
  other arithmetic  19.1 us (9%)
  local copies, waits for them, and re-layouts  7.54 us (3%)
    pallas_call x4, Pallas kernels, contract(): pl.pallas_call(kernel, in_specs=[pl.BlockSpec(memory_space=pl.ANY)] * n_i...  29.8 us
    pallas_call x2, Pallas kernels, expand(): pl.pallas_call(functools.partial(expand_kernel, len(lefts)), grid=(width...  24.6 us
    ppermute x41, starting transfers between devices, swap(): return lax.ppermute(block, 'col', [(i, i ^ bit) for i in range(n)])  24.1 us
    pallas_call x2, Pallas kernels, down_products(): pl.pallas_call(functools.partial(down_kernel, len(pieces)), grid=(width /...  22.2 us
    ppermute x41, waiting for transfers between devices, swap(): return lax.ppermute(block, 'col', [(i, i ^ bit) for i in range(n)])  21.3 us
    ppermute x12, starting transfers between devices, shift(): return lax.ppermute(block, 'depth', [(i, (i + step) % n) for i in range(n)])  21 us
    pallas_call x1, Pallas kernels, wide_grads(): pl.pallas_call(functools.partial(wide_grad_kernel, len(pieces)), grid=(wi...  17.8 us
    convert_element_type x13, other arithmetic, narrow(): return block.astype(jnp.bfloat16)  15.6 us
  transfers between devices with their start and end apart: 59, of which 13 were waited for; matrix products, arithmetic and copies ran while one was open for 9% of the time, Pallas kernels for 49%

profile of v11, /device:TPU:0, one launch (start us, length us, event | category | flops | bytes accessed | tf_op | source)
XLA Modules:
  0.0 220.5 jit_solution(7702478648691339145)
XLA Ops:
  0.6 3.1 %collective-permute-start.1 = (bf16[48,4096]{1,0:T(8,128)(2,1)}, bf16[48,4096]{1,0:T(8,128)(2,1)S(1)}, u32[]{:S(2)}, u32[]{:S(2)}) collective-permute-start(bf16[48,4096]{1,0:T(8,128)(2,1)} %refs_0_.6), channel_id=1, source_target_pairs={{0,1},{1,2},{2,3},{3,0},{4,5},{5,6},{6,7},{7,4},{8,9},{9,10},{10,1... | collective-permute-start | bytes 1179656 | tf_op jit(solution)/shard_map/ppermute | solution.py:223
  3.7 1.5 collective-permute-start
  6.1 1.7 slice.187
  7.8 7.2 %collective-permute-done.1.refs_0_.refs_4_ = bf16[48,4096]{1,0:T(8,128)(2,1)S(1)} collective-permute-done((bf16[48,4096]{1,0:T(8,128)(2,1)}, bf16[48,4096]{1,0:T(8,128)(2,1)S(1)}, u32[]{:S(2)}, u32[]{:S(2)}) %collective-permute-start.1) | collective-permute-done | bytes 393248 | tf_op jit(solution)/shard_map/ppermute | solution.py:223
  15.6 1.7 collective-permute-start.4
  17.4 1.5 collective-permute-start.3
  18.9 1.7 collective-permute-start.5
  21.3 7.5 %shard_map.92 = bf16[384,896]{1,0:T(8,128)(2,1)} custom-call(bf16[48,4096]{1,0:T(8,128)(2,1)} %refs_0_.6, bf16[48,4096]{1,0:T(8,128)(2,1)} %copy-done.23, bf16[48,4096]{1,0:T(8,128)(2,1)} %copy-done.24, bf16[48,4096]{1,0:T(8,128)(2,1)} %copy-done.25, bf16[4096,896]{1,0:T(8,128)(2,1)} %refs_4_.11, bf16[4096,896]{1,0:T(8,128)(2,1)} %refs_5_.11), custom_call_target="tpu_custom_call" | custom-call | flops 2818572288 | bytes 16252928 | tf_op jit(solution)/shard_map/pallas_call | solution.py:78
  29.8 1.6 collective-permute-start.14
  32.3 1.5 collective-permute-start.11
  34.4 2.9 %collective-permute-start.10 = (bf16[32,4096]{1,0:T(8,128)(2,1)}, bf16[32,4096]{1,0:T(8,128)(2,1)S(1)}, u32[]{:S(2)}, u32[]{:S(2)}) collective-permute-start(bf16[32,4096]{1,0:T(8,128)(2,1)} %slice.187), channel_id=1, source_target_pairs={{0,3},{1,0},{2,1},{3,2},{4,7},{5,4},{6,5},{7,6},{8,11},{9,8},{10,9... | collective-permute-start | bytes 786440 | tf_op jit(solution)/shard_map/ppermute | solution.py:223
  37.3 7.5 %shard_map.93 = bf16[384,896]{1,0:T(8,128)(2,1)} custom-call(bf16[48,4096]{1,0:T(8,128)(2,1)} %copy-done.22, bf16[48,4096]{1,0:T(8,128)(2,1)} %copy-done.28, bf16[48,4096]{1,0:T(8,128)(2,1)} %copy-done.27, bf16[48,4096]{1,0:T(8,128)(2,1)} %copy-done.30, bf16[4096,896]{1,0:T(8,128)(2,1)} %refs_4_.11, bf16[4096,896]{1,0:T(8,128)(2,1)} %refs_5_.11), custom_call_target="tpu_custom_call" | custom-call | flops 2818572288 | bytes 16252928 | tf_op jit(solution)/shard_map/pallas_call | solution.py:78
  44.8 1.9 collective-permute-done.12.refs_1_
  46.6 2.1 collective-permute-done.10
  50.0 2.3 %collective-permute-start.15 = (bf16[48,4096]{1,0:T(8,128)(2,1)S(1)}, bf16[48,4096]{1,0:T(8,128)(2,1)S(1)}, u32[]{:S(2)}, u32[]{:S(2)}) collective-permute-start(bf16[48,4096]{1,0:T(8,128)(2,1)S(1)} %constant_dynamic-update-slice_fusion.refs_0_.refs_10_), channel_id=1, source_target_pairs={{0,3},{1,0},{2,1},{3,2},{4,7},{5,4},{6,5},{7,6},{8,11},{9,8},{10,9... | collective-permute-start | bytes 1179656 | tf_op jit(solution)/shard_map/ppermute | solution.py:223
  52.3 1.5 collective-permute-start.16
  54.7 7.5 %shard_map.94 = bf16[384,896]{1,0:T(8,128)(2,1)} custom-call(bf16[48,4096]{1,0:T(8,128)(2,1)} %copy-done.26, bf16[48,4096]{1,0:T(8,128)(2,1)} %copy-done.31, bf16[48,4096]{1,0:T(8,128)(2,1)} %copy-done.32, bf16[48,4096]{1,0:T(8,128)(2,1)} %copy-done.33, bf16[4096,896]{1,0:T(8,128)(2,1)} %refs_4_.11, bf16[4096,896]{1,0:T(8,128)(2,1)} %refs_5_.11), custom_call_target="tpu_custom_call" | custom-call | flops 2818572288 | bytes 16252928 | tf_op jit(solution)/shard_map/pallas_call | solution.py:78
  62.2 6.5 %collective-permute-done.17.refs_2_.refs_12_ = bf16[32,4096]{1,0:T(8,128)(2,1)S(1)} collective-permute-done((bf16[32,4096]{1,0:T(8,128)(2,1)S(1)}, bf16[32,4096]{1,0:T(8,128)(2,1)S(1)}, u32[]{:S(2)}, u32[]{:S(2)}) %collective-permute-start.17) | collective-permute-done | bytes 262176 | tf_op jit(solution)/shard_map/ppermute | solution.py:228
  69.8 1.5 collective-permute-start.24
  72.6 2.7 %collective-permute-done.24.refs_1_.refs_11_ = bf16[16,4096]{1,0:T(8,128)(2,1)S(1)} collective-permute-done((bf16[16,4096]{1,0:T(8,128)(2,1)S(1)}, bf16[16,4096]{1,0:T(8,128)(2,1)S(1)}, u32[]{:S(2)}, u32[]{:S(2)}) %collective-permute-start.24) | collective-permute-done | bytes 131104 | tf_op jit(solution)/shard_map/ppermute | solution.py:228
  75.4 1.6 collective-permute-start.23
  78.7 7.5 %shard_map.95 = bf16[384,896]{1,0:T(8,128)(2,1)} custom-call(bf16[48,4096]{1,0:T(8,128)(2,1)} %copy-done.29, bf16[48,4096]{1,0:T(8,128)(2,1)} %copy-done.34, bf16[48,4096]{1,0:T(8,128)(2,1)} %copy-done.35, bf16[48,4096]{1,0:T(8,128)(2,1)} %copy-done.36, bf16[4096,896]{1,0:T(8,128)(2,1)} %refs_4_.11, bf16[4096,896]{1,0:T(8,128)(2,1)} %refs_5_.11), custom_call_target="tpu_custom_call" | custom-call | flops 2818572288 | bytes 16252928 | tf_op jit(solution)/shard_map/pallas_call | solution.py:78
  88.6 1.5 collective-permute-start.31
  90.1 1.3 collective-permute-start.30
  93.0 11.1 %shard_map.96 = (bf16[384,896]{1,0:T(8,128)(2,1)}, bf16[96,4096]{1,0:T(8,128)(2,1)}, bf16[96,4096]{1,0:T(8,128)(2,1)}, bf16[96,4096]{1,0:T(8,128)(2,1)}, bf16[96,4096]{1,0:T(8,128)(2,1)}) custom-call(bf16[48,4096]{1,0:T(8,128)(2,1)} %copy-done.14, bf16[16,4096]{1,0:T(8,128)(2,1)} %copy-done.56, bf16[32,4096]{1,0:T(8,128)(2,1)} %copy-done.49, ...), custom_call_target="tpu_custom_call" | custom-call | flops 5637144576 | bytes 14319616 | tf_op jit(solution)/shard_map/pallas_call | solution.py:150
  104.1 1.8 collective-permute-done.30.refs_7_
  112.0 1.5 collective-permute-start.37
  114.3 11.1 %shard_map.97 = (bf16[384,896]{1,0:T(8,128)(2,1)}, bf16[96,4096]{1,0:T(8,128)(2,1)}, bf16[96,4096]{1,0:T(8,128)(2,1)}, bf16[96,4096]{1,0:T(8,128)(2,1)}, bf16[96,4096]{1,0:T(8,128)(2,1)}) custom-call(bf16[48,4096]{1,0:T(8,128)(2,1)} %refs_0_.5, bf16[16,4096]{1,0:T(8,128)(2,1)} %copy-done.54, bf16[32,4096]{1,0:T(8,128)(2,1)} %copy-done.51, ...), custom_call_target="tpu_custom_call" | custom-call | flops 5637144576 | bytes 14319616 | tf_op jit(solution)/shard_map/pallas_call | solution.py:150
  126.9 1.5 collective-permute-done.43
  128.4 1.3 add_convert_fusion.11
  129.8 1.6 collective-permute-start.44
  131.4 2.8 %multiply_convert_fusion.4 = (bf16[192,896]{1,0:T(8,128)(2,1)}, bf16[192,896]{1,0:T(8,128)(2,1)}, bf16[192,896]{1,0:T(8,128)(2,1)}, bf16[192,896]{1,0:T(8,128)(2,1)}) fusion(bf16[384,896]{1,0:T(8,128)(2,1)} %collective-permute-done.42, bf16[384,896]{1,0:T(8,128)(2,1)S(1)} %copy-done.16, f32[384,896]{1,0:T(8,128)S(1)} %convert_add_fusion, ...), kind=kLoop, calls=%fused_computation.28 | loop fusion | flops 5505024 | bytes 5505024 | tf_op jit(solution)/shard_map/convert_element_type | solution.py:29
  134.2 12.3 %shard_map.98 = (bf16[96,4096]{1,0:T(8,128)(2,1)}, bf16[96,4096]{1,0:T(8,128)(2,1)}, bf16[96,4096]{1,0:T(8,128)(2,1)}, bf16[96,4096]{1,0:T(8,128)(2,1)}) custom-call(bf16[192,896]{1,0:T(8,128)(2,1)} %get-tuple-element.261.refs_0_.refs_18_, bf16[192,896]{1,0:T(8,128)(2,1)} %get-tuple-element.244.refs_1_.refs_19_, ...), custom_call_target="tpu_custom_call" | custom-call | flops 5637144576 | bytes 19202048 | tf_op jit(solution)/shard_map/pallas_call | solution.py:113
  146.5 3.0 %collective-permute-done.44 = bf16[96,4096]{1,0:T(8,128)(2,1)S(1)} collective-permute-done((bf16[96,4096]{1,0:T(8,128)(2,1)S(1)}, bf16[96,4096]{1,0:T(8,128)(2,1)S(1)}, u32[]{:S(2)}, u32[]{:S(2)}) %collective-permute-start.44) | collective-permute-done | bytes 786464 | tf_op jit(solution)/shard_map/ppermute | solution.py:228
  149.4 1.2 add_convert_fusion.6
  152.9 2.4 %multiply_convert_fusion.1 = (bf16[192,896]{1,0:T(8,128)(2,1)}, bf16[192,896]{1,0:T(8,128)(2,1)}) fusion(bf16[384,896]{1,0:T(8,128)(2,1)} %collective-permute-done.46, bf16[384,896]{1,0:T(8,128)(2,1)S(1)} %copy-done.17, bf16[384,896]{1,0:T(8,128)(2,1)S(1)} %collective-permute-done.14, bf16[384,896]{1,0:T(8,128)(2,1)S(1)} %copy-done), kind=kLoop, calls=%fused_computation.23 | loop fusion | flops 3784704 | bytes 2752512 | tf_op jit(solution)/shard_map/convert_element_type | solution.py:29
  155.4 1.5 collective-permute-start.48
  156.9 2.3 %multiply_convert_fusion = (bf16[192,896]{1,0:T(8,128)(2,1)}, bf16[192,896]{1,0:T(8,128)(2,1)}) fusion(bf16[384,896]{1,0:T(8,128)(2,1)} %collective-permute-done.46, bf16[384,896]{1,0:T(8,128)(2,1)S(1)} %copy-done.17, bf16[384,896]{1,0:T(8,128)(2,1)S(1)} %collective-permute-done.21, bf16[384,896]{1,0:T(8,128)(2,1)S(1)} %copy-done.1), kind=kLoop, calls=%fused_computation.22 | loop fusion | flops 3784704 | bytes 2752512 | tf_op jit(solution)/shard_map/convert_element_type | solution.py:29
  159.2 12.3 %shard_map.99 = (bf16[96,4096]{1,0:T(8,128)(2,1)}, bf16[96,4096]{1,0:T(8,128)(2,1)}, bf16[96,4096]{1,0:T(8,128)(2,1)}, bf16[96,4096]{1,0:T(8,128)(2,1)}) custom-call(bf16[192,896]{1,0:T(8,128)(2,1)} %get-tuple-element.242.refs_0_.refs_16_, bf16[192,896]{1,0:T(8,128)(2,1)} %get-tuple-element.240.refs_1_.refs_17_, ...), custom_call_target="tpu_custom_call" | custom-call | flops 5637144576 | bytes 19202048 | tf_op jit(solution)/shard_map/pallas_call | solution.py:113
  171.6 3.2 %collective-permute-done.48 = bf16[96,4096]{1,0:T(8,128)(2,1)S(1)} collective-permute-done((bf16[96,4096]{1,0:T(8,128)(2,1)S(1)}, bf16[96,4096]{1,0:T(8,128)(2,1)S(1)}, u32[]{:S(2)}, u32[]{:S(2)}) %collective-permute-start.48) | collective-permute-done | bytes 786464 | tf_op jit(solution)/shard_map/ppermute | solution.py:228
  176.3 2.7 %collective-permute-start.55 = (bf16[48,4096]{1,0:T(8,128)(2,1)S(1)}, bf16[48,4096]{1,0:T(8,128)(2,1)S(1)}, u32[]{:S(2)}, u32[]{:S(2)}) collective-permute-start(bf16[48,4096]{1,0:T(8,128)(2,1)S(1)} %get-tuple-element.248), channel_id=1, source_target_pairs={{0,3},{1,0},{2,1},{3,2},{4,7},{5,4},{6,5},{7,6},{8,11},{9,8},{10,9... | collective-permute-start | bytes 1179656 | tf_op jit(solution)/shard_map/ppermute | solution.py:223
  179.5 1.6 collective-permute-start.53
  181.1 13.2 %shard_map.100 = f32[896,4096]{1,0:T(8,128)} custom-call(bf16[48,4096]{1,0:T(8,128)(2,1)} %refs_0_.5, bf16[16,4096]{1,0:T(8,128)(2,1)} %copy-done.54, bf16[32,4096]{1,0:T(8,128)(2,1)} %copy-done.51, bf16[48,4096]{1,0:T(8,128)(2,1)} %collective-permute-done.2.refs_3_, bf16[16,4096]{1,0:T(8,128)(2,1)} %copy-done.55, bf16[32,4096]{1,0:T(8,128)(2,1)} %copy-done.53, ...), custom_call_target="tpu_custom_call" | custom-call | flops 5637144576 | bytes 22347776 | tf_op jit(solution)/shard_map/pallas_call | solution.py:209
  194.3 1.6 collective-permute-done.55
  196.2 2.1 collective-permute-start.58
  198.4 1.6 collective-permute-start.57
  200.0 17.8 %shard_map.101 = (f32[4096,896]{1,0:T(8,128)}, f32[4096,896]{1,0:T(8,128)}) custom-call(bf16[48,4096]{1,0:T(8,128)(2,1)} %refs_0_.6, bf16[48,4096]{1,0:T(8,128)(2,1)} %copy-done.23, bf16[48,4096]{1,0:T(8,128)(2,1)} %copy-done.24, bf16[48,4096]{1,0:T(8,128)(2,1)} %copy-done.25, bf16[48,4096]{1,0:T(8,128)(2,1)} %copy-done.22, bf16[48,4096]{1,0:T(8,128)(2,1)} %copy-done.28, ...), custom_call_target="tpu_custom_call" | custom-call | flops 11274289152 | bytes 38404096 | tf_op jit(solution)/shard_map/pallas_call | solution.py:185
  217.8 2.7 %convert_add_fusion.2 = (f32[48,4096]{1,0:T(8,128)}, f32[48,4096]{1,0:T(8,128)}) fusion(bf16[48,4096]{1,0:T(8,128)(2,1)} %collective-permute-done.56, bf16[96,4096]{1,0:T(8,128)(2,1)S(1)} %collective-permute-done.58, bf16[96,4096]{1,0:T(8,128)(2,1)S(1)} %collective-permute-done.57, bf16[96,4096]{1,0:T(8,128)(2,1)S(1)} %collective-permute-done.54, ...), kind=kLoop, calls=%fused_computation.6 | loop fusion | flops 3538944 | bytes 5505024 | tf_op jit(solution)/shard_map/add | solution.py:276
  (224 shorter events, 27.6 us)
Async XLA Ops:
  0.6 14.4 %collective-permute-start.1 = (bf16[48,4096]{1,0:T(8,128)(2,1)}, bf16[48,4096]{1,0:T(8,128)(2,1)S(1)}, u32[]{:S(2)}, u32[]{:S(2)}) collective-permute-start(bf16[48,4096]{1,0:T(8,128)(2,1)} %refs_0_.6), channel_id=1, source_target_pairs={{0,1},{1,2},{2,3},{3,0},{4,5},{5,6},{6,7},{7,4},{8,9},{9,10},{10,1... | collective-permute-start | bytes 1179656 | tf_op jit(solution)/shard_map/ppermute | solution.py:223
  3.7 11.4 %collective-permute-start = (bf16[48,4096]{1,0:T(8,128)(2,1)}, bf16[48,4096]{1,0:T(8,128)(2,1)S(1)}, u32[]{:S(2)}, u32[]{:S(2)}) collective-permute-start(bf16[48,4096]{1,0:T(8,128)(2,1)} %refs_0_.6), channel_id=1, source_target_pairs={{0,8},{4,12},{8,0},{12,4},{1,9},{5,13},{9,1},{13,5},{2,10},{6,14},... | collective-permute-start | bytes 1179656 | tf_op jit(solution)/shard_map/ppermute | solution.py:228
  5.2 9.8 %collective-permute-start.2 = (bf16[48,4096]{1,0:T(8,128)(2,1)}, bf16[48,4096]{1,0:T(8,128)(2,1)}, u32[]{:S(2)}, u32[]{:S(2)}) collective-permute-start(bf16[48,4096]{1,0:T(8,128)(2,1)} %refs_0_.5), channel_id=1, source_target_pairs={{0,4},{4,0},{8,12},{12,8},{1,5},{5,1},{9,13},{13,9},{2,6},{6,2},{1... | collective-permute-start | bytes 1179656 | tf_op jit(solution)/shard_map/ppermute | solution.py:228
  15.2 5.4 %collective-permute-start.8 = (bf16[48,4096]{1,0:T(8,128)(2,1)S(1)}, bf16[48,4096]{1,0:T(8,128)(2,1)S(1)}, u32[]{:S(2)}, u32[]{:S(2)}) collective-permute-start(bf16[48,4096]{1,0:T(8,128)(2,1)S(1)} %collective-permute-done.refs_1_), channel_id=1, source_target_pairs={{0,4},{4,0},{8,12},{12,8},{1,5},{5,1},{9,13},{13,9},{2,6},{6,2},{1... | collective-permute-start | bytes 1179656 | tf_op jit(solution)/shard_map/ppermute | solution.py:228
  15.6 14.1 %collective-permute-start.4 = (bf16[48,4096]{1,0:T(8,128)(2,1)}, bf16[48,4096]{1,0:T(8,128)(2,1)S(1)}, u32[]{:S(2)}, u32[]{:S(2)}) collective-permute-start(bf16[48,4096]{1,0:T(8,128)(2,1)} %refs_0_.6), channel_id=1, source_target_pairs={{0,3},{1,0},{2,1},{3,2},{4,7},{5,4},{6,5},{7,6},{8,11},{9,8},{10,9... | collective-permute-start | bytes 1179656 | tf_op jit(solution)/shard_map/ppermute | solution.py:223
  17.4 12.4 %collective-permute-start.6 = (bf16[48,4096]{1,0:T(8,128)(2,1)S(1)}, bf16[48,4096]{1,0:T(8,128)(2,1)S(1)}, u32[]{:S(2)}, u32[]{:S(2)}) collective-permute-start(bf16[48,4096]{1,0:T(8,128)(2,1)S(1)} %collective-permute-done.1.refs_0_.refs_4_), channel_id=1, source_target_pairs={{0,4},{4,0},{8,12},{12,8},{1,5},{5,1},{9,13},{13,9},{2,6},{6,2},{1... | collective-permute-start | bytes 1179656 | tf_op jit(solution)/shard_map/ppermute | solution.py:228
  17.4 12.4 %collective-permute-start.3 = (bf16[48,4096]{1,0:T(8,128)(2,1)S(1)}, bf16[48,4096]{1,0:T(8,128)(2,1)S(1)}, u32[]{:S(2)}, u32[]{:S(2)}) collective-permute-start(bf16[48,4096]{1,0:T(8,128)(2,1)S(1)} %collective-permute-done.1.refs_0_.refs_4_), channel_id=1, source_target_pairs={{0,8},{4,12},{8,0},{12,4},{1,9},{5,13},{9,1},{13,5},{2,10},{6,14},... | collective-permute-start | bytes 1179656 | tf_op jit(solution)/shard_map/ppermute | solution.py:228
  18.9 10.8 %collective-permute-start.5 = (bf16[16,4096]{1,0:T(8,128)(2,1)S(1)}, bf16[16,4096]{1,0:T(8,128)(2,1)S(1)}, u32[]{:S(2)}, u32[]{:S(2)}) collective-permute-start(bf16[16,4096]{1,0:T(8,128)(2,1)S(1)} %slice.186), channel_id=1, source_target_pairs={{0,3},{1,0},{2,1},{3,2},{4,7},{5,4},{6,5},{7,6},{8,11},{9,8},{10,9... | collective-permute-start | bytes 393224 | tf_op jit(solution)/shard_map/ppermute | solution.py:223
  29.8 19.0 %collective-permute-start.14 = (bf16[384,896]{1,0:T(8,128)(2,1)}, bf16[384,896]{1,0:T(8,128)(2,1)S(1)}, u32[]{:S(2)}, u32[]{:S(2)}) collective-permute-start(bf16[384,896]{1,0:T(8,128)(2,1)} %shard_map.92), channel_id=1, source_target_pairs={{0,16},{16,0},{1,17},{17,1},{2,18},{18,2},{3,19},{19,3},{4,20},{20... | collective-permute-start | bytes 2064392 | tf_op jit(solution)/shard_map/ppermute | solution.py:234
  31.4 17.4 %collective-permute-start.9 = (bf16[48,4096]{1,0:T(8,128)(2,1)S(1)}, bf16[48,4096]{1,0:T(8,128)(2,1)S(1)}, u32[]{:S(2)}, u32[]{:S(2)}) collective-permute-start(bf16[48,4096]{1,0:T(8,128)(2,1)S(1)} %collective-permute-done.1.refs_0_.refs_4_), channel_id=1, source_target_pairs={{0,1},{1,2},{2,3},{3,0},{4,5},{5,6},{6,7},{7,4},{8,9},{9,10},{10,1... | collective-permute-start | bytes 1179656 | tf_op jit(solution)/shard_map/ppermute | solution.py:223
  32.3 16.5 %collective-permute-start.11 = (bf16[48,4096]{1,0:T(8,128)(2,1)S(1)}, bf16[48,4096]{1,0:T(8,128)(2,1)S(1)}, u32[]{:S(2)}, u32[]{:S(2)}) collective-permute-start(bf16[48,4096]{1,0:T(8,128)(2,1)S(1)} %collective-permute-done.4.refs_0_.refs_8_), channel_id=1, source_target_pairs={{0,8},{4,12},{8,0},{12,4},{1,9},{5,13},{9,1},{13,5},{2,10},{6,14},... | collective-permute-start | bytes 1179656 | tf_op jit(solution)/shard_map/ppermute | solution.py:228
  33.8 12.8 %collective-permute-start.12 = (bf16[16,4096]{1,0:T(8,128)(2,1)S(1)}, bf16[16,4096]{1,0:T(8,128)(2,1)S(1)}, u32[]{:S(2)}, u32[]{:S(2)}) collective-permute-start(bf16[16,4096]{1,0:T(8,128)(2,1)S(1)} %slice.186), channel_id=1, source_target_pairs={{0,8},{4,12},{8,0},{12,4},{1,9},{5,13},{9,1},{13,5},{2,10},{6,14},... | collective-permute-start | bytes 393224 | tf_op jit(solution)/shard_map/ppermute | solution.py:228
  34.4 14.4 %collective-permute-start.10 = (bf16[32,4096]{1,0:T(8,128)(2,1)}, bf16[32,4096]{1,0:T(8,128)(2,1)S(1)}, u32[]{:S(2)}, u32[]{:S(2)}) collective-permute-start(bf16[32,4096]{1,0:T(8,128)(2,1)} %slice.187), channel_id=1, source_target_pairs={{0,3},{1,0},{2,1},{3,2},{4,7},{5,4},{6,5},{7,6},{8,11},{9,8},{10,9... | collective-permute-start | bytes 786440 | tf_op jit(solution)/shard_map/ppermute | solution.py:223
  48.8 19.9 %collective-permute-start.21 = (bf16[384,896]{1,0:T(8,128)(2,1)}, bf16[384,896]{1,0:T(8,128)(2,1)S(1)}, u32[]{:S(2)}, u32[]{:S(2)}) collective-permute-start(bf16[384,896]{1,0:T(8,128)(2,1)} %shard_map.93), channel_id=1, source_target_pairs={{0,16},{16,0},{1,17},{17,1},{2,18},{18,2},{3,19},{19,3},{4,20},{20... | collective-permute-start | bytes 2064392 | tf_op jit(solution)/shard_map/ppermute | solution.py:234
  50.0 18.7 %collective-permute-start.15 = (bf16[48,4096]{1,0:T(8,128)(2,1)S(1)}, bf16[48,4096]{1,0:T(8,128)(2,1)S(1)}, u32[]{:S(2)}, u32[]{:S(2)}) collective-permute-start(bf16[48,4096]{1,0:T(8,128)(2,1)S(1)} %constant_dynamic-update-slice_fusion.refs_0_.refs_10_), channel_id=1, source_target_pairs={{0,3},{1,0},{2,1},{3,2},{4,7},{5,4},{6,5},{7,6},{8,11},{9,8},{10,9... | collective-permute-start | bytes 1179656 | tf_op jit(solution)/shard_map/ppermute | solution.py:223
  52.3 16.4 %collective-permute-start.16 = (bf16[48,4096]{1,0:T(8,128)(2,1)S(1)}, bf16[48,4096]{1,0:T(8,128)(2,1)S(1)}, u32[]{:S(2)}, u32[]{:S(2)}) collective-permute-start(bf16[48,4096]{1,0:T(8,128)(2,1)S(1)} %collective-permute-done.9.refs_0_.refs_12_), channel_id=1, source_target_pairs={{0,8},{4,12},{8,0},{12,4},{1,9},{5,13},{9,1},{13,5},{2,10},{6,14},... | collective-permute-start | bytes 1179656 | tf_op jit(solution)/shard_map/ppermute | solution.py:228
  53.8 8.4 %collective-permute-start.20 = (bf16[16,4096]{1,0:T(8,128)(2,1)S(1)}, bf16[16,4096]{1,0:T(8,128)(2,1)S(1)}, u32[]{:S(2)}, u32[]{:S(2)}) collective-permute-start(bf16[16,4096]{1,0:T(8,128)(2,1)S(1)} %collective-permute-done.12.refs_1_), channel_id=1, source_target_pairs={{0,4},{4,0},{8,12},{12,8},{1,5},{5,1},{9,13},{13,9},{2,6},{6,2},{1... | collective-permute-start | bytes 393224 | tf_op jit(solution)/shard_map/ppermute | solution.py:228
  53.9 14.8 %collective-permute-start.17 = (bf16[32,4096]{1,0:T(8,128)(2,1)S(1)}, bf16[32,4096]{1,0:T(8,128)(2,1)S(1)}, u32[]{:S(2)}, u32[]{:S(2)}) collective-permute-start(bf16[32,4096]{1,0:T(8,128)(2,1)S(1)} %collective-permute-done.10), channel_id=1, source_target_pairs={{0,8},{4,12},{8,0},{12,4},{1,9},{5,13},{9,1},{13,5},{2,10},{6,14},... | collective-permute-start | bytes 786440 | tf_op jit(solution)/shard_map/ppermute | solution.py:228
  68.7 6.6 %collective-permute-start.25 = (bf16[48,4096]{1,0:T(8,128)(2,1)S(1)}, bf16[48,4096]{1,0:T(8,128)(2,1)S(1)}, u32[]{:S(2)}, u32[]{:S(2)}) collective-permute-start(bf16[48,4096]{1,0:T(8,128)(2,1)S(1)} %collective-permute-done.9.refs_0_.refs_12_), channel_id=1, source_target_pairs={{0,4},{4,0},{8,12},{12,8},{1,5},{5,1},{9,13},{13,9},{2,6},{6,2},{1... | collective-permute-start | bytes 1179656 | tf_op jit(solution)/shard_map/ppermute | solution.py:228
  68.8 18.1 %collective-permute-start.29 = (bf16[384,896]{1,0:T(8,128)(2,1)}, bf16[384,896]{1,0:T(8,128)(2,1)S(1)}, u32[]{:S(2)}, u32[]{:S(2)}) collective-permute-start(bf16[384,896]{1,0:T(8,128)(2,1)} %shard_map.94), channel_id=1, source_target_pairs={{0,16},{16,0},{1,17},{17,1},{2,18},{18,2},{3,19},{19,3},{4,20},{20... | collective-permute-start | bytes 2064392 | tf_op jit(solution)/shard_map/ppermute | solution.py:234
  69.8 5.6 %collective-permute-start.24 = (bf16[16,4096]{1,0:T(8,128)(2,1)S(1)}, bf16[16,4096]{1,0:T(8,128)(2,1)S(1)}, u32[]{:S(2)}, u32[]{:S(2)}) collective-permute-start(bf16[16,4096]{1,0:T(8,128)(2,1)S(1)} %collective-permute-done.5), channel_id=1, source_target_pairs={{0,8},{4,12},{8,0},{12,4},{1,9},{5,13},{9,1},{13,5},{2,10},{6,14},... | collective-permute-start | bytes 393224 | tf_op jit(solution)/shard_map/ppermute | solution.py:228
  71.3 6.7 %collective-permute-start.26 = (bf16[48,4096]{1,0:T(8,128)(2,1)S(1)}, bf16[48,4096]{1,0:T(8,128)(2,1)S(1)}, u32[]{:S(2)}, u32[]{:S(2)}) collective-permute-start(bf16[48,4096]{1,0:T(8,128)(2,1)S(1)} %collective-permute-done.16.refs_1_.refs_13_), channel_id=1, source_target_pairs={{0,4},{4,0},{8,12},{12,8},{1,5},{5,1},{9,13},{13,9},{2,6},{6,2},{1... | collective-permute-start | bytes 1179656 | tf_op jit(solution)/shard_map/ppermute | solution.py:228
  72.3 13.9 %collective-permute-start.22 = (bf16[48,4096]{1,0:T(8,128)(2,1)S(1)}, bf16[48,4096]{1,0:T(8,128)(2,1)S(1)}, u32[]{:S(2)}, u32[]{:S(2)}) collective-permute-start(bf16[48,4096]{1,0:T(8,128)(2,1)S(1)} %copy-done.4), channel_id=1, source_target_pairs={{0,1},{1,2},{2,3},{3,0},{4,5},{5,6},{6,7},{7,4},{8,9},{9,10},{10,1... | collective-permute-start | bytes 1179656 | tf_op jit(solution)/shard_map/ppermute | solution.py:223
  75.3 10.9 %collective-permute-start.27 = (bf16[48,4096]{1,0:T(8,128)(2,1)S(1)}, bf16[48,4096]{1,0:T(8,128)(2,1)S(1)}, u32[]{:S(2)}, u32[]{:S(2)}) collective-permute-start(bf16[48,4096]{1,0:T(8,128)(2,1)S(1)} %constant_dynamic-update-slice_fusion.refs_0_.refs_10_), channel_id=1, source_target_pairs={{0,4},{4,0},{8,12},{12,8},{1,5},{5,1},{9,13},{13,9},{2,6},{6,2},{1... | collective-permute-start | bytes 1179656 | tf_op jit(solution)/shard_map/ppermute | solution.py:228
  75.4 11.5 %collective-permute-start.23 = (bf16[48,4096]{1,0:T(8,128)(2,1)S(1)}, bf16[48,4096]{1,0:T(8,128)(2,1)S(1)}, u32[]{:S(2)}, u32[]{:S(2)}) collective-permute-start(bf16[48,4096]{1,0:T(8,128)(2,1)S(1)} %collective-permute-done.15.refs_6_.refs_16_), channel_id=1, source_target_pairs={{0,8},{4,12},{8,0},{12,4},{1,9},{5,13},{9,1},{13,5},{2,10},{6,14},... | collective-permute-start | bytes 1179656 | tf_op jit(solution)/shard_map/ppermute | solution.py:228
  78.0 8.2 %collective-permute-start.28 = (bf16[32,4096]{1,0:T(8,128)(2,1)S(1)}, bf16[32,4096]{1,0:T(8,128)(2,1)S(1)}, u32[]{:S(2)}, u32[]{:S(2)}) collective-permute-start(bf16[32,4096]{1,0:T(8,128)(2,1)S(1)} %collective-permute-done.17.refs_2_.refs_12_), channel_id=1, source_target_pairs={{0,4},{4,0},{8,12},{12,8},{1,5},{5,1},{9,13},{13,9},{2,6},{6,2},{1... | collective-permute-start | bytes 786440 | tf_op jit(solution)/shard_map/ppermute | solution.py:228
  86.9 4.6 %collective-permute-start.33 = (bf16[48,4096]{1,0:T(8,128)(2,1)S(1)}, bf16[48,4096]{1,0:T(8,128)(2,1)S(1)}, u32[]{:S(2)}, u32[]{:S(2)}) collective-permute-start(bf16[48,4096]{1,0:T(8,128)(2,1)S(1)} %collective-permute-done.15.refs_6_.refs_16_), channel_id=1, source_target_pairs={{0,4},{4,0},{8,12},{12,8},{1,5},{5,1},{9,13},{13,9},{2,6},{6,2},{1... | collective-permute-start | bytes 1179656 | tf_op jit(solution)/shard_map/ppermute | solution.py:228
  87.5 18.5 %collective-permute-start.35 = (bf16[384,896]{1,0:T(8,128)(2,1)}, bf16[384,896]{1,0:T(8,128)(2,1)S(1)}, u32[]{:S(2)}, u32[]{:S(2)}) collective-permute-start(bf16[384,896]{1,0:T(8,128)(2,1)} %shard_map.95), channel_id=1, source_target_pairs={{0,16},{16,0},{1,17},{17,1},{2,18},{18,2},{3,19},{19,3},{4,20},{20... | collective-permute-start | bytes 2064392 | tf_op jit(solution)/shard_map/ppermute | solution.py:234
  88.6 15.5 %collective-permute-start.31 = (bf16[32,4096]{1,0:T(8,128)(2,1)}, bf16[32,4096]{1,0:T(8,128)(2,1)S(1)}, u32[]{:S(2)}, u32[]{:S(2)}) collective-permute-start(bf16[32,4096]{1,0:T(8,128)(2,1)} %slice.187), channel_id=1, source_target_pairs={{0,8},{4,12},{8,0},{12,4},{1,9},{5,13},{9,1},{13,5},{2,10},{6,14},... | collective-permute-start | bytes 786440 | tf_op jit(solution)/shard_map/ppermute | solution.py:228
  90.1 15.8 %collective-permute-start.30 = (bf16[48,4096]{1,0:T(8,128)(2,1)S(1)}, bf16[48,4096]{1,0:T(8,128)(2,1)S(1)}, u32[]{:S(2)}, u32[]{:S(2)}) collective-permute-start(bf16[48,4096]{1,0:T(8,128)(2,1)S(1)} %collective-permute-done.22.refs_6_), channel_id=1, source_target_pairs={{0,8},{4,12},{8,0},{12,4},{1,9},{5,13},{9,1},{13,5},{2,10},{6,14},... | collective-permute-start | bytes 1179656 | tf_op jit(solution)/shard_map/ppermute | solution.py:228
  108.0 17.7 %collective-permute-start.42 = (bf16[384,896]{1,0:T(8,128)(2,1)S(1)}, bf16[384,896]{1,0:T(8,128)(2,1)}, u32[]{:S(2)}, u32[]{:S(2)}) collective-permute-start(bf16[384,896]{1,0:T(8,128)(2,1)S(1)} %copy-done.15), channel_id=1, source_target_pairs={{0,16},{16,0},{1,17},{17,1},{2,18},{18,2},{3,19},{19,3},{4,20},{20... | collective-permute-start | bytes 2064392 | tf_op jit(solution)/shard_map/ppermute | solution.py:234
  109.0 4.6 %collective-permute-start.40 = (bf16[48,4096]{1,0:T(8,128)(2,1)S(1)}, bf16[48,4096]{1,0:T(8,128)(2,1)S(1)}, u32[]{:S(2)}, u32[]{:S(2)}) collective-permute-start(bf16[48,4096]{1,0:T(8,128)(2,1)S(1)} %copy-done.39), channel_id=1, source_target_pairs={{0,4},{4,0},{8,12},{12,8},{1,5},{5,1},{9,13},{13,9},{2,6},{6,2},{1... | collective-permute-start | bytes 1179656 | tf_op jit(solution)/shard_map/ppermute | solution.py:228
  109.5 4.8 %collective-permute-start.41 = (bf16[48,4096]{1,0:T(8,128)(2,1)S(1)}, bf16[48,4096]{1,0:T(8,128)(2,1)}, u32[]{:S(2)}, u32[]{:S(2)}) collective-permute-start(bf16[48,4096]{1,0:T(8,128)(2,1)S(1)} %copy-done.45), channel_id=1, source_target_pairs={{0,4},{4,0},{8,12},{12,8},{1,5},{5,1},{9,13},{13,9},{2,6},{6,2},{1... | collective-permute-start | bytes 1179656 | tf_op jit(solution)/shard_map/ppermute | solution.py:228
  110.5 15.3 %collective-permute-start.38 = (bf16[96,4096]{1,0:T(8,128)(2,1)}, bf16[96,4096]{1,0:T(8,128)(2,1)S(1)}, u32[]{:S(2)}, u32[]{:S(2)}) collective-permute-start(bf16[96,4096]{1,0:T(8,128)(2,1)} %get-tuple-element.174), channel_id=1, source_target_pairs={{0,4},{4,0},{8,12},{12,8},{1,5},{5,1},{9,13},{13,9},{2,6},{6,2},{1... | collective-permute-start | bytes 2359304 | tf_op jit(solution)/shard_map/ppermute | solution.py:228
  112.0 13.8 %collective-permute-start.37 = (bf16[48,4096]{1,0:T(8,128)(2,1)}, bf16[48,4096]{1,0:T(8,128)(2,1)S(1)}, u32[]{:S(2)}, u32[]{:S(2)}) collective-permute-start(bf16[48,4096]{1,0:T(8,128)(2,1)} %get-tuple-element.260), channel_id=1, source_target_pairs={{0,8},{4,12},{8,0},{12,4},{1,9},{5,13},{9,1},{13,5},{2,10},{6,14},... | collective-permute-start | bytes 1179656 | tf_op jit(solution)/shard_map/ppermute | solution.py:228
  125.9 20.6 %collective-permute-start.46 = (bf16[384,896]{1,0:T(8,128)(2,1)}, bf16[384,896]{1,0:T(8,128)(2,1)}, u32[]{:S(2)}, u32[]{:S(2)}) collective-permute-start(bf16[384,896]{1,0:T(8,128)(2,1)} %get-tuple-element.199), channel_id=1, source_target_pairs={{0,16},{16,0},{1,17},{17,1},{2,18},{18,2},{3,19},{19,3},{4,20},{20... | collective-permute-start | bytes 2064392 | tf_op jit(solution)/shard_map/ppermute | solution.py:234
  129.8 19.6 %collective-permute-start.44 = (bf16[96,4096]{1,0:T(8,128)(2,1)S(1)}, bf16[96,4096]{1,0:T(8,128)(2,1)S(1)}, u32[]{:S(2)}, u32[]{:S(2)}) collective-permute-start(bf16[96,4096]{1,0:T(8,128)(2,1)S(1)} %pad_maximum_fusion), channel_id=1, source_target_pairs={{0,8},{4,12},{8,0},{12,4},{1,9},{5,13},{9,1},{13,5},{2,10},{6,14},... | collective-permute-start | bytes 2359304 | tf_op jit(solution)/shard_map/ppermute | solution.py:228
  131.4 18.1 %collective-permute-start.45 = (bf16[96,4096]{1,0:T(8,128)(2,1)}, bf16[96,4096]{1,0:T(8,128)(2,1)S(1)}, u32[]{:S(2)}, u32[]{:S(2)}) collective-permute-start(bf16[96,4096]{1,0:T(8,128)(2,1)} %get-tuple-element.193), channel_id=1, source_target_pairs={{0,4},{4,0},{8,12},{12,8},{1,5},{5,1},{9,13},{13,9},{2,6},{6,2},{1... | collective-permute-start | bytes 2359304 | tf_op jit(solution)/shard_map/ppermute | solution.py:228
  150.6 20.9 %collective-permute-start.51 = (bf16[48,4096]{1,0:T(8,128)(2,1)}, bf16[48,4096]{1,0:T(8,128)(2,1)S(1)}, u32[]{:S(2)}, u32[]{:S(2)}) collective-permute-start(bf16[48,4096]{1,0:T(8,128)(2,1)} %get-tuple-element.249), channel_id=1, source_target_pairs={{0,3},{1,0},{2,1},{3,2},{4,7},{5,4},{6,5},{7,6},{8,11},{9,8},{10,9... | collective-permute-start | bytes 1179656 | tf_op jit(solution)/shard_map/ppermute | solution.py:223
  151.5 20.1 %collective-permute-start.50 = (bf16[48,4096]{1,0:T(8,128)(2,1)}, bf16[48,4096]{1,0:T(8,128)(2,1)S(1)}, u32[]{:S(2)}, u32[]{:S(2)}) collective-permute-start(bf16[48,4096]{1,0:T(8,128)(2,1)} %get-tuple-element.250), channel_id=1, source_target_pairs={{0,1},{1,2},{2,3},{3,0},{4,5},{5,6},{6,7},{7,4},{8,9},{9,10},{10,1... | collective-permute-start | bytes 1179656 | tf_op jit(solution)/shard_map/ppermute | solution.py:223
  155.4 19.4 %collective-permute-start.48 = (bf16[96,4096]{1,0:T(8,128)(2,1)S(1)}, bf16[96,4096]{1,0:T(8,128)(2,1)S(1)}, u32[]{:S(2)}, u32[]{:S(2)}) collective-permute-start(bf16[96,4096]{1,0:T(8,128)(2,1)S(1)} %pad_maximum_fusion.1), channel_id=1, source_target_pairs={{0,8},{4,12},{8,0},{12,4},{1,9},{5,13},{9,1},{13,5},{2,10},{6,14},... | collective-permute-start | bytes 2359304 | tf_op jit(solution)/shard_map/ppermute | solution.py:228
  156.9 17.9 %collective-permute-start.49 = (bf16[96,4096]{1,0:T(8,128)(2,1)S(1)}, bf16[96,4096]{1,0:T(8,128)(2,1)S(1)}, u32[]{:S(2)}, u32[]{:S(2)}) collective-permute-start(bf16[96,4096]{1,0:T(8,128)(2,1)S(1)} %copy-done.58), channel_id=1, source_target_pairs={{0,4},{4,0},{8,12},{12,8},{1,5},{5,1},{9,13},{13,9},{2,6},{6,2},{1... | collective-permute-start | bytes 2359304 | tf_op jit(solution)/shard_map/ppermute | solution.py:228
  175.1 19.2 %collective-permute-start.56 = (bf16[48,4096]{1,0:T(8,128)(2,1)S(1)}, bf16[48,4096]{1,0:T(8,128)(2,1)}, u32[]{:S(2)}, u32[]{:S(2)}) collective-permute-start(bf16[48,4096]{1,0:T(8,128)(2,1)S(1)} %get-tuple-element.247), channel_id=1, source_target_pairs={{0,1},{1,2},{2,3},{3,0},{4,5},{5,6},{6,7},{7,4},{8,9},{9,10},{10,1... | collective-permute-start | bytes 1179656 | tf_op jit(solution)/shard_map/ppermute | solution.py:223
  176.3 19.7 %collective-permute-start.55 = (bf16[48,4096]{1,0:T(8,128)(2,1)S(1)}, bf16[48,4096]{1,0:T(8,128)(2,1)S(1)}, u32[]{:S(2)}, u32[]{:S(2)}) collective-permute-start(bf16[48,4096]{1,0:T(8,128)(2,1)S(1)} %get-tuple-element.248), channel_id=1, source_target_pairs={{0,3},{1,0},{2,1},{3,2},{4,7},{5,4},{6,5},{7,6},{8,11},{9,8},{10,9... | collective-permute-start | bytes 1179656 | tf_op jit(solution)/shard_map/ppermute | solution.py:223
  179.2 16.7 %collective-permute-start.54 = (bf16[96,4096]{1,0:T(8,128)(2,1)}, bf16[96,4096]{1,0:T(8,128)(2,1)S(1)}, u32[]{:S(2)}, u32[]{:S(2)}) collective-permute-start(bf16[96,4096]{1,0:T(8,128)(2,1)} %get-tuple-element.216), channel_id=1, source_target_pairs={{0,4},{4,0},{8,12},{12,8},{1,5},{5,1},{9,13},{13,9},{2,6},{6,2},{1... | collective-permute-start | bytes 2359304 | tf_op jit(solution)/shard_map/ppermute | solution.py:228
  179.5 16.4 %collective-permute-start.53 = (bf16[48,4096]{1,0:T(8,128)(2,1)S(1)}, bf16[48,4096]{1,0:T(8,128)(2,1)S(1)}, u32[]{:S(2)}, u32[]{:S(2)}) collective-permute-start(bf16[48,4096]{1,0:T(8,128)(2,1)S(1)} %get-tuple-element.254), channel_id=1, source_target_pairs={{0,8},{4,12},{8,0},{12,4},{1,9},{5,13},{9,1},{13,5},{2,10},{6,14},... | collective-permute-start | bytes 1179656 | tf_op jit(solution)/shard_map/ppermute | solution.py:228
  196.2 21.6 %collective-permute-start.58 = (bf16[96,4096]{1,0:T(8,128)(2,1)S(1)}, bf16[96,4096]{1,0:T(8,128)(2,1)S(1)}, u32[]{:S(2)}, u32[]{:S(2)}) collective-permute-start(bf16[96,4096]{1,0:T(8,128)(2,1)S(1)} %pad_maximum_fusion.3), channel_id=1, source_target_pairs={{0,3},{1,0},{2,1},{3,2},{4,7},{5,4},{6,5},{7,6},{8,11},{9,8},{10,9... | collective-permute-start | bytes 2359304 | tf_op jit(solution)/shard_map/ppermute | solution.py:223
  198.4 19.4 %collective-permute-start.57 = (bf16[96,4096]{1,0:T(8,128)(2,1)S(1)}, bf16[96,4096]{1,0:T(8,128)(2,1)S(1)}, u32[]{:S(2)}, u32[]{:S(2)}) collective-permute-start(bf16[96,4096]{1,0:T(8,128)(2,1)S(1)} %pad_maximum_fusion.2), channel_id=1, source_target_pairs={{0,8},{4,12},{8,0},{12,4},{1,9},{5,13},{9,1},{13,5},{2,10},{6,14},... | collective-permute-start | bytes 2359304 | tf_op jit(solution)/shard_map/ppermute | solution.py:228
  (70 other events, 461.1 us)

commit v12 on v11

--- a/solution.py
+++ b/solution.py
@@ -108,7 +108,7 @@
     blocks = sum(lefts, [])
     rows, units = blocks[0].shape
     width = weights[0].shape[0]
-    block = min(512, width)
+    block = min(1024, width)
     out = jax.ShapeDtypeStruct((rows // 2, width), jnp.bfloat16)
     return pl.pallas_call(
         functools.partial(expand_kernel, len(lefts)),
@@ -283,9 +283,8 @@
 def body(tokens, gate_weight, up_weight, down_weight, cotangent):
     pair = [gate_weight, up_weight]
 
-    def half_sums(partial, moved, *others):
+    def half_sums(partial, moved):
         half = partial.shape[0] // 2
-        moved = [after(block, *others) for block in moved]
         return [
             row_sum(partial[at], [block[at] for block in moved])
             for at in (slice(0, half), slice(half, 2 * half))
@@ -314,11 +313,11 @@
 
     pair0_moved = row_moves(pair0)
     near2, tail3 = (shift(after(x, pair0), k) for x, k in ((near1, 1), (cot_tail, 3)))
-    far3, far_head0 = swap(near3, CHIP), swap(after(cot_head, pair0), CHIP)
+    far3, far_tail0 = swap(near3, CHIP), swap(after(cot_tail, pair0), CHIP)
     token1 = quad([near1], [far1], [core1, swap(far1, CORE)])
     pair1 = contract(token1, pair)
-    near2, tail3, far3, far_head0, pair1, *pair0_moved = sync(
-        near2, tail3, far3, far_head0, pair1, *pair0_moved
+    near2, tail3, far3, far_tail0, pair1, *pair0_moved = sync(
+        near2, tail3, far3, far_tail0, pair1, *pair0_moved
     )
 
     gate0, up0 = half_sums(pair0, pair0_moved)
@@ -329,9 +328,9 @@
     far2, far_tail3 = swap(near2, CHIP), swap(after(tail3, pair1), CHIP)
     token3 = quad([near3], [far3], other_cores([after(near3, pair1), far3]))
     pair3 = contract(token3, pair)
-    far_head0_core = swap(after(far_head0, pair1), CORE)
-    cot_near2, far2, far_tail3, pair3, far_head0_core, *pair1_moved = sync(
-        cot_near2, far2, far_tail3, pair3, far_head0_core, *pair1_moved
+    far_tail0_core = swap(after(far_tail0, pair1), CORE)
+    cot_near2, far2, far_tail3, pair3, far_tail0_core, *pair1_moved = sync(
+        cot_near2, far2, far_tail3, pair3, far_tail0_core, *pair1_moved
     )
 
     gate1, up1 = half_sums(pair1, pair1_moved)
@@ -351,12 +350,12 @@
     gate3, up3 = pair_sums(pair3, pair3_moved)
     hidden3 = hidden_of(gate3, up3)
     pair2_moved = row_moves(pair2)
-    cot_far1, far_tail0 = swap(cot_near1, CHIP), swap(after(cot_tail, pair2), CHIP)
+    cot_far1, far_head0 = swap(cot_near1, CHIP), swap(after(cot_head, pair2), CHIP)
     cot_far3 = [far_head3, far_tail3]
     cot3 = quad([cot_near3], cot_far3, [core3, swap(far_head3, CORE), far_tail3_core])
     cot2 = quad([cot_near2], [cot_far2], other_cores([after(cot_near2, pair2), cot_far2]))
     products = down_products(cot3 + cot2, [hidden0, hidden1], down_weight)
-    cot_far1, far_tail0, grad_b, *rest = sync(cot_far1, far_tail0, *products, *pair2_moved)
+    cot_far1, far_head0, grad_b, *rest = sync(cot_far1, far_head0, *products, *pair2_moved)
     parts, pair2_moved = rest[:4], rest[4:]
 
     gate2, up2 = pair_sums(pair2, pair2_moved)
@@ -365,7 +364,7 @@
     (mixed_sent0, sent), mixed_a = chip_part(parts)
     mixed_a_moved = swap(sent, CHIP)
     cot_far0 = [far_head0, far_tail0]
-    cot0 = quad([cotangent], cot_far0, [cot_core0, far_head0_core, swap(far_tail0, CORE)])
+    cot0 = quad([cotangent], cot_far0, [cot_core0, swap(far_head0, CORE), far_tail0_core])
     cot1 = quad([cot_near1], [cot_far1], other_cores([after(cot_near1, grad_b), cot_far1]))
     products = down_products(cot0 + cot1, [hidden3, hidden2], down_weight)
     mixed_a_moved, mixed_a[1], mixed_sent0, grad_a, *rest = sync(
@@ -376,7 +375,7 @@
     grad_a_moved = row_moves(grad_a)
     sent, mixed_b = chip_part(parts)
     mixed_b_moved = swap(jnp.concatenate(sent, axis=0), CHIP)
-    grad3, grad2 = half_sums(grad_b, grad_b_moved)
+    grad3, grad2 = pair_sums(grad_b, grad_b_moved)
     grads3, grads2 = grads_of(gate3, up3, grad3), grads_of(gate2, up2, grad2)
     parts = expand([[x, y] for x, y in zip(grads3, grads2)], pair)
     mixed_b_moved, mixed_b[1], *rest = sync(mixed_b_moved, mixed_b[1], *parts, *grad_a_moved)
@@ -384,7 +383,7 @@
 
     sent, token_grad_b = chip_part(parts)
     token_b_moved = swap(jnp.concatenate(sent, axis=0), CHIP)
-    grad0, grad1 = half_sums(grad_a, grad_a_moved, *sent)
+    grad0, grad1 = pair_sums(grad_a, grad_a_moved)
     size = tokens.shape[0]
     mixed_part3 = shift(narrow(block_sum(mixed_b, 0, mixed_b_moved[:size])), 1)
     mixed_part2 = shift(narrow(block_sum(mixed_b, 1, mixed_b_moved[size:])), -1)

time: 223 us -> 218 us (0.978)
  waiting for transfers between devices: 33.6 us -> 45.6 us
  starting transfers between devices: 51.3 us -> 43.1 us
  Pallas kernels: 108 us -> 104 us
  other arithmetic: 19.1 us -> 15.4 us
    ppermute x41, starting transfers between devices: 24.1 us -> 16.5 us  [swap(): return lax.ppermute(block, 'col', [(i, i ^ bit) for i in range(n)])]
    ppermute x6, waiting for transfers between devices: 0.37 us -> 6.23 us  [row_moves(): lax.ppermute(partial, 'row', [(i, (i + step) % n) for i in range(n)])]
    ppermute x12, waiting for transfers between devices: 12 us -> 17.8 us  [shift(): return lax.ppermute(block, 'depth', [(i, (i + step) % n) for i in range(n)])]
    convert_element_type x13 -> x12, other arithmetic: 15.6 us -> 10.4 us  [narrow(): return block.astype(jnp.bfloat16)]
    pallas_call x2, Pallas kernels: 24.6 us -> 21.4 us  [expand(): pl.pallas_call(functools.partial(expand_kernel, len(lefts)), grid=(width...]
    add x2 -> x4, other arithmetic: 0.27 us -> 2.74 us  [row_sum(): return sum([wide(block) for block in moved], wide(partial))]
    unnamed x119 -> x125, local copies, waits for them, and re-layouts: 4.93 us -> 4.51 us
  transfers between devices with their start and end apart: 59 -> 59, of which waited for: 13 -> 16; matrix products, arithmetic and copies ran while one was open for 9% -> 7% of each run, Pallas kernels for 49% -> 48%
where the time goes in v12:
time: 218 us; the launch traced here: 216 us
  Pallas kernels  104 us (48%)
  waiting for transfers between devices  45.6 us (21%)
  starting transfers between devices  43.1 us (20%)
  other arithmetic  15.4 us (7%)
  local copies, waits for them, and re-layouts  6.46 us (3%)
    pallas_call x4, Pallas kernels, contract(): pl.pallas_call(kernel, in_specs=[pl.BlockSpec(memory_space=pl.ANY)] * n_i...  29.9 us
    pallas_call x2, Pallas kernels, down_products(): pl.pallas_call(functools.partial(down_kernel, len(pieces)), grid=(width /...  22.2 us
    ppermute x41, waiting for transfers between devices, swap(): return lax.ppermute(block, 'col', [(i, i ^ bit) for i in range(n)])  21.6 us
    pallas_call x2, Pallas kernels, expand(): pl.pallas_call(functools.partial(expand_kernel, len(lefts)), grid=(width...  21.4 us
    ppermute x12, starting transfers between devices, shift(): return lax.ppermute(block, 'depth', [(i, (i + step) % n) for i in range(n)])  20.4 us
    ppermute x12, waiting for transfers between devices, shift(): return lax.ppermute(block, 'depth', [(i, (i + step) % n) for i in range(n)])  17.8 us
    pallas_call x1, Pallas kernels, wide_grads(): pl.pallas_call(functools.partial(wide_grad_kernel, len(pieces)), grid=(wi...  17.8 us
    ppermute x41, starting transfers between devices, swap(): return lax.ppermute(block, 'col', [(i, i ^ bit) for i in range(n)])  16.5 us
  transfers between devices with their start and end apart: 59, of which 16 were waited for; matrix products, arithmetic and copies ran while one was open for 7% of the time, Pallas kernels for 48%

profile of v12, /device:TPU:0, one launch (start us, length us, event | category | flops | bytes accessed | tf_op | source)
XLA Modules:
  0.0 216.4 jit_solution(18052525714560138631)
XLA Ops:
  0.6 3.1 %collective-permute-start.1 = (bf16[48,4096]{1,0:T(8,128)(2,1)}, bf16[48,4096]{1,0:T(8,128)(2,1)S(1)}, u32[]{:S(2)}, u32[]{:S(2)}) collective-permute-start(bf16[48,4096]{1,0:T(8,128)(2,1)} %refs_0_.6), channel_id=1, source_target_pairs={{0,1},{1,2},{2,3},{3,0},{4,5},{5,6},{6,7},{7,4},{8,9},{9,10},{10,1... | collective-permute-start | bytes 1179656 | tf_op jit(solution)/shard_map/ppermute | solution.py:223
  3.7 1.5 collective-permute-start
  6.2 1.0 slice.175
  7.2 7.9 %collective-permute-done.1.refs_0_.refs_4_ = bf16[48,4096]{1,0:T(8,128)(2,1)S(1)} collective-permute-done((bf16[48,4096]{1,0:T(8,128)(2,1)}, bf16[48,4096]{1,0:T(8,128)(2,1)S(1)}, u32[]{:S(2)}, u32[]{:S(2)}) %collective-permute-start.1) | collective-permute-done | bytes 393248 | tf_op jit(solution)/shard_map/ppermute | solution.py:223
  15.6 1.7 collective-permute-start.4
  17.4 1.5 collective-permute-start.3
  18.9 1.7 collective-permute-start.5
  21.3 7.4 %shard_map.92 = bf16[384,896]{1,0:T(8,128)(2,1)} custom-call(bf16[48,4096]{1,0:T(8,128)(2,1)} %refs_0_.6, bf16[48,4096]{1,0:T(8,128)(2,1)} %copy-done.23, bf16[48,4096]{1,0:T(8,128)(2,1)} %copy-done.24, bf16[48,4096]{1,0:T(8,128)(2,1)} %copy-done.25, bf16[4096,896]{1,0:T(8,128)(2,1)} %refs_4_.11, bf16[4096,896]{1,0:T(8,128)(2,1)} %refs_5_.11), custom_call_target="tpu_custom_call" | custom-call | flops 2818572288 | bytes 16252928 | tf_op jit(solution)/shard_map/pallas_call | solution.py:78
  28.8 1.0 collective-permute-done.5
  29.8 1.6 collective-permute-start.14
  31.4 1.5 collective-permute-start.12
  34.3 1.2 collective-permute-done.13.refs_3_.refs_7_
  35.5 2.9 %collective-permute-start.10 = (bf16[32,4096]{1,0:T(8,128)(2,1)S(1)}, bf16[32,4096]{1,0:T(8,128)(2,1)S(1)}, u32[]{:S(2)}, u32[]{:S(2)}) collective-permute-start(bf16[32,4096]{1,0:T(8,128)(2,1)S(1)} %slice.175), channel_id=1, source_target_pairs={{0,3},{1,0},{2,1},{3,2},{4,7},{5,4},{6,5},{7,6},{8,11},{9,8},{10,9... | collective-permute-start | bytes 786440 | tf_op jit(solution)/shard_map/ppermute | solution.py:223
  38.4 7.5 %shard_map.93 = bf16[384,896]{1,0:T(8,128)(2,1)} custom-call(bf16[48,4096]{1,0:T(8,128)(2,1)} %copy-done.22, bf16[48,4096]{1,0:T(8,128)(2,1)} %copy-done.28, bf16[48,4096]{1,0:T(8,128)(2,1)} %copy-done.27, bf16[48,4096]{1,0:T(8,128)(2,1)} %copy-done.30, bf16[4096,896]{1,0:T(8,128)(2,1)} %refs_4_.11, bf16[4096,896]{1,0:T(8,128)(2,1)} %refs_5_.11), custom_call_target="tpu_custom_call" | custom-call | flops 2818572288 | bytes 16252928 | tf_op jit(solution)/shard_map/pallas_call | solution.py:78
  45.9 4.1 %collective-permute-done.10 = bf16[32,4096]{1,0:T(8,128)(2,1)S(1)} collective-permute-done((bf16[32,4096]{1,0:T(8,128)(2,1)S(1)}, bf16[32,4096]{1,0:T(8,128)(2,1)S(1)}, u32[]{:S(2)}, u32[]{:S(2)}) %collective-permute-start.10) | collective-permute-done | bytes 262176 | tf_op jit(solution)/shard_map/ppermute | solution.py:223
  51.2 1.8 collective-permute-start.15
  53.9 1.2 collective-permute-start.17
  55.1 7.5 %shard_map.94 = bf16[384,896]{1,0:T(8,128)(2,1)} custom-call(bf16[48,4096]{1,0:T(8,128)(2,1)} %copy-done.26, bf16[48,4096]{1,0:T(8,128)(2,1)} %copy-done.31, bf16[48,4096]{1,0:T(8,128)(2,1)} %copy-done.32, bf16[48,4096]{1,0:T(8,128)(2,1)} %copy-done.33, bf16[4096,896]{1,0:T(8,128)(2,1)} %refs_4_.11, bf16[4096,896]{1,0:T(8,128)(2,1)} %refs_5_.11), custom_call_target="tpu_custom_call" | custom-call | flops 2818572288 | bytes 16252928 | tf_op jit(solution)/shard_map/pallas_call | solution.py:78
  62.6 6.7 %collective-permute-done.17.refs_2_.refs_12_ = bf16[32,4096]{1,0:T(8,128)(2,1)S(1)} collective-permute-done((bf16[32,4096]{1,0:T(8,128)(2,1)S(1)}, bf16[32,4096]{1,0:T(8,128)(2,1)S(1)}, u32[]{:S(2)}, u32[]{:S(2)}) %collective-permute-start.17) | collective-permute-done | bytes 262176 | tf_op jit(solution)/shard_map/ppermute | solution.py:228
  69.5 1.6 collective-permute-start.29
  71.5 1.0 multiply_convert_fusion.11.refs_10_.refs_20_
  72.9 3.7 %collective-permute-done.24.refs_1_.refs_11_ = bf16[16,4096]{1,0:T(8,128)(2,1)S(1)} collective-permute-done((bf16[16,4096]{1,0:T(8,128)(2,1)S(1)}, bf16[16,4096]{1,0:T(8,128)(2,1)S(1)}, u32[]{:S(2)}, u32[]{:S(2)}) %collective-permute-start.24) | collective-permute-done | bytes 131104 | tf_op jit(solution)/shard_map/ppermute | solution.py:228
  77.2 1.0 multiply_convert_fusion.10.refs_11_.refs_21_
  79.0 7.5 %shard_map.95 = bf16[384,896]{1,0:T(8,128)(2,1)} custom-call(bf16[48,4096]{1,0:T(8,128)(2,1)} %copy-done.29, bf16[48,4096]{1,0:T(8,128)(2,1)} %copy-done.34, bf16[48,4096]{1,0:T(8,128)(2,1)} %copy-done.35, bf16[48,4096]{1,0:T(8,128)(2,1)} %copy-done.36, bf16[4096,896]{1,0:T(8,128)(2,1)} %refs_4_.11, bf16[4096,896]{1,0:T(8,128)(2,1)} %refs_5_.11), custom_call_target="tpu_custom_call" | custom-call | flops 2818572288 | bytes 16252928 | tf_op jit(solution)/shard_map/pallas_call | solution.py:78
  86.5 1.7 collective-permute-done.23.refs_7_.refs_17_
  93.1 11.1 %shard_map.96 = (bf16[384,896]{1,0:T(8,128)(2,1)}, bf16[96,4096]{1,0:T(8,128)(2,1)}, bf16[96,4096]{1,0:T(8,128)(2,1)}, bf16[96,4096]{1,0:T(8,128)(2,1)}, bf16[96,4096]{1,0:T(8,128)(2,1)}) custom-call(bf16[48,4096]{1,0:T(8,128)(2,1)} %copy-done.15, bf16[16,4096]{1,0:T(8,128)(2,1)} %copy-done.55, bf16[32,4096]{1,0:T(8,128)(2,1)} %copy-done.53, ...), custom_call_target="tpu_custom_call" | custom-call | flops 5637144576 | bytes 14319616 | tf_op jit(solution)/shard_map/pallas_call | solution.py:150
  104.2 2.1 collective-permute-done.35
  113.0 11.1 %shard_map.97 = (bf16[384,896]{1,0:T(8,128)(2,1)}, bf16[96,4096]{1,0:T(8,128)(2,1)}, bf16[96,4096]{1,0:T(8,128)(2,1)}, bf16[96,4096]{1,0:T(8,128)(2,1)}, bf16[96,4096]{1,0:T(8,128)(2,1)}) custom-call(bf16[48,4096]{1,0:T(8,128)(2,1)} %refs_0_.5, bf16[16,4096]{1,0:T(8,128)(2,1)} %copy-done.57, bf16[32,4096]{1,0:T(8,128)(2,1)} %copy-done.51, ...), custom_call_target="tpu_custom_call" | custom-call | flops 5637144576 | bytes 14319616 | tf_op jit(solution)/shard_map/pallas_call | solution.py:150
  124.1 1.6 collective-permute-done.42
  126.7 1.2 convert_add_fusion.1
  129.2 1.7 multiply_convert_fusion.4
  130.9 10.7 %shard_map.98 = (bf16[96,4096]{1,0:T(8,128)(2,1)}, bf16[96,4096]{1,0:T(8,128)(2,1)}, bf16[96,4096]{1,0:T(8,128)(2,1)}, bf16[96,4096]{1,0:T(8,128)(2,1)}) custom-call(bf16[192,896]{1,0:T(8,128)(2,1)} %get-tuple-element.259.refs_0_.refs_18_, bf16[192,896]{1,0:T(8,128)(2,1)} %get-tuple-element.240.refs_1_.refs_19_, ...), custom_call_target="tpu_custom_call" | custom-call | flops 5637144576 | bytes 19202048 | tf_op jit(solution)/shard_map/pallas_call | solution.py:113
  141.6 2.5 %collective-permute-done.46 = bf16[384,896]{1,0:T(8,128)(2,1)} collective-permute-done((bf16[384,896]{1,0:T(8,128)(2,1)}, bf16[384,896]{1,0:T(8,128)(2,1)}, u32[]{:S(2)}, u32[]{:S(2)}) %collective-permute-start.46) | collective-permute-done | bytes 688160 | tf_op jit(solution)/shard_map/ppermute | solution.py:234
  144.0 4.2 %collective-permute-done.44 = bf16[96,4096]{1,0:T(8,128)(2,1)S(1)} collective-permute-done((bf16[96,4096]{1,0:T(8,128)(2,1)S(1)}, bf16[96,4096]{1,0:T(8,128)(2,1)S(1)}, u32[]{:S(2)}, u32[]{:S(2)}) %collective-permute-start.44) | collective-permute-done | bytes 786464 | tf_op jit(solution)/shard_map/ppermute | solution.py:228
  148.3 1.1 add_convert_fusion.6
  149.7 1.7 collective-permute-start.50
  151.4 1.2 convert_add_fusion
  154.0 1.9 multiply_convert_fusion
  155.9 10.7 %shard_map.99 = (bf16[96,4096]{1,0:T(8,128)(2,1)}, bf16[96,4096]{1,0:T(8,128)(2,1)}, bf16[96,4096]{1,0:T(8,128)(2,1)}, bf16[96,4096]{1,0:T(8,128)(2,1)}) custom-call(bf16[192,896]{1,0:T(8,128)(2,1)} %get-tuple-element.257.refs_0_.refs_16_, bf16[192,896]{1,0:T(8,128)(2,1)} %get-tuple-element.236.refs_1_.refs_17_, ...), custom_call_target="tpu_custom_call" | custom-call | flops 5637144576 | bytes 19202048 | tf_op jit(solution)/shard_map/pallas_call | solution.py:113
  166.6 2.9 %collective-permute-done.51 = bf16[48,4096]{1,0:T(8,128)(2,1)S(1)} collective-permute-done((bf16[48,4096]{1,0:T(8,128)(2,1)}, bf16[48,4096]{1,0:T(8,128)(2,1)S(1)}, u32[]{:S(2)}, u32[]{:S(2)}) %collective-permute-start.51) | collective-permute-done | bytes 393248 | tf_op jit(solution)/shard_map/ppermute | solution.py:223
  169.5 2.9 %collective-permute-done.48 = bf16[96,4096]{1,0:T(8,128)(2,1)S(1)} collective-permute-done((bf16[96,4096]{1,0:T(8,128)(2,1)S(1)}, bf16[96,4096]{1,0:T(8,128)(2,1)S(1)}, u32[]{:S(2)}, u32[]{:S(2)}) %collective-permute-start.48) | collective-permute-done | bytes 786464 | tf_op jit(solution)/shard_map/ppermute | solution.py:228
  173.2 3.4 %collective-permute-start.55 = (bf16[48,4096]{1,0:T(8,128)(2,1)S(1)}, bf16[48,4096]{1,0:T(8,128)(2,1)S(1)}, u32[]{:S(2)}, u32[]{:S(2)}) collective-permute-start(bf16[48,4096]{1,0:T(8,128)(2,1)S(1)} %get-tuple-element.244), channel_id=1, source_target_pairs={{0,3},{1,0},{2,1},{3,2},{4,7},{5,4},{6,5},{7,6},{8,11},{9,8},{10,9... | collective-permute-start | bytes 1179656 | tf_op jit(solution)/shard_map/ppermute | solution.py:223
  177.7 13.2 %shard_map.100 = f32[896,4096]{1,0:T(8,128)} custom-call(bf16[48,4096]{1,0:T(8,128)(2,1)} %refs_0_.5, bf16[16,4096]{1,0:T(8,128)(2,1)} %copy-done.57, bf16[32,4096]{1,0:T(8,128)(2,1)} %copy-done.51, bf16[48,4096]{1,0:T(8,128)(2,1)} %collective-permute-done.2.refs_3_, bf16[16,4096]{1,0:T(8,128)(2,1)} %copy-done.59, bf16[32,4096]{1,0:T(8,128)(2,1)} %copy-done.52, ...), custom_call_target="tpu_custom_call" | custom-call | flops 5637144576 | bytes 22347776 | tf_op jit(solution)/shard_map/pallas_call | solution.py:209
  190.9 1.9 collective-permute-done.55
  193.1 2.1 collective-permute-start.58
  195.3 1.6 collective-permute-start.57
  196.9 17.8 %shard_map.101 = (f32[4096,896]{1,0:T(8,128)}, f32[4096,896]{1,0:T(8,128)}) custom-call(bf16[48,4096]{1,0:T(8,128)(2,1)} %refs_0_.6, bf16[48,4096]{1,0:T(8,128)(2,1)} %copy-done.23, bf16[48,4096]{1,0:T(8,128)(2,1)} %copy-done.24, bf16[48,4096]{1,0:T(8,128)(2,1)} %copy-done.25, bf16[48,4096]{1,0:T(8,128)(2,1)} %copy-done.22, bf16[48,4096]{1,0:T(8,128)(2,1)} %copy-done.28, ...), custom_call_target="tpu_custom_call" | custom-call | flops 11274289152 | bytes 38404096 | tf_op jit(solution)/shard_map/pallas_call | solution.py:185
  214.7 1.7 convert_add_fusion.4
  (231 shorter events, 25.5 us)
Async XLA Ops:
  0.6 14.4 %collective-permute-start.1 = (bf16[48,4096]{1,0:T(8,128)(2,1)}, bf16[48,4096]{1,0:T(8,128)(2,1)S(1)}, u32[]{:S(2)}, u32[]{:S(2)}) collective-permute-start(bf16[48,4096]{1,0:T(8,128)(2,1)} %refs_0_.6), channel_id=1, source_target_pairs={{0,1},{1,2},{2,3},{3,0},{4,5},{5,6},{6,7},{7,4},{8,9},{9,10},{10,1... | collective-permute-start | bytes 1179656 | tf_op jit(solution)/shard_map/ppermute | solution.py:223
  3.7 11.4 %collective-permute-start = (bf16[48,4096]{1,0:T(8,128)(2,1)}, bf16[48,4096]{1,0:T(8,128)(2,1)S(1)}, u32[]{:S(2)}, u32[]{:S(2)}) collective-permute-start(bf16[48,4096]{1,0:T(8,128)(2,1)} %refs_0_.6), channel_id=1, source_target_pairs={{0,8},{4,12},{8,0},{12,4},{1,9},{5,13},{9,1},{13,5},{2,10},{6,14},... | collective-permute-start | bytes 1179656 | tf_op jit(solution)/shard_map/ppermute | solution.py:228
  5.2 9.8 %collective-permute-start.2 = (bf16[48,4096]{1,0:T(8,128)(2,1)}, bf16[48,4096]{1,0:T(8,128)(2,1)}, u32[]{:S(2)}, u32[]{:S(2)}) collective-permute-start(bf16[48,4096]{1,0:T(8,128)(2,1)} %refs_0_.5), channel_id=1, source_target_pairs={{0,4},{4,0},{8,12},{12,8},{1,5},{5,1},{9,13},{13,9},{2,6},{6,2},{1... | collective-permute-start | bytes 1179656 | tf_op jit(solution)/shard_map/ppermute | solution.py:228
  15.2 5.4 %collective-permute-start.8 = (bf16[48,4096]{1,0:T(8,128)(2,1)S(1)}, bf16[48,4096]{1,0:T(8,128)(2,1)S(1)}, u32[]{:S(2)}, u32[]{:S(2)}) collective-permute-start(bf16[48,4096]{1,0:T(8,128)(2,1)S(1)} %collective-permute-done.refs_1_), channel_id=1, source_target_pairs={{0,4},{4,0},{8,12},{12,8},{1,5},{5,1},{9,13},{13,9},{2,6},{6,2},{1... | collective-permute-start | bytes 1179656 | tf_op jit(solution)/shard_map/ppermute | solution.py:228
  15.6 14.1 %collective-permute-start.4 = (bf16[48,4096]{1,0:T(8,128)(2,1)}, bf16[48,4096]{1,0:T(8,128)(2,1)S(1)}, u32[]{:S(2)}, u32[]{:S(2)}) collective-permute-start(bf16[48,4096]{1,0:T(8,128)(2,1)} %refs_0_.6), channel_id=1, source_target_pairs={{0,3},{1,0},{2,1},{3,2},{4,7},{5,4},{6,5},{7,6},{8,11},{9,8},{10,9... | collective-permute-start | bytes 1179656 | tf_op jit(solution)/shard_map/ppermute | solution.py:223
  17.4 12.4 %collective-permute-start.6 = (bf16[48,4096]{1,0:T(8,128)(2,1)S(1)}, bf16[48,4096]{1,0:T(8,128)(2,1)S(1)}, u32[]{:S(2)}, u32[]{:S(2)}) collective-permute-start(bf16[48,4096]{1,0:T(8,128)(2,1)S(1)} %collective-permute-done.1.refs_0_.refs_4_), channel_id=1, source_target_pairs={{0,4},{4,0},{8,12},{12,8},{1,5},{5,1},{9,13},{13,9},{2,6},{6,2},{1... | collective-permute-start | bytes 1179656 | tf_op jit(solution)/shard_map/ppermute | solution.py:228
  17.4 12.4 %collective-permute-start.3 = (bf16[48,4096]{1,0:T(8,128)(2,1)S(1)}, bf16[48,4096]{1,0:T(8,128)(2,1)S(1)}, u32[]{:S(2)}, u32[]{:S(2)}) collective-permute-start(bf16[48,4096]{1,0:T(8,128)(2,1)S(1)} %collective-permute-done.1.refs_0_.refs_4_), channel_id=1, source_target_pairs={{0,8},{4,12},{8,0},{12,4},{1,9},{5,13},{9,1},{13,5},{2,10},{6,14},... | collective-permute-start | bytes 1179656 | tf_op jit(solution)/shard_map/ppermute | solution.py:228
  18.9 10.8 %collective-permute-start.5 = (bf16[16,4096]{1,0:T(8,128)(2,1)S(1)}, bf16[16,4096]{1,0:T(8,128)(2,1)S(1)}, u32[]{:S(2)}, u32[]{:S(2)}) collective-permute-start(bf16[16,4096]{1,0:T(8,128)(2,1)S(1)} %slice.174), channel_id=1, source_target_pairs={{0,3},{1,0},{2,1},{3,2},{4,7},{5,4},{6,5},{7,6},{8,11},{9,8},{10,9... | collective-permute-start | bytes 393224 | tf_op jit(solution)/shard_map/ppermute | solution.py:223
  29.8 20.2 %collective-permute-start.14 = (bf16[384,896]{1,0:T(8,128)(2,1)}, bf16[384,896]{1,0:T(8,128)(2,1)S(1)}, u32[]{:S(2)}, u32[]{:S(2)}) collective-permute-start(bf16[384,896]{1,0:T(8,128)(2,1)} %shard_map.92), channel_id=1, source_target_pairs={{0,16},{16,0},{1,17},{17,1},{2,18},{18,2},{3,19},{19,3},{4,20},{20... | collective-permute-start | bytes 2064392 | tf_op jit(solution)/shard_map/ppermute | solution.py:234
  31.4 14.5 %collective-permute-start.12 = (bf16[32,4096]{1,0:T(8,128)(2,1)S(1)}, bf16[32,4096]{1,0:T(8,128)(2,1)S(1)}, u32[]{:S(2)}, u32[]{:S(2)}) collective-permute-start(bf16[32,4096]{1,0:T(8,128)(2,1)S(1)} %slice.175), channel_id=1, source_target_pairs={{0,8},{4,12},{8,0},{12,4},{1,9},{5,13},{9,1},{13,5},{2,10},{6,14},... | collective-permute-start | bytes 786440 | tf_op jit(solution)/shard_map/ppermute | solution.py:228
  32.9 17.1 %collective-permute-start.9 = (bf16[48,4096]{1,0:T(8,128)(2,1)S(1)}, bf16[48,4096]{1,0:T(8,128)(2,1)S(1)}, u32[]{:S(2)}, u32[]{:S(2)}) collective-permute-start(bf16[48,4096]{1,0:T(8,128)(2,1)S(1)} %collective-permute-done.1.refs_0_.refs_4_), channel_id=1, source_target_pairs={{0,1},{1,2},{2,3},{3,0},{4,5},{5,6},{6,7},{7,4},{8,9},{9,10},{10,1... | collective-permute-start | bytes 1179656 | tf_op jit(solution)/shard_map/ppermute | solution.py:223
  33.8 16.2 %collective-permute-start.11 = (bf16[48,4096]{1,0:T(8,128)(2,1)S(1)}, bf16[48,4096]{1,0:T(8,128)(2,1)S(1)}, u32[]{:S(2)}, u32[]{:S(2)}) collective-permute-start(bf16[48,4096]{1,0:T(8,128)(2,1)S(1)} %collective-permute-done.4.refs_0_.refs_8_), channel_id=1, source_target_pairs={{0,8},{4,12},{8,0},{12,4},{1,9},{5,13},{9,1},{13,5},{2,10},{6,14},... | collective-permute-start | bytes 1179656 | tf_op jit(solution)/shard_map/ppermute | solution.py:228
  35.5 14.5 %collective-permute-start.10 = (bf16[32,4096]{1,0:T(8,128)(2,1)S(1)}, bf16[32,4096]{1,0:T(8,128)(2,1)S(1)}, u32[]{:S(2)}, u32[]{:S(2)}) collective-permute-start(bf16[32,4096]{1,0:T(8,128)(2,1)S(1)} %slice.175), channel_id=1, source_target_pairs={{0,3},{1,0},{2,1},{3,2},{4,7},{5,4},{6,5},{7,6},{8,11},{9,8},{10,9... | collective-permute-start | bytes 786440 | tf_op jit(solution)/shard_map/ppermute | solution.py:223
  50.0 19.3 %collective-permute-start.21 = (bf16[384,896]{1,0:T(8,128)(2,1)}, bf16[384,896]{1,0:T(8,128)(2,1)S(1)}, u32[]{:S(2)}, u32[]{:S(2)}) collective-permute-start(bf16[384,896]{1,0:T(8,128)(2,1)} %shard_map.93), channel_id=1, source_target_pairs={{0,16},{16,0},{1,17},{17,1},{2,18},{18,2},{3,19},{19,3},{4,20},{20... | collective-permute-start | bytes 2064392 | tf_op jit(solution)/shard_map/ppermute | solution.py:234
  51.2 18.1 %collective-permute-start.15 = (bf16[48,4096]{1,0:T(8,128)(2,1)S(1)}, bf16[48,4096]{1,0:T(8,128)(2,1)S(1)}, u32[]{:S(2)}, u32[]{:S(2)}) collective-permute-start(bf16[48,4096]{1,0:T(8,128)(2,1)S(1)} %constant_dynamic-update-slice_fusion.refs_0_.refs_10_), channel_id=1, source_target_pairs={{0,3},{1,0},{2,1},{3,2},{4,7},{5,4},{6,5},{7,6},{8,11},{9,8},{10,9... | collective-permute-start | bytes 1179656 | tf_op jit(solution)/shard_map/ppermute | solution.py:223
  53.0 16.4 %collective-permute-start.16 = (bf16[48,4096]{1,0:T(8,128)(2,1)S(1)}, bf16[48,4096]{1,0:T(8,128)(2,1)S(1)}, u32[]{:S(2)}, u32[]{:S(2)}) collective-permute-start(bf16[48,4096]{1,0:T(8,128)(2,1)S(1)} %collective-permute-done.9.refs_0_.refs_12_), channel_id=1, source_target_pairs={{0,8},{4,12},{8,0},{12,4},{1,9},{5,13},{9,1},{13,5},{2,10},{6,14},... | collective-permute-start | bytes 1179656 | tf_op jit(solution)/shard_map/ppermute | solution.py:228
  53.8 8.8 %collective-permute-start.20 = (bf16[32,4096]{1,0:T(8,128)(2,1)S(1)}, bf16[32,4096]{1,0:T(8,128)(2,1)S(1)}, u32[]{:S(2)}, u32[]{:S(2)}) collective-permute-start(bf16[32,4096]{1,0:T(8,128)(2,1)S(1)} %collective-permute-done.12.refs_2_), channel_id=1, source_target_pairs={{0,4},{4,0},{8,12},{12,8},{1,5},{5,1},{9,13},{13,9},{2,6},{6,2},{1... | collective-permute-start | bytes 786440 | tf_op jit(solution)/shard_map/ppermute | solution.py:228
  53.9 15.5 %collective-permute-start.17 = (bf16[32,4096]{1,0:T(8,128)(2,1)S(1)}, bf16[32,4096]{1,0:T(8,128)(2,1)S(1)}, u32[]{:S(2)}, u32[]{:S(2)}) collective-permute-start(bf16[32,4096]{1,0:T(8,128)(2,1)S(1)} %collective-permute-done.10), channel_id=1, source_target_pairs={{0,8},{4,12},{8,0},{12,4},{1,9},{5,13},{9,1},{13,5},{2,10},{6,14},... | collective-permute-start | bytes 786440 | tf_op jit(solution)/shard_map/ppermute | solution.py:228
  69.4 7.2 %collective-permute-start.25 = (bf16[48,4096]{1,0:T(8,128)(2,1)S(1)}, bf16[48,4096]{1,0:T(8,128)(2,1)S(1)}, u32[]{:S(2)}, u32[]{:S(2)}) collective-permute-start(bf16[48,4096]{1,0:T(8,128)(2,1)S(1)} %collective-permute-done.9.refs_0_.refs_12_), channel_id=1, source_target_pairs={{0,4},{4,0},{8,12},{12,8},{1,5},{5,1},{9,13},{13,9},{2,6},{6,2},{1... | collective-permute-start | bytes 1179656 | tf_op jit(solution)/shard_map/ppermute | solution.py:228
  69.5 18.7 %collective-permute-start.29 = (bf16[384,896]{1,0:T(8,128)(2,1)}, bf16[384,896]{1,0:T(8,128)(2,1)S(1)}, u32[]{:S(2)}, u32[]{:S(2)}) collective-permute-start(bf16[384,896]{1,0:T(8,128)(2,1)} %shard_map.94), channel_id=1, source_target_pairs={{0,16},{16,0},{1,17},{17,1},{2,18},{18,2},{3,19},{19,3},{4,20},{20... | collective-permute-start | bytes 2064392 | tf_op jit(solution)/shard_map/ppermute | solution.py:234
  71.0 5.6 %collective-permute-start.24 = (bf16[16,4096]{1,0:T(8,128)(2,1)S(1)}, bf16[16,4096]{1,0:T(8,128)(2,1)S(1)}, u32[]{:S(2)}, u32[]{:S(2)}) collective-permute-start(bf16[16,4096]{1,0:T(8,128)(2,1)S(1)} %collective-permute-done.5), channel_id=1, source_target_pairs={{0,8},{4,12},{8,0},{12,4},{1,9},{5,13},{9,1},{13,5},{2,10},{6,14},... | collective-permute-start | bytes 393224 | tf_op jit(solution)/shard_map/ppermute | solution.py:228
  71.5 6.7 %collective-permute-start.26 = (bf16[48,4096]{1,0:T(8,128)(2,1)S(1)}, bf16[48,4096]{1,0:T(8,128)(2,1)S(1)}, u32[]{:S(2)}, u32[]{:S(2)}) collective-permute-start(bf16[48,4096]{1,0:T(8,128)(2,1)S(1)} %collective-permute-done.16.refs_1_.refs_13_), channel_id=1, source_target_pairs={{0,4},{4,0},{8,12},{12,8},{1,5},{5,1},{9,13},{13,9},{2,6},{6,2},{1... | collective-permute-start | bytes 1179656 | tf_op jit(solution)/shard_map/ppermute | solution.py:228
  72.6 13.9 %collective-permute-start.22 = (bf16[48,4096]{1,0:T(8,128)(2,1)S(1)}, bf16[48,4096]{1,0:T(8,128)(2,1)S(1)}, u32[]{:S(2)}, u32[]{:S(2)}) collective-permute-start(bf16[48,4096]{1,0:T(8,128)(2,1)S(1)} %copy-done.4), channel_id=1, source_target_pairs={{0,1},{1,2},{2,3},{3,0},{4,5},{5,6},{6,7},{7,4},{8,9},{9,10},{10,1... | collective-permute-start | bytes 1179656 | tf_op jit(solution)/shard_map/ppermute | solution.py:223
  76.6 9.9 %collective-permute-start.27 = (bf16[48,4096]{1,0:T(8,128)(2,1)S(1)}, bf16[48,4096]{1,0:T(8,128)(2,1)S(1)}, u32[]{:S(2)}, u32[]{:S(2)}) collective-permute-start(bf16[48,4096]{1,0:T(8,128)(2,1)S(1)} %constant_dynamic-update-slice_fusion.refs_0_.refs_10_), channel_id=1, source_target_pairs={{0,4},{4,0},{8,12},{12,8},{1,5},{5,1},{9,13},{13,9},{2,6},{6,2},{1... | collective-permute-start | bytes 1179656 | tf_op jit(solution)/shard_map/ppermute | solution.py:228
  76.6 11.5 %collective-permute-start.23 = (bf16[48,4096]{1,0:T(8,128)(2,1)S(1)}, bf16[48,4096]{1,0:T(8,128)(2,1)S(1)}, u32[]{:S(2)}, u32[]{:S(2)}) collective-permute-start(bf16[48,4096]{1,0:T(8,128)(2,1)S(1)} %collective-permute-done.15.refs_6_.refs_16_), channel_id=1, source_target_pairs={{0,8},{4,12},{8,0},{12,4},{1,9},{5,13},{9,1},{13,5},{2,10},{6,14},... | collective-permute-start | bytes 1179656 | tf_op jit(solution)/shard_map/ppermute | solution.py:228
  78.2 8.2 %collective-permute-start.28 = (bf16[32,4096]{1,0:T(8,128)(2,1)S(1)}, bf16[32,4096]{1,0:T(8,128)(2,1)S(1)}, u32[]{:S(2)}, u32[]{:S(2)}) collective-permute-start(bf16[32,4096]{1,0:T(8,128)(2,1)S(1)} %collective-permute-done.17.refs_2_.refs_12_), channel_id=1, source_target_pairs={{0,4},{4,0},{8,12},{12,8},{1,5},{5,1},{9,13},{13,9},{2,6},{6,2},{1... | collective-permute-start | bytes 786440 | tf_op jit(solution)/shard_map/ppermute | solution.py:228
  88.7 17.6 %collective-permute-start.35 = (bf16[384,896]{1,0:T(8,128)(2,1)}, bf16[384,896]{1,0:T(8,128)(2,1)S(1)}, u32[]{:S(2)}, u32[]{:S(2)}) collective-permute-start(bf16[384,896]{1,0:T(8,128)(2,1)} %shard_map.95), channel_id=1, source_target_pairs={{0,16},{16,0},{1,17},{17,1},{2,18},{18,2},{3,19},{19,3},{4,20},{20... | collective-permute-start | bytes 2064392 | tf_op jit(solution)/shard_map/ppermute | solution.py:234
  89.5 14.7 %collective-permute-start.31 = (bf16[16,4096]{1,0:T(8,128)(2,1)}, bf16[16,4096]{1,0:T(8,128)(2,1)S(1)}, u32[]{:S(2)}, u32[]{:S(2)}) collective-permute-start(bf16[16,4096]{1,0:T(8,128)(2,1)} %copy-done.60), channel_id=1, source_target_pairs={{0,8},{4,12},{8,0},{12,4},{1,9},{5,13},{9,1},{13,5},{2,10},{6,14},... | collective-permute-start | bytes 393224 | tf_op jit(solution)/shard_map/ppermute | solution.py:228
  90.9 13.3 %collective-permute-start.30 = (bf16[48,4096]{1,0:T(8,128)(2,1)S(1)}, bf16[48,4096]{1,0:T(8,128)(2,1)S(1)}, u32[]{:S(2)}, u32[]{:S(2)}) collective-permute-start(bf16[48,4096]{1,0:T(8,128)(2,1)S(1)} %collective-permute-done.22.refs_6_), channel_id=1, source_target_pairs={{0,8},{4,12},{8,0},{12,4},{1,9},{5,13},{9,1},{13,5},{2,10},{6,14},... | collective-permute-start | bytes 1179656 | tf_op jit(solution)/shard_map/ppermute | solution.py:228
  107.8 18.0 %collective-permute-start.42 = (bf16[384,896]{1,0:T(8,128)(2,1)S(1)}, bf16[384,896]{1,0:T(8,128)(2,1)}, u32[]{:S(2)}, u32[]{:S(2)}) collective-permute-start(bf16[384,896]{1,0:T(8,128)(2,1)S(1)} %copy-done.16), channel_id=1, source_target_pairs={{0,16},{16,0},{1,17},{17,1},{2,18},{18,2},{3,19},{19,3},{4,20},{20... | collective-permute-start | bytes 2064392 | tf_op jit(solution)/shard_map/ppermute | solution.py:234
  109.1 3.9 %collective-permute-start.41 = (bf16[48,4096]{1,0:T(8,128)(2,1)S(1)}, bf16[48,4096]{1,0:T(8,128)(2,1)}, u32[]{:S(2)}, u32[]{:S(2)}) collective-permute-start(bf16[48,4096]{1,0:T(8,128)(2,1)S(1)} %copy-done.45), channel_id=1, source_target_pairs={{0,4},{4,0},{8,12},{12,8},{1,5},{5,1},{9,13},{13,9},{2,6},{6,2},{1... | collective-permute-start | bytes 1179656 | tf_op jit(solution)/shard_map/ppermute | solution.py:228
  110.3 15.5 %collective-permute-start.38 = (bf16[96,4096]{1,0:T(8,128)(2,1)}, bf16[96,4096]{1,0:T(8,128)(2,1)S(1)}, u32[]{:S(2)}, u32[]{:S(2)}) collective-permute-start(bf16[96,4096]{1,0:T(8,128)(2,1)} %get-tuple-element.171), channel_id=1, source_target_pairs={{0,4},{4,0},{8,12},{12,8},{1,5},{5,1},{9,13},{13,9},{2,6},{6,2},{1... | collective-permute-start | bytes 2359304 | tf_op jit(solution)/shard_map/ppermute | solution.py:228
  111.6 14.1 %collective-permute-start.37 = (bf16[48,4096]{1,0:T(8,128)(2,1)}, bf16[48,4096]{1,0:T(8,128)(2,1)S(1)}, u32[]{:S(2)}, u32[]{:S(2)}) collective-permute-start(bf16[48,4096]{1,0:T(8,128)(2,1)} %get-tuple-element.256), channel_id=1, source_target_pairs={{0,8},{4,12},{8,0},{12,4},{1,9},{5,13},{9,1},{13,5},{2,10},{6,14},... | collective-permute-start | bytes 1179656 | tf_op jit(solution)/shard_map/ppermute | solution.py:228
  125.9 18.2 %collective-permute-start.46 = (bf16[384,896]{1,0:T(8,128)(2,1)}, bf16[384,896]{1,0:T(8,128)(2,1)}, u32[]{:S(2)}, u32[]{:S(2)}) collective-permute-start(bf16[384,896]{1,0:T(8,128)(2,1)} %get-tuple-element.196), channel_id=1, source_target_pairs={{0,16},{16,0},{1,17},{17,1},{2,18},{18,2},{3,19},{19,3},{4,20},{20... | collective-permute-start | bytes 2064392 | tf_op jit(solution)/shard_map/ppermute | solution.py:234
  128.6 19.6 %collective-permute-start.44 = (bf16[96,4096]{1,0:T(8,128)(2,1)S(1)}, bf16[96,4096]{1,0:T(8,128)(2,1)S(1)}, u32[]{:S(2)}, u32[]{:S(2)}) collective-permute-start(bf16[96,4096]{1,0:T(8,128)(2,1)S(1)} %pad_maximum_fusion), channel_id=1, source_target_pairs={{0,8},{4,12},{8,0},{12,4},{1,9},{5,13},{9,1},{13,5},{2,10},{6,14},... | collective-permute-start | bytes 2359304 | tf_op jit(solution)/shard_map/ppermute | solution.py:228
  129.2 19.1 %collective-permute-start.45 = (bf16[96,4096]{1,0:T(8,128)(2,1)}, bf16[96,4096]{1,0:T(8,128)(2,1)S(1)}, u32[]{:S(2)}, u32[]{:S(2)}) collective-permute-start(bf16[96,4096]{1,0:T(8,128)(2,1)} %get-tuple-element.190), channel_id=1, source_target_pairs={{0,4},{4,0},{8,12},{12,8},{1,5},{5,1},{9,13},{13,9},{2,6},{6,2},{1... | collective-permute-start | bytes 2359304 | tf_op jit(solution)/shard_map/ppermute | solution.py:228
  148.3 4.3 %collective-permute-start.47 = (bf16[96,4096]{1,0:T(8,128)(2,1)}, bf16[96,4096]{1,0:T(8,128)(2,1)S(1)}, u32[]{:S(2)}, u32[]{:S(2)}) collective-permute-start(bf16[96,4096]{1,0:T(8,128)(2,1)} %get-tuple-element.198), channel_id=1, source_target_pairs={{0,4},{4,0},{8,12},{12,8},{1,5},{5,1},{9,13},{13,9},{2,6},{6,2},{1... | collective-permute-start | bytes 2359304 | tf_op jit(solution)/shard_map/ppermute | solution.py:228
  149.3 20.2 %collective-permute-start.51 = (bf16[48,4096]{1,0:T(8,128)(2,1)}, bf16[48,4096]{1,0:T(8,128)(2,1)S(1)}, u32[]{:S(2)}, u32[]{:S(2)}) collective-permute-start(bf16[48,4096]{1,0:T(8,128)(2,1)} %get-tuple-element.245), channel_id=1, source_target_pairs={{0,3},{1,0},{2,1},{3,2},{4,7},{5,4},{6,5},{7,6},{8,11},{9,8},{10,9... | collective-permute-start | bytes 1179656 | tf_op jit(solution)/shard_map/ppermute | solution.py:223
  149.7 19.8 %collective-permute-start.50 = (bf16[48,4096]{1,0:T(8,128)(2,1)S(1)}, bf16[48,4096]{1,0:T(8,128)(2,1)S(1)}, u32[]{:S(2)}, u32[]{:S(2)}) collective-permute-start(bf16[48,4096]{1,0:T(8,128)(2,1)S(1)} %get-tuple-element.246), channel_id=1, source_target_pairs={{0,1},{1,2},{2,3},{3,0},{4,5},{5,6},{6,7},{7,4},{8,9},{9,10},{10,1... | collective-permute-start | bytes 1179656 | tf_op jit(solution)/shard_map/ppermute | solution.py:223
  152.9 19.4 %collective-permute-start.48 = (bf16[96,4096]{1,0:T(8,128)(2,1)S(1)}, bf16[96,4096]{1,0:T(8,128)(2,1)S(1)}, u32[]{:S(2)}, u32[]{:S(2)}) collective-permute-start(bf16[96,4096]{1,0:T(8,128)(2,1)S(1)} %pad_maximum_fusion.1), channel_id=1, source_target_pairs={{0,8},{4,12},{8,0},{12,4},{1,9},{5,13},{9,1},{13,5},{2,10},{6,14},... | collective-permute-start | bytes 2359304 | tf_op jit(solution)/shard_map/ppermute | solution.py:228
  154.0 18.4 %collective-permute-start.49 = (bf16[96,4096]{1,0:T(8,128)(2,1)S(1)}, bf16[96,4096]{1,0:T(8,128)(2,1)S(1)}, u32[]{:S(2)}, u32[]{:S(2)}) collective-permute-start(bf16[96,4096]{1,0:T(8,128)(2,1)S(1)} %copy-done.61), channel_id=1, source_target_pairs={{0,4},{4,0},{8,12},{12,8},{1,5},{5,1},{9,13},{13,9},{2,6},{6,2},{1... | collective-permute-start | bytes 2359304 | tf_op jit(solution)/shard_map/ppermute | solution.py:228
  172.4 4.3 %collective-permute-start.52 = (bf16[96,4096]{1,0:T(8,128)(2,1)}, bf16[96,4096]{1,0:T(8,128)(2,1)S(1)}, u32[]{:S(2)}, u32[]{:S(2)}) collective-permute-start(bf16[96,4096]{1,0:T(8,128)(2,1)} %get-tuple-element.210), channel_id=1, source_target_pairs={{0,4},{4,0},{8,12},{12,8},{1,5},{5,1},{9,13},{13,9},{2,6},{6,2},{1... | collective-permute-start | bytes 2359304 | tf_op jit(solution)/shard_map/ppermute | solution.py:228
  172.7 18.2 %collective-permute-start.56 = (bf16[48,4096]{1,0:T(8,128)(2,1)S(1)}, bf16[48,4096]{1,0:T(8,128)(2,1)S(1)}, u32[]{:S(2)}, u32[]{:S(2)}) collective-permute-start(bf16[48,4096]{1,0:T(8,128)(2,1)S(1)} %get-tuple-element.243), channel_id=1, source_target_pairs={{0,1},{1,2},{2,3},{3,0},{4,5},{5,6},{6,7},{7,4},{8,9},{9,10},{10,1... | collective-permute-start | bytes 1179656 | tf_op jit(solution)/shard_map/ppermute | solution.py:223
  173.2 19.7 %collective-permute-start.55 = (bf16[48,4096]{1,0:T(8,128)(2,1)S(1)}, bf16[48,4096]{1,0:T(8,128)(2,1)S(1)}, u32[]{:S(2)}, u32[]{:S(2)}) collective-permute-start(bf16[48,4096]{1,0:T(8,128)(2,1)S(1)} %get-tuple-element.244), channel_id=1, source_target_pairs={{0,3},{1,0},{2,1},{3,2},{4,7},{5,4},{6,5},{7,6},{8,11},{9,8},{10,9... | collective-permute-start | bytes 1179656 | tf_op jit(solution)/shard_map/ppermute | solution.py:223
  176.8 16.0 %collective-permute-start.54 = (bf16[96,4096]{1,0:T(8,128)(2,1)}, bf16[96,4096]{1,0:T(8,128)(2,1)S(1)}, u32[]{:S(2)}, u32[]{:S(2)}) collective-permute-start(bf16[96,4096]{1,0:T(8,128)(2,1)} %get-tuple-element.212), channel_id=1, source_target_pairs={{0,4},{4,0},{8,12},{12,8},{1,5},{5,1},{9,13},{13,9},{2,6},{6,2},{1... | collective-permute-start | bytes 2359304 | tf_op jit(solution)/shard_map/ppermute | solution.py:228
  177.2 15.7 %collective-permute-start.53 = (bf16[48,4096]{1,0:T(8,128)(2,1)S(1)}, bf16[48,4096]{1,0:T(8,128)(2,1)S(1)}, u32[]{:S(2)}, u32[]{:S(2)}) collective-permute-start(bf16[48,4096]{1,0:T(8,128)(2,1)S(1)} %get-tuple-element.250), channel_id=1, source_target_pairs={{0,8},{4,12},{8,0},{12,4},{1,9},{5,13},{9,1},{13,5},{2,10},{6,14},... | collective-permute-start | bytes 1179656 | tf_op jit(solution)/shard_map/ppermute | solution.py:228
  193.1 21.6 %collective-permute-start.58 = (bf16[96,4096]{1,0:T(8,128)(2,1)S(1)}, bf16[96,4096]{1,0:T(8,128)(2,1)S(1)}, u32[]{:S(2)}, u32[]{:S(2)}) collective-permute-start(bf16[96,4096]{1,0:T(8,128)(2,1)S(1)} %pad_maximum_fusion.3), channel_id=1, source_target_pairs={{0,3},{1,0},{2,1},{3,2},{4,7},{5,4},{6,5},{7,6},{8,11},{9,8},{10,9... | collective-permute-start | bytes 2359304 | tf_op jit(solution)/shard_map/ppermute | solution.py:223
  195.3 19.4 %collective-permute-start.57 = (bf16[96,4096]{1,0:T(8,128)(2,1)S(1)}, bf16[96,4096]{1,0:T(8,128)(2,1)S(1)}, u32[]{:S(2)}, u32[]{:S(2)}) collective-permute-start(bf16[96,4096]{1,0:T(8,128)(2,1)S(1)} %pad_maximum_fusion.2), channel_id=1, source_target_pairs={{0,8},{4,12},{8,0},{12,4},{1,9},{5,13},{9,1},{13,5},{2,10},{6,14},... | collective-permute-start | bytes 2359304 | tf_op jit(solution)/shard_map/ppermute | solution.py:228
  (73 other events, 497.2 us)

commit v13 on v12

--- a/solution.py
+++ b/solution.py
@@ -179,7 +179,7 @@
 def wide_grads(pieces, gate_grads, up_grads):
     grads = [*gate_grads, *up_grads]
     width, units = pieces[0].shape[1], grads[0].shape[1]
-    block = min(512, width)
+    block = min(1024, width)
     rows = sum(piece.shape[0] for piece in pieces)
     out = jax.ShapeDtypeStruct((width, units), jnp.float32)
     return pl.pallas_call(

time: 218 us -> 217 us (level)
  transfers between devices with their start and end apart: 59 -> 59, of which waited for: 16 -> 17; matrix products, arithmetic and copies ran while one was open for 7% -> 7% of each run, Pallas kernels for 48% -> 48%
where the time goes in v13:
time: 217 us; the launch traced here: 216 us
  Pallas kernels  104 us (48%)
  waiting for transfers between devices  45.7 us (21%)
  starting transfers between devices  43.1 us (20%)
  other arithmetic  15.4 us (7%)
  local copies, waits for them, and re-layouts  6.46 us (3%)
    pallas_call x4, Pallas kernels, contract(): pl.pallas_call(kernel, in_specs=[pl.BlockSpec(memory_space=pl.ANY)] * n_i...  29.9 us
    pallas_call x2, Pallas kernels, down_products(): pl.pallas_call(functools.partial(down_kernel, len(pieces)), grid=(width /...  22.2 us
    ppermute x41, waiting for transfers between devices, swap(): return lax.ppermute(block, 'col', [(i, i ^ bit) for i in range(n)])  21.7 us
    pallas_call x2, Pallas kernels, expand(): pl.pallas_call(functools.partial(expand_kernel, len(lefts)), grid=(width...  21.4 us
    ppermute x12, starting transfers between devices, shift(): return lax.ppermute(block, 'depth', [(i, (i + step) % n) for i in range(n)])  20.4 us
    ppermute x12, waiting for transfers between devices, shift(): return lax.ppermute(block, 'depth', [(i, (i + step) % n) for i in range(n)])  17.8 us
    pallas_call x1, Pallas kernels, wide_grads(): pl.pallas_call(functools.partial(wide_grad_kernel, len(pieces)), grid=(wi...  17.2 us
    ppermute x41, starting transfers between devices, swap(): return lax.ppermute(block, 'col', [(i, i ^ bit) for i in range(n)])  16.5 us
  transfers between devices with their start and end apart: 59, of which 17 were waited for; matrix products, arithmetic and copies ran while one was open for 7% of the time, Pallas kernels for 48%

profile of v13, /device:TPU:0, one launch (start us, length us, event | category | flops | bytes accessed | tf_op | source)
XLA Modules:
  0.0 216.0 jit_solution(9066961252224821661)
XLA Ops:
  0.6 3.1 %collective-permute-start.1 = (bf16[48,4096]{1,0:T(8,128)(2,1)}, bf16[48,4096]{1,0:T(8,128)(2,1)S(1)}, u32[]{:S(2)}, u32[]{:S(2)}) collective-permute-start(bf16[48,4096]{1,0:T(8,128)(2,1)} %refs_0_.6), channel_id=1, source_target_pairs={{0,1},{1,2},{2,3},{3,0},{4,5},{5,6},{6,7},{7,4},{8,9},{9,10},{10,1... | collective-permute-start | bytes 1179656 | tf_op jit(solution)/shard_map/ppermute | solution.py:223
  3.7 1.5 collective-permute-start
  6.2 1.0 slice.175
  7.2 7.9 %collective-permute-done.1.refs_0_.refs_4_ = bf16[48,4096]{1,0:T(8,128)(2,1)S(1)} collective-permute-done((bf16[48,4096]{1,0:T(8,128)(2,1)}, bf16[48,4096]{1,0:T(8,128)(2,1)S(1)}, u32[]{:S(2)}, u32[]{:S(2)}) %collective-permute-start.1) | collective-permute-done | bytes 393248 | tf_op jit(solution)/shard_map/ppermute | solution.py:223
  15.6 1.7 collective-permute-start.4
  17.4 1.5 collective-permute-start.3
  18.9 1.7 collective-permute-start.5
  21.3 7.4 %shard_map.92 = bf16[384,896]{1,0:T(8,128)(2,1)} custom-call(bf16[48,4096]{1,0:T(8,128)(2,1)} %refs_0_.6, bf16[48,4096]{1,0:T(8,128)(2,1)} %copy-done.23, bf16[48,4096]{1,0:T(8,128)(2,1)} %copy-done.24, bf16[48,4096]{1,0:T(8,128)(2,1)} %copy-done.25, bf16[4096,896]{1,0:T(8,128)(2,1)} %refs_4_.11, bf16[4096,896]{1,0:T(8,128)(2,1)} %refs_5_.11), custom_call_target="tpu_custom_call" | custom-call | flops 2818572288 | bytes 16252928 | tf_op jit(solution)/shard_map/pallas_call | solution.py:78
  28.8 1.0 collective-permute-done.5
  29.8 1.6 collective-permute-start.14
  31.4 1.5 collective-permute-start.12
  34.3 1.2 collective-permute-done.13.refs_3_.refs_7_
  35.5 2.9 %collective-permute-start.10 = (bf16[32,4096]{1,0:T(8,128)(2,1)S(1)}, bf16[32,4096]{1,0:T(8,128)(2,1)S(1)}, u32[]{:S(2)}, u32[]{:S(2)}) collective-permute-start(bf16[32,4096]{1,0:T(8,128)(2,1)S(1)} %slice.175), channel_id=1, source_target_pairs={{0,3},{1,0},{2,1},{3,2},{4,7},{5,4},{6,5},{7,6},{8,11},{9,8},{10,9... | collective-permute-start | bytes 786440 | tf_op jit(solution)/shard_map/ppermute | solution.py:223
  38.4 7.5 %shard_map.93 = bf16[384,896]{1,0:T(8,128)(2,1)} custom-call(bf16[48,4096]{1,0:T(8,128)(2,1)} %copy-done.22, bf16[48,4096]{1,0:T(8,128)(2,1)} %copy-done.28, bf16[48,4096]{1,0:T(8,128)(2,1)} %copy-done.27, bf16[48,4096]{1,0:T(8,128)(2,1)} %copy-done.30, bf16[4096,896]{1,0:T(8,128)(2,1)} %refs_4_.11, bf16[4096,896]{1,0:T(8,128)(2,1)} %refs_5_.11), custom_call_target="tpu_custom_call" | custom-call | flops 2818572288 | bytes 16252928 | tf_op jit(solution)/shard_map/pallas_call | solution.py:78
  45.9 4.1 %collective-permute-done.10 = bf16[32,4096]{1,0:T(8,128)(2,1)S(1)} collective-permute-done((bf16[32,4096]{1,0:T(8,128)(2,1)S(1)}, bf16[32,4096]{1,0:T(8,128)(2,1)S(1)}, u32[]{:S(2)}, u32[]{:S(2)}) %collective-permute-start.10) | collective-permute-done | bytes 262176 | tf_op jit(solution)/shard_map/ppermute | solution.py:223
  51.2 1.8 collective-permute-start.15
  53.9 1.2 collective-permute-start.17
  55.1 7.5 %shard_map.94 = bf16[384,896]{1,0:T(8,128)(2,1)} custom-call(bf16[48,4096]{1,0:T(8,128)(2,1)} %copy-done.26, bf16[48,4096]{1,0:T(8,128)(2,1)} %copy-done.31, bf16[48,4096]{1,0:T(8,128)(2,1)} %copy-done.32, bf16[48,4096]{1,0:T(8,128)(2,1)} %copy-done.33, bf16[4096,896]{1,0:T(8,128)(2,1)} %refs_4_.11, bf16[4096,896]{1,0:T(8,128)(2,1)} %refs_5_.11), custom_call_target="tpu_custom_call" | custom-call | flops 2818572288 | bytes 16252928 | tf_op jit(solution)/shard_map/pallas_call | solution.py:78
  62.6 6.7 %collective-permute-done.17.refs_2_.refs_12_ = bf16[32,4096]{1,0:T(8,128)(2,1)S(1)} collective-permute-done((bf16[32,4096]{1,0:T(8,128)(2,1)S(1)}, bf16[32,4096]{1,0:T(8,128)(2,1)S(1)}, u32[]{:S(2)}, u32[]{:S(2)}) %collective-permute-start.17) | collective-permute-done | bytes 262176 | tf_op jit(solution)/shard_map/ppermute | solution.py:228
  69.5 1.6 collective-permute-start.29
  71.5 1.0 multiply_convert_fusion.11.refs_10_.refs_20_
  72.9 3.7 %collective-permute-done.24.refs_1_.refs_11_ = bf16[16,4096]{1,0:T(8,128)(2,1)S(1)} collective-permute-done((bf16[16,4096]{1,0:T(8,128)(2,1)S(1)}, bf16[16,4096]{1,0:T(8,128)(2,1)S(1)}, u32[]{:S(2)}, u32[]{:S(2)}) %collective-permute-start.24) | collective-permute-done | bytes 131104 | tf_op jit(solution)/shard_map/ppermute | solution.py:228
  77.2 1.0 multiply_convert_fusion.10.refs_11_.refs_21_
  79.0 7.5 %shard_map.95 = bf16[384,896]{1,0:T(8,128)(2,1)} custom-call(bf16[48,4096]{1,0:T(8,128)(2,1)} %copy-done.29, bf16[48,4096]{1,0:T(8,128)(2,1)} %copy-done.34, bf16[48,4096]{1,0:T(8,128)(2,1)} %copy-done.35, bf16[48,4096]{1,0:T(8,128)(2,1)} %copy-done.36, bf16[4096,896]{1,0:T(8,128)(2,1)} %refs_4_.11, bf16[4096,896]{1,0:T(8,128)(2,1)} %refs_5_.11), custom_call_target="tpu_custom_call" | custom-call | flops 2818572288 | bytes 16252928 | tf_op jit(solution)/shard_map/pallas_call | solution.py:78
  86.5 1.7 collective-permute-done.23.refs_7_.refs_17_
  93.1 11.1 %shard_map.96 = (bf16[384,896]{1,0:T(8,128)(2,1)}, bf16[96,4096]{1,0:T(8,128)(2,1)}, bf16[96,4096]{1,0:T(8,128)(2,1)}, bf16[96,4096]{1,0:T(8,128)(2,1)}, bf16[96,4096]{1,0:T(8,128)(2,1)}) custom-call(bf16[48,4096]{1,0:T(8,128)(2,1)} %copy-done.15, bf16[16,4096]{1,0:T(8,128)(2,1)} %copy-done.55, bf16[32,4096]{1,0:T(8,128)(2,1)} %copy-done.53, ...), custom_call_target="tpu_custom_call" | custom-call | flops 5637144576 | bytes 14319616 | tf_op jit(solution)/shard_map/pallas_call | solution.py:150
  104.2 2.1 collective-permute-done.35
  113.0 11.1 %shard_map.97 = (bf16[384,896]{1,0:T(8,128)(2,1)}, bf16[96,4096]{1,0:T(8,128)(2,1)}, bf16[96,4096]{1,0:T(8,128)(2,1)}, bf16[96,4096]{1,0:T(8,128)(2,1)}, bf16[96,4096]{1,0:T(8,128)(2,1)}) custom-call(bf16[48,4096]{1,0:T(8,128)(2,1)} %refs_0_.5, bf16[16,4096]{1,0:T(8,128)(2,1)} %copy-done.57, bf16[32,4096]{1,0:T(8,128)(2,1)} %copy-done.51, ...), custom_call_target="tpu_custom_call" | custom-call | flops 5637144576 | bytes 14319616 | tf_op jit(solution)/shard_map/pallas_call | solution.py:150
  124.1 1.6 collective-permute-done.42
  126.7 1.2 convert_add_fusion.1
  129.2 1.7 multiply_convert_fusion.4
  130.9 10.7 %shard_map.98 = (bf16[96,4096]{1,0:T(8,128)(2,1)}, bf16[96,4096]{1,0:T(8,128)(2,1)}, bf16[96,4096]{1,0:T(8,128)(2,1)}, bf16[96,4096]{1,0:T(8,128)(2,1)}) custom-call(bf16[192,896]{1,0:T(8,128)(2,1)} %get-tuple-element.259.refs_0_.refs_18_, bf16[192,896]{1,0:T(8,128)(2,1)} %get-tuple-element.240.refs_1_.refs_19_, ...), custom_call_target="tpu_custom_call" | custom-call | flops 5637144576 | bytes 19202048 | tf_op jit(solution)/shard_map/pallas_call | solution.py:113
  141.6 2.5 %collective-permute-done.46 = bf16[384,896]{1,0:T(8,128)(2,1)} collective-permute-done((bf16[384,896]{1,0:T(8,128)(2,1)}, bf16[384,896]{1,0:T(8,128)(2,1)}, u32[]{:S(2)}, u32[]{:S(2)}) %collective-permute-start.46) | collective-permute-done | bytes 688160 | tf_op jit(solution)/shard_map/ppermute | solution.py:234
  144.0 4.2 %collective-permute-done.44 = bf16[96,4096]{1,0:T(8,128)(2,1)S(1)} collective-permute-done((bf16[96,4096]{1,0:T(8,128)(2,1)S(1)}, bf16[96,4096]{1,0:T(8,128)(2,1)S(1)}, u32[]{:S(2)}, u32[]{:S(2)}) %collective-permute-start.44) | collective-permute-done | bytes 786464 | tf_op jit(solution)/shard_map/ppermute | solution.py:228
  148.3 1.1 add_convert_fusion.6
  149.7 1.7 collective-permute-start.50
  151.4 1.2 convert_add_fusion
  154.0 1.9 multiply_convert_fusion
  155.9 10.7 %shard_map.99 = (bf16[96,4096]{1,0:T(8,128)(2,1)}, bf16[96,4096]{1,0:T(8,128)(2,1)}, bf16[96,4096]{1,0:T(8,128)(2,1)}, bf16[96,4096]{1,0:T(8,128)(2,1)}) custom-call(bf16[192,896]{1,0:T(8,128)(2,1)} %get-tuple-element.257.refs_0_.refs_16_, bf16[192,896]{1,0:T(8,128)(2,1)} %get-tuple-element.236.refs_1_.refs_17_, ...), custom_call_target="tpu_custom_call" | custom-call | flops 5637144576 | bytes 19202048 | tf_op jit(solution)/shard_map/pallas_call | solution.py:113
  166.6 2.9 %collective-permute-done.51 = bf16[48,4096]{1,0:T(8,128)(2,1)S(1)} collective-permute-done((bf16[48,4096]{1,0:T(8,128)(2,1)}, bf16[48,4096]{1,0:T(8,128)(2,1)S(1)}, u32[]{:S(2)}, u32[]{:S(2)}) %collective-permute-start.51) | collective-permute-done | bytes 393248 | tf_op jit(solution)/shard_map/ppermute | solution.py:223
  169.5 2.9 %collective-permute-done.48 = bf16[96,4096]{1,0:T(8,128)(2,1)S(1)} collective-permute-done((bf16[96,4096]{1,0:T(8,128)(2,1)S(1)}, bf16[96,4096]{1,0:T(8,128)(2,1)S(1)}, u32[]{:S(2)}, u32[]{:S(2)}) %collective-permute-start.48) | collective-permute-done | bytes 786464 | tf_op jit(solution)/shard_map/ppermute | solution.py:228
  173.2 3.4 %collective-permute-start.55 = (bf16[48,4096]{1,0:T(8,128)(2,1)S(1)}, bf16[48,4096]{1,0:T(8,128)(2,1)S(1)}, u32[]{:S(2)}, u32[]{:S(2)}) collective-permute-start(bf16[48,4096]{1,0:T(8,128)(2,1)S(1)} %get-tuple-element.244), channel_id=1, source_target_pairs={{0,3},{1,0},{2,1},{3,2},{4,7},{5,4},{6,5},{7,6},{8,11},{9,8},{10,9... | collective-permute-start | bytes 1179656 | tf_op jit(solution)/shard_map/ppermute | solution.py:223
  177.7 13.2 %shard_map.100 = f32[896,4096]{1,0:T(8,128)} custom-call(bf16[48,4096]{1,0:T(8,128)(2,1)} %refs_0_.5, bf16[16,4096]{1,0:T(8,128)(2,1)} %copy-done.57, bf16[32,4096]{1,0:T(8,128)(2,1)} %copy-done.51, bf16[48,4096]{1,0:T(8,128)(2,1)} %collective-permute-done.2.refs_3_, bf16[16,4096]{1,0:T(8,128)(2,1)} %copy-done.59, bf16[32,4096]{1,0:T(8,128)(2,1)} %copy-done.52, ...), custom_call_target="tpu_custom_call" | custom-call | flops 5637144576 | bytes 22347776 | tf_op jit(solution)/shard_map/pallas_call | solution.py:209
  190.9 1.9 collective-permute-done.55
  193.1 2.1 collective-permute-start.58
  195.3 1.6 collective-permute-start.57
  196.9 17.2 %shard_map.101 = (f32[4096,896]{1,0:T(8,128)}, f32[4096,896]{1,0:T(8,128)}) custom-call(bf16[48,4096]{1,0:T(8,128)(2,1)} %refs_0_.6, bf16[48,4096]{1,0:T(8,128)(2,1)} %copy-done.23, bf16[48,4096]{1,0:T(8,128)(2,1)} %copy-done.24, bf16[48,4096]{1,0:T(8,128)(2,1)} %copy-done.25, bf16[48,4096]{1,0:T(8,128)(2,1)} %copy-done.22, bf16[48,4096]{1,0:T(8,128)(2,1)} %copy-done.28, ...), custom_call_target="tpu_custom_call" | custom-call | flops 11274289152 | bytes 38404096 | tf_op jit(solution)/shard_map/pallas_call | solution.py:185
  214.3 1.7 convert_add_fusion.4
  (231 shorter events, 25.6 us)
Async XLA Ops:
  0.6 14.4 %collective-permute-start.1 = (bf16[48,4096]{1,0:T(8,128)(2,1)}, bf16[48,4096]{1,0:T(8,128)(2,1)S(1)}, u32[]{:S(2)}, u32[]{:S(2)}) collective-permute-start(bf16[48,4096]{1,0:T(8,128)(2,1)} %refs_0_.6), channel_id=1, source_target_pairs={{0,1},{1,2},{2,3},{3,0},{4,5},{5,6},{6,7},{7,4},{8,9},{9,10},{10,1... | collective-permute-start | bytes 1179656 | tf_op jit(solution)/shard_map/ppermute | solution.py:223
  3.7 11.4 %collective-permute-start = (bf16[48,4096]{1,0:T(8,128)(2,1)}, bf16[48,4096]{1,0:T(8,128)(2,1)S(1)}, u32[]{:S(2)}, u32[]{:S(2)}) collective-permute-start(bf16[48,4096]{1,0:T(8,128)(2,1)} %refs_0_.6), channel_id=1, source_target_pairs={{0,8},{4,12},{8,0},{12,4},{1,9},{5,13},{9,1},{13,5},{2,10},{6,14},... | collective-permute-start | bytes 1179656 | tf_op jit(solution)/shard_map/ppermute | solution.py:228
  5.2 9.8 %collective-permute-start.2 = (bf16[48,4096]{1,0:T(8,128)(2,1)}, bf16[48,4096]{1,0:T(8,128)(2,1)}, u32[]{:S(2)}, u32[]{:S(2)}) collective-permute-start(bf16[48,4096]{1,0:T(8,128)(2,1)} %refs_0_.5), channel_id=1, source_target_pairs={{0,4},{4,0},{8,12},{12,8},{1,5},{5,1},{9,13},{13,9},{2,6},{6,2},{1... | collective-permute-start | bytes 1179656 | tf_op jit(solution)/shard_map/ppermute | solution.py:228
  15.2 5.4 %collective-permute-start.8 = (bf16[48,4096]{1,0:T(8,128)(2,1)S(1)}, bf16[48,4096]{1,0:T(8,128)(2,1)S(1)}, u32[]{:S(2)}, u32[]{:S(2)}) collective-permute-start(bf16[48,4096]{1,0:T(8,128)(2,1)S(1)} %collective-permute-done.refs_1_), channel_id=1, source_target_pairs={{0,4},{4,0},{8,12},{12,8},{1,5},{5,1},{9,13},{13,9},{2,6},{6,2},{1... | collective-permute-start | bytes 1179656 | tf_op jit(solution)/shard_map/ppermute | solution.py:228
  15.6 14.1 %collective-permute-start.4 = (bf16[48,4096]{1,0:T(8,128)(2,1)}, bf16[48,4096]{1,0:T(8,128)(2,1)S(1)}, u32[]{:S(2)}, u32[]{:S(2)}) collective-permute-start(bf16[48,4096]{1,0:T(8,128)(2,1)} %refs_0_.6), channel_id=1, source_target_pairs={{0,3},{1,0},{2,1},{3,2},{4,7},{5,4},{6,5},{7,6},{8,11},{9,8},{10,9... | collective-permute-start | bytes 1179656 | tf_op jit(solution)/shard_map/ppermute | solution.py:223
  17.4 12.4 %collective-permute-start.6 = (bf16[48,4096]{1,0:T(8,128)(2,1)S(1)}, bf16[48,4096]{1,0:T(8,128)(2,1)S(1)}, u32[]{:S(2)}, u32[]{:S(2)}) collective-permute-start(bf16[48,4096]{1,0:T(8,128)(2,1)S(1)} %collective-permute-done.1.refs_0_.refs_4_), channel_id=1, source_target_pairs={{0,4},{4,0},{8,12},{12,8},{1,5},{5,1},{9,13},{13,9},{2,6},{6,2},{1... | collective-permute-start | bytes 1179656 | tf_op jit(solution)/shard_map/ppermute | solution.py:228
  17.4 12.4 %collective-permute-start.3 = (bf16[48,4096]{1,0:T(8,128)(2,1)S(1)}, bf16[48,4096]{1,0:T(8,128)(2,1)S(1)}, u32[]{:S(2)}, u32[]{:S(2)}) collective-permute-start(bf16[48,4096]{1,0:T(8,128)(2,1)S(1)} %collective-permute-done.1.refs_0_.refs_4_), channel_id=1, source_target_pairs={{0,8},{4,12},{8,0},{12,4},{1,9},{5,13},{9,1},{13,5},{2,10},{6,14},... | collective-permute-start | bytes 1179656 | tf_op jit(solution)/shard_map/ppermute | solution.py:228
  18.9 10.8 %collective-permute-start.5 = (bf16[16,4096]{1,0:T(8,128)(2,1)S(1)}, bf16[16,4096]{1,0:T(8,128)(2,1)S(1)}, u32[]{:S(2)}, u32[]{:S(2)}) collective-permute-start(bf16[16,4096]{1,0:T(8,128)(2,1)S(1)} %slice.174), channel_id=1, source_target_pairs={{0,3},{1,0},{2,1},{3,2},{4,7},{5,4},{6,5},{7,6},{8,11},{9,8},{10,9... | collective-permute-start | bytes 393224 | tf_op jit(solution)/shard_map/ppermute | solution.py:223
  29.8 20.2 %collective-permute-start.14 = (bf16[384,896]{1,0:T(8,128)(2,1)}, bf16[384,896]{1,0:T(8,128)(2,1)S(1)}, u32[]{:S(2)}, u32[]{:S(2)}) collective-permute-start(bf16[384,896]{1,0:T(8,128)(2,1)} %shard_map.92), channel_id=1, source_target_pairs={{0,16},{16,0},{1,17},{17,1},{2,18},{18,2},{3,19},{19,3},{4,20},{20... | collective-permute-start | bytes 2064392 | tf_op jit(solution)/shard_map/ppermute | solution.py:234
  31.4 14.5 %collective-permute-start.12 = (bf16[32,4096]{1,0:T(8,128)(2,1)S(1)}, bf16[32,4096]{1,0:T(8,128)(2,1)S(1)}, u32[]{:S(2)}, u32[]{:S(2)}) collective-permute-start(bf16[32,4096]{1,0:T(8,128)(2,1)S(1)} %slice.175), channel_id=1, source_target_pairs={{0,8},{4,12},{8,0},{12,4},{1,9},{5,13},{9,1},{13,5},{2,10},{6,14},... | collective-permute-start | bytes 786440 | tf_op jit(solution)/shard_map/ppermute | solution.py:228
  32.9 17.1 %collective-permute-start.9 = (bf16[48,4096]{1,0:T(8,128)(2,1)S(1)}, bf16[48,4096]{1,0:T(8,128)(2,1)S(1)}, u32[]{:S(2)}, u32[]{:S(2)}) collective-permute-start(bf16[48,4096]{1,0:T(8,128)(2,1)S(1)} %collective-permute-done.1.refs_0_.refs_4_), channel_id=1, source_target_pairs={{0,1},{1,2},{2,3},{3,0},{4,5},{5,6},{6,7},{7,4},{8,9},{9,10},{10,1... | collective-permute-start | bytes 1179656 | tf_op jit(solution)/shard_map/ppermute | solution.py:223
  33.8 16.2 %collective-permute-start.11 = (bf16[48,4096]{1,0:T(8,128)(2,1)S(1)}, bf16[48,4096]{1,0:T(8,128)(2,1)S(1)}, u32[]{:S(2)}, u32[]{:S(2)}) collective-permute-start(bf16[48,4096]{1,0:T(8,128)(2,1)S(1)} %collective-permute-done.4.refs_0_.refs_8_), channel_id=1, source_target_pairs={{0,8},{4,12},{8,0},{12,4},{1,9},{5,13},{9,1},{13,5},{2,10},{6,14},... | collective-permute-start | bytes 1179656 | tf_op jit(solution)/shard_map/ppermute | solution.py:228
  35.5 14.5 %collective-permute-start.10 = (bf16[32,4096]{1,0:T(8,128)(2,1)S(1)}, bf16[32,4096]{1,0:T(8,128)(2,1)S(1)}, u32[]{:S(2)}, u32[]{:S(2)}) collective-permute-start(bf16[32,4096]{1,0:T(8,128)(2,1)S(1)} %slice.175), channel_id=1, source_target_pairs={{0,3},{1,0},{2,1},{3,2},{4,7},{5,4},{6,5},{7,6},{8,11},{9,8},{10,9... | collective-permute-start | bytes 786440 | tf_op jit(solution)/shard_map/ppermute | solution.py:223
  50.0 19.3 %collective-permute-start.21 = (bf16[384,896]{1,0:T(8,128)(2,1)}, bf16[384,896]{1,0:T(8,128)(2,1)S(1)}, u32[]{:S(2)}, u32[]{:S(2)}) collective-permute-start(bf16[384,896]{1,0:T(8,128)(2,1)} %shard_map.93), channel_id=1, source_target_pairs={{0,16},{16,0},{1,17},{17,1},{2,18},{18,2},{3,19},{19,3},{4,20},{20... | collective-permute-start | bytes 2064392 | tf_op jit(solution)/shard_map/ppermute | solution.py:234
  51.2 18.1 %collective-permute-start.15 = (bf16[48,4096]{1,0:T(8,128)(2,1)S(1)}, bf16[48,4096]{1,0:T(8,128)(2,1)S(1)}, u32[]{:S(2)}, u32[]{:S(2)}) collective-permute-start(bf16[48,4096]{1,0:T(8,128)(2,1)S(1)} %constant_dynamic-update-slice_fusion.refs_0_.refs_10_), channel_id=1, source_target_pairs={{0,3},{1,0},{2,1},{3,2},{4,7},{5,4},{6,5},{7,6},{8,11},{9,8},{10,9... | collective-permute-start | bytes 1179656 | tf_op jit(solution)/shard_map/ppermute | solution.py:223
  53.0 16.4 %collective-permute-start.16 = (bf16[48,4096]{1,0:T(8,128)(2,1)S(1)}, bf16[48,4096]{1,0:T(8,128)(2,1)S(1)}, u32[]{:S(2)}, u32[]{:S(2)}) collective-permute-start(bf16[48,4096]{1,0:T(8,128)(2,1)S(1)} %collective-permute-done.9.refs_0_.refs_12_), channel_id=1, source_target_pairs={{0,8},{4,12},{8,0},{12,4},{1,9},{5,13},{9,1},{13,5},{2,10},{6,14},... | collective-permute-start | bytes 1179656 | tf_op jit(solution)/shard_map/ppermute | solution.py:228
  53.8 8.8 %collective-permute-start.20 = (bf16[32,4096]{1,0:T(8,128)(2,1)S(1)}, bf16[32,4096]{1,0:T(8,128)(2,1)S(1)}, u32[]{:S(2)}, u32[]{:S(2)}) collective-permute-start(bf16[32,4096]{1,0:T(8,128)(2,1)S(1)} %collective-permute-done.12.refs_2_), channel_id=1, source_target_pairs={{0,4},{4,0},{8,12},{12,8},{1,5},{5,1},{9,13},{13,9},{2,6},{6,2},{1... | collective-permute-start | bytes 786440 | tf_op jit(solution)/shard_map/ppermute | solution.py:228
  53.9 15.5 %collective-permute-start.17 = (bf16[32,4096]{1,0:T(8,128)(2,1)S(1)}, bf16[32,4096]{1,0:T(8,128)(2,1)S(1)}, u32[]{:S(2)}, u32[]{:S(2)}) collective-permute-start(bf16[32,4096]{1,0:T(8,128)(2,1)S(1)} %collective-permute-done.10), channel_id=1, source_target_pairs={{0,8},{4,12},{8,0},{12,4},{1,9},{5,13},{9,1},{13,5},{2,10},{6,14},... | collective-permute-start | bytes 786440 | tf_op jit(solution)/shard_map/ppermute | solution.py:228
  69.4 7.2 %collective-permute-start.25 = (bf16[48,4096]{1,0:T(8,128)(2,1)S(1)}, bf16[48,4096]{1,0:T(8,128)(2,1)S(1)}, u32[]{:S(2)}, u32[]{:S(2)}) collective-permute-start(bf16[48,4096]{1,0:T(8,128)(2,1)S(1)} %collective-permute-done.9.refs_0_.refs_12_), channel_id=1, source_target_pairs={{0,4},{4,0},{8,12},{12,8},{1,5},{5,1},{9,13},{13,9},{2,6},{6,2},{1... | collective-permute-start | bytes 1179656 | tf_op jit(solution)/shard_map/ppermute | solution.py:228
  69.5 18.7 %collective-permute-start.29 = (bf16[384,896]{1,0:T(8,128)(2,1)}, bf16[384,896]{1,0:T(8,128)(2,1)S(1)}, u32[]{:S(2)}, u32[]{:S(2)}) collective-permute-start(bf16[384,896]{1,0:T(8,128)(2,1)} %shard_map.94), channel_id=1, source_target_pairs={{0,16},{16,0},{1,17},{17,1},{2,18},{18,2},{3,19},{19,3},{4,20},{20... | collective-permute-start | bytes 2064392 | tf_op jit(solution)/shard_map/ppermute | solution.py:234
  71.0 5.6 %collective-permute-start.24 = (bf16[16,4096]{1,0:T(8,128)(2,1)S(1)}, bf16[16,4096]{1,0:T(8,128)(2,1)S(1)}, u32[]{:S(2)}, u32[]{:S(2)}) collective-permute-start(bf16[16,4096]{1,0:T(8,128)(2,1)S(1)} %collective-permute-done.5), channel_id=1, source_target_pairs={{0,8},{4,12},{8,0},{12,4},{1,9},{5,13},{9,1},{13,5},{2,10},{6,14},... | collective-permute-start | bytes 393224 | tf_op jit(solution)/shard_map/ppermute | solution.py:228
  71.5 6.7 %collective-permute-start.26 = (bf16[48,4096]{1,0:T(8,128)(2,1)S(1)}, bf16[48,4096]{1,0:T(8,128)(2,1)S(1)}, u32[]{:S(2)}, u32[]{:S(2)}) collective-permute-start(bf16[48,4096]{1,0:T(8,128)(2,1)S(1)} %collective-permute-done.16.refs_1_.refs_13_), channel_id=1, source_target_pairs={{0,4},{4,0},{8,12},{12,8},{1,5},{5,1},{9,13},{13,9},{2,6},{6,2},{1... | collective-permute-start | bytes 1179656 | tf_op jit(solution)/shard_map/ppermute | solution.py:228
  72.6 13.9 %collective-permute-start.22 = (bf16[48,4096]{1,0:T(8,128)(2,1)S(1)}, bf16[48,4096]{1,0:T(8,128)(2,1)S(1)}, u32[]{:S(2)}, u32[]{:S(2)}) collective-permute-start(bf16[48,4096]{1,0:T(8,128)(2,1)S(1)} %copy-done.4), channel_id=1, source_target_pairs={{0,1},{1,2},{2,3},{3,0},{4,5},{5,6},{6,7},{7,4},{8,9},{9,10},{10,1... | collective-permute-start | bytes 1179656 | tf_op jit(solution)/shard_map/ppermute | solution.py:223
  76.6 9.9 %collective-permute-start.27 = (bf16[48,4096]{1,0:T(8,128)(2,1)S(1)}, bf16[48,4096]{1,0:T(8,128)(2,1)S(1)}, u32[]{:S(2)}, u32[]{:S(2)}) collective-permute-start(bf16[48,4096]{1,0:T(8,128)(2,1)S(1)} %constant_dynamic-update-slice_fusion.refs_0_.refs_10_), channel_id=1, source_target_pairs={{0,4},{4,0},{8,12},{12,8},{1,5},{5,1},{9,13},{13,9},{2,6},{6,2},{1... | collective-permute-start | bytes 1179656 | tf_op jit(solution)/shard_map/ppermute | solution.py:228
  76.6 11.5 %collective-permute-start.23 = (bf16[48,4096]{1,0:T(8,128)(2,1)S(1)}, bf16[48,4096]{1,0:T(8,128)(2,1)S(1)}, u32[]{:S(2)}, u32[]{:S(2)}) collective-permute-start(bf16[48,4096]{1,0:T(8,128)(2,1)S(1)} %collective-permute-done.15.refs_6_.refs_16_), channel_id=1, source_target_pairs={{0,8},{4,12},{8,0},{12,4},{1,9},{5,13},{9,1},{13,5},{2,10},{6,14},... | collective-permute-start | bytes 1179656 | tf_op jit(solution)/shard_map/ppermute | solution.py:228
  78.2 8.2 %collective-permute-start.28 = (bf16[32,4096]{1,0:T(8,128)(2,1)S(1)}, bf16[32,4096]{1,0:T(8,128)(2,1)S(1)}, u32[]{:S(2)}, u32[]{:S(2)}) collective-permute-start(bf16[32,4096]{1,0:T(8,128)(2,1)S(1)} %collective-permute-done.17.refs_2_.refs_12_), channel_id=1, source_target_pairs={{0,4},{4,0},{8,12},{12,8},{1,5},{5,1},{9,13},{13,9},{2,6},{6,2},{1... | collective-permute-start | bytes 786440 | tf_op jit(solution)/shard_map/ppermute | solution.py:228
  88.7 17.6 %collective-permute-start.35 = (bf16[384,896]{1,0:T(8,128)(2,1)}, bf16[384,896]{1,0:T(8,128)(2,1)S(1)}, u32[]{:S(2)}, u32[]{:S(2)}) collective-permute-start(bf16[384,896]{1,0:T(8,128)(2,1)} %shard_map.95), channel_id=1, source_target_pairs={{0,16},{16,0},{1,17},{17,1},{2,18},{18,2},{3,19},{19,3},{4,20},{20... | collective-permute-start | bytes 2064392 | tf_op jit(solution)/shard_map/ppermute | solution.py:234
  89.5 14.7 %collective-permute-start.31 = (bf16[16,4096]{1,0:T(8,128)(2,1)}, bf16[16,4096]{1,0:T(8,128)(2,1)S(1)}, u32[]{:S(2)}, u32[]{:S(2)}) collective-permute-start(bf16[16,4096]{1,0:T(8,128)(2,1)} %copy-done.60), channel_id=1, source_target_pairs={{0,8},{4,12},{8,0},{12,4},{1,9},{5,13},{9,1},{13,5},{2,10},{6,14},... | collective-permute-start | bytes 393224 | tf_op jit(solution)/shard_map/ppermute | solution.py:228
  90.9 13.3 %collective-permute-start.30 = (bf16[48,4096]{1,0:T(8,128)(2,1)S(1)}, bf16[48,4096]{1,0:T(8,128)(2,1)S(1)}, u32[]{:S(2)}, u32[]{:S(2)}) collective-permute-start(bf16[48,4096]{1,0:T(8,128)(2,1)S(1)} %collective-permute-done.22.refs_6_), channel_id=1, source_target_pairs={{0,8},{4,12},{8,0},{12,4},{1,9},{5,13},{9,1},{13,5},{2,10},{6,14},... | collective-permute-start | bytes 1179656 | tf_op jit(solution)/shard_map/ppermute | solution.py:228
  107.8 18.0 %collective-permute-start.42 = (bf16[384,896]{1,0:T(8,128)(2,1)S(1)}, bf16[384,896]{1,0:T(8,128)(2,1)}, u32[]{:S(2)}, u32[]{:S(2)}) collective-permute-start(bf16[384,896]{1,0:T(8,128)(2,1)S(1)} %copy-done.16), channel_id=1, source_target_pairs={{0,16},{16,0},{1,17},{17,1},{2,18},{18,2},{3,19},{19,3},{4,20},{20... | collective-permute-start | bytes 2064392 | tf_op jit(solution)/shard_map/ppermute | solution.py:234
  109.1 3.9 %collective-permute-start.41 = (bf16[48,4096]{1,0:T(8,128)(2,1)S(1)}, bf16[48,4096]{1,0:T(8,128)(2,1)}, u32[]{:S(2)}, u32[]{:S(2)}) collective-permute-start(bf16[48,4096]{1,0:T(8,128)(2,1)S(1)} %copy-done.45), channel_id=1, source_target_pairs={{0,4},{4,0},{8,12},{12,8},{1,5},{5,1},{9,13},{13,9},{2,6},{6,2},{1... | collective-permute-start | bytes 1179656 | tf_op jit(solution)/shard_map/ppermute | solution.py:228
  110.3 15.5 %collective-permute-start.38 = (bf16[96,4096]{1,0:T(8,128)(2,1)}, bf16[96,4096]{1,0:T(8,128)(2,1)S(1)}, u32[]{:S(2)}, u32[]{:S(2)}) collective-permute-start(bf16[96,4096]{1,0:T(8,128)(2,1)} %get-tuple-element.171), channel_id=1, source_target_pairs={{0,4},{4,0},{8,12},{12,8},{1,5},{5,1},{9,13},{13,9},{2,6},{6,2},{1... | collective-permute-start | bytes 2359304 | tf_op jit(solution)/shard_map/ppermute | solution.py:228
  111.6 14.1 %collective-permute-start.37 = (bf16[48,4096]{1,0:T(8,128)(2,1)}, bf16[48,4096]{1,0:T(8,128)(2,1)S(1)}, u32[]{:S(2)}, u32[]{:S(2)}) collective-permute-start(bf16[48,4096]{1,0:T(8,128)(2,1)} %get-tuple-element.256), channel_id=1, source_target_pairs={{0,8},{4,12},{8,0},{12,4},{1,9},{5,13},{9,1},{13,5},{2,10},{6,14},... | collective-permute-start | bytes 1179656 | tf_op jit(solution)/shard_map/ppermute | solution.py:228
  125.9 18.2 %collective-permute-start.46 = (bf16[384,896]{1,0:T(8,128)(2,1)}, bf16[384,896]{1,0:T(8,128)(2,1)}, u32[]{:S(2)}, u32[]{:S(2)}) collective-permute-start(bf16[384,896]{1,0:T(8,128)(2,1)} %get-tuple-element.196), channel_id=1, source_target_pairs={{0,16},{16,0},{1,17},{17,1},{2,18},{18,2},{3,19},{19,3},{4,20},{20... | collective-permute-start | bytes 2064392 | tf_op jit(solution)/shard_map/ppermute | solution.py:234
  128.6 19.6 %collective-permute-start.44 = (bf16[96,4096]{1,0:T(8,128)(2,1)S(1)}, bf16[96,4096]{1,0:T(8,128)(2,1)S(1)}, u32[]{:S(2)}, u32[]{:S(2)}) collective-permute-start(bf16[96,4096]{1,0:T(8,128)(2,1)S(1)} %pad_maximum_fusion), channel_id=1, source_target_pairs={{0,8},{4,12},{8,0},{12,4},{1,9},{5,13},{9,1},{13,5},{2,10},{6,14},... | collective-permute-start | bytes 2359304 | tf_op jit(solution)/shard_map/ppermute | solution.py:228
  129.2 19.1 %collective-permute-start.45 = (bf16[96,4096]{1,0:T(8,128)(2,1)}, bf16[96,4096]{1,0:T(8,128)(2,1)S(1)}, u32[]{:S(2)}, u32[]{:S(2)}) collective-permute-start(bf16[96,4096]{1,0:T(8,128)(2,1)} %get-tuple-element.190), channel_id=1, source_target_pairs={{0,4},{4,0},{8,12},{12,8},{1,5},{5,1},{9,13},{13,9},{2,6},{6,2},{1... | collective-permute-start | bytes 2359304 | tf_op jit(solution)/shard_map/ppermute | solution.py:228
  148.3 4.3 %collective-permute-start.47 = (bf16[96,4096]{1,0:T(8,128)(2,1)}, bf16[96,4096]{1,0:T(8,128)(2,1)S(1)}, u32[]{:S(2)}, u32[]{:S(2)}) collective-permute-start(bf16[96,4096]{1,0:T(8,128)(2,1)} %get-tuple-element.198), channel_id=1, source_target_pairs={{0,4},{4,0},{8,12},{12,8},{1,5},{5,1},{9,13},{13,9},{2,6},{6,2},{1... | collective-permute-start | bytes 2359304 | tf_op jit(solution)/shard_map/ppermute | solution.py:228
  149.3 20.2 %collective-permute-start.51 = (bf16[48,4096]{1,0:T(8,128)(2,1)}, bf16[48,4096]{1,0:T(8,128)(2,1)S(1)}, u32[]{:S(2)}, u32[]{:S(2)}) collective-permute-start(bf16[48,4096]{1,0:T(8,128)(2,1)} %get-tuple-element.245), channel_id=1, source_target_pairs={{0,3},{1,0},{2,1},{3,2},{4,7},{5,4},{6,5},{7,6},{8,11},{9,8},{10,9... | collective-permute-start | bytes 1179656 | tf_op jit(solution)/shard_map/ppermute | solution.py:223
  149.7 19.8 %collective-permute-start.50 = (bf16[48,4096]{1,0:T(8,128)(2,1)S(1)}, bf16[48,4096]{1,0:T(8,128)(2,1)S(1)}, u32[]{:S(2)}, u32[]{:S(2)}) collective-permute-start(bf16[48,4096]{1,0:T(8,128)(2,1)S(1)} %get-tuple-element.246), channel_id=1, source_target_pairs={{0,1},{1,2},{2,3},{3,0},{4,5},{5,6},{6,7},{7,4},{8,9},{9,10},{10,1... | collective-permute-start | bytes 1179656 | tf_op jit(solution)/shard_map/ppermute | solution.py:223
  152.9 19.4 %collective-permute-start.48 = (bf16[96,4096]{1,0:T(8,128)(2,1)S(1)}, bf16[96,4096]{1,0:T(8,128)(2,1)S(1)}, u32[]{:S(2)}, u32[]{:S(2)}) collective-permute-start(bf16[96,4096]{1,0:T(8,128)(2,1)S(1)} %pad_maximum_fusion.1), channel_id=1, source_target_pairs={{0,8},{4,12},{8,0},{12,4},{1,9},{5,13},{9,1},{13,5},{2,10},{6,14},... | collective-permute-start | bytes 2359304 | tf_op jit(solution)/shard_map/ppermute | solution.py:228
  154.0 18.4 %collective-permute-start.49 = (bf16[96,4096]{1,0:T(8,128)(2,1)S(1)}, bf16[96,4096]{1,0:T(8,128)(2,1)S(1)}, u32[]{:S(2)}, u32[]{:S(2)}) collective-permute-start(bf16[96,4096]{1,0:T(8,128)(2,1)S(1)} %copy-done.61), channel_id=1, source_target_pairs={{0,4},{4,0},{8,12},{12,8},{1,5},{5,1},{9,13},{13,9},{2,6},{6,2},{1... | collective-permute-start | bytes 2359304 | tf_op jit(solution)/shard_map/ppermute | solution.py:228
  172.4 4.3 %collective-permute-start.52 = (bf16[96,4096]{1,0:T(8,128)(2,1)}, bf16[96,4096]{1,0:T(8,128)(2,1)S(1)}, u32[]{:S(2)}, u32[]{:S(2)}) collective-permute-start(bf16[96,4096]{1,0:T(8,128)(2,1)} %get-tuple-element.210), channel_id=1, source_target_pairs={{0,4},{4,0},{8,12},{12,8},{1,5},{5,1},{9,13},{13,9},{2,6},{6,2},{1... | collective-permute-start | bytes 2359304 | tf_op jit(solution)/shard_map/ppermute | solution.py:228
  172.7 18.2 %collective-permute-start.56 = (bf16[48,4096]{1,0:T(8,128)(2,1)S(1)}, bf16[48,4096]{1,0:T(8,128)(2,1)S(1)}, u32[]{:S(2)}, u32[]{:S(2)}) collective-permute-start(bf16[48,4096]{1,0:T(8,128)(2,1)S(1)} %get-tuple-element.243), channel_id=1, source_target_pairs={{0,1},{1,2},{2,3},{3,0},{4,5},{5,6},{6,7},{7,4},{8,9},{9,10},{10,1... | collective-permute-start | bytes 1179656 | tf_op jit(solution)/shard_map/ppermute | solution.py:223
  173.2 19.7 %collective-permute-start.55 = (bf16[48,4096]{1,0:T(8,128)(2,1)S(1)}, bf16[48,4096]{1,0:T(8,128)(2,1)S(1)}, u32[]{:S(2)}, u32[]{:S(2)}) collective-permute-start(bf16[48,4096]{1,0:T(8,128)(2,1)S(1)} %get-tuple-element.244), channel_id=1, source_target_pairs={{0,3},{1,0},{2,1},{3,2},{4,7},{5,4},{6,5},{7,6},{8,11},{9,8},{10,9... | collective-permute-start | bytes 1179656 | tf_op jit(solution)/shard_map/ppermute | solution.py:223
  176.8 16.0 %collective-permute-start.54 = (bf16[96,4096]{1,0:T(8,128)(2,1)}, bf16[96,4096]{1,0:T(8,128)(2,1)S(1)}, u32[]{:S(2)}, u32[]{:S(2)}) collective-permute-start(bf16[96,4096]{1,0:T(8,128)(2,1)} %get-tuple-element.212), channel_id=1, source_target_pairs={{0,4},{4,0},{8,12},{12,8},{1,5},{5,1},{9,13},{13,9},{2,6},{6,2},{1... | collective-permute-start | bytes 2359304 | tf_op jit(solution)/shard_map/ppermute | solution.py:228
  177.2 15.7 %collective-permute-start.53 = (bf16[48,4096]{1,0:T(8,128)(2,1)S(1)}, bf16[48,4096]{1,0:T(8,128)(2,1)S(1)}, u32[]{:S(2)}, u32[]{:S(2)}) collective-permute-start(bf16[48,4096]{1,0:T(8,128)(2,1)S(1)} %get-tuple-element.250), channel_id=1, source_target_pairs={{0,8},{4,12},{8,0},{12,4},{1,9},{5,13},{9,1},{13,5},{2,10},{6,14},... | collective-permute-start | bytes 1179656 | tf_op jit(solution)/shard_map/ppermute | solution.py:228
  193.1 21.0 %collective-permute-start.58 = (bf16[96,4096]{1,0:T(8,128)(2,1)S(1)}, bf16[96,4096]{1,0:T(8,128)(2,1)S(1)}, u32[]{:S(2)}, u32[]{:S(2)}) collective-permute-start(bf16[96,4096]{1,0:T(8,128)(2,1)S(1)} %pad_maximum_fusion.3), channel_id=1, source_target_pairs={{0,3},{1,0},{2,1},{3,2},{4,7},{5,4},{6,5},{7,6},{8,11},{9,8},{10,9... | collective-permute-start | bytes 2359304 | tf_op jit(solution)/shard_map/ppermute | solution.py:223
  195.3 18.9 %collective-permute-start.57 = (bf16[96,4096]{1,0:T(8,128)(2,1)S(1)}, bf16[96,4096]{1,0:T(8,128)(2,1)S(1)}, u32[]{:S(2)}, u32[]{:S(2)}) collective-permute-start(bf16[96,4096]{1,0:T(8,128)(2,1)S(1)} %pad_maximum_fusion.2), channel_id=1, source_target_pairs={{0,8},{4,12},{8,0},{12,4},{1,9},{5,13},{9,1},{13,5},{2,10},{6,14},... | collective-permute-start | bytes 2359304 | tf_op jit(solution)/shard_map/ppermute | solution.py:228
  (73 other events, 496.3 us)

commit v14 on v13

--- a/solution.py
+++ b/solution.py
@@ -57,7 +57,7 @@
 def contract(pieces, weights):
     width = pieces[0].shape[1]
     units = weights[0].shape[1]
-    block = min(512, width)
+    block = min(1024, width)
     deep = pl.Buffered(4)
     rows = sum(piece.shape[0] for piece in pieces)
     out = jax.ShapeDtypeStruct((rows * len(weights), units), jnp.bfloat16)
@@ -203,7 +203,7 @@
 
 def tall_grad(pieces, hiddens):
     width, units = pieces[0].shape[1], hiddens[0].shape[1]
-    block = min(512, width)
+    block = min(1024, width)
     rows = sum(piece.shape[0] for piece in pieces)
     out = jax.ShapeDtypeStruct((units, width), jnp.float32)
     return pl.pallas_call(

time: 217 us -> 217 us (level)
  no operation moved by 1% of the time
where the time goes in v14:
time: 217 us; the launch traced here: 216 us
  Pallas kernels  103 us (47%)
  waiting for transfers between devices  46.3 us (21%)
  starting transfers between devices  43.5 us (20%)
  other arithmetic  15.4 us (7%)
  local copies, waits for them, and re-layouts  6.35 us (3%)
    pallas_call x4, Pallas kernels, contract(): pl.pallas_call(kernel, in_specs=[pl.BlockSpec(memory_space=pl.ANY)] * n_i...  30.6 us
    pallas_call x2, Pallas kernels, down_products(): pl.pallas_call(functools.partial(down_kernel, len(pieces)), grid=(width /...  22.2 us
    pallas_call x2, Pallas kernels, expand(): pl.pallas_call(functools.partial(expand_kernel, len(lefts)), grid=(width...  21.4 us
    ppermute x41, waiting for transfers between devices, swap(): return lax.ppermute(block, 'col', [(i, i ^ bit) for i in range(n)])  21.3 us
    ppermute x12, starting transfers between devices, shift(): return lax.ppermute(block, 'depth', [(i, (i + step) % n) for i in range(n)])  20.4 us
    ppermute x12, waiting for transfers between devices, shift(): return lax.ppermute(block, 'depth', [(i, (i + step) % n) for i in range(n)])  18.8 us
    pallas_call x1, Pallas kernels, wide_grads(): pl.pallas_call(functools.partial(wide_grad_kernel, len(pieces)), grid=(wi...  17.2 us
    ppermute x41, starting transfers between devices, swap(): return lax.ppermute(block, 'col', [(i, i ^ bit) for i in range(n)])  16.9 us
  transfers between devices with their start and end apart: 59, of which 17 were waited for; matrix products, arithmetic and copies ran while one was open for 7% of the time, Pallas kernels for 48%

profile of v14, /device:TPU:0, one launch (start us, length us, event | category | flops | bytes accessed | tf_op | source)
XLA Modules:
  0.0 216.0 jit_solution(8527750980370644242)
XLA Ops:
  0.6 3.1 %collective-permute-start.1 = (bf16[48,4096]{1,0:T(8,128)(2,1)}, bf16[48,4096]{1,0:T(8,128)(2,1)S(1)}, u32[]{:S(2)}, u32[]{:S(2)}) collective-permute-start(bf16[48,4096]{1,0:T(8,128)(2,1)} %refs_0_.6), channel_id=1, source_target_pairs={{0,1},{1,2},{2,3},{3,0},{4,5},{5,6},{6,7},{7,4},{8,9},{9,10},{10,1... | collective-permute-start | bytes 1179656 | tf_op jit(solution)/shard_map/ppermute | solution.py:223
  3.7 1.5 collective-permute-start
  6.2 1.0 slice.175
  7.2 7.9 %collective-permute-done.1.refs_0_.refs_4_ = bf16[48,4096]{1,0:T(8,128)(2,1)S(1)} collective-permute-done((bf16[48,4096]{1,0:T(8,128)(2,1)}, bf16[48,4096]{1,0:T(8,128)(2,1)S(1)}, u32[]{:S(2)}, u32[]{:S(2)}) %collective-permute-start.1) | collective-permute-done | bytes 393248 | tf_op jit(solution)/shard_map/ppermute | solution.py:223
  15.6 1.7 collective-permute-start.4
  17.4 1.5 collective-permute-start.3
  18.9 1.7 collective-permute-start.5
  21.3 7.6 %shard_map.92 = bf16[384,896]{1,0:T(8,128)(2,1)} custom-call(bf16[48,4096]{1,0:T(8,128)(2,1)} %refs_0_.6, bf16[48,4096]{1,0:T(8,128)(2,1)} %copy-done.23, bf16[48,4096]{1,0:T(8,128)(2,1)} %copy-done.24, bf16[48,4096]{1,0:T(8,128)(2,1)} %copy-done.25, bf16[4096,896]{1,0:T(8,128)(2,1)} %refs_4_.11, bf16[4096,896]{1,0:T(8,128)(2,1)} %refs_5_.11), custom_call_target="tpu_custom_call" | custom-call | flops 2818572288 | bytes 16252928 | tf_op jit(solution)/shard_map/pallas_call | solution.py:78
  29.8 1.6 collective-permute-start.14
  31.4 1.5 collective-permute-start.12
  34.3 1.2 collective-permute-done.13.refs_3_.refs_7_
  35.5 2.9 %collective-permute-start.10 = (bf16[32,4096]{1,0:T(8,128)(2,1)S(1)}, bf16[32,4096]{1,0:T(8,128)(2,1)S(1)}, u32[]{:S(2)}, u32[]{:S(2)}) collective-permute-start(bf16[32,4096]{1,0:T(8,128)(2,1)S(1)} %slice.175), channel_id=1, source_target_pairs={{0,3},{1,0},{2,1},{3,2},{4,7},{5,4},{6,5},{7,6},{8,11},{9,8},{10,9... | collective-permute-start | bytes 786440 | tf_op jit(solution)/shard_map/ppermute | solution.py:223
  38.4 7.6 %shard_map.93 = bf16[384,896]{1,0:T(8,128)(2,1)} custom-call(bf16[48,4096]{1,0:T(8,128)(2,1)} %copy-done.22, bf16[48,4096]{1,0:T(8,128)(2,1)} %copy-done.28, bf16[48,4096]{1,0:T(8,128)(2,1)} %copy-done.27, bf16[48,4096]{1,0:T(8,128)(2,1)} %copy-done.30, bf16[4096,896]{1,0:T(8,128)(2,1)} %refs_4_.11, bf16[4096,896]{1,0:T(8,128)(2,1)} %refs_5_.11), custom_call_target="tpu_custom_call" | custom-call | flops 2818572288 | bytes 16252928 | tf_op jit(solution)/shard_map/pallas_call | solution.py:78
  46.1 3.9 %collective-permute-done.10 = bf16[32,4096]{1,0:T(8,128)(2,1)S(1)} collective-permute-done((bf16[32,4096]{1,0:T(8,128)(2,1)S(1)}, bf16[32,4096]{1,0:T(8,128)(2,1)S(1)}, u32[]{:S(2)}, u32[]{:S(2)}) %collective-permute-start.10) | collective-permute-done | bytes 262176 | tf_op jit(solution)/shard_map/ppermute | solution.py:223
  51.2 1.8 collective-permute-start.15
  53.9 1.2 collective-permute-start.17
  55.1 7.7 %shard_map.94 = bf16[384,896]{1,0:T(8,128)(2,1)} custom-call(bf16[48,4096]{1,0:T(8,128)(2,1)} %copy-done.26, bf16[48,4096]{1,0:T(8,128)(2,1)} %copy-done.31, bf16[48,4096]{1,0:T(8,128)(2,1)} %copy-done.32, bf16[48,4096]{1,0:T(8,128)(2,1)} %copy-done.33, bf16[4096,896]{1,0:T(8,128)(2,1)} %refs_4_.11, bf16[4096,896]{1,0:T(8,128)(2,1)} %refs_5_.11), custom_call_target="tpu_custom_call" | custom-call | flops 2818572288 | bytes 16252928 | tf_op jit(solution)/shard_map/pallas_call | solution.py:78
  62.8 6.5 %collective-permute-done.17.refs_2_.refs_12_ = bf16[32,4096]{1,0:T(8,128)(2,1)S(1)} collective-permute-done((bf16[32,4096]{1,0:T(8,128)(2,1)S(1)}, bf16[32,4096]{1,0:T(8,128)(2,1)S(1)}, u32[]{:S(2)}, u32[]{:S(2)}) %collective-permute-start.17) | collective-permute-done | bytes 262176 | tf_op jit(solution)/shard_map/ppermute | solution.py:228
  69.5 1.6 collective-permute-start.29
  71.5 1.0 multiply_convert_fusion.11.refs_10_.refs_20_
  72.9 3.7 %collective-permute-done.24.refs_1_.refs_11_ = bf16[16,4096]{1,0:T(8,128)(2,1)S(1)} collective-permute-done((bf16[16,4096]{1,0:T(8,128)(2,1)S(1)}, bf16[16,4096]{1,0:T(8,128)(2,1)S(1)}, u32[]{:S(2)}, u32[]{:S(2)}) %collective-permute-start.24) | collective-permute-done | bytes 131104 | tf_op jit(solution)/shard_map/ppermute | solution.py:228
  77.2 1.0 multiply_convert_fusion.10.refs_11_.refs_21_
  79.0 7.7 %shard_map.95 = bf16[384,896]{1,0:T(8,128)(2,1)} custom-call(bf16[48,4096]{1,0:T(8,128)(2,1)} %copy-done.29, bf16[48,4096]{1,0:T(8,128)(2,1)} %copy-done.34, bf16[48,4096]{1,0:T(8,128)(2,1)} %copy-done.35, bf16[48,4096]{1,0:T(8,128)(2,1)} %copy-done.36, bf16[4096,896]{1,0:T(8,128)(2,1)} %refs_4_.11, bf16[4096,896]{1,0:T(8,128)(2,1)} %refs_5_.11), custom_call_target="tpu_custom_call" | custom-call | flops 2818572288 | bytes 16252928 | tf_op jit(solution)/shard_map/pallas_call | solution.py:78
  86.7 1.5 collective-permute-done.23.refs_7_.refs_17_
  93.1 11.1 %shard_map.96 = (bf16[384,896]{1,0:T(8,128)(2,1)}, bf16[96,4096]{1,0:T(8,128)(2,1)}, bf16[96,4096]{1,0:T(8,128)(2,1)}, bf16[96,4096]{1,0:T(8,128)(2,1)}, bf16[96,4096]{1,0:T(8,128)(2,1)}) custom-call(bf16[48,4096]{1,0:T(8,128)(2,1)} %copy-done.15, bf16[16,4096]{1,0:T(8,128)(2,1)} %copy-done.55, bf16[32,4096]{1,0:T(8,128)(2,1)} %copy-done.53, ...), custom_call_target="tpu_custom_call" | custom-call | flops 5637144576 | bytes 14319616 | tf_op jit(solution)/shard_map/pallas_call | solution.py:150
  104.2 2.1 collective-permute-done.35
  109.3 0.9 add_convert_fusion.12
  113.0 11.1 %shard_map.97 = (bf16[384,896]{1,0:T(8,128)(2,1)}, bf16[96,4096]{1,0:T(8,128)(2,1)}, bf16[96,4096]{1,0:T(8,128)(2,1)}, bf16[96,4096]{1,0:T(8,128)(2,1)}, bf16[96,4096]{1,0:T(8,128)(2,1)}) custom-call(bf16[48,4096]{1,0:T(8,128)(2,1)} %refs_0_.5, bf16[16,4096]{1,0:T(8,128)(2,1)} %copy-done.57, bf16[32,4096]{1,0:T(8,128)(2,1)} %copy-done.51, ...), custom_call_target="tpu_custom_call" | custom-call | flops 5637144576 | bytes 14319616 | tf_op jit(solution)/shard_map/pallas_call | solution.py:150
  124.1 1.6 collective-permute-done.42
  126.7 1.2 convert_add_fusion.1
  129.3 1.7 multiply_convert_fusion.4
  131.0 10.7 %shard_map.98 = (bf16[96,4096]{1,0:T(8,128)(2,1)}, bf16[96,4096]{1,0:T(8,128)(2,1)}, bf16[96,4096]{1,0:T(8,128)(2,1)}, bf16[96,4096]{1,0:T(8,128)(2,1)}) custom-call(bf16[192,896]{1,0:T(8,128)(2,1)} %get-tuple-element.259.refs_0_.refs_18_, bf16[192,896]{1,0:T(8,128)(2,1)} %get-tuple-element.240.refs_1_.refs_19_, ...), custom_call_target="tpu_custom_call" | custom-call | flops 5637144576 | bytes 19202048 | tf_op jit(solution)/shard_map/pallas_call | solution.py:113
  141.7 2.4 %collective-permute-done.46 = bf16[384,896]{1,0:T(8,128)(2,1)} collective-permute-done((bf16[384,896]{1,0:T(8,128)(2,1)}, bf16[384,896]{1,0:T(8,128)(2,1)}, u32[]{:S(2)}, u32[]{:S(2)}) %collective-permute-start.46) | collective-permute-done | bytes 688160 | tf_op jit(solution)/shard_map/ppermute | solution.py:234
  144.0 4.2 %collective-permute-done.44 = bf16[96,4096]{1,0:T(8,128)(2,1)S(1)} collective-permute-done((bf16[96,4096]{1,0:T(8,128)(2,1)S(1)}, bf16[96,4096]{1,0:T(8,128)(2,1)S(1)}, u32[]{:S(2)}, u32[]{:S(2)}) %collective-permute-start.44) | collective-permute-done | bytes 786464 | tf_op jit(solution)/shard_map/ppermute | solution.py:228
  148.3 1.1 add_convert_fusion.6
  149.7 1.7 collective-permute-start.50
  151.4 1.2 convert_add_fusion
  154.0 1.9 multiply_convert_fusion
  155.9 10.7 %shard_map.99 = (bf16[96,4096]{1,0:T(8,128)(2,1)}, bf16[96,4096]{1,0:T(8,128)(2,1)}, bf16[96,4096]{1,0:T(8,128)(2,1)}, bf16[96,4096]{1,0:T(8,128)(2,1)}) custom-call(bf16[192,896]{1,0:T(8,128)(2,1)} %get-tuple-element.257.refs_0_.refs_16_, bf16[192,896]{1,0:T(8,128)(2,1)} %get-tuple-element.236.refs_1_.refs_17_, ...), custom_call_target="tpu_custom_call" | custom-call | flops 5637144576 | bytes 19202048 | tf_op jit(solution)/shard_map/pallas_call | solution.py:113
  166.6 2.9 %collective-permute-done.51 = bf16[48,4096]{1,0:T(8,128)(2,1)S(1)} collective-permute-done((bf16[48,4096]{1,0:T(8,128)(2,1)}, bf16[48,4096]{1,0:T(8,128)(2,1)S(1)}, u32[]{:S(2)}, u32[]{:S(2)}) %collective-permute-start.51) | collective-permute-done | bytes 393248 | tf_op jit(solution)/shard_map/ppermute | solution.py:223
  169.5 2.9 %collective-permute-done.48 = bf16[96,4096]{1,0:T(8,128)(2,1)S(1)} collective-permute-done((bf16[96,4096]{1,0:T(8,128)(2,1)S(1)}, bf16[96,4096]{1,0:T(8,128)(2,1)S(1)}, u32[]{:S(2)}, u32[]{:S(2)}) %collective-permute-start.48) | collective-permute-done | bytes 786464 | tf_op jit(solution)/shard_map/ppermute | solution.py:228
  173.2 3.4 %collective-permute-start.55 = (bf16[48,4096]{1,0:T(8,128)(2,1)S(1)}, bf16[48,4096]{1,0:T(8,128)(2,1)S(1)}, u32[]{:S(2)}, u32[]{:S(2)}) collective-permute-start(bf16[48,4096]{1,0:T(8,128)(2,1)S(1)} %get-tuple-element.244), channel_id=1, source_target_pairs={{0,3},{1,0},{2,1},{3,2},{4,7},{5,4},{6,5},{7,6},{8,11},{9,8},{10,9... | collective-permute-start | bytes 1179656 | tf_op jit(solution)/shard_map/ppermute | solution.py:223
  177.9 11.6 %shard_map.100 = f32[896,4096]{1,0:T(8,128)} custom-call(bf16[48,4096]{1,0:T(8,128)(2,1)} %refs_0_.5, bf16[16,4096]{1,0:T(8,128)(2,1)} %copy-done.57, bf16[32,4096]{1,0:T(8,128)(2,1)} %copy-done.51, bf16[48,4096]{1,0:T(8,128)(2,1)} %collective-permute-done.2.refs_3_, bf16[16,4096]{1,0:T(8,128)(2,1)} %copy-done.59, bf16[32,4096]{1,0:T(8,128)(2,1)} %copy-done.52, ...), custom_call_target="tpu_custom_call" | custom-call | flops 5637144576 | bytes 22347776 | tf_op jit(solution)/shard_map/pallas_call | solution.py:209
  189.5 3.3 %collective-permute-done.55 = bf16[48,4096]{1,0:T(8,128)(2,1)S(1)} collective-permute-done((bf16[48,4096]{1,0:T(8,128)(2,1)S(1)}, bf16[48,4096]{1,0:T(8,128)(2,1)S(1)}, u32[]{:S(2)}, u32[]{:S(2)}) %collective-permute-start.55) | collective-permute-done | bytes 393248 | tf_op jit(solution)/shard_map/ppermute | solution.py:223
  193.1 2.1 collective-permute-start.58
  195.3 1.6 collective-permute-start.57
  196.9 17.2 %shard_map.101 = (f32[4096,896]{1,0:T(8,128)}, f32[4096,896]{1,0:T(8,128)}) custom-call(bf16[48,4096]{1,0:T(8,128)(2,1)} %refs_0_.6, bf16[48,4096]{1,0:T(8,128)(2,1)} %copy-done.23, bf16[48,4096]{1,0:T(8,128)(2,1)} %copy-done.24, bf16[48,4096]{1,0:T(8,128)(2,1)} %copy-done.25, bf16[48,4096]{1,0:T(8,128)(2,1)} %copy-done.22, bf16[48,4096]{1,0:T(8,128)(2,1)} %copy-done.28, ...), custom_call_target="tpu_custom_call" | custom-call | flops 11274289152 | bytes 38404096 | tf_op jit(solution)/shard_map/pallas_call | solution.py:185
  214.3 1.7 convert_add_fusion.4
  (231 shorter events, 25.6 us)
Async XLA Ops:
  0.6 14.4 %collective-permute-start.1 = (bf16[48,4096]{1,0:T(8,128)(2,1)}, bf16[48,4096]{1,0:T(8,128)(2,1)S(1)}, u32[]{:S(2)}, u32[]{:S(2)}) collective-permute-start(bf16[48,4096]{1,0:T(8,128)(2,1)} %refs_0_.6), channel_id=1, source_target_pairs={{0,1},{1,2},{2,3},{3,0},{4,5},{5,6},{6,7},{7,4},{8,9},{9,10},{10,1... | collective-permute-start | bytes 1179656 | tf_op jit(solution)/shard_map/ppermute | solution.py:223
  3.7 11.4 %collective-permute-start = (bf16[48,4096]{1,0:T(8,128)(2,1)}, bf16[48,4096]{1,0:T(8,128)(2,1)S(1)}, u32[]{:S(2)}, u32[]{:S(2)}) collective-permute-start(bf16[48,4096]{1,0:T(8,128)(2,1)} %refs_0_.6), channel_id=1, source_target_pairs={{0,8},{4,12},{8,0},{12,4},{1,9},{5,13},{9,1},{13,5},{2,10},{6,14},... | collective-permute-start | bytes 1179656 | tf_op jit(solution)/shard_map/ppermute | solution.py:228
  5.2 9.8 %collective-permute-start.2 = (bf16[48,4096]{1,0:T(8,128)(2,1)}, bf16[48,4096]{1,0:T(8,128)(2,1)}, u32[]{:S(2)}, u32[]{:S(2)}) collective-permute-start(bf16[48,4096]{1,0:T(8,128)(2,1)} %refs_0_.5), channel_id=1, source_target_pairs={{0,4},{4,0},{8,12},{12,8},{1,5},{5,1},{9,13},{13,9},{2,6},{6,2},{1... | collective-permute-start | bytes 1179656 | tf_op jit(solution)/shard_map/ppermute | solution.py:228
  15.2 5.4 %collective-permute-start.8 = (bf16[48,4096]{1,0:T(8,128)(2,1)S(1)}, bf16[48,4096]{1,0:T(8,128)(2,1)S(1)}, u32[]{:S(2)}, u32[]{:S(2)}) collective-permute-start(bf16[48,4096]{1,0:T(8,128)(2,1)S(1)} %collective-permute-done.refs_1_), channel_id=1, source_target_pairs={{0,4},{4,0},{8,12},{12,8},{1,5},{5,1},{9,13},{13,9},{2,6},{6,2},{1... | collective-permute-start | bytes 1179656 | tf_op jit(solution)/shard_map/ppermute | solution.py:228
  15.6 14.1 %collective-permute-start.4 = (bf16[48,4096]{1,0:T(8,128)(2,1)}, bf16[48,4096]{1,0:T(8,128)(2,1)S(1)}, u32[]{:S(2)}, u32[]{:S(2)}) collective-permute-start(bf16[48,4096]{1,0:T(8,128)(2,1)} %refs_0_.6), channel_id=1, source_target_pairs={{0,3},{1,0},{2,1},{3,2},{4,7},{5,4},{6,5},{7,6},{8,11},{9,8},{10,9... | collective-permute-start | bytes 1179656 | tf_op jit(solution)/shard_map/ppermute | solution.py:223
  17.4 12.4 %collective-permute-start.6 = (bf16[48,4096]{1,0:T(8,128)(2,1)S(1)}, bf16[48,4096]{1,0:T(8,128)(2,1)S(1)}, u32[]{:S(2)}, u32[]{:S(2)}) collective-permute-start(bf16[48,4096]{1,0:T(8,128)(2,1)S(1)} %collective-permute-done.1.refs_0_.refs_4_), channel_id=1, source_target_pairs={{0,4},{4,0},{8,12},{12,8},{1,5},{5,1},{9,13},{13,9},{2,6},{6,2},{1... | collective-permute-start | bytes 1179656 | tf_op jit(solution)/shard_map/ppermute | solution.py:228
  17.4 12.4 %collective-permute-start.3 = (bf16[48,4096]{1,0:T(8,128)(2,1)S(1)}, bf16[48,4096]{1,0:T(8,128)(2,1)S(1)}, u32[]{:S(2)}, u32[]{:S(2)}) collective-permute-start(bf16[48,4096]{1,0:T(8,128)(2,1)S(1)} %collective-permute-done.1.refs_0_.refs_4_), channel_id=1, source_target_pairs={{0,8},{4,12},{8,0},{12,4},{1,9},{5,13},{9,1},{13,5},{2,10},{6,14},... | collective-permute-start | bytes 1179656 | tf_op jit(solution)/shard_map/ppermute | solution.py:228
  18.9 10.8 %collective-permute-start.5 = (bf16[16,4096]{1,0:T(8,128)(2,1)S(1)}, bf16[16,4096]{1,0:T(8,128)(2,1)S(1)}, u32[]{:S(2)}, u32[]{:S(2)}) collective-permute-start(bf16[16,4096]{1,0:T(8,128)(2,1)S(1)} %slice.174), channel_id=1, source_target_pairs={{0,3},{1,0},{2,1},{3,2},{4,7},{5,4},{6,5},{7,6},{8,11},{9,8},{10,9... | collective-permute-start | bytes 393224 | tf_op jit(solution)/shard_map/ppermute | solution.py:223
  29.8 20.2 %collective-permute-start.14 = (bf16[384,896]{1,0:T(8,128)(2,1)}, bf16[384,896]{1,0:T(8,128)(2,1)S(1)}, u32[]{:S(2)}, u32[]{:S(2)}) collective-permute-start(bf16[384,896]{1,0:T(8,128)(2,1)} %shard_map.92), channel_id=1, source_target_pairs={{0,16},{16,0},{1,17},{17,1},{2,18},{18,2},{3,19},{19,3},{4,20},{20... | collective-permute-start | bytes 2064392 | tf_op jit(solution)/shard_map/ppermute | solution.py:234
  31.4 14.7 %collective-permute-start.12 = (bf16[32,4096]{1,0:T(8,128)(2,1)S(1)}, bf16[32,4096]{1,0:T(8,128)(2,1)S(1)}, u32[]{:S(2)}, u32[]{:S(2)}) collective-permute-start(bf16[32,4096]{1,0:T(8,128)(2,1)S(1)} %slice.175), channel_id=1, source_target_pairs={{0,8},{4,12},{8,0},{12,4},{1,9},{5,13},{9,1},{13,5},{2,10},{6,14},... | collective-permute-start | bytes 786440 | tf_op jit(solution)/shard_map/ppermute | solution.py:228
  32.9 17.1 %collective-permute-start.9 = (bf16[48,4096]{1,0:T(8,128)(2,1)S(1)}, bf16[48,4096]{1,0:T(8,128)(2,1)S(1)}, u32[]{:S(2)}, u32[]{:S(2)}) collective-permute-start(bf16[48,4096]{1,0:T(8,128)(2,1)S(1)} %collective-permute-done.1.refs_0_.refs_4_), channel_id=1, source_target_pairs={{0,1},{1,2},{2,3},{3,0},{4,5},{5,6},{6,7},{7,4},{8,9},{9,10},{10,1... | collective-permute-start | bytes 1179656 | tf_op jit(solution)/shard_map/ppermute | solution.py:223
  33.8 16.2 %collective-permute-start.11 = (bf16[48,4096]{1,0:T(8,128)(2,1)S(1)}, bf16[48,4096]{1,0:T(8,128)(2,1)S(1)}, u32[]{:S(2)}, u32[]{:S(2)}) collective-permute-start(bf16[48,4096]{1,0:T(8,128)(2,1)S(1)} %collective-permute-done.4.refs_0_.refs_8_), channel_id=1, source_target_pairs={{0,8},{4,12},{8,0},{12,4},{1,9},{5,13},{9,1},{13,5},{2,10},{6,14},... | collective-permute-start | bytes 1179656 | tf_op jit(solution)/shard_map/ppermute | solution.py:228
  35.5 14.5 %collective-permute-start.10 = (bf16[32,4096]{1,0:T(8,128)(2,1)S(1)}, bf16[32,4096]{1,0:T(8,128)(2,1)S(1)}, u32[]{:S(2)}, u32[]{:S(2)}) collective-permute-start(bf16[32,4096]{1,0:T(8,128)(2,1)S(1)} %slice.175), channel_id=1, source_target_pairs={{0,3},{1,0},{2,1},{3,2},{4,7},{5,4},{6,5},{7,6},{8,11},{9,8},{10,9... | collective-permute-start | bytes 786440 | tf_op jit(solution)/shard_map/ppermute | solution.py:223
  50.0 19.3 %collective-permute-start.21 = (bf16[384,896]{1,0:T(8,128)(2,1)}, bf16[384,896]{1,0:T(8,128)(2,1)S(1)}, u32[]{:S(2)}, u32[]{:S(2)}) collective-permute-start(bf16[384,896]{1,0:T(8,128)(2,1)} %shard_map.93), channel_id=1, source_target_pairs={{0,16},{16,0},{1,17},{17,1},{2,18},{18,2},{3,19},{19,3},{4,20},{20... | collective-permute-start | bytes 2064392 | tf_op jit(solution)/shard_map/ppermute | solution.py:234
  51.2 18.1 %collective-permute-start.15 = (bf16[48,4096]{1,0:T(8,128)(2,1)S(1)}, bf16[48,4096]{1,0:T(8,128)(2,1)S(1)}, u32[]{:S(2)}, u32[]{:S(2)}) collective-permute-start(bf16[48,4096]{1,0:T(8,128)(2,1)S(1)} %constant_dynamic-update-slice_fusion.refs_0_.refs_10_), channel_id=1, source_target_pairs={{0,3},{1,0},{2,1},{3,2},{4,7},{5,4},{6,5},{7,6},{8,11},{9,8},{10,9... | collective-permute-start | bytes 1179656 | tf_op jit(solution)/shard_map/ppermute | solution.py:223
  53.0 16.4 %collective-permute-start.16 = (bf16[48,4096]{1,0:T(8,128)(2,1)S(1)}, bf16[48,4096]{1,0:T(8,128)(2,1)S(1)}, u32[]{:S(2)}, u32[]{:S(2)}) collective-permute-start(bf16[48,4096]{1,0:T(8,128)(2,1)S(1)} %collective-permute-done.9.refs_0_.refs_12_), channel_id=1, source_target_pairs={{0,8},{4,12},{8,0},{12,4},{1,9},{5,13},{9,1},{13,5},{2,10},{6,14},... | collective-permute-start | bytes 1179656 | tf_op jit(solution)/shard_map/ppermute | solution.py:228
  53.8 9.0 %collective-permute-start.20 = (bf16[32,4096]{1,0:T(8,128)(2,1)S(1)}, bf16[32,4096]{1,0:T(8,128)(2,1)S(1)}, u32[]{:S(2)}, u32[]{:S(2)}) collective-permute-start(bf16[32,4096]{1,0:T(8,128)(2,1)S(1)} %collective-permute-done.12.refs_2_), channel_id=1, source_target_pairs={{0,4},{4,0},{8,12},{12,8},{1,5},{5,1},{9,13},{13,9},{2,6},{6,2},{1... | collective-permute-start | bytes 786440 | tf_op jit(solution)/shard_map/ppermute | solution.py:228
  53.9 15.5 %collective-permute-start.17 = (bf16[32,4096]{1,0:T(8,128)(2,1)S(1)}, bf16[32,4096]{1,0:T(8,128)(2,1)S(1)}, u32[]{:S(2)}, u32[]{:S(2)}) collective-permute-start(bf16[32,4096]{1,0:T(8,128)(2,1)S(1)} %collective-permute-done.10), channel_id=1, source_target_pairs={{0,8},{4,12},{8,0},{12,4},{1,9},{5,13},{9,1},{13,5},{2,10},{6,14},... | collective-permute-start | bytes 786440 | tf_op jit(solution)/shard_map/ppermute | solution.py:228
  69.4 7.2 %collective-permute-start.25 = (bf16[48,4096]{1,0:T(8,128)(2,1)S(1)}, bf16[48,4096]{1,0:T(8,128)(2,1)S(1)}, u32[]{:S(2)}, u32[]{:S(2)}) collective-permute-start(bf16[48,4096]{1,0:T(8,128)(2,1)S(1)} %collective-permute-done.9.refs_0_.refs_12_), channel_id=1, source_target_pairs={{0,4},{4,0},{8,12},{12,8},{1,5},{5,1},{9,13},{13,9},{2,6},{6,2},{1... | collective-permute-start | bytes 1179656 | tf_op jit(solution)/shard_map/ppermute | solution.py:228
  69.5 18.7 %collective-permute-start.29 = (bf16[384,896]{1,0:T(8,128)(2,1)}, bf16[384,896]{1,0:T(8,128)(2,1)S(1)}, u32[]{:S(2)}, u32[]{:S(2)}) collective-permute-start(bf16[384,896]{1,0:T(8,128)(2,1)} %shard_map.94), channel_id=1, source_target_pairs={{0,16},{16,0},{1,17},{17,1},{2,18},{18,2},{3,19},{19,3},{4,20},{20... | collective-permute-start | bytes 2064392 | tf_op jit(solution)/shard_map/ppermute | solution.py:234
  71.0 5.6 %collective-permute-start.24 = (bf16[16,4096]{1,0:T(8,128)(2,1)S(1)}, bf16[16,4096]{1,0:T(8,128)(2,1)S(1)}, u32[]{:S(2)}, u32[]{:S(2)}) collective-permute-start(bf16[16,4096]{1,0:T(8,128)(2,1)S(1)} %collective-permute-done.5), channel_id=1, source_target_pairs={{0,8},{4,12},{8,0},{12,4},{1,9},{5,13},{9,1},{13,5},{2,10},{6,14},... | collective-permute-start | bytes 393224 | tf_op jit(solution)/shard_map/ppermute | solution.py:228
  71.5 6.7 %collective-permute-start.26 = (bf16[48,4096]{1,0:T(8,128)(2,1)S(1)}, bf16[48,4096]{1,0:T(8,128)(2,1)S(1)}, u32[]{:S(2)}, u32[]{:S(2)}) collective-permute-start(bf16[48,4096]{1,0:T(8,128)(2,1)S(1)} %collective-permute-done.16.refs_1_.refs_13_), channel_id=1, source_target_pairs={{0,4},{4,0},{8,12},{12,8},{1,5},{5,1},{9,13},{13,9},{2,6},{6,2},{1... | collective-permute-start | bytes 1179656 | tf_op jit(solution)/shard_map/ppermute | solution.py:228
  72.6 14.1 %collective-permute-start.22 = (bf16[48,4096]{1,0:T(8,128)(2,1)S(1)}, bf16[48,4096]{1,0:T(8,128)(2,1)S(1)}, u32[]{:S(2)}, u32[]{:S(2)}) collective-permute-start(bf16[48,4096]{1,0:T(8,128)(2,1)S(1)} %copy-done.4), channel_id=1, source_target_pairs={{0,1},{1,2},{2,3},{3,0},{4,5},{5,6},{6,7},{7,4},{8,9},{9,10},{10,1... | collective-permute-start | bytes 1179656 | tf_op jit(solution)/shard_map/ppermute | solution.py:223
  76.6 10.1 %collective-permute-start.27 = (bf16[48,4096]{1,0:T(8,128)(2,1)S(1)}, bf16[48,4096]{1,0:T(8,128)(2,1)S(1)}, u32[]{:S(2)}, u32[]{:S(2)}) collective-permute-start(bf16[48,4096]{1,0:T(8,128)(2,1)S(1)} %constant_dynamic-update-slice_fusion.refs_0_.refs_10_), channel_id=1, source_target_pairs={{0,4},{4,0},{8,12},{12,8},{1,5},{5,1},{9,13},{13,9},{2,6},{6,2},{1... | collective-permute-start | bytes 1179656 | tf_op jit(solution)/shard_map/ppermute | solution.py:228
  76.6 11.5 %collective-permute-start.23 = (bf16[48,4096]{1,0:T(8,128)(2,1)S(1)}, bf16[48,4096]{1,0:T(8,128)(2,1)S(1)}, u32[]{:S(2)}, u32[]{:S(2)}) collective-permute-start(bf16[48,4096]{1,0:T(8,128)(2,1)S(1)} %collective-permute-done.15.refs_6_.refs_16_), channel_id=1, source_target_pairs={{0,8},{4,12},{8,0},{12,4},{1,9},{5,13},{9,1},{13,5},{2,10},{6,14},... | collective-permute-start | bytes 1179656 | tf_op jit(solution)/shard_map/ppermute | solution.py:228
  78.2 8.4 %collective-permute-start.28 = (bf16[32,4096]{1,0:T(8,128)(2,1)S(1)}, bf16[32,4096]{1,0:T(8,128)(2,1)S(1)}, u32[]{:S(2)}, u32[]{:S(2)}) collective-permute-start(bf16[32,4096]{1,0:T(8,128)(2,1)S(1)} %collective-permute-done.17.refs_2_.refs_12_), channel_id=1, source_target_pairs={{0,4},{4,0},{8,12},{12,8},{1,5},{5,1},{9,13},{13,9},{2,6},{6,2},{1... | collective-permute-start | bytes 786440 | tf_op jit(solution)/shard_map/ppermute | solution.py:228
  88.7 17.6 %collective-permute-start.35 = (bf16[384,896]{1,0:T(8,128)(2,1)}, bf16[384,896]{1,0:T(8,128)(2,1)S(1)}, u32[]{:S(2)}, u32[]{:S(2)}) collective-permute-start(bf16[384,896]{1,0:T(8,128)(2,1)} %shard_map.95), channel_id=1, source_target_pairs={{0,16},{16,0},{1,17},{17,1},{2,18},{18,2},{3,19},{19,3},{4,20},{20... | collective-permute-start | bytes 2064392 | tf_op jit(solution)/shard_map/ppermute | solution.py:234
  89.5 14.7 %collective-permute-start.31 = (bf16[16,4096]{1,0:T(8,128)(2,1)}, bf16[16,4096]{1,0:T(8,128)(2,1)S(1)}, u32[]{:S(2)}, u32[]{:S(2)}) collective-permute-start(bf16[16,4096]{1,0:T(8,128)(2,1)} %copy-done.60), channel_id=1, source_target_pairs={{0,8},{4,12},{8,0},{12,4},{1,9},{5,13},{9,1},{13,5},{2,10},{6,14},... | collective-permute-start | bytes 393224 | tf_op jit(solution)/shard_map/ppermute | solution.py:228
  90.9 13.3 %collective-permute-start.30 = (bf16[48,4096]{1,0:T(8,128)(2,1)S(1)}, bf16[48,4096]{1,0:T(8,128)(2,1)S(1)}, u32[]{:S(2)}, u32[]{:S(2)}) collective-permute-start(bf16[48,4096]{1,0:T(8,128)(2,1)S(1)} %collective-permute-done.22.refs_6_), channel_id=1, source_target_pairs={{0,8},{4,12},{8,0},{12,4},{1,9},{5,13},{9,1},{13,5},{2,10},{6,14},... | collective-permute-start | bytes 1179656 | tf_op jit(solution)/shard_map/ppermute | solution.py:228
  107.8 18.0 %collective-permute-start.42 = (bf16[384,896]{1,0:T(8,128)(2,1)S(1)}, bf16[384,896]{1,0:T(8,128)(2,1)}, u32[]{:S(2)}, u32[]{:S(2)}) collective-permute-start(bf16[384,896]{1,0:T(8,128)(2,1)S(1)} %copy-done.16), channel_id=1, source_target_pairs={{0,16},{16,0},{1,17},{17,1},{2,18},{18,2},{3,19},{19,3},{4,20},{20... | collective-permute-start | bytes 2064392 | tf_op jit(solution)/shard_map/ppermute | solution.py:234
  109.1 3.9 %collective-permute-start.41 = (bf16[48,4096]{1,0:T(8,128)(2,1)S(1)}, bf16[48,4096]{1,0:T(8,128)(2,1)}, u32[]{:S(2)}, u32[]{:S(2)}) collective-permute-start(bf16[48,4096]{1,0:T(8,128)(2,1)S(1)} %copy-done.45), channel_id=1, source_target_pairs={{0,4},{4,0},{8,12},{12,8},{1,5},{5,1},{9,13},{13,9},{2,6},{6,2},{1... | collective-permute-start | bytes 1179656 | tf_op jit(solution)/shard_map/ppermute | solution.py:228
  110.3 15.5 %collective-permute-start.38 = (bf16[96,4096]{1,0:T(8,128)(2,1)}, bf16[96,4096]{1,0:T(8,128)(2,1)S(1)}, u32[]{:S(2)}, u32[]{:S(2)}) collective-permute-start(bf16[96,4096]{1,0:T(8,128)(2,1)} %get-tuple-element.171), channel_id=1, source_target_pairs={{0,4},{4,0},{8,12},{12,8},{1,5},{5,1},{9,13},{13,9},{2,6},{6,2},{1... | collective-permute-start | bytes 2359304 | tf_op jit(solution)/shard_map/ppermute | solution.py:228
  111.6 14.1 %collective-permute-start.37 = (bf16[48,4096]{1,0:T(8,128)(2,1)}, bf16[48,4096]{1,0:T(8,128)(2,1)S(1)}, u32[]{:S(2)}, u32[]{:S(2)}) collective-permute-start(bf16[48,4096]{1,0:T(8,128)(2,1)} %get-tuple-element.256), channel_id=1, source_target_pairs={{0,8},{4,12},{8,0},{12,4},{1,9},{5,13},{9,1},{13,5},{2,10},{6,14},... | collective-permute-start | bytes 1179656 | tf_op jit(solution)/shard_map/ppermute | solution.py:228
  125.9 18.2 %collective-permute-start.46 = (bf16[384,896]{1,0:T(8,128)(2,1)}, bf16[384,896]{1,0:T(8,128)(2,1)}, u32[]{:S(2)}, u32[]{:S(2)}) collective-permute-start(bf16[384,896]{1,0:T(8,128)(2,1)} %get-tuple-element.196), channel_id=1, source_target_pairs={{0,16},{16,0},{1,17},{17,1},{2,18},{18,2},{3,19},{19,3},{4,20},{20... | collective-permute-start | bytes 2064392 | tf_op jit(solution)/shard_map/ppermute | solution.py:234
  128.6 19.6 %collective-permute-start.44 = (bf16[96,4096]{1,0:T(8,128)(2,1)S(1)}, bf16[96,4096]{1,0:T(8,128)(2,1)S(1)}, u32[]{:S(2)}, u32[]{:S(2)}) collective-permute-start(bf16[96,4096]{1,0:T(8,128)(2,1)S(1)} %pad_maximum_fusion), channel_id=1, source_target_pairs={{0,8},{4,12},{8,0},{12,4},{1,9},{5,13},{9,1},{13,5},{2,10},{6,14},... | collective-permute-start | bytes 2359304 | tf_op jit(solution)/shard_map/ppermute | solution.py:228
  129.3 19.0 %collective-permute-start.45 = (bf16[96,4096]{1,0:T(8,128)(2,1)}, bf16[96,4096]{1,0:T(8,128)(2,1)S(1)}, u32[]{:S(2)}, u32[]{:S(2)}) collective-permute-start(bf16[96,4096]{1,0:T(8,128)(2,1)} %get-tuple-element.190), channel_id=1, source_target_pairs={{0,4},{4,0},{8,12},{12,8},{1,5},{5,1},{9,13},{13,9},{2,6},{6,2},{1... | collective-permute-start | bytes 2359304 | tf_op jit(solution)/shard_map/ppermute | solution.py:228
  148.3 4.3 %collective-permute-start.47 = (bf16[96,4096]{1,0:T(8,128)(2,1)}, bf16[96,4096]{1,0:T(8,128)(2,1)S(1)}, u32[]{:S(2)}, u32[]{:S(2)}) collective-permute-start(bf16[96,4096]{1,0:T(8,128)(2,1)} %get-tuple-element.198), channel_id=1, source_target_pairs={{0,4},{4,0},{8,12},{12,8},{1,5},{5,1},{9,13},{13,9},{2,6},{6,2},{1... | collective-permute-start | bytes 2359304 | tf_op jit(solution)/shard_map/ppermute | solution.py:228
  149.3 20.2 %collective-permute-start.51 = (bf16[48,4096]{1,0:T(8,128)(2,1)}, bf16[48,4096]{1,0:T(8,128)(2,1)S(1)}, u32[]{:S(2)}, u32[]{:S(2)}) collective-permute-start(bf16[48,4096]{1,0:T(8,128)(2,1)} %get-tuple-element.245), channel_id=1, source_target_pairs={{0,3},{1,0},{2,1},{3,2},{4,7},{5,4},{6,5},{7,6},{8,11},{9,8},{10,9... | collective-permute-start | bytes 1179656 | tf_op jit(solution)/shard_map/ppermute | solution.py:223
  149.7 19.8 %collective-permute-start.50 = (bf16[48,4096]{1,0:T(8,128)(2,1)S(1)}, bf16[48,4096]{1,0:T(8,128)(2,1)S(1)}, u32[]{:S(2)}, u32[]{:S(2)}) collective-permute-start(bf16[48,4096]{1,0:T(8,128)(2,1)S(1)} %get-tuple-element.246), channel_id=1, source_target_pairs={{0,1},{1,2},{2,3},{3,0},{4,5},{5,6},{6,7},{7,4},{8,9},{9,10},{10,1... | collective-permute-start | bytes 1179656 | tf_op jit(solution)/shard_map/ppermute | solution.py:223
  152.9 19.4 %collective-permute-start.48 = (bf16[96,4096]{1,0:T(8,128)(2,1)S(1)}, bf16[96,4096]{1,0:T(8,128)(2,1)S(1)}, u32[]{:S(2)}, u32[]{:S(2)}) collective-permute-start(bf16[96,4096]{1,0:T(8,128)(2,1)S(1)} %pad_maximum_fusion.1), channel_id=1, source_target_pairs={{0,8},{4,12},{8,0},{12,4},{1,9},{5,13},{9,1},{13,5},{2,10},{6,14},... | collective-permute-start | bytes 2359304 | tf_op jit(solution)/shard_map/ppermute | solution.py:228
  154.0 18.4 %collective-permute-start.49 = (bf16[96,4096]{1,0:T(8,128)(2,1)S(1)}, bf16[96,4096]{1,0:T(8,128)(2,1)S(1)}, u32[]{:S(2)}, u32[]{:S(2)}) collective-permute-start(bf16[96,4096]{1,0:T(8,128)(2,1)S(1)} %copy-done.61), channel_id=1, source_target_pairs={{0,4},{4,0},{8,12},{12,8},{1,5},{5,1},{9,13},{13,9},{2,6},{6,2},{1... | collective-permute-start | bytes 2359304 | tf_op jit(solution)/shard_map/ppermute | solution.py:228
  172.4 4.3 %collective-permute-start.52 = (bf16[96,4096]{1,0:T(8,128)(2,1)}, bf16[96,4096]{1,0:T(8,128)(2,1)S(1)}, u32[]{:S(2)}, u32[]{:S(2)}) collective-permute-start(bf16[96,4096]{1,0:T(8,128)(2,1)} %get-tuple-element.210), channel_id=1, source_target_pairs={{0,4},{4,0},{8,12},{12,8},{1,5},{5,1},{9,13},{13,9},{2,6},{6,2},{1... | collective-permute-start | bytes 2359304 | tf_op jit(solution)/shard_map/ppermute | solution.py:228
  172.7 16.8 %collective-permute-start.56 = (bf16[48,4096]{1,0:T(8,128)(2,1)S(1)}, bf16[48,4096]{1,0:T(8,128)(2,1)S(1)}, u32[]{:S(2)}, u32[]{:S(2)}) collective-permute-start(bf16[48,4096]{1,0:T(8,128)(2,1)S(1)} %get-tuple-element.243), channel_id=1, source_target_pairs={{0,1},{1,2},{2,3},{3,0},{4,5},{5,6},{6,7},{7,4},{8,9},{9,10},{10,1... | collective-permute-start | bytes 1179656 | tf_op jit(solution)/shard_map/ppermute | solution.py:223
  173.2 19.7 %collective-permute-start.55 = (bf16[48,4096]{1,0:T(8,128)(2,1)S(1)}, bf16[48,4096]{1,0:T(8,128)(2,1)S(1)}, u32[]{:S(2)}, u32[]{:S(2)}) collective-permute-start(bf16[48,4096]{1,0:T(8,128)(2,1)S(1)} %get-tuple-element.244), channel_id=1, source_target_pairs={{0,3},{1,0},{2,1},{3,2},{4,7},{5,4},{6,5},{7,6},{8,11},{9,8},{10,9... | collective-permute-start | bytes 1179656 | tf_op jit(solution)/shard_map/ppermute | solution.py:223
  176.8 16.0 %collective-permute-start.54 = (bf16[96,4096]{1,0:T(8,128)(2,1)}, bf16[96,4096]{1,0:T(8,128)(2,1)S(1)}, u32[]{:S(2)}, u32[]{:S(2)}) collective-permute-start(bf16[96,4096]{1,0:T(8,128)(2,1)} %get-tuple-element.212), channel_id=1, source_target_pairs={{0,4},{4,0},{8,12},{12,8},{1,5},{5,1},{9,13},{13,9},{2,6},{6,2},{1... | collective-permute-start | bytes 2359304 | tf_op jit(solution)/shard_map/ppermute | solution.py:228
  177.2 15.7 %collective-permute-start.53 = (bf16[48,4096]{1,0:T(8,128)(2,1)S(1)}, bf16[48,4096]{1,0:T(8,128)(2,1)S(1)}, u32[]{:S(2)}, u32[]{:S(2)}) collective-permute-start(bf16[48,4096]{1,0:T(8,128)(2,1)S(1)} %get-tuple-element.250), channel_id=1, source_target_pairs={{0,8},{4,12},{8,0},{12,4},{1,9},{5,13},{9,1},{13,5},{2,10},{6,14},... | collective-permute-start | bytes 1179656 | tf_op jit(solution)/shard_map/ppermute | solution.py:228
  193.1 21.0 %collective-permute-start.58 = (bf16[96,4096]{1,0:T(8,128)(2,1)S(1)}, bf16[96,4096]{1,0:T(8,128)(2,1)S(1)}, u32[]{:S(2)}, u32[]{:S(2)}) collective-permute-start(bf16[96,4096]{1,0:T(8,128)(2,1)S(1)} %pad_maximum_fusion.3), channel_id=1, source_target_pairs={{0,3},{1,0},{2,1},{3,2},{4,7},{5,4},{6,5},{7,6},{8,11},{9,8},{10,9... | collective-permute-start | bytes 2359304 | tf_op jit(solution)/shard_map/ppermute | solution.py:223
  195.3 18.9 %collective-permute-start.57 = (bf16[96,4096]{1,0:T(8,128)(2,1)S(1)}, bf16[96,4096]{1,0:T(8,128)(2,1)S(1)}, u32[]{:S(2)}, u32[]{:S(2)}) collective-permute-start(bf16[96,4096]{1,0:T(8,128)(2,1)S(1)} %pad_maximum_fusion.2), channel_id=1, source_target_pairs={{0,8},{4,12},{8,0},{12,4},{1,9},{5,13},{9,1},{13,5},{2,10},{6,14},... | collective-permute-start | bytes 2359304 | tf_op jit(solution)/shard_map/ppermute | solution.py:228
  (73 other events, 496.5 us)
